TPU v7x, 32 devices: a whole 2x2x4 slice. The times are simulated.
32 devices in a mesh: dp: 8 (over z, x), own: 4 (over y, core).
Axes of the slice: x: 2, y: 2, z: 4, core: 2. Of those that a mesh axis runs over, the one named last changes fastest.
Arguments:
- frames: bfloat16 [8192, 21, 21, 64], P(('dp', 'own')), may hold values from -6 to 6
- actions: int32 [32, 256], P(('dp', 'own')), may hold values from 0 to 17
- dones: int32 [32, 256], P(('dp', 'own')), may hold values 0 or 1
- lengths: int32 [32], P(('dp', 'own')), may hold values from 32 to 256, as said below
- rewards: float32 [32, 256], P(('dp', 'own')), may hold values from -6 to 6
- old_values: float32 [32, 256], P(('dp', 'own')), may hold values from -6 to 6
- old_logp: float32 [32, 256], P(('dp', 'own')), may hold values from -3.6 to -2.2
- conv_first: float32 [256, 32], replicated, may hold values from -0.375 to 0.375
- conv_second: float32 [512, 64], replicated, may hold values from -0.25 to 0.25
- conv_third: float32 [576, 64], replicated, may hold values from -0.25 to 0.25
- dense_hidden: float32 [3136, 512], P('dp', 'own'), may hold values from -0.109375 to 0.109375
- dense_heads: float32 [512, 19], replicated, may hold values from -1 to 1
- bias_all: float32 [691], replicated, may hold values from -1.5 to 1.5
- mean_first: float32 [256, 32], replicated, may hold values from -0.01953125 to 0.01953125
- mean_second: float32 [512, 64], replicated, may hold values from -0.01953125 to 0.01953125
- mean_third: float32 [576, 64], replicated, may hold values from -0.01953125 to 0.01953125
- mean_dense: float32 [3136, 512], P('dp', 'own'), may hold values from -0.015625 to 0.015625
- mean_heads: float32 [512, 19], replicated, may hold values from -0.0390625 to 0.0390625
- mean_bias: float32 [691], replicated, may hold values from -0.02734375 to 0.02734375
- square_first: float32 [256, 32], replicated, may hold values from 1.0986329e-05 to 4.3945314e-05
- square_second: float32 [512, 64], replicated, may hold values from 1.0986329e-05 to 4.3945314e-05
- square_third: float32 [576, 64], replicated, may hold values from 1.0986329e-05 to 4.3945314e-05
- square_dense: float32 [3136, 512], P('dp', 'own'), may hold values from 7.6293945e-06 to 3.0517578e-05
- square_heads: float32 [512, 19], replicated, may hold values from 4.3945314e-05 to 0.00017578126
- square_bias: float32 [691], replicated, may hold values from 1.953125e-05 to 7.8125e-05
- left_first: float32 [256, 256], replicated, may hold values from -1 to 1, as said below
- right_first: float32 [32, 32], replicated, may hold values from -1 to 1, as said below
- left_second: float32 [512, 512], replicated, may hold values from -1 to 1, as said below
- right_second: float32 [64, 64], replicated, may hold values from -1 to 1, as said below
- left_third: float32 [576, 576], replicated, may hold values from -1 to 1, as said below
- right_third: float32 [64, 64], replicated, may hold values from -1 to 1, as said below
- right_dense: float32 [4, 128, 128], P('own'), may hold values from -1 to 1, as said below
- left_heads: float32 [512, 512], replicated, may hold values from -1 to 1, as said below
- right_heads: float32 [19, 19], replicated, may hold values from -1 to 1, as said below
Outputs:
- frames_grad: bfloat16 [8192, 21, 21, 64], P(('dp', 'own'))
- grad_first: float32 [256, 32], replicated
- grad_second: float32 [512, 64], replicated
- grad_third: float32 [576, 64], replicated
- grad_dense: float32 [3136, 512], P('dp', 'own')
- grad_heads: float32 [512, 19], replicated
- grad_bias: float32 [691], replicated
- momentum_first: float32 [256, 32], replicated
- momentum_second: float32 [512, 64], replicated
- momentum_third: float32 [576, 64], replicated
- momentum_dense: float32 [3136, 512], P('dp', 'own')
- momentum_heads: float32 [512, 19], replicated
- momentum_bias: float32 [691], replicated
- variance_first: float32 [256, 32], replicated
- variance_second: float32 [512, 64], replicated
- variance_third: float32 [576, 64], replicated
- variance_dense: float32 [3136, 512], P('dp', 'own')
- variance_heads: float32 [512, 19], replicated
- variance_bias: float32 [691], replicated
- updated_first: float32 [256, 32], replicated
- updated_second: float32 [512, 64], replicated
- updated_third: float32 [576, 64], replicated
- updated_dense: float32 [3136, 512], P('dp', 'own')
- updated_heads: float32 [512, 19], replicated
- updated_bias: float32 [691], replicated
Inputs may be any that keep to these rules, and one draw needn't show every extreme that they name: `lengths`: the last trajectory has all 256 steps valid. `left_first`: an orthogonal matrix. `right_first`: an orthogonal matrix. `left_second`: an orthogonal matrix. `right_second`: an orthogonal matrix. `left_third`: an orthogonal matrix. `right_third`: an orthogonal matrix. `right_dense`: each block is an orthogonal matrix. `left_heads`: an orthogonal matrix. `right_heads`: an orthogonal matrix.
All inputs are finite; a program needn't handle non-finite values. No bound on the sum of `dones` on one device may be relied on, other than what follows from the above.
Results may differ from a plain program's by a relative error of at most 0.013.
The roundings to bfloat16 on the way count: a program that leaves them out, or rounds other values in their place, can miss the bound.
Values may be sent and summed in bfloat16 or wider, within the bound.
No kernel may reach another device: no remote copies, remote signals or barrier semaphores. Data moves between devices by JAX's collectives and lax.ppermute only.
A program may use at most 384 MiB of HBM per device.

v0:
```python
import math

import jax
import jax.numpy as jnp
from jax import lax
from jax.sharding import PartitionSpec as P

HID = 512
STEP = 10
FLAT = 3136
K1 = 256
K2 = 512
K3 = 576


GAMMA = 0.99
LAMBDA = 0.95
CLIP = 0.1
ENTROPY_COEF = 0.01
VALUE_COEF = 0.5
BETA = 0.5
EPSILON = 1e-08
RATE = 1.0
BIAS_RATE = 0.1
HIGH = lax.Precision.HIGHEST


def advantage_terms(lengths, dones, rewards, old_values):
    count_traj, steps = rewards.shape
    position = lax.broadcasted_iota(jnp.int32, rewards.shape, 1)
    mask = (position < lengths[:, None]).astype(jnp.float32)
    next_live = (position + 1 < lengths[:, None]).astype(jnp.float32)
    shifted = jnp.concatenate([old_values[:, 1:], jnp.zeros((count_traj, 1), jnp.float32)], axis=1)
    going = 1.0 - dones.astype(jnp.float32)
    delta = rewards + GAMMA * going * shifted * next_live - old_values
    width = math.gcd(steps, 16)
    blocks = steps // width
    source = (mask * delta).reshape(count_traj, blocks, width)
    passing = ((1 - dones) * (position < lengths[:, None]).astype(jnp.int32)).reshape(
        count_traj, blocks, width
    )
    breaks = 1 - passing
    before = jnp.cumsum(breaks, axis=-1) - breaks
    after_all = jnp.sum(breaks, axis=-1, keepdims=True)
    here = lax.broadcasted_iota(jnp.int32, (width, width), 0)
    later = lax.broadcasted_iota(jnp.int32, (width, width), 1)
    factor = GAMMA * LAMBDA
    powers = jnp.where(
        later >= here, jnp.power(jnp.float32(factor), (later - here).astype(jnp.float32)), 0.0
    )
    joined = (before[..., :, None] == before[..., None, :]).astype(jnp.float32)
    weights = joined * powers
    local = jnp.einsum("jkts,jks->jkt", weights, source, precision=HIGH)
    spots = lax.broadcasted_iota(jnp.int32, (width,), 0)
    tail_power = jnp.power(jnp.float32(factor), (width - spots).astype(jnp.float32))
    tail = (before == after_all).astype(jnp.float32) * tail_power

    def block_step(carry, item):
        first_local, first_tail = item
        return (first_local + first_tail * carry, carry)

    _, incoming = lax.scan(
        block_step,
        jnp.zeros((count_traj,), jnp.float32),
        (local[:, :, 0].T, tail[:, :, 0].T),
        reverse=True,
    )
    advantage = (local + tail * incoming.T[:, :, None]).reshape(count_traj, steps)
    return (mask, advantage, advantage + old_values)


def policy_loss(heads, actions, norm_adv, returns, mask, old_logp, count):
    acts = heads.shape[1] - 1
    logits = heads[:, :acts]
    value = heads[:, acts]
    logp_all = jax.nn.log_softmax(logits, axis=-1)
    choose = (lax.broadcasted_iota(jnp.int32, logits.shape, 1) == actions[:, None]).astype(
        jnp.float32
    )
    logp = jnp.sum(logp_all * choose, axis=-1)
    entropy = -jnp.sum(jnp.exp(logp_all) * logp_all, axis=-1)
    ratio = jnp.exp(logp - old_logp)
    soft = 1.0 + CLIP * jnp.tanh((ratio - 1.0) / CLIP)
    policy = -jnp.minimum(ratio * norm_adv, soft * norm_adv)
    each = policy + VALUE_COEF * 0.5 * (value - returns) ** 2 - ENTROPY_COEF * entropy
    return jnp.sum(mask * each) / count


def cell_patches(inputs, kernel, out):
    return jnp.concatenate(
        [inputs[:, i : i + out, j : j + out, :] for i in range(kernel) for j in range(kernel)],
        axis=-1,
    )


def fold_cells(inputs):
    count_rows, height, width, chans = inputs.shape
    shaped = inputs.reshape(count_rows, height // 2, 2, width // 2, 2, chans).transpose(
        0, 1, 3, 2, 4, 5
    )
    return shaped.reshape(count_rows, height // 2, width // 2, 4 * chans)


def unfold_cells(inputs):
    count_rows, height, width, merged = inputs.shape
    chans = merged // 4
    shaped = inputs.reshape(count_rows, height, width, 2, 2, chans).transpose(0, 1, 3, 2, 4, 5)
    return shaped.reshape(count_rows, 2 * height, 2 * width, chans)


def patches_back(spread, kernel, size):
    out = spread.shape[1]
    chans = spread.shape[-1] // (kernel * kernel)
    total = jnp.zeros((spread.shape[0], size, size, chans), jnp.float32)
    for index in range(kernel * kernel):
        row_off = index // kernel
        col_off = index % kernel
        piece = spread[..., index * chans : (index + 1) * chans]
        total = total + jnp.pad(
            piece,
            ((0, 0), (row_off, size - out - row_off), (col_off, size - out - col_off), (0, 0)),
        )
    return total


def apply_weight(inputs, weight):
    shape = inputs.shape
    out = jnp.dot(inputs.reshape(-1, shape[-1]), weight, preferred_element_type=jnp.float32)
    return out.reshape(shape[:-1] + (weight.shape[1],))


def weight_grad(inputs, upstream):
    left_rows = inputs.reshape(-1, inputs.shape[-1])
    right_rows = upstream.reshape(-1, upstream.shape[-1])
    return lax.dot_general(
        left_rows, right_rows, (((0,), (0,)), ((), ())), preferred_element_type=jnp.float32
    )


def input_grad(upstream, weight):
    shape = upstream.shape
    rows = upstream.reshape(-1, shape[-1])
    out = lax.dot_general(
        rows, weight, (((1,), (1,)), ((), ())), preferred_element_type=jnp.float32
    )
    return out.reshape(shape[:-1] + (weight.shape[0],))


def gelu_grad(pre, upstream):
    _, back = jax.vjp(jax.nn.gelu, pre)
    return back(upstream)[0]


def column_sum(values):
    return jnp.sum(values.astype(jnp.float32).reshape(-1, values.shape[-1]), axis=0)


def adam_terms(grad, mean, square):
    momentum = BETA * mean + (1.0 - BETA) * grad
    variance = BETA * square + (1.0 - BETA) * grad * grad
    fix = 1.0 - BETA**STEP
    direction = momentum / fix / (jnp.sqrt(variance / fix) + EPSILON)
    return (momentum, variance, direction)


def rotated_step(weight, grad, mean, square, left, right, rate):
    turned = jnp.dot(
        lax.dot_general(left, grad, (((0,), (0,)), ((), ())), precision=HIGH), right, precision=HIGH
    )
    momentum, variance, direction = adam_terms(turned, mean, square)
    back = lax.dot_general(
        jnp.dot(left, direction, precision=HIGH), right, (((1,), (1,)), ((), ())), precision=HIGH
    )
    return (momentum, variance, weight - rate * back)


def dense_step(weight, grad, mean, square, blocks, rate):
    split = grad.reshape(grad.shape[0], blocks.shape[0], blocks.shape[1])
    turned = jnp.einsum("rbk,bkl->rbl", split, blocks, precision=HIGH).reshape(grad.shape)
    momentum, variance, direction = adam_terms(turned, mean, square)
    back = jnp.einsum(
        "rbl,bkl->rbk", direction.reshape(split.shape), blocks, precision=HIGH
    ).reshape(grad.shape)
    return (momentum, variance, weight - rate * back)


def shards(
    frames,
    actions,
    dones,
    lengths,
    rewards,
    old_values,
    old_logp,
    conv_first,
    conv_second,
    conv_third,
    dense_hidden,
    dense_heads,
    bias_all,
    mean_first,
    mean_second,
    mean_third,
    mean_dense,
    mean_heads,
    mean_bias,
    square_first,
    square_second,
    square_third,
    square_dense,
    square_heads,
    square_bias,
    left_first,
    right_first,
    left_second,
    right_second,
    left_third,
    right_third,
    right_dense,
    left_heads,
    right_heads,
):
    mask, advantage, returns = advantage_terms(lengths, dones, rewards, old_values)
    count_here = jnp.sum(mask)
    total_here = jnp.sum(mask * advantage)
    count, total = lax.psum((count_here, total_here), ("dp", "own"))
    centre = total / count
    spread = lax.psum(jnp.sum(mask * (advantage - centre) ** 2), ("dp", "own"))
    var = spread / count
    norm_adv = (advantage - centre) * lax.rsqrt(var + 1e-05)
    c_one = conv_first.shape[1]
    c_two = conv_second.shape[1]
    hid = dense_heads.shape[0]
    bias_one = bias_all[:c_one]
    bias_two = bias_all[c_one : c_one + c_two]
    bias_three = bias_all[c_one + c_two : c_one + 2 * c_two]
    bias_dense = bias_all[c_one + 2 * c_two : c_one + 2 * c_two + hid]
    bias_heads = bias_all[c_one + 2 * c_two + hid :]
    weight_first = conv_first.astype(jnp.bfloat16)
    weight_second = conv_second.astype(jnp.bfloat16)
    weight_third = conv_third.astype(jnp.bfloat16)
    weight_heads = dense_heads.astype(jnp.bfloat16)
    tokens = frames.shape[0]
    grid = frames.shape[1]
    patches_one = cell_patches(frames, 2, grid - 1)
    pre_one = apply_weight(patches_one, weight_first) + bias_one
    act_one = jax.nn.gelu(pre_one).astype(jnp.bfloat16)
    folded = fold_cells(act_one)
    patches_two = cell_patches(folded, 2, folded.shape[1] - 1)
    pre_two = apply_weight(patches_two, weight_second) + bias_two
    act_two = jax.nn.gelu(pre_two).astype(jnp.bfloat16)
    patches_three = cell_patches(act_two, 3, act_two.shape[1] - 2)
    pre_three = apply_weight(patches_three, weight_third) + bias_three
    act_three = jax.nn.gelu(pre_three).astype(jnp.bfloat16)
    flat = act_three.reshape(tokens, -1)
    columns = lax.all_gather(dense_hidden.astype(jnp.bfloat16), "own", axis=1, tiled=True)
    dense_full = lax.all_gather(columns, "dp", axis=0, tiled=True)
    pre_dense = jnp.dot(flat, dense_full, preferred_element_type=jnp.float32)
    pre_dense = pre_dense + bias_dense
    hidden = jax.nn.gelu(pre_dense).astype(jnp.bfloat16)
    heads = jnp.dot(hidden, weight_heads, preferred_element_type=jnp.float32) + bias_heads

    def total_loss(values):
        return policy_loss(
            values,
            actions.reshape(-1),
            norm_adv.reshape(-1),
            returns.reshape(-1),
            mask.reshape(-1),
            old_logp.reshape(-1),
            count,
        )

    _, loss_back = jax.vjp(total_loss, heads)
    d_heads = loss_back(jnp.float32(1.0))[0].astype(jnp.bfloat16)
    heads_here = weight_grad(hidden, d_heads)
    d_hidden = input_grad(d_heads, weight_heads)
    d_dense = gelu_grad(pre_dense, d_hidden).astype(jnp.bfloat16)
    d_flat = input_grad(d_dense, dense_full)
    row_sums = lax.psum_scatter(
        lax.dot_general(
            flat, d_dense, (((0,), (0,)), ((), ())), preferred_element_type=jnp.float32
        ),
        "dp",
        scatter_dimension=0,
        tiled=True,
    )
    grad_dense = lax.psum_scatter(row_sums, "own", scatter_dimension=1, tiled=True)
    d_three = gelu_grad(pre_three, d_flat.reshape(pre_three.shape)).astype(jnp.bfloat16)
    third_here = weight_grad(patches_three, d_three)
    d_act_two = patches_back(input_grad(d_three, weight_third), 3, act_two.shape[1])
    d_two = gelu_grad(pre_two, d_act_two).astype(jnp.bfloat16)
    second_here = weight_grad(patches_two, d_two)
    d_act_one = unfold_cells(patches_back(input_grad(d_two, weight_second), 2, folded.shape[1]))
    d_one = gelu_grad(pre_one, d_act_one).astype(jnp.bfloat16)
    first_here = weight_grad(patches_one, d_one)
    frames_grad = patches_back(input_grad(d_one, weight_first), 2, grid).astype(jnp.bfloat16)
    bias_here = jnp.concatenate(
        [
            column_sum(d_one),
            column_sum(d_two),
            column_sum(d_three),
            column_sum(d_dense),
            column_sum(d_heads),
        ]
    )
    grad_first, grad_second, grad_third, grad_heads, grad_bias = lax.psum(
        (first_here, second_here, third_here, heads_here, bias_here), ("dp", "own")
    )
    mom_one, var_one, new_one = rotated_step(
        conv_first,
        grad_first,
        mean_first,
        square_first,
        left_first,
        right_first,
        RATE / math.sqrt(K1),
    )
    mom_two, var_two, new_two = rotated_step(
        conv_second,
        grad_second,
        mean_second,
        square_second,
        left_second,
        right_second,
        RATE / math.sqrt(K2),
    )
    mom_three, var_three, new_three = rotated_step(
        conv_third,
        grad_third,
        mean_third,
        square_third,
        left_third,
        right_third,
        RATE / math.sqrt(K3),
    )
    mom_dense, var_dense, new_dense = dense_step(
        dense_hidden, grad_dense, mean_dense, square_dense, right_dense, RATE / math.sqrt(FLAT)
    )
    mom_heads, var_heads, new_heads = rotated_step(
        dense_heads,
        grad_heads,
        mean_heads,
        square_heads,
        left_heads,
        right_heads,
        RATE / math.sqrt(HID),
    )
    mom_bias, var_bias, bias_dir = adam_terms(grad_bias, mean_bias, square_bias)
    new_bias = bias_all - BIAS_RATE * bias_dir
    return (
        frames_grad,
        grad_first,
        grad_second,
        grad_third,
        grad_dense,
        grad_heads,
        grad_bias,
        mom_one,
        mom_two,
        mom_three,
        mom_dense,
        mom_heads,
        mom_bias,
        var_one,
        var_two,
        var_three,
        var_dense,
        var_heads,
        var_bias,
        new_one,
        new_two,
        new_three,
        new_dense,
        new_heads,
        new_bias,
    )


def solution(mesh):
    in_specs = (
        P(("dp", "own"), None, None, None),
        P(("dp", "own"), None),
        P(("dp", "own"), None),
        P(("dp", "own")),
        P(("dp", "own"), None),
        P(("dp", "own"), None),
        P(("dp", "own"), None),
        P(),
        P(),
        P(),
        P("dp", "own"),
        P(),
        P(),
        P(),
        P(),
        P(),
        P("dp", "own"),
        P(),
        P(),
        P(),
        P(),
        P(),
        P("dp", "own"),
        P(),
        P(),
        P(),
        P(),
        P(),
        P(),
        P(),
        P(),
        P("own", None, None),
        P(),
        P(),
    )
    out_specs = (
        P(("dp", "own"), None, None, None),
        P(),
        P(),
        P(),
        P("dp", "own"),
        P(),
        P(),
        P(),
        P(),
        P(),
        P("dp", "own"),
        P(),
        P(),
        P(),
        P(),
        P(),
        P("dp", "own"),
        P(),
        P(),
        P(),
        P(),
        P(),
        P("dp", "own"),
        P(),
        P(),
    )
    return jax.shard_map(shards, mesh=mesh, in_specs=in_specs, out_specs=out_specs, check_vma=False)
```

profile of v0, /device:TPU:0, one launch (start us, length us, event | category | flops | bytes accessed | tf_op | source)
XLA Modules:
  0.0 1036.0 jit_solution(1087293904836730523)
XLA Ops:
  27.4 32.2 %while.16 = (s32[]{:T(128)}, f32[1]{0:T(128)}, f32[16,1]{0,1:T(1,128)S(1)}, f32[16,1]{0,1:T(1,128)S(1)}, f32[16,1]{0,1:T(1,128)S(1)}, /*index=5*/s32[]{:T(128)}, s32[]{:T(128)}, s32[]{:T(128)}) while((s32[]{:T(128)}, f32[1]{0:T(128)}, f32[16,1]{0,1:T(1,128)S(1)}, f32[16,1]{0,1:T(1,128)S(1)}, f32[16,1]{0,1:T(1,128)S(1)}, /*index=5*/s32[]{:T(128)}, ...), condition=%wide.region_5.6_spmd, body=%wide.region_4.5_spmd.sunk | while | flops 5 | bytes 153 | solution.py:62
  61.0 40.4 %all-reduce.20 = (f32[]{:T(128)}, f32[]{:T(128)}) all-reduce(f32[]{:T(128)} %get-tuple-element.157, f32[]{:T(128)} %get-tuple-element.211), channel_id=1, replica_groups=mesh['dp'=8,'own'=4] {'dp','own'}, use_global_device_ids=true, to_apply=%region_10.11 | all-reduce | flops 2 | bytes 16 | tf_op jit(solution)/shard_map/psum | solution.py:226
  104.1 40.9 %psum.58 = f32[]{:T(128)} all-reduce(f32[]{:T(128)} %select_reduce_fusion.1), channel_id=1, replica_groups=mesh['dp'=8,'own'=4] {'dp','own'}, use_global_device_ids=true, to_apply=%region_12.13 | all-reduce | flops 1 | bytes 8 | tf_op jit(solution)/shard_map/psum | solution.py:228
  147.0 35.6 %fusion.150 = (bf16[256,20,20,64]{0,3,2,1:T(8,128)(2,1)}, bf16[256,20,20,64]{0,3,2,1:T(8,128)(2,1)}, bf16[256,20,20,64]{0,3,2,1:T(8,128)(2,1)}, bf16[256,20,20,64]{0,3,2,1:T(8,128)(2,1)}) fusion(bf16[256,21,21,64]{0,3,2,1:T(8,128)(2,1)} %param.36), kind=kLoop, calls=%fused_computation.235 | loop fusion | bytes 104857600 | tf_op jit(solution)/shard_map/slice | solution.py:91
  182.6 24.1 %copy.84 = bf16[256,20,20,64]{3,0,2,1:T(8,128)(2,1)} copy(bf16[256,20,20,64]{0,3,2,1:T(8,128)(2,1)} %get-tuple-element.180) | data formatting | bytes 26214400
  206.7 24.1 %copy.86 = bf16[256,20,20,64]{3,0,2,1:T(8,128)(2,1)} copy(bf16[256,20,20,64]{0,3,2,1:T(8,128)(2,1)} %get-tuple-element.181) | data formatting | bytes 26214400
  230.8 24.1 %copy.85 = bf16[256,20,20,64]{3,0,2,1:T(8,128)(2,1)} copy(bf16[256,20,20,64]{0,3,2,1:T(8,128)(2,1)} %get-tuple-element.182) | data formatting | bytes 26214400
  254.9 24.2 %copy.87 = bf16[256,20,20,64]{3,0,2,1:T(8,128)(2,1)} copy(bf16[256,20,20,64]{0,3,2,1:T(8,128)(2,1)} %get-tuple-element.183) | data formatting | bytes 26214400
  279.1 48.4 %multiply_convert_fusion = (bf16[256,20,20,32]{0,3,2,1:T(8,128)(2,1)S(1)}, f32[256,20,20,32]{0,3,2,1:T(8,128)}) fusion(f32[32]{0:T(128)S(1)} %slice.136, f32[256,32]{0,1:T(8,128)S(1)} %copy-done.31, bf16[256,20,20,64]{3,0,2,1:T(8,128)(2,1)} %copy.87, bf16[256,20,20,64]{3,0,2,1:T(8,128)(2,1)} %copy.86, bf16[256,20,20,64]{3,0,2,1:T(8,128)(2,1)} %copy.85, ...), kind=kOutput, calls=%fused_computation.16 | convolution fusion | flops 1920212992 | bytes 72122496 | tf_op jit(solution)/shard_map/dot_general | solution.py:128
  336.4 8.5 copy.88
  344.9 8.5 copy.90
  353.4 8.5 copy.89
  361.9 8.5 copy.91
  370.5 13.6 %multiply_convert_fusion.1 = (bf16[256,9,9,64]{0,3,2,1:T(8,128)(2,1)S(1)}, f32[256,9,9,64]{0,3,2,1:T(8,128)}) fusion(f32[64]{0:T(128)S(1)} %copy-done.50, f32[512,64]{0,1:T(8,128)S(1)} %copy-done.16, bf16[256,9,9,128]{3,0,2,1:T(8,128)(2,1)} %copy.91, bf16[256,9,9,128]{3,0,2,1:T(8,128)(2,1)} %copy.90, bf16[256,9,9,128]{3,0,2,1:T(8,128)(2,1)} %copy.89, ...), kind=kOutput, calls=%fused_computation.27 | convolution fusion | flops 1457192960 | bytes 29327616 | tf_op jit(solution)/shard_map/dot_general | solution.py:128
  407.6 11.6 %fusion.61 = f32[256,7,7,576]{0,3,2,1:T(8,128)} fusion(bf16[256,7,7,64]{0,3,2,1:T(8,128)(2,1)S(1)} %get-tuple-element.152, f32[576,64]{0,1:T(8,128)S(1)} %copy-done.8), kind=kOutput, calls=%fused_computation.107 | convolution fusion | flops 924880896 | bytes 30654464 | tf_op jit(solution)/shard_map/dot_general | solution.py:143
  419.2 17.9 %fusion.149 = (f32[256,7,7,64]{0,3,2,1:T(8,128)}, f32[256,7,7,64]{0,3,2,1:T(8,128)}, f32[256,7,7,64]{0,3,2,1:T(8,128)}, f32[256,7,7,64]{0,3,2,1:T(8,128)}, f32[2...) fusion(f32[256,7,7,576]{0,3,2,1:T(8,128)} %fusion.61), kind=kLoop, calls=%fused_computation.234 | loop fusion | bytes 57802752 | tf_op jit(solution)/shard_map/slice | solution.py:118
  437.1 13.2 %convert_reduce_fusion.1 = (f32[64]{0:T(128)}, bf16[256,9,9,64]{0,3,2,1:T(8,128)(2,1)S(1)}) fusion(f32[256,9,9,64]{0,3,2,1:T(8,128)} %get-tuple-element.203, f32[64]{0:T(128)S(1)} %copy-done.50, f32[256,7,7,64]{0,3,2,1:T(8,128)} %get-tuple-element.172, f32[256,7,7,64]{0,3,2,1:T(8,128)} %get-tuple-element.173, f32[256,7,7,64]{0,3,2,1:T(8,128)} %get-tuple-element.174, ...), kind=kLoop, calls=%fused_computation.26 | loop fusion | flops 41140160 | bytes 36864512 | tf_op jit(solution)/shard_map/reduce_sum | solution.py:155
  450.4 11.6 %fusion.26 = f32[512,64]{0,1:T(8,128)} fusion(bf16[256,9,9,64]{0,3,2,1:T(8,128)(2,1)S(1)} %get-tuple-element.154, bf16[256,9,9,128]{3,0,2,1:T(8,128)(2,1)} %copy.91, bf16[256,9,9,128]{3,0,2,1:T(8,128)(2,1)} %copy.90, bf16[256,9,9,128]{3,0,2,1:T(8,128)(2,1)} %copy.89, bf16[256,9,9,128]{3,0,2,1:T(8,128)(2,1)} %copy.88), kind=kOutput, calls=%fused_computation.58 | convolution fusion | flops 1443889152 | bytes 24018944 | tf_op jit(solution)/shard_map/dot_general | solution.py:135
  462.0 16.4 %fusion.67 = f32[256,9,9,512]{3,0,2,1:T(8,128)} fusion(bf16[256,9,9,64]{0,3,2,1:T(8,128)(2,1)S(1)} %get-tuple-element.154, f32[512,64]{0,1:T(8,128)S(1)} %copy-done.16), kind=kOutput, calls=%fused_computation.115 | convolution fusion | flops 1358987264 | bytes 45252608 | tf_op jit(solution)/shard_map/dot_general | solution.py:143
  478.4 28.7 %fusion.148 = (f32[256,9,9,128]{3,0,2,1:T(8,128)}, f32[256,9,9,128]{3,0,2,1:T(8,128)}, f32[256,9,9,128]{3,0,2,1:T(8,128)}, f32[256,9,9,128]{3,0,2,1:T(8,128)}) fusion(f32[256,9,9,512]{3,0,2,1:T(8,128)} %fusion.67), kind=kLoop, calls=%fused_computation.233 | loop fusion | bytes 84934656 | tf_op jit(solution)/shard_map/slice | solution.py:118
  507.1 19.8 %pad_add_fusion = f32[256,10,10,128]{3,0,2,1:T(8,128)} fusion(f32[256,9,9,128]{3,0,2,1:T(8,128)} %get-tuple-element.168, f32[256,9,9,128]{3,0,2,1:T(8,128)} %get-tuple-element.169, f32[256,9,9,128]{3,0,2,1:T(8,128)} %get-tuple-element.170, f32[256,9,9,128]{3,0,2,1:T(8,128)} %get-tuple-element.167), kind=kLoop, calls=%fused_computation.15 | loop fusion | flops 9830400 | bytes 55574528 | tf_op jit(solution)/shard_map/add | solution.py:119
  526.9 14.0 %copy.74 = f32[256,10,10,128]{0,3,2,1:T(8,128)} copy(f32[256,10,10,128]{3,0,2,1:T(8,128)} %pad_add_fusion) | data formatting | bytes 26214400 | tf_op jit(solution)/shard_map/add | solution.py:119
  540.9 12.3 %copy.75 = f32[256,10,2,10,2,32]{0,5,4,3,2,1:T(8,128)} copy(f32[256,10,2,10,2,32]{0,5,4,2,3,1:T(8,128)} %bitcast.140) | data formatting | bytes 26214400 | tf_op jit(solution)/shard_map/transpose | solution.py:107
  553.2 15.4 %convert_reduce_fusion = (f32[32]{0:T(128)S(1)}, bf16[256,20,20,32]{0,3,2,1:T(8,128)(2,1)}) fusion(f32[256,20,20,32]{0,3,2,1:T(8,128)} %bitcast.139, f32[256,20,20,32]{0,3,2,1:T(8,128)} %get-tuple-element.201, f32[32]{0:T(128)S(1)} %copy-done.55), kind=kLoop, calls=%fused_computation.14 | loop fusion | flops 75366368 | bytes 32768256 | tf_op jit(solution)/shard_map/reduce_sum | solution.py:155
  568.7 46.2 %convolution_bitcast_fusion.1 = f32[256,32]{0,1:T(8,128)} fusion(bf16[256,20,20,32]{0,3,2,1:T(8,128)(2,1)} %get-tuple-element.156, bf16[256,20,20,64]{3,0,2,1:T(8,128)(2,1)} %copy.87, bf16[256,20,20,64]{3,0,2,1:T(8,128)(2,1)} %copy.86, bf16[256,20,20,64]{3,0,2,1:T(8,128)(2,1)} %copy.85, bf16[256,20,20,64]{3,0,2,1:T(8,128)(2,1)} %copy.84), kind=kOutput, calls=%fused_computation.61 | convolution fusion | flops 1887436800 | bytes 59015168 | tf_op jit(solution)/shard_map/dot_general | solution.py:135
  615.6 10.1 convolution_bitcast_fusion
  631.2 39.0 %fusion.99 = f32[256,20,20,256]{0,3,2,1:T(8,128)} fusion(bf16[256,20,20,32]{0,3,2,1:T(8,128)(2,1)} %get-tuple-element.156, f32[256,32]{0,1:T(8,128)S(1)} %copy-done.32), kind=kOutput, calls=%fused_computation.158 | convolution fusion | flops 1677729792 | bytes 111443968 | tf_op jit(solution)/shard_map/dot_general | solution.py:143
  670.2 65.9 %fusion.147 = (f32[256,20,20,64]{0,3,2,1:T(8,128)}, f32[256,20,20,64]{0,3,2,1:T(8,128)}, f32[256,20,20,64]{0,3,2,1:T(8,128)}, f32[256,20,20,64]{0,3,2,1:T(8,128)}) fusion(f32[256,20,20,256]{0,3,2,1:T(8,128)} %fusion.99), kind=kLoop, calls=%fused_computation.232 | loop fusion | bytes 209715200 | tf_op jit(solution)/shard_map/slice | solution.py:118
  736.2 38.2 %add_convert_fusion = bf16[256,21,21,64]{0,3,2,1:T(8,128)(2,1)} fusion(f32[256,20,20,64]{0,3,2,1:T(8,128)} %get-tuple-element.164, f32[256,20,20,64]{0,3,2,1:T(8,128)} %get-tuple-element.165, f32[256,20,20,64]{0,3,2,1:T(8,128)} %get-tuple-element.166, f32[256,20,20,64]{0,3,2,1:T(8,128)} %get-tuple-element.163), kind=kLoop, calls=%fused_computation.3 | loop fusion | flops 28901376 | bytes 119308288 | tf_op jit(solution)/shard_map/convert_element_type | solution.py:297
  783.5 87.5 %all-reduce.27.cloned.1.call-done = (f32[512,64]{0,1:T(8,128)}, f32[576,64]{0,1:T(8,128)}) async-done(((f32[512,64]{0,1:T(8,128)}, f32[576,64]{0,1:T(8,128)}), (f32[512,64]{0,1:T(8,128)}, f32[576,64]{0,1:T(8,128)})) %all-reduce.27.cloned.1.call-update) | async-done | bytes 278544 | tf_op jit(solution)/shard_map/psum | solution.py:307
  872.7 123.0 %reduce-scatter.3.cloned.1.call-done = f32[392,512]{1,0:T(8,128)} async-done(((f32[3136,512]{1,0:T(8,128)}), f32[392,512]{1,0:T(8,128)}) %reduce-scatter.3.cloned.1.call-update) | async-done | bytes 802832 | tf_op jit(solution)/shard_map/reduce_scatter | solution.py:280
  1006.4 14.8 %reduce-scatter.5.cloned.1.call-done = f32[392,128]{1,0:T(8,128)} async-done(((f32[392,512]{1,0:T(8,128)}), f32[392,128]{1,0:T(8,128)}) %reduce-scatter.5.cloned.1.call-update) | async-done | bytes 200720 | tf_op jit(solution)/shard_map/reduce_scatter | solution.py:288
  (240 shorter events, 100.5 us)
Async XLA Ops:
  7.2 992.7 %copy-start = (f32[576,576]{1,0:T(8,128)S(1)}, f32[576,576]{1,0:T(8,128)}, u32[]{:S(2)}) copy-start(f32[576,576]{1,0:T(8,128)} %param.65) | copy-start | bytes 3981316
  7.2 388.3 %all-gather.2.cloned.1.call-start = ((), (), s32[]{:S(2)}) async-start(), calls=%async_computation.2 | async-start | bytes 3612672 | tf_op jit(solution)/shard_map/all_gather | solution.py:257
  16.8 757.7 %all-reduce.25.cloned.1.call-start = ((), (), s32[]{:S(2)}) async-start(), calls=%async_computation.5 | async-start | bytes 172032 | tf_op jit(solution)/shard_map/psum | solution.py:307
  17.5 261.6 %copy-start.54 = (f32[32]{0:T(128)}, f32[32]{0:T(128)S(1)}, u32[]{:S(2)}) copy-start(f32[32]{0:T(128)S(1)} %slice.136) | copy-start | bytes 388
  568.6 46.2 %copy-start.47 = (f32[19]{0:T(128)S(1)}, f32[19]{0:T(128)}, u32[]{:S(2)}) copy-start(f32[19]{0:T(128)} %get-tuple-element.149) | copy-start | bytes 232
  568.6 46.2 %copy-start.48 = (f32[64]{0:T(128)S(1)}, f32[64]{0:T(128)}, u32[]{:S(2)}) copy-start(f32[64]{0:T(128)} %get-tuple-element.151) | copy-start | bytes 772
  568.6 46.2 %copy-start.49 = (f32[64]{0:T(128)S(1)}, f32[64]{0:T(128)}, u32[]{:S(2)}) copy-start(f32[64]{0:T(128)} %get-tuple-element.153) | copy-start | bytes 772
  568.7 46.2 %copy-start.52 = (f32[512]{0:T(512)S(1)}, f32[512]{0:T(512)}, u32[]{:S(2)}) copy-start(f32[512]{0:T(512)} %get-tuple-element.208) | copy-start | bytes 6148
  568.7 47.0 %copy-start.3 = (bf16[256,7,7,64]{0,3,2,1:T(8,128)(2,1)S(1)}, bf16[256,7,7,64]{0,3,2,1:T(8,128)(2,1)}, u32[]{:S(2)}) copy-start(bf16[256,7,7,64]{0,3,2,1:T(8,128)(2,1)} %copy-done.2) | copy-start | bytes 4816900
  615.6 255.4 %all-reduce.27.cloned.1.call-start = ((), (), s32[]{:S(2)}) async-start(), calls=%async_computation.6 | async-start | bytes 589824 | tf_op jit(solution)/shard_map/psum | solution.py:307
  625.8 369.9 %reduce-scatter.3.cloned.1.call-start = ((), (), s32[]{:S(2)}) async-start(), calls=%async_computation.3 | async-start | bytes 7225344 | tf_op jit(solution)/shard_map/reduce_scatter | solution.py:280
  631.1 390.1 %reduce-scatter.5.cloned.1.call-start = ((), (), s32[]{:S(2)}) async-start(), calls=%async_computation.4 | async-start | bytes 1003520 | tf_op jit(solution)/shard_map/reduce_scatter | solution.py:288
  736.1 38.4 %copy-start.39 = (f32[691]{0:T(1024)S(1)}, f32[691]{0:T(1024)}, u32[]{:S(2)}) copy-start(f32[691]{0:T(1024)} %param.48) | copy-start | bytes 8296
  736.1 38.4 %copy-start.43 = (f32[691]{0:T(1024)S(1)}, f32[691]{0:T(1024)}, u32[]{:S(2)}) copy-start(f32[691]{0:T(1024)} %param.60) | copy-start | bytes 8296
  736.1 38.4 %copy-start.44 = (f32[691]{0:T(1024)S(1)}, f32[691]{0:T(1024)}, u32[]{:S(2)}) copy-start(f32[691]{0:T(1024)} %param.54) | copy-start | bytes 8296
  736.1 39.7 %copy-start.12 = (f32[256,256]{1,0:T(8,128)S(1)}, f32[256,256]{1,0:T(8,128)}, u32[]{:S(2)}) copy-start(f32[256,256]{1,0:T(8,128)} %param.61) | copy-start | bytes 786436
  736.1 40.7 %copy-start.33 = (f32[32,32]{1,0:T(8,128)S(1)}, f32[32,32]{1,0:T(8,128)}, u32[]{:S(2)}) copy-start(f32[32,32]{1,0:T(8,128)} %param.62) | copy-start | bytes 12292
  736.1 40.7 %copy-start.37 = (f32[256,32]{0,1:T(8,128)S(1)}, f32[256,32]{0,1:T(8,128)}, u32[]{:S(2)}) copy-start(f32[256,32]{0,1:T(8,128)} %param.55) | copy-start | bytes 98308
  736.1 40.7 %copy-start.38 = (f32[256,32]{0,1:T(8,128)S(1)}, f32[256,32]{0,1:T(8,128)}, u32[]{:S(2)}) copy-start(f32[256,32]{0,1:T(8,128)} %param.49) | copy-start | bytes 98308
  736.1 44.0 %copy-start.34 = (f32[19,19]{1,0:T(8,128)S(1)}, f32[19,19]{1,0:T(8,128)}, u32[]{:S(2)}) copy-start(f32[19,19]{1,0:T(8,128)} %param.69) | copy-start | bytes 4336
  736.1 44.0 %copy-start.35 = (f32[512,19]{0,1:T(8,128)S(1)}, f32[512,19]{0,1:T(8,128)}, u32[]{:S(2)}) copy-start(f32[512,19]{0,1:T(8,128)} %param.59) | copy-start | bytes 116740
  736.2 44.0 %copy-start.36 = (f32[512,19]{0,1:T(8,128)S(1)}, f32[512,19]{0,1:T(8,128)}, u32[]{:S(2)}) copy-start(f32[512,19]{0,1:T(8,128)} %param.53) | copy-start | bytes 116740
  736.2 46.5 %copy-start.27 = (f32[512,19]{0,1:T(8,128)S(1)}, f32[512,19]{0,1:T(8,128)}, u32[]{:S(2)}) copy-start(f32[512,19]{0,1:T(8,128)} %param.47) | copy-start | bytes 116740
  736.2 134.8 %copy-start.6 = (f32[512,512]{1,0:T(8,128)S(1)}, f32[512,512]{1,0:T(8,128)}, u32[]{:S(2)}) copy-start(f32[512,512]{1,0:T(8,128)} %param.63) | copy-start | bytes 3145732
  774.4 223.8 %copy-start.17 = (f32[512,64]{0,1:T(8,128)S(1)}, f32[512,64]{0,1:T(8,128)}, u32[]{:S(2)}) copy-start(f32[512,64]{0,1:T(8,128)} %param.44) | copy-start | bytes 393220
  776.8 227.9 %copy-start.9 = (f32[576,64]{0,1:T(8,128)S(1)}, f32[576,64]{0,1:T(8,128)}, u32[]{:S(2)}) copy-start(f32[576,64]{0,1:T(8,128)} %param.45) | copy-start | bytes 442372
  780.4 244.8 %copy-start.28 = (f32[256,32]{0,1:T(8,128)S(1)}, f32[256,32]{0,1:T(8,128)}, u32[]{:S(2)}) copy-start(f32[256,32]{0,1:T(8,128)} %get-tuple-element.272) | copy-start | bytes 98308
  782.6 244.5 %copy-start.23 = (f32[512,19]{0,1:T(8,128)S(1)}, f32[512,19]{0,1:T(8,128)}, u32[]{:S(2)}) copy-start(f32[512,19]{0,1:T(8,128)} %get-tuple-element.276) | copy-start | bytes 116740
  871.0 154.8 %copy-start.18 = (f32[512,64]{0,1:T(8,128)S(1)}, f32[512,64]{0,1:T(8,128)}, u32[]{:S(2)}) copy-start(f32[512,64]{0,1:T(8,128)} %get-tuple-element.273) | copy-start | bytes 393220
  871.0 155.5 %copy-start.13 = (f32[576,64]{0,1:T(8,128)S(1)}, f32[576,64]{0,1:T(8,128)}, u32[]{:S(2)}) copy-start(f32[576,64]{0,1:T(8,128)} %get-tuple-element.274) | copy-start | bytes 442372
  997.1 31.9 %copy-start.19 = (f32[512,64]{0,1:T(8,128)}, f32[512,64]{0,1:T(8,128)S(1)}, u32[]{:S(2)}) copy-start(f32[512,64]{0,1:T(8,128)S(1)} %get-tuple-element.285) | copy-start | bytes 393220
  1003.2 25.8 %copy-start.14 = (f32[576,64]{0,1:T(8,128)}, f32[576,64]{0,1:T(8,128)S(1)}, u32[]{:S(2)}) copy-start(f32[576,64]{0,1:T(8,128)S(1)} %get-tuple-element.286) | copy-start | bytes 442372
  (30 other events, 190.2 us)
Sparse Core Ops, SparseCore 0:
  16.9 62.0 all-gather.1
  615.7 121.5 all-reduce.24
  743.3 127.6 all-reduce.26
  874.9 120.8 reduce-scatter.2
  998.7 22.5 reduce-scatter.4
where the time goes:
time: 1050 us; the launch traced here: 1040 us
  local copies, waits for them, and re-layouts  345 us (33%)
  matrix products  237 us (23%)
  waiting for transfers between devices  225 us (21%)
  other arithmetic  97.6 us (9%)
  blocking collectives  89.7 us (9%)
  loops' own time  21.1 us (2%)
  between operations  19.2 us (2%)
    unnamed x135, local copies, waits for them, and re-layouts  143 us
    reduce_scatter x1, waiting for transfers between devices, shards(): lax.psum_scatter(lax.dot_general(flat, d_dense, (((0,), (0,)), ((), ())),...  123 us
    slice x3, local copies, waits for them, and re-layouts, patches_back(): piece = spread[..., index * chans:(index + 1) * chans]  112 us
    psum x2, waiting for transfers between devices, shards(): lax.psum((first_here, second_here, third_here, heads_here, bias_here), ('...  87.5 us
    dot_general x5, matrix products, input_grad(): lax.dot_general(rows, weight, (((1,), (1,)), ((), ())), preferred_element...  69.1 us
    dot_general x4, matrix products, weight_grad(): lax.dot_general(left_rows, right_rows, (((0,), (0,)), ((), ())), preferre...  68.7 us
    dot_general x3, matrix products, apply_weight(): jnp.dot(inputs.reshape(-1, shape[-1]), weight, preferred_element_type=jnp...  66.3 us
    slice x2, local copies, waits for them, and re-layouts, cell_patches(): inputs[:, i:i + out, j:j + out, :]  43 us
  transfers between devices with their start and end apart: 5, of which 3 were waited for; matrix products, arithmetic and copies ran while one was open for 43% of the time, Pallas kernels for 0%

commit v1 on v0

v1 whole, which is shorter than its diff:
```python
import functools
import math

import jax
import jax.numpy as jnp
from jax import lax
from jax.experimental import pallas as pl
from jax.experimental.pallas import tpu as pltpu
from jax.sharding import PartitionSpec as P

STEP = 10
GAMMA = 0.99
LAMBDA = 0.95
CLIP = 0.1
ENTROPY_COEF = 0.01
VALUE_COEF = 0.5
BETA = 0.5
EPSILON = 1e-08
RATE = 1.0
BIAS_RATE = 0.1
HIGH = lax.Precision.HIGHEST
ROOT = math.sqrt(2.0 / math.pi)
CUBE = 0.044715
BF = jnp.bfloat16
F32 = jnp.float32
MIB = 2**20

NN = (((1,), (0,)), ((), ()))
NT = (((1,), (1,)), ((), ()))
TN = (((0,), (0,)), ((), ()))


def dot(a, b, dims=NN, precision=None):
    return lax.dot_general(a, b, dims, precision=precision, preferred_element_type=F32)


def params(limit=48, **more):
    return pltpu.CompilerParams(vmem_limit_bytes=limit * MIB, **more)


def gelu_both(x):
    x2 = x * x
    t = jnp.tanh(x * (ROOT + (ROOT * CUBE) * x2))
    h = 0.5 * x
    act = h + h * t
    slope = (0.5 + 0.5 * t) + h * (1.0 - t * t) * (ROOT + (3.0 * ROOT * CUBE) * x2)
    return act, slope


def wide(column, rows, n):
    k = column.shape[0]
    tall = jnp.concatenate([column] * (rows // k), axis=0) if rows > k else column
    return jnp.concatenate([tall] * (n // 128), axis=1)


def band_forward(weight, kernel, feats, count):
    ch = weight.shape[1]
    w = weight.astype(BF).T.reshape(ch, kernel, kernel, feats)
    parts = [
        jnp.pad(w, ((0, 0), (0, 0), (j, count - 1 - j), (0, 0))) for j in range(count)
    ]
    return jnp.stack(parts).reshape(count * ch, kernel * (kernel + count - 1) * feats)


def band_square(weight, feats):
    ch = weight.shape[1]
    w = weight.astype(BF).T.reshape(ch, 2, 2, feats)
    parts = [
        jnp.pad(w, ((0, 0), (dy, 1 - dy), (dx, 1 - dx), (0, 0)))
        for dy in range(2)
        for dx in range(2)
    ]
    return jnp.stack(parts).reshape(4 * ch, 9 * feats)


def band_back(weight, kernel, feats, count):
    ch = weight.shape[1]
    w = weight.astype(BF).reshape(kernel, kernel, feats, ch)[::-1, ::-1].transpose(2, 0, 1, 3)
    parts = [
        jnp.pad(w, ((0, 0), (0, 0), (i, count - 1 - i), (0, 0))) for i in range(count)
    ]
    return jnp.stack(parts).reshape(count * feats, kernel * (kernel + count - 1) * ch)


def advantage_kernel(lengths_ref, dones_ref, rewards_ref, values_ref, adv_ref, stat_ref):
    n = rewards_ref.shape[1]
    length = lengths_ref[0]
    position = lax.broadcasted_iota(jnp.int32, (8, n), 1)
    live = position < length
    mask = jnp.where(live, 1.0, 0.0)
    next_live = jnp.where(position + 1 < length, 1.0, 0.0)
    values = jnp.broadcast_to(values_ref[...], (8, n))
    rewards = jnp.broadcast_to(rewards_ref[...], (8, n))
    going = 1.0 - jnp.broadcast_to(dones_ref[...], (8, n)).astype(F32)

    def ahead(v, k, fill):
        return jnp.concatenate([v[:, k:], jnp.full((8, k), fill, F32)], axis=1)

    delta = rewards + GAMMA * going * ahead(values, 1, 0.0) * next_live - values
    total = mask * delta
    carry = mask * (GAMMA * LAMBDA) * going
    k = 1
    while k < n:
        total = total + carry * ahead(total, k, 0.0)
        carry = carry * ahead(carry, k, 0.0)
        k *= 2
    adv_ref[...] = total[0:1]
    count = jnp.sum(mask, axis=1, keepdims=True)
    mean = jnp.sum(mask * total, axis=1, keepdims=True) / count
    spread = jnp.sum(mask * (total - mean) ** 2, axis=1, keepdims=True)
    lane = lax.broadcasted_iota(jnp.int32, (8, 128), 1)
    stat = jnp.where(lane == 0, count, jnp.where(lane == 1, mean, jnp.where(lane == 2, spread, 0.0)))
    stat_ref[...] = stat[0:1]


def advantages(lengths, dones, rewards, old_values):
    n = rewards.shape[1]
    vmem = pl.BlockSpec(memory_space=pltpu.VMEM)
    return pl.pallas_call(
        advantage_kernel,
        out_shape=(jax.ShapeDtypeStruct((1, n), F32), jax.ShapeDtypeStruct((1, 128), F32)),
        in_specs=[pl.BlockSpec(memory_space=pltpu.SMEM), vmem, vmem, vmem],
        out_specs=(vmem, vmem),
        name="advantages",
    )(lengths, dones, rewards, old_values)


def join_stats(mine, other):
    n_a, m_a, s_a = mine[0, 0], mine[0, 1], mine[0, 2]
    n_b, m_b, s_b = other[0, 0], other[0, 1], other[0, 2]
    count = n_a + n_b
    mean = (n_a * m_a + n_b * m_b) / count
    gap = m_a - m_b
    spread = (s_a + s_b) + gap * gap * (n_a * n_b) / count
    lane = lax.broadcasted_iota(jnp.int32, mine.shape, 1)
    return jnp.where(lane == 0, count, jnp.where(lane == 1, mean, jnp.where(lane == 2, spread, 0.0)))


def conv_one_kernel(top_ref, bottom_ref, band_ref, bias_ref, act_ref, slope_ref):
    n = act_ref.shape[-1]
    cells = act_ref.shape[1]
    bias = wide(bias_ref[0:32, :], 128, n)
    for col in range(cells):
        span = slice(col * 128, col * 128 + 192)
        patch = jnp.concatenate(
            [top_ref[0, span, :], top_ref[1, span, :], bottom_ref[0, span, :]], axis=0
        )
        act, slope = gelu_both(dot(band_ref[...], patch) + bias)
        act_ref[0, col] = act.astype(BF)
        slope_ref[0, col] = slope.astype(BF)


def conv_one(frames, band, bias):
    grid, _, n = frames.shape
    half = grid // 2
    whole = lambda r: (0, 0)
    row = pl.BlockSpec((1, half, 128, n), lambda r: (r, 0, 0, 0))
    shape = jax.ShapeDtypeStruct((half, half, 128, n), BF)
    return pl.pallas_call(
        conv_one_kernel,
        out_shape=(shape, shape),
        grid=(half,),
        in_specs=[
            pl.BlockSpec((2,) + frames.shape[1:], lambda r: (r, 0, 0)),
            pl.BlockSpec((1,) + frames.shape[1:], lambda r: (2 * r + 2, 0, 0)),
            pl.BlockSpec(band.shape, whole),
            pl.BlockSpec(bias.shape, whole),
        ],
        out_specs=(row, row),
        compiler_params=params(),
        name="conv_one",
    )(frames, frames, band, bias)


def conv_two_three_kernel(
    top_ref, bottom_ref, band_two_ref, band_three_ref, bias_ref,
    act_ref, slope_ref, flat_ref, slope_three_ref, keep_ref,
):
    n = act_ref.shape[-1]
    step = pl.program_id(0)
    bias_two = wide(bias_ref[32:96, :], 192, n)
    for part in range(3):
        span = slice(3 * part, 3 * part + 4)
        patch = jnp.concatenate(
            [top_ref[0, span].reshape(512, n), bottom_ref[0, span].reshape(512, n)], axis=0
        )
        act, slope = gelu_both(dot(band_two_ref[...], patch) + bias_two)
        rows = slice(part * 192, part * 192 + 192)
        act = act.astype(BF)
        act_ref[0, rows, :] = act
        keep_ref[step, rows, :] = act
        slope_ref[0, rows, :] = slope.astype(BF)

    @pl.when(step >= 2)
    def _():
        bias_three = wide(bias_ref[96:160, :], 256, n)
        for first, start in ((0, 0), (1, 3)):
            patch = jnp.concatenate(
                [keep_ref[step - 2 + a, start * 64 : start * 64 + 384, :] for a in range(3)], axis=0
            )
            pre = dot(band_three_ref[first * 64 :, :], patch) + bias_three[first * 64 :]
            act, slope = gelu_both(pre)
            rows = slice((start + first) * 64, (start + 4) * 64)
            flat_ref[rows, :] = act.astype(BF)
            slope_three_ref[rows, :] = slope.astype(BF)


def conv_two_three(act_one, band_two, band_three, bias):
    n = act_one.shape[-1]
    whole = lambda r: (0, 0)
    row = pl.BlockSpec((1, 576, n), lambda r: (r, 0, 0))
    late = pl.BlockSpec((448, n), lambda r: (jnp.maximum(r - 2, 0), 0))
    two = jax.ShapeDtypeStruct((9, 576, n), BF)
    three = jax.ShapeDtypeStruct((3136, n), BF)
    return pl.pallas_call(
        conv_two_three_kernel,
        out_shape=(two, two, three, three),
        grid=(9,),
        in_specs=[
            pl.BlockSpec((1,) + act_one.shape[1:], lambda r: (r, 0, 0, 0)),
            pl.BlockSpec((1,) + act_one.shape[1:], lambda r: (r + 1, 0, 0, 0)),
            pl.BlockSpec(band_two.shape, whole),
            pl.BlockSpec(band_three.shape, whole),
            pl.BlockSpec(bias.shape, whole),
        ],
        out_specs=(row, row, late, late),
        scratch_shapes=[pltpu.VMEM((9, 576, n), BF)],
        compiler_params=params(),
        name="conv_two_three",
    )(act_one, act_one, band_two, band_three, bias)


def head_gradient(heads, actions, adv, values, old_logp, mask, count, centre, var):
    rows, n = heads.shape
    acts = rows - 1
    norm_adv = (adv - centre) * lax.rsqrt(var + 1e-05)
    returns = adv + values
    index = lax.broadcasted_iota(jnp.int32, (rows, n), 0)
    is_logit = index < acts
    top = jnp.max(jnp.where(is_logit, heads, -jnp.inf), axis=0, keepdims=True)
    shifted = heads - top
    grown = jnp.where(is_logit, jnp.exp(jnp.where(is_logit, shifted, 0.0)), 0.0)
    total = jnp.sum(grown, axis=0, keepdims=True)
    logp_all = jnp.where(is_logit, shifted - jnp.log(total), 0.0)
    prob = jnp.where(is_logit, jnp.exp(logp_all), 0.0)
    chosen = jnp.where(index == actions, 1.0, 0.0)
    logp = jnp.sum(logp_all * chosen, axis=0, keepdims=True)
    plogp = jnp.sum(prob * logp_all, axis=0, keepdims=True)
    value = jnp.sum(jnp.where(index == acts, heads, 0.0), axis=0, keepdims=True)
    ratio = jnp.exp(logp - old_logp)
    bent = jnp.tanh((ratio - 1.0) / CLIP)
    soft = 1.0 + CLIP * bent
    plain = ratio * norm_adv
    clipped = soft * norm_adv
    share = jnp.where(plain < clipped, 1.0, jnp.where(plain > clipped, 0.0, 0.5))
    by_ratio = -norm_adv * (share + (1.0 - share) * (1.0 - bent * bent))
    scale = mask / count
    by_logp = by_ratio * ratio
    by_logit = by_logp * (chosen - prob) + ENTROPY_COEF * prob * (logp_all - plogp)
    by_value = VALUE_COEF * (value - returns)
    return jnp.where(is_logit, by_logit, by_value) * scale


def dense_kernel(
    place_ref, lengths_ref, flat_ref, slope_three_ref, pieces_ref, heads_ref, bias_ref,
    actions_ref, adv_ref, values_ref, logp_ref, stat_ref,
    d_three_ref, keep_ref, send_ref, grad_heads_ref, sum_three_ref, sum_dense_ref, sum_heads_ref,
    weight_ref, d_dense_ref,
):
    n = flat_ref.shape[-1]
    n_dp, n_own, rows, cols = pieces_ref.shape
    dp, own = place_ref[0], place_ref[1]
    for i in range(n_dp):
        for j in range(n_own):
            weight_ref[i * rows : (i + 1) * rows, j * cols : (j + 1) * cols] = pieces_ref[
                i ^ dp, j ^ own
            ]
    hid = n_own * cols
    bias_dense = wide(bias_ref[160 : 160 + hid, :], hid, n)
    bias_heads = wide(bias_ref[160 + hid : 160 + hid + 19, :], 19, n)
    pre = dot(weight_ref[...], flat_ref[...], TN) + bias_dense
    hidden, slope = gelu_both(pre)
    hidden = hidden.astype(BF)
    head_weight = heads_ref[...].astype(BF)
    heads = dot(head_weight, hidden) + bias_heads
    position = lax.broadcasted_iota(jnp.int32, (1, n), 1)
    mask = jnp.where(position < lengths_ref[0], 1.0, 0.0)
    count = stat_ref[0:1, 0:1]
    centre = stat_ref[0:1, 1:2]
    var = stat_ref[0:1, 2:3] / count
    d_heads = head_gradient(
        heads, actions_ref[...], adv_ref[...], values_ref[...], logp_ref[...], mask, count, centre, var
    ).astype(BF)
    ones = jnp.ones((8, n), BF)
    grad_heads_ref[...] = dot(d_heads, hidden, NT)
    sum_heads_ref[...] = dot(ones, d_heads, NT)[0:1]
    d_dense = (dot(head_weight, d_heads, TN) * slope).astype(BF)
    sum_dense_ref[...] = dot(ones, d_dense, NT)[0:1]
    for j in range(n_own):
        d_dense_ref[j] = d_dense[j * cols : (j + 1) * cols]
    for k in range(n_own):
        block = dot(flat_ref[...], d_dense_ref[own ^ k], NT).astype(BF)
        if k % 2 == 0:
            keep_ref[k // 2] = block
        else:
            send_ref[k // 2] = block
    total = jnp.zeros((64, n), F32)
    for part in range(7):
        span = slice(part * 448, part * 448 + 448)
        d_three = (dot(weight_ref[span, :], d_dense) * slope_three_ref[span, :].astype(F32)).astype(BF)
        d_three_ref[span, :] = d_three
        back = d_three.astype(F32)
        for c in range(7):
            total = total + back[c * 64 : c * 64 + 64]
    sum_three_ref[...] = dot(jnp.ones((8, n), F32), total, NT, HIGH)[0:1]


def dense(place, lengths, flat, slope_three, pieces, heads, bias, actions, adv, values, logp, stat):
    n = flat.shape[-1]
    n_dp, n_own, rows, cols = pieces.shape
    hid = n_own * cols
    full = n_dp * rows
    vmem = pl.BlockSpec(memory_space=pltpu.VMEM)
    smem = pl.BlockSpec(memory_space=pltpu.SMEM)
    half = jax.ShapeDtypeStruct((n_own // 2, full, cols), BF)
    return pl.pallas_call(
        dense_kernel,
        out_shape=(
            jax.ShapeDtypeStruct((full, n), BF),
            half,
            half,
            jax.ShapeDtypeStruct(heads.shape, F32),
            jax.ShapeDtypeStruct((1, 64), F32),
            jax.ShapeDtypeStruct((1, hid), F32),
            jax.ShapeDtypeStruct((1, heads.shape[0]), F32),
        ),
        in_specs=[smem, smem] + [vmem] * 10,
        out_specs=(vmem,) * 7,
        scratch_shapes=[pltpu.VMEM((full, hid), BF), pltpu.VMEM((n_own, cols, n), BF)],
        compiler_params=params(56),
        name="dense",
    )(place, lengths, flat, slope_three, pieces, heads, bias, actions, adv, values, logp, stat)


def conv_three_back_kernel(
    d_three_ref, act_ref, slope_ref, band_ref, d_two_ref, grad_ref, sum_ref, pad_ref, acc_ref, tot_ref
):
    n = act_ref.shape[-1]
    step = pl.program_id(0)

    @pl.when(step == 0)
    def _():
        pad_ref[...] = jnp.zeros_like(pad_ref)
        acc_ref[...] = jnp.zeros_like(acc_ref)
        tot_ref[...] = jnp.zeros_like(tot_ref)
        for r in range(7):
            pad_ref[r + 2, 128 : 128 + 448, :] = d_three_ref[r * 448 : r * 448 + 448, :]

    total = tot_ref[...]
    for part in range(3):
        patch = jnp.concatenate(
            [pad_ref[step + a, part * 192 : part * 192 + 320, :] for a in range(3)], axis=0
        )
        rows = slice(part * 192, part * 192 + 192)
        d_two = (dot(band_ref[...], patch) * slope_ref[0, rows, :].astype(F32)).astype(BF)
        d_two_ref[0, rows, :] = d_two
        back = d_two.astype(F32)
        total = total + (back[0:64] + back[64:128]) + back[128:192]
    tot_ref[...] = total

    @pl.when(step < 7)
    def _():
        row = pad_ref[step + 2, 128 : 128 + 448, :]
        second = jnp.concatenate([jnp.zeros((64, n), BF), row[256:448]], axis=0)
        for d_rows, start in ((row[0:256], 0), (second, 3)):
            cells = jnp.concatenate(
                [act_ref[step + a, start * 64 : start * 64 + 384, :] for a in range(3)], axis=0
            )
            acc_ref[...] += dot(d_rows, cells, NT)

    @pl.when(step == 8)
    def _():
        for a in range(3):
            out = None
            for c in range(4):
                piece = acc_ref[c * 64 : c * 64 + 64, a * 384 + c * 64 : a * 384 + c * 64 + 192]
                out = piece if out is None else out + piece
            grad_ref[:, a * 192 : a * 192 + 192] = out
        sum_ref[...] = dot(jnp.ones((8, n), F32), tot_ref[...], NT, HIGH)[0:1]


def conv_three_back(d_three, act_two, slope_two, band):
    n = act_two.shape[-1]
    whole = lambda r: (0, 0)
    row = pl.BlockSpec((1, 576, n), lambda r: (r, 0, 0))
    return pl.pallas_call(
        conv_three_back_kernel,
        out_shape=(
            jax.ShapeDtypeStruct(act_two.shape, BF),
            jax.ShapeDtypeStruct((64, 576), F32),
            jax.ShapeDtypeStruct((1, 64), F32),
        ),
        grid=(9,),
        in_specs=[
            pl.BlockSpec(d_three.shape, whole),
            pl.BlockSpec(act_two.shape, lambda r: (0, 0, 0)),
            row,
            pl.BlockSpec(band.shape, whole),
        ],
        out_specs=(row, pl.BlockSpec((64, 576), whole), pl.BlockSpec((1, 64), whole)),
        scratch_shapes=[
            pltpu.VMEM((11, 704, n), BF),
            pltpu.VMEM((256, 1152), F32),
            pltpu.VMEM((64, n), F32),
        ],
        compiler_params=params(),
        name="conv_three_back",
    )(d_three, act_two, slope_two, band)


def conv_two_back_kernel(
    d_two_ref, top_ref, bottom_ref, slope_ref, band_ref, d_one_ref, grad_ref, sum_ref,
    pad_ref, acc_ref, tot_ref,
):
    n = d_one_ref.shape[-1]
    step = pl.program_id(0)

    @pl.when(step == 0)
    def _():
        pad_ref[...] = jnp.zeros_like(pad_ref)
        acc_ref[...] = jnp.zeros_like(acc_ref)
        tot_ref[...] = jnp.zeros_like(tot_ref)
        for r in range(9):
            pad_ref[r + 1, 64 : 64 + 576, :] = d_two_ref[r]

    total = tot_ref[...]
    for col in range(10):
        patch = jnp.concatenate(
            [pad_ref[step + a, col * 64 : col * 64 + 128, :] for a in range(2)], axis=0
        )
        d_one = (dot(band_ref[...], patch) * slope_ref[0, col].astype(F32)).astype(BF)
        d_one_ref[0, col] = d_one
        total = total + d_one.astype(F32)
    tot_ref[...] = total

    @pl.when(step < 9)
    def _():
        for part in range(3):
            span = slice(3 * part, 3 * part + 4)
            cells = jnp.concatenate(
                [top_ref[0, span].reshape(512, n), bottom_ref[0, span].reshape(512, n)], axis=0
            )
            rows = pad_ref[step + 1, 64 + part * 192 : 64 + part * 192 + 192, :]
            acc_ref[...] += dot(rows, cells, NT)

    @pl.when(step == 9)
    def _():
        for a in range(2):
            out = None
            for c in range(3):
                piece = acc_ref[c * 64 : c * 64 + 64, a * 512 + c * 128 : a * 512 + c * 128 + 256]
                out = piece if out is None else out + piece
            grad_ref[:, a * 256 : a * 256 + 256] = out
        sums = dot(jnp.ones((8, n), F32), tot_ref[...], NT, HIGH)[0:1]
        sum_ref[...] = (sums[:, 0:32] + sums[:, 32:64]) + (sums[:, 64:96] + sums[:, 96:128])


def conv_two_back(d_two, act_one, slope_one, band):
    n = act_one.shape[-1]
    half = act_one.shape[0]
    whole = lambda r: (0, 0)
    row = pl.BlockSpec((1,) + act_one.shape[1:], lambda r: (r, 0, 0, 0))
    return pl.pallas_call(
        conv_two_back_kernel,
        out_shape=(
            jax.ShapeDtypeStruct(act_one.shape, BF),
            jax.ShapeDtypeStruct((64, 512), F32),
            jax.ShapeDtypeStruct((1, 32), F32),
        ),
        grid=(half,),
        in_specs=[
            pl.BlockSpec(d_two.shape, lambda r: (0, 0, 0)),
            row,
            pl.BlockSpec((1,) + act_one.shape[1:], lambda r: (jnp.minimum(r + 1, half - 1), 0, 0, 0)),
            row,
            pl.BlockSpec(band.shape, whole),
        ],
        out_specs=(row, pl.BlockSpec((64, 512), whole), pl.BlockSpec((1, 32), whole)),
        scratch_shapes=[
            pltpu.VMEM((11, 704, n), BF),
            pltpu.VMEM((192, 1024), F32),
            pltpu.VMEM((128, n), F32),
        ],
        compiler_params=params(),
        name="conv_two_back",
    )(d_two, act_one, act_one, slope_one, band)


def conv_one_grad_kernel(top_ref, bottom_ref, d_one_ref, grad_ref, acc_ref):
    n = d_one_ref.shape[-1]
    step = pl.program_id(0)

    @pl.when(step == 0)
    def _():
        acc_ref[...] = jnp.zeros_like(acc_ref)

    for pair in range(d_one_ref.shape[1] // 2):
        span = slice(pair * 256, pair * 256 + 320)
        cells = jnp.concatenate(
            [top_ref[0, span, :], top_ref[1, span, :], bottom_ref[0, span, :]], axis=0
        )
        rows = d_one_ref[0, 2 * pair : 2 * pair + 2].reshape(256, n)
        acc_ref[...] += dot(rows, cells, NT)

    @pl.when(step == pl.num_programs(0) - 1)
    def _():
        for a in range(2):
            out = None
            for k in range(2):
                for dy in range(2):
                    for dx in range(2):
                        row = ((k * 2 + dy) * 2 + dx) * 32
                        lane = (dy + a) * 320 + (2 * k + dx) * 64
                        piece = acc_ref[row : row + 32, lane : lane + 128]
                        out = piece if out is None else out + piece
            grad_ref[:, a * 128 : a * 128 + 128] = out


def conv_one_grad(frames, d_one):
    n = frames.shape[-1]
    half = d_one.shape[0]
    return pl.pallas_call(
        conv_one_grad_kernel,
        out_shape=jax.ShapeDtypeStruct((32, 256), F32),
        grid=(half,),
        in_specs=[
            pl.BlockSpec((2,) + frames.shape[1:], lambda r: (r, 0, 0)),
            pl.BlockSpec((1,) + frames.shape[1:], lambda r: (2 * r + 2, 0, 0)),
            pl.BlockSpec((1,) + d_one.shape[1:], lambda r: (r, 0, 0, 0)),
        ],
        out_specs=pl.BlockSpec((32, 256), lambda r: (0, 0)),
        scratch_shapes=[pltpu.VMEM((256, 960), F32)],
        compiler_params=params(),
        name="conv_one_grad",
    )(frames, frames, d_one)


def frames_back_kernel(above_ref, here_ref, band_ref, out_ref):
    n = out_ref.shape[-1]
    step = pl.program_id(0)
    last = pl.num_programs(0) - 1
    cells = here_ref.shape[1]
    zero = jnp.zeros((32, n), BF)

    def slab(ref, dy, first, alive):
        parts = []
        for c in range(first, first + 4):
            if c < 0 or c >= 2 * cells:
                parts.append(zero)
            else:
                start = (dy * 2 + c % 2) * 32
                parts.append(ref[0, c // 2, start : start + 32, :])
        whole = jnp.concatenate(parts, axis=0)
        return whole if alive is None else jnp.where(alive, whole, jnp.zeros_like(whole))

    for block in range(7):
        first = 3 * block - 1
        up = slab(above_ref, 1, first, step > 0)
        mid = slab(here_ref, 0, first, step < last)
        rows = slice(block * 192, block * 192 + 192)
        out_ref[0, rows, :] = dot(band_ref[...], jnp.concatenate([up, mid], axis=0)).astype(BF)

    @pl.when(step < last)
    def _():
        for block in range(7):
            first = 3 * block - 1
            mid = slab(here_ref, 0, first, None)
            low = slab(here_ref, 1, first, None)
            rows = slice(block * 192, block * 192 + 192)
            out_ref[1, rows, :] = dot(band_ref[...], jnp.concatenate([mid, low], axis=0)).astype(BF)


def frames_back(d_one, band, shape):
    half = d_one.shape[0]
    block = (1,) + d_one.shape[1:]
    return pl.pallas_call(
        frames_back_kernel,
        out_shape=jax.ShapeDtypeStruct(shape, BF),
        grid=(half + 1,),
        in_specs=[
            pl.BlockSpec(block, lambda r: (jnp.maximum(r - 1, 0), 0, 0, 0)),
            pl.BlockSpec(block, lambda r: (jnp.minimum(r, half - 1), 0, 0, 0)),
            pl.BlockSpec(band.shape, lambda r: (0, 0)),
        ],
        out_specs=pl.BlockSpec((2,) + shape[1:], lambda r: (r, 0, 0)),
        compiler_params=params(),
        name="frames_back",
    )(d_one, d_one, band)


def adam_terms(grad, mean, square):
    momentum = BETA * mean + (1.0 - BETA) * grad
    variance = BETA * square + (1.0 - BETA) * grad * grad
    fix = 1.0 - BETA**STEP
    direction = momentum / fix / (jnp.sqrt(variance / fix) + EPSILON)
    return (momentum, variance, direction)


def turned_step(weight, grad, mean, square, left, right):
    rate = RATE / math.sqrt(weight.shape[1])
    turned = dot(dot(right, grad, TN, HIGH), left, NN, HIGH)
    momentum, variance, direction = adam_terms(turned, mean, square)
    back = dot(dot(right, direction, NN, HIGH), left, NT, HIGH)
    return momentum, variance, weight - rate * back


def step_kernel(*refs):
    ins, outs = refs[:6], refs[6:]
    results = turned_step(*[ref[...] for ref in ins])
    for ref, value in zip(outs, results):
        ref[...] = value


def rotated_step(weight, grad, mean, square, left, right):
    vmem = pl.BlockSpec(memory_space=pltpu.VMEM)
    shape = jax.ShapeDtypeStruct(grad.shape, F32)
    return pl.pallas_call(
        step_kernel,
        out_shape=(shape,) * 3,
        in_specs=[vmem] * 6,
        out_specs=(vmem,) * 3,
        compiler_params=params(),
        name="rotated_step",
    )(weight.T, grad, mean.T, square.T, left, right)


def dense_step_kernel(weight_ref, grad_ref, mean_ref, square_ref, block_ref, mom_ref, var_ref, new_ref, *, rate):
    turned = dot(grad_ref[...], block_ref[0], NN, HIGH)
    momentum, variance, direction = adam_terms(turned, mean_ref[...], square_ref[...])
    mom_ref[...] = momentum
    var_ref[...] = variance
    new_ref[...] = weight_ref[...] - rate * dot(direction, block_ref[0], NT, HIGH)


def dense_step(weight, grad, mean, square, block, rate):
    vmem = pl.BlockSpec(memory_space=pltpu.VMEM)
    shape = jax.ShapeDtypeStruct(grad.shape, F32)
    return pl.pallas_call(
        functools.partial(dense_step_kernel, rate=rate),
        out_shape=(shape,) * 3,
        in_specs=[vmem] * 5,
        out_specs=(vmem,) * 3,
        compiler_params=params(),
        name="dense_step",
    )(weight, grad, mean, square, block)


def swap(x, axis, bit, size):
    return lax.ppermute(x, axis, [(i, i ^ bit) for i in range(size)])


def bits_of(size):
    return [1 << b for b in range(size.bit_length() - 1)]


def gather_pieces(piece, n_dp, n_own):
    pieces = piece[None, None]
    for bit in bits_of(n_dp):
        pieces = jnp.concatenate([pieces, swap(pieces, "dp", bit, n_dp)], axis=0)
    for bit in bits_of(n_own):
        pieces = jnp.concatenate([pieces, swap(pieces, "own", bit, n_own)], axis=1)
    return pieces


def sum_everywhere(x, n_dp, n_own):
    for bit in bits_of(n_own):
        x = x + swap(x, "own", bit, n_own)
    for bit in bits_of(n_dp):
        x = x + swap(x, "dp", bit, n_dp)
    return x


def add_low(a, b):
    return (a.astype(F32) + b.astype(F32)).astype(BF)


def scatter_sum(keep, send, n_dp, n_own):
    own, dp = lax.axis_index("own"), lax.axis_index("dp")
    block = add_low(keep, swap(send, "own", 1, n_own))
    size = n_own // 2
    bit = n_own // 2
    while size > 1:
        size //= 2
        block = add_low(block[:size], swap(block[size:], "own", bit, n_own))
        bit //= 2
    block = block[0]
    rows = block.shape[0] // n_dp
    blocks = block.reshape((2,) * len(bits_of(n_dp)) + (rows, block.shape[1]))
    for bit in bits_of(n_dp):
        axis = blocks.ndim - 3
        mine = (dp // bit) % 2
        kept = lax.dynamic_index_in_dim(blocks, mine, axis, keepdims=False)
        gone = lax.dynamic_index_in_dim(blocks, 1 - mine, axis, keepdims=False)
        came = swap(gone, "dp", bit, n_dp)
        if blocks.ndim > 3:
            blocks = add_low(kept, came)
        else:
            blocks = kept.astype(F32) + came.astype(F32)
    return blocks


def shards(
    frames, actions, dones, lengths, rewards, old_values, old_logp,
    conv_first, conv_second, conv_third, dense_hidden, dense_heads, bias_all,
    mean_first, mean_second, mean_third, mean_dense, mean_heads, mean_bias,
    square_first, square_second, square_third, square_dense, square_heads, square_bias,
    left_first, right_first, left_second, right_second, left_third, right_third,
    right_dense, left_heads, right_heads, *, n_dp, n_own,
):
    tokens, grid = frames.shape[0], frames.shape[1]
    planes = frames.shape[3]
    place = jnp.stack([lax.axis_index("dp"), lax.axis_index("own")]).astype(jnp.int32)
    pieces = gather_pieces(dense_hidden.astype(BF), n_dp, n_own)
    adv, stat = advantages(lengths, dones, rewards, old_values)
    for bit in bits_of(n_own):
        stat = join_stats(stat, swap(stat, "own", bit, n_own))
    for bit in bits_of(n_dp):
        stat = join_stats(stat, swap(stat, "dp", bit, n_dp))
    bias = jnp.broadcast_to(bias_all[:, None], (bias_all.shape[0], 128))
    cells = frames.transpose(1, 2, 3, 0).reshape(grid, grid * planes, tokens)
    act_one, slope_one = conv_one(cells, band_square(conv_first, planes), bias)
    act_two, slope_two, flat, slope_three = conv_two_three(
        act_one, band_forward(conv_second, 2, 128, 3), band_forward(conv_third, 3, 64, 4), bias
    )
    d_three, keep, send, here_heads, sum_three, sum_dense, sum_heads = dense(
        place, lengths, flat, slope_three, pieces, dense_heads.T, bias,
        actions, adv, old_values, old_logp, stat,
    )
    grad_dense = scatter_sum(keep, send, n_dp, n_own)
    d_two, here_third, sum_two = conv_three_back(d_three, act_two, slope_two, band_back(conv_third, 3, 64, 3))
    d_one, here_second, sum_one = conv_two_back(d_two, act_one, slope_one, band_back(conv_second, 2, 128, 1))
    here_first = conv_one_grad(cells, d_one)
    frames_grad = frames_back(d_one, band_back(conv_first, 2, planes, 3), cells.shape)
    frames_grad = frames_grad.reshape(grid, grid, planes, tokens).transpose(3, 0, 1, 2)
    here_bias = jnp.concatenate([sum_one, sum_two, sum_three, sum_dense, sum_heads], axis=1)
    here = (here_first, here_second, here_third, here_heads, here_bias)
    packed = jnp.concatenate([h.reshape(-1) for h in here])
    packed = sum_everywhere(packed, n_dp, n_own)
    grads = []
    start = 0
    for h in here:
        grads.append(packed[start : start + h.size].reshape(h.shape))
        start += h.size
    grad_first, grad_second, grad_third, grad_heads, grad_bias = grads
    one = rotated_step(conv_first, grad_first, mean_first, square_first, left_first, right_first)
    two = rotated_step(conv_second, grad_second, mean_second, square_second, left_second, right_second)
    three = rotated_step(conv_third, grad_third, mean_third, square_third, left_third, right_third)
    top = rotated_step(dense_heads, grad_heads, mean_heads, square_heads, left_heads, right_heads)
    flat_rows = dense_hidden.shape[0] * n_dp
    wide_step = dense_step(
        dense_hidden, grad_dense, mean_dense, square_dense, right_dense, RATE / math.sqrt(flat_rows)
    )
    grad_bias = grad_bias.reshape(-1)
    mom_bias, var_bias, bias_dir = adam_terms(grad_bias, mean_bias, square_bias)
    new_bias = bias_all - BIAS_RATE * bias_dir
    outs = [frames_grad, grad_first.T, grad_second.T, grad_third.T, grad_dense, grad_heads.T, grad_bias]
    for index, bias_part in enumerate((mom_bias, var_bias, new_bias)):
        outs += [one[index].T, two[index].T, three[index].T, wide_step[index], top[index].T, bias_part]
    return tuple(outs)


def solution(mesh):
    n_dp, n_own = mesh.shape["dp"], mesh.shape["own"]
    both = ("dp", "own")
    rep = P()
    in_specs = (
        (P(both, None, None, None), P(both, None), P(both, None), P(both))
        + (P(both, None),) * 3
        + (rep, rep, rep, P("dp", "own"), rep, rep) * 3
        + (rep,) * 6
        + (P("own", None, None), rep, rep)
    )
    out_specs = (P(both, None, None, None),) + (rep, rep, rep, P("dp", "own"), rep, rep) * 4
    body = functools.partial(shards, n_dp=n_dp, n_own=n_own)
    return jax.shard_map(body, mesh=mesh, in_specs=in_specs, out_specs=out_specs, check_vma=False)
```

time: 1050 us -> 294 us (0.28); the launches traced: 1040 us -> 292 us
  local copies, waits for them, and re-layouts: 345 us -> 27.9 us
  matrix products: 237 us -> 0 us
  waiting for transfers between devices: 225 us -> 66 us
  Pallas kernels: 0 us -> 118 us
  blocking collectives: 89.7 us -> 0 us
  other arithmetic: 97.6 us -> 16.9 us
  between operations: 19.2 us -> 41.5 us
  starting transfers between devices: 0.21 us -> 21.7 us
  loops' own time: 21.1 us -> 0 us
    dot_general x34 -> x0, matrix products: 237 us -> none  [the longest x5 69.1 us: input_grad(): lax.dot_general(rows, weight, (((1,), (1,)), ((), ())), preferred_element...]
    slice x11 -> x15, local copies, waits for them, and re-layouts: 161 us -> 8.7 us  [the longest x5 2.93 us: join_stats(): n_b, m_b, s_b = (other[0, 0], other[0, 1], other[0, 2])]
    unnamed x135 -> x103, local copies, waits for them, and re-layouts: 143 us -> 4.46 us
    reduce_scatter x2 -> x0, waiting for transfers between devices: 138 us -> none  [the longest x1 123 us: shards(): lax.psum_scatter(lax.dot_general(flat, d_dense, (((0,), (0,)), ((), ())),...]
    pallas_call x0 -> x13, Pallas kernels: none -> 118 us  [the longest x1 18.2 us: conv_one(): pl.pallas_call(conv_one_kernel, out_shape=(shape, shape), grid=(half,), i...]
    psum x2 -> x0, waiting for transfers between devices: 87.5 us -> none  [shards(): lax.psum((first_here, second_here, third_here, heads_here, bias_here), ('...]
    psum x2 -> x0, blocking collectives: 81.3 us -> none  [the longest x1 40.9 us: shards(): spread = lax.psum(jnp.sum(mask * (advantage - centre) ** 2), ('dp', 'own'))]
    ppermute x0 -> x20, waiting for transfers between devices: none -> 66 us  [swap(): return lax.ppermute(x, axis, [(i, i ^ bit) for i in range(size)])]
  transfers between devices with their start and end apart: 5 -> 20, of which waited for: 3 -> 11; matrix products, arithmetic and copies ran while one was open for 43% -> 11% of each run, Pallas kernels for 0% -> 36%
where the time goes in v1:
time: 294 us; the launch traced here: 292 us
  Pallas kernels  118 us (40%)
  waiting for transfers between devices  66 us (22%)
  between operations  41.5 us (14%)
  local copies, waits for them, and re-layouts  27.9 us (9%)
  starting transfers between devices  21.7 us (7%)
  other arithmetic  16.9 us (6%)
    ppermute x20, waiting for transfers between devices, swap(): return lax.ppermute(x, axis, [(i, i ^ bit) for i in range(size)])  66 us
    ppermute x20, starting transfers between devices, swap(): return lax.ppermute(x, axis, [(i, i ^ bit) for i in range(size)])  21.7 us
    pallas_call x1, Pallas kernels, conv_one(): pl.pallas_call(conv_one_kernel, out_shape=(shape, shape), grid=(half,), i...  18.2 us
    pallas_call x1, Pallas kernels, frames_back(): pl.pallas_call(frames_back_kernel, out_shape=jax.ShapeDtypeStruct(shape,...  16.7 us
    pallas_call x1, Pallas kernels, conv_two_back(): pl.pallas_call(conv_two_back_kernel, out_shape=(jax.ShapeDtypeStruct(act_...  16 us
    pallas_call x1, Pallas kernels, conv_one_grad(): pl.pallas_call(conv_one_grad_kernel, out_shape=jax.ShapeDtypeStruct((32,...  15 us
    pallas_call x1, Pallas kernels, conv_two_three(): pl.pallas_call(conv_two_three_kernel, out_shape=(two, two, three, three),...  14.9 us
    pallas_call x1, Pallas kernels, conv_three_back(): pl.pallas_call(conv_three_back_kernel, out_shape=(jax.ShapeDtypeStruct(ac...  11.8 us
  transfers between devices with their start and end apart: 20, of which 11 were waited for; matrix products, arithmetic and copies ran while one was open for 11% of the time, Pallas kernels for 36%

profile of v1, /device:TPU:0, one launch (start us, length us, event | category | flops | bytes accessed | tf_op | source)
XLA Modules:
  0.0 291.9 jit_solution(5165004510474401497)
XLA Ops:
  1.7 3.0 %collective-permute-start = (bf16[1,1,392,128]{3,2,1,0:T(8,128)(2,1)S(1)}, bf16[1,1,392,128]{3,2,1,0:T(8,128)(2,1)S(1)}, u32[]{:S(2)}, u32[]{:S(2)}) collective-permute-start(bf16[1,1,392,128]{3,2,1,0:T(8,128)(2,1)S(1)} %convert_bitcast_fusion), channel_id=1, source_target_pairs={{0,4},{4,0},{8,12},{12,8},{16,20},{20,16},{24,28},{28,24},{1,5},{5... | collective-permute-start | bytes 301064 | tf_op jit(solution)/shard_map/ppermute | solution.py:659
  4.7 2.8 collective-permute-done
  7.5 2.0 collective-permute-start.1
  10.1 2.0 advantages.1
  12.1 1.7 collective-permute-done.1
  13.8 2.5 collective-permute-start.2
  17.1 16.1 %collective-permute-done.2 = bf16[4,1,392,128]{3,2,1,0:T(8,128)(2,1)S(1)} collective-permute-done((bf16[4,1,392,128]{3,2,1,0:T(8,128)(2,1)S(1)}, bf16[4,1,392,128]{3,2,1,0:T(8,128)(2,1)S(1)}, u32[]{:S(2)}, u32[]{:S(2)}) %collective-permute-start.2) | collective-permute-done | bytes 401440 | tf_op jit(solution)/shard_map/ppermute | solution.py:659
  40.0 1.6 collective-permute-start.4
  42.5 2.1 copy.98
  48.3 18.2 %conv_one.1 = (bf16[10,10,128,256]{3,2,1,0:T(8,128)(2,1)}, bf16[10,10,128,256]{3,2,1,0:T(8,128)(2,1)}) custom-call(bf16[21,1344,256]{2,1,0:T(8,128)(2,1)} %bitcast.151, bf16[21,1344,256]{2,1,0:T(8,128)(2,1)} %bitcast.152, bf16[128,576]{1,0:T(8,128)(2,1)S(1)} %reshape.254.band_ref, f32[691,128]{1,0:T(8,128)S(1)} %broadcast_in_dim.64.bias_ref), custom_call_target="tpu_custom_call" | custom-call | tf_op jit(solution)/shard_map/conv_one/pallas_call | solution.py:159
  66.6 14.9 %conv_two_three.1 = (bf16[9,576,256]{2,1,0:T(8,128)(2,1)}, bf16[9,576,256]{2,1,0:T(8,128)(2,1)}, bf16[3136,256]{1,0:T(8,128)(2,1)S(1)}, bf16[3136,256]{1,0:T(8,128)(2,1)S(1)}) custom-call(bf16[10,10,128,256]{3,2,1,0:T(8,128)(2,1)} %get-tuple-element.61.top_ref.bottom_ref, bf16[10,10,128,256]{3,2,1,0:T(8,128)(2,1)} %get-tuple-element.61.top_ref.bottom_ref, ...), custom_call_target="tpu_custom_call" | custom-call | tf_op jit(solution)/shard_map/conv_two_three/pallas_call | solution.py:215
  114.5 1.6 collective-permute-done.8
  123.3 1.6 collective-permute-start.9
  135.4 3.3 %pad_maximum_fusion.pieces_ref = bf16[8,4,392,128]{3,2,1,0:T(8,128)(2,1)} fusion(bf16[8,2,392,128]{3,2,1,0:T(8,128)(2,1)} %collective-permute-done.4, bf16[8,1,392,128]{3,2,1,0:T(8,128)(2,1)S(1)} %copy-done.34, bf16[4,1,392,128]{3,2,1,0:T(8,128)(2,1)S(1)} %collective-permute-done.2, bf16[2,1,392,128]{3,2,1,0:T(8,128)(2,1)S(1)} %collective-permute-done.1, ...), kind=kLoop, calls=%fused_computation | loop fusion | flops 8028160 | bytes 6422528 | tf_op jit(solution)/shard_map/concatenate | solution.py:671
  138.7 10.6 %dense.1 = (bf16[3136,256]{1,0:T(8,128)(2,1)}, bf16[2,3136,128]{2,1,0:T(8,128)(2,1)}, bf16[2,3136,128]{2,1,0:T(8,128)(2,1)}, f32[19,512]{1,0:T(8,128)}, f32[1,64...) custom-call(s32[2]{0:T(128)} %pad_add_fusion.place_ref, s32[1]{0:T(128)S(6)} %copy.117.lengths_ref, ...), custom_call_target="tpu_custom_call" | custom-call | tf_op jit(solution)/shard_map/dense/pallas_call | solution.py:326
  149.7 1.6 copy.99
  151.3 1.8 reshape.278.band_ref
  153.7 11.8 %conv_three_back.1 = (bf16[9,576,256]{2,1,0:T(8,128)(2,1)S(1)}, f32[64,576]{1,0:T(8,128)S(1)}, f32[1,64]{1,0:T(1,128)S(1)}) custom-call(bf16[3136,256]{1,0:T(8,128)(2,1)S(1)} %copy-done.1, bf16[9,576,256]{2,1,0:T(8,128)(2,1)} %get-tuple-element.67.act_ref, bf16[9,576,256]{2,1,0:T(8,128)(2,1)} %get-tuple-element.68.slope_ref, ...), custom_call_target="tpu_custom_call" | custom-call | tf_op jit(solution)/shard_map/conv_three_back/pallas_call | solution.py:396
  165.4 16.0 %conv_two_back.1 = (bf16[10,10,128,256]{3,2,1,0:T(8,128)(2,1)}, f32[64,512]{1,0:T(8,128)S(1)}, f32[1,32]{1,0:T(1,128)S(1)}) custom-call(bf16[9,576,256]{2,1,0:T(8,128)(2,1)S(1)} %get-tuple-element.69.d_two_ref, bf16[10,10,128,256]{3,2,1,0:T(8,128)(2,1)} %get-tuple-element.61.top_ref.bottom_ref, ...), custom_call_target="tpu_custom_call" | custom-call | tf_op jit(solution)/shard_map/conv_two_back/pallas_call | solution.py:473
  181.4 15.0 %conv_one_grad.1 = f32[32,256]{1,0:T(8,128)S(1)} custom-call(bf16[21,1344,256]{2,1,0:T(8,128)(2,1)} %bitcast.153, bf16[21,1344,256]{2,1,0:T(8,128)(2,1)} %bitcast.154, bf16[10,10,128,256]{3,2,1,0:T(8,128)(2,1)} %get-tuple-element.71.above_ref.here_ref.d_one_ref), custom_call_target="tpu_custom_call" | custom-call | tf_op jit(solution)/shard_map/conv_one_grad/pallas_call | solution.py:532
  196.9 1.8 add_convert_fusion
  201.7 1.7 collective-permute-start.11
  203.5 24.3 %collective-permute-done.11 = f32[88243]{0:T(1024)S(1)} collective-permute-done((f32[88243]{0:T(1024)S(1)}, f32[88243]{0:T(1024)S(1)}, u32[]{:S(2)}, u32[]{:S(2)}) %collective-permute-start.11) | collective-permute-done | bytes 353004 | tf_op jit(solution)/shard_map/ppermute | solution.py:659
  230.3 8.8 %collective-permute-done.12 = f32[88243]{0:T(1024)S(1)} collective-permute-done((f32[88243]{0:T(1024)S(1)}, f32[88243]{0:T(1024)S(1)}, u32[]{:S(2)}, u32[]{:S(2)}) %collective-permute-start.12) | collective-permute-done | bytes 353004 | tf_op jit(solution)/shard_map/ppermute | solution.py:659
  240.0 6.8 %collective-permute-done.13 = f32[88243]{0:T(1024)S(1)} collective-permute-done((f32[88243]{0:T(1024)S(1)}, f32[88243]{0:T(1024)S(1)}, u32[]{:S(2)}, u32[]{:S(2)}) %collective-permute-start.13) | collective-permute-done | bytes 353004 | tf_op jit(solution)/shard_map/ppermute | solution.py:659
  246.9 2.1 collective-permute-start.14
  251.8 16.7 %frames_back.1 = bf16[21,1344,256]{2,1,0:T(8,128)(2,1)} custom-call(bf16[10,10,128,256]{3,2,1,0:T(8,128)(2,1)} %get-tuple-element.71.above_ref.here_ref.d_one_ref, bf16[10,10,128,256]{3,2,1,0:T(8,128)(2,1)} %get-tuple-element.71.above_ref.here_ref.d_one_ref, bf16[192,256]{1,0:T(8,128)(2,1)S(1)} %reshape.279.band_ref), custom_call_target="tpu_custom_call" | custom-call | tf_op jit(solution)/shard_map/frames_back/pallas_call | solution.py:586
  276.3 2.5 rotated_step.7
  280.5 3.4 %rotated_step.6 = (f32[64,576]{1,0:T(8,128)}, f32[64,576]{1,0:T(8,128)}, f32[64,576]{1,0:T(8,128)}) custom-call(f32[64,576]{1,0:T(8,128)S(1)} %bitcast.133, f32[64,576]{1,0:T(8,128)S(1)} %reshape.272.refs_1_, f32[64,576]{1,0:T(8,128)S(1)} %bitcast.140, f32[64,576]{1,0:T(8,128)S(1)} %bitcast.141, f32[576,576]{1,0:T(8,128)S(1)} %copy-done.4, ...), custom_call_target="tpu_custom_call" | custom-call | tf_op jit(solution)/shard_map/rotated_step/pallas_call | solution.py:627
  284.0 3.0 %rotated_step.5 = (f32[64,512]{1,0:T(8,128)}, f32[64,512]{1,0:T(8,128)}, f32[64,512]{1,0:T(8,128)}) custom-call(f32[64,512]{1,0:T(8,128)S(1)} %bitcast.132, f32[64,512]{1,0:T(8,128)S(1)} %reshape.271.refs_1_, f32[64,512]{1,0:T(8,128)S(1)} %bitcast.143, f32[64,512]{1,0:T(8,128)S(1)} %bitcast.144, f32[512,512]{1,0:T(8,128)S(1)} %copy-done.7, ...), custom_call_target="tpu_custom_call" | custom-call | tf_op jit(solution)/shard_map/rotated_step/pallas_call | solution.py:627
  287.0 1.7 rotated_step.4
  289.7 2.2 dense_step.1
  (207 shorter events, 45.3 us)
Async XLA Ops:
  0.7 16.4 %copy-start.5 = (f32[512,64]{0,1:T(8,128)S(1)}, f32[512,64]{0,1:T(8,128)}, u32[]{:S(2)}) copy-start(f32[512,64]{0,1:T(8,128)} %param.42) | copy-start | bytes 393220
  1.7 33.3 %copy-start.10 = (f32[576,64]{0,1:T(8,128)S(1)}, f32[576,64]{0,1:T(8,128)}, u32[]{:S(2)}) copy-start(f32[576,64]{0,1:T(8,128)} %param.43) | copy-start | bytes 442372
  1.7 5.8 %collective-permute-start = (bf16[1,1,392,128]{3,2,1,0:T(8,128)(2,1)S(1)}, bf16[1,1,392,128]{3,2,1,0:T(8,128)(2,1)S(1)}, u32[]{:S(2)}, u32[]{:S(2)}) collective-permute-start(bf16[1,1,392,128]{3,2,1,0:T(8,128)(2,1)S(1)} %convert_bitcast_fusion), channel_id=1, source_target_pairs={{0,4},{4,0},{8,12},{12,8},{16,20},{20,16},{24,28},{28,24},{1,5},{5... | collective-permute-start | bytes 301064 | tf_op jit(solution)/shard_map/ppermute | solution.py:659
  7.5 6.2 %collective-permute-start.1 = (bf16[2,1,392,128]{3,2,1,0:T(8,128)(2,1)S(1)}, bf16[2,1,392,128]{3,2,1,0:T(8,128)(2,1)S(1)}, u32[]{:S(2)}, u32[]{:S(2)}) collective-permute-start(bf16[2,1,392,128]{3,2,1,0:T(8,128)(2,1)S(1)} %pad_maximum_fusion.8), channel_id=1, source_target_pairs={{0,8},{4,12},{8,0},{12,4},{16,24},{20,28},{24,16},{28,20},{1,9},{5... | collective-permute-start | bytes 602120 | tf_op jit(solution)/shard_map/ppermute | solution.py:659
  12.1 22.1 %copy-start.42 = (f32[1,128]{1,0:T(1,128)S(1)}, f32[1,128]{1,0:T(1,128)}, u32[]{:S(2)}) copy-start(f32[1,128]{1,0:T(1,128)} %get-tuple-element.65) | copy-start | bytes 1540
  12.1 71.7 %collective-permute-start.5 = (f32[1,128]{1,0:T(1,128)}, f32[1,128]{1,0:T(1,128)S(1)}, u32[]{:S(2)}, u32[]{:S(2)}) collective-permute-start(f32[1,128]{1,0:T(1,128)} %get-tuple-element.65), channel_id=1, source_target_pairs={{0,1},{1,0},{2,3},{3,2},{4,5},{5,4},{6,7},{7,6},{8,9},{9,8},{10,11... | collective-permute-start | bytes 1544 | tf_op jit(solution)/shard_map/ppermute | solution.py:659
  13.8 19.4 %collective-permute-start.2 = (bf16[4,1,392,128]{3,2,1,0:T(8,128)(2,1)S(1)}, bf16[4,1,392,128]{3,2,1,0:T(8,128)(2,1)S(1)}, u32[]{:S(2)}, u32[]{:S(2)}) collective-permute-start(bf16[4,1,392,128]{3,2,1,0:T(8,128)(2,1)S(1)} %pad_maximum_fusion.5), channel_id=1, source_target_pairs={{0,16},{4,20},{8,24},{12,28},{16,0},{20,4},{24,8},{28,12},{1,17},{... | collective-permute-start | bytes 1204232 | tf_op jit(solution)/shard_map/ppermute | solution.py:659
  34.2 4.3 %collective-permute-start.3 = (bf16[8,1,392,128]{3,2,1,0:T(8,128)(2,1)}, bf16[8,1,392,128]{3,2,1,0:T(8,128)(2,1)S(1)}, u32[]{:S(2)}, u32[]{:S(2)}) collective-permute-start(bf16[8,1,392,128]{3,2,1,0:T(8,128)(2,1)} %pad_maximum_fusion.3), channel_id=1, source_target_pairs={{0,1},{1,0},{2,3},{3,2},{4,5},{5,4},{6,7},{7,6},{8,9},{9,8},{10,11... | collective-permute-start | bytes 2408456 | tf_op jit(solution)/shard_map/ppermute | solution.py:659
  40.0 95.4 %collective-permute-start.4 = (bf16[8,2,392,128]{3,2,1,0:T(8,128)(2,1)}, bf16[8,2,392,128]{3,2,1,0:T(8,128)(2,1)}, u32[]{:S(2)}, u32[]{:S(2)}) collective-permute-start(bf16[8,2,392,128]{3,2,1,0:T(8,128)(2,1)} %pad_maximum_fusion.1), channel_id=1, source_target_pairs={{0,2},{1,3},{2,0},{3,1},{4,6},{5,7},{6,4},{7,5},{8,10},{9,11},{10,... | collective-permute-start | bytes 4816904 | tf_op jit(solution)/shard_map/ppermute | solution.py:659
  48.3 18.2 %copy-start = (f32[691,128]{1,0:T(8,128)}, f32[691,128]{1,0:T(8,128)S(1)}, u32[]{:S(2)}) copy-start(f32[691,128]{1,0:T(8,128)S(1)} %broadcast_in_dim.64.bias_ref) | copy-start | bytes 1061380
  66.6 68.9 %copy-start.34 = (bf16[8,1,392,128]{3,2,1,0:T(8,128)(2,1)S(1)}, bf16[8,1,392,128]{3,2,1,0:T(8,128)(2,1)}, u32[]{:S(2)}) copy-start(bf16[8,1,392,128]{3,2,1,0:T(8,128)(2,1)} %copy-done.33) | copy-start | bytes 2408452
  91.0 3.6 %collective-permute-start.6 = (f32[1,128]{1,0:T(1,128)S(1)}, f32[1,128]{1,0:T(1,128)S(1)}, u32[]{:S(2)}, u32[]{:S(2)}) collective-permute-start(f32[1,128]{1,0:T(1,128)S(1)} %select_select_fusion.4), channel_id=1, source_target_pairs={{0,2},{1,3},{2,0},{3,1},{4,6},{5,7},{6,4},{7,5},{8,10},{9,11},{10,... | collective-permute-start | bytes 1544 | tf_op jit(solution)/shard_map/ppermute | solution.py:659
  101.7 3.6 %collective-permute-start.7 = (f32[1,128]{1,0:T(1,128)S(1)}, f32[1,128]{1,0:T(1,128)S(1)}, u32[]{:S(2)}, u32[]{:S(2)}) collective-permute-start(f32[1,128]{1,0:T(1,128)S(1)} %select_select_fusion.3), channel_id=1, source_target_pairs={{0,4},{4,0},{8,12},{12,8},{16,20},{20,16},{24,28},{28,24},{1,5},{5... | collective-permute-start | bytes 1544 | tf_op jit(solution)/shard_map/ppermute | solution.py:659
  112.5 3.6 %collective-permute-start.8 = (f32[1,128]{1,0:T(1,128)S(1)}, f32[1,128]{1,0:T(1,128)S(1)}, u32[]{:S(2)}, u32[]{:S(2)}) collective-permute-start(f32[1,128]{1,0:T(1,128)S(1)} %select_select_fusion.2), channel_id=1, source_target_pairs={{0,8},{4,12},{8,0},{12,4},{16,24},{20,28},{24,16},{28,20},{1,9},{5... | collective-permute-start | bytes 1544 | tf_op jit(solution)/shard_map/ppermute | solution.py:659
  123.3 4.5 %collective-permute-start.9 = (f32[1,128]{1,0:T(1,128)S(1)}, f32[1,128]{1,0:T(1,128)S(1)}, u32[]{:S(2)}, u32[]{:S(2)}) collective-permute-start(f32[1,128]{1,0:T(1,128)S(1)} %select_select_fusion.1), channel_id=1, source_target_pairs={{0,16},{4,20},{8,24},{12,28},{16,0},{20,4},{24,8},{28,12},{1,17},{... | collective-permute-start | bytes 1544 | tf_op jit(solution)/shard_map/ppermute | solution.py:659
  138.7 10.7 %copy-start.37 = (bf16[576,64]{1,0:T(8,128)(2,1)S(1)}, bf16[576,64]{1,0:T(8,128)(2,1)}, u32[]{:S(2)}) copy-start(bf16[576,64]{1,0:T(8,128)(2,1)} %copy-done.36) | copy-start | bytes 221188
  149.3 47.6 %collective-permute-start.15 = (bf16[2,3136,128]{2,1,0:T(8,128)(2,1)}, bf16[2,3136,128]{2,1,0:T(8,128)(2,1)}, u32[]{:S(2)}, u32[]{:S(2)}) collective-permute-start(bf16[2,3136,128]{2,1,0:T(8,128)(2,1)} %get-tuple-element.81), channel_id=1, source_target_pairs={{0,1},{1,0},{2,3},{3,2},{4,5},{5,4},{6,7},{7,6},{8,9},{9,8},{10,11... | collective-permute-start | bytes 4816904 | tf_op jit(solution)/shard_map/ppermute | solution.py:659
  181.4 15.2 %copy-start.40 = (f32[19,512]{1,0:T(8,128)S(1)}, f32[19,512]{1,0:T(8,128)}, u32[]{:S(2)}) copy-start(f32[19,512]{1,0:T(8,128)} %get-tuple-element.74) | copy-start | bytes 116740
  181.4 15.2 %copy-start.45 = (f32[1,512]{1,0:T(1,128)S(1)}, f32[1,512]{1,0:T(1,128)}, u32[]{:S(2)}) copy-start(f32[1,512]{1,0:T(1,128)} %get-tuple-element.78) | copy-start | bytes 6148
  181.4 15.2 %copy-start.46 = (f32[1,64]{1,0:T(1,128)S(1)}, f32[1,64]{1,0:T(1,128)}, u32[]{:S(2)}) copy-start(f32[1,64]{1,0:T(1,128)} %get-tuple-element.77) | copy-start | bytes 772
  181.4 15.2 %copy-start.47 = (f32[1,19]{1,0:T(1,128)S(1)}, f32[1,19]{1,0:T(1,128)}, u32[]{:S(2)}) copy-start(f32[1,19]{1,0:T(1,128)} %get-tuple-element.79) | copy-start | bytes 232
  181.4 15.4 %copy-start.35 = (bf16[2,3136,128]{2,1,0:T(8,128)(2,1)S(1)}, bf16[2,3136,128]{2,1,0:T(8,128)(2,1)}, u32[]{:S(2)}) copy-start(bf16[2,3136,128]{2,1,0:T(8,128)(2,1)} %get-tuple-element.80) | copy-start | bytes 4816900
  199.6 29.7 %collective-permute-start.16 = (bf16[1,3136,128]{2,1,0:T(8,128)(2,1)}, bf16[1,3136,128]{2,1,0:T(8,128)(2,1)S(1)}, u32[]{:S(2)}, u32[]{:S(2)}) collective-permute-start(bf16[1,3136,128]{2,1,0:T(8,128)(2,1)} %slice.152), channel_id=1, source_target_pairs={{0,2},{1,3},{2,0},{3,1},{4,6},{5,7},{6,4},{7,5},{8,10},{9,11},{10,... | collective-permute-start | bytes 2408456 | tf_op jit(solution)/shard_map/ppermute | solution.py:659
  200.0 1.7 collective-permute-start.10
  201.7 26.0 %collective-permute-start.11 = (f32[88243]{0:T(1024)S(1)}, f32[88243]{0:T(1024)S(1)}, u32[]{:S(2)}, u32[]{:S(2)}) collective-permute-start(f32[88243]{0:T(1024)S(1)} %add.253), channel_id=1, source_target_pairs={{0,2},{1,3},{2,0},{3,1},{4,6},{5,7},{6,4},{7,5},{8,10},{9,11},{10,... | collective-permute-start | bytes 1058924 | tf_op jit(solution)/shard_map/ppermute | solution.py:659
  227.8 11.3 %collective-permute-start.12 = (f32[88243]{0:T(1024)S(1)}, f32[88243]{0:T(1024)S(1)}, u32[]{:S(2)}, u32[]{:S(2)}) collective-permute-start(f32[88243]{0:T(1024)S(1)} %add.254), channel_id=1, source_target_pairs={{0,4},{4,0},{8,12},{12,8},{16,20},{20,16},{24,28},{28,24},{1,5},{5... | collective-permute-start | bytes 1058924 | tf_op jit(solution)/shard_map/ppermute | solution.py:659
  229.6 19.3 %collective-permute-start.17 = (bf16[2,2,392,128]{3,2,0,1:T(8,128)(2,1)S(1)}, bf16[2,2,392,128]{3,2,0,1:T(8,128)(2,1)S(1)}, u32[]{:S(2)}, u32[]{:S(2)}) collective-permute-start(bf16[2,2,392,128]{3,2,0,1:T(8,128)(2,1)S(1)} %bitcast.160), channel_id=1, source_target_pairs={{0,4},{4,0},{8,12},{12,8},{16,20},{20,16},{24,28},{28,24},{1,5},{5... | collective-permute-start | bytes 1204232 | tf_op jit(solution)/shard_map/ppermute | solution.py:659
  239.1 7.7 %collective-permute-start.13 = (f32[88243]{0:T(1024)S(1)}, f32[88243]{0:T(1024)S(1)}, u32[]{:S(2)}, u32[]{:S(2)}) collective-permute-start(f32[88243]{0:T(1024)S(1)} %add.255), channel_id=1, source_target_pairs={{0,8},{4,12},{8,0},{12,4},{16,24},{20,28},{24,16},{28,20},{1,9},{5... | collective-permute-start | bytes 1058924 | tf_op jit(solution)/shard_map/ppermute | solution.py:659
  246.9 21.7 %collective-permute-start.14 = (f32[88243]{0:T(1024)S(1)}, f32[88243]{0:T(1024)}, u32[]{:S(2)}, u32[]{:S(2)}) collective-permute-start(f32[88243]{0:T(1024)S(1)} %add.256), channel_id=1, source_target_pairs={{0,16},{4,20},{8,24},{12,28},{16,0},{20,4},{24,8},{28,12},{1,17},{... | collective-permute-start | bytes 1058924 | tf_op jit(solution)/shard_map/ppermute | solution.py:659
  249.7 19.9 %collective-permute-start.18 = (bf16[2,392,128]{2,1,0:T(8,128)(2,1)}, bf16[2,392,128]{2,1,0:T(8,128)(2,1)S(1)}, u32[]{:S(2)}, u32[]{:S(2)}) collective-permute-start(bf16[2,392,128]{2,1,0:T(8,128)(2,1)} %dynamic-slice_bitcast_fusion), channel_id=1, source_target_pairs={{0,8},{4,12},{8,0},{12,4},{16,24},{20,28},{24,16},{28,20},{1,9},{5... | collective-permute-start | bytes 602120 | tf_op jit(solution)/shard_map/ppermute | solution.py:659
  270.4 18.3 %collective-permute-start.19 = (bf16[392,128]{1,0:T(8,128)(2,1)}, bf16[392,128]{1,0:T(8,128)(2,1)}, u32[]{:S(2)}, u32[]{:S(2)}) collective-permute-start(bf16[392,128]{1,0:T(8,128)(2,1)} %dynamic-slice_bitcast_fusion.1), channel_id=1, source_target_pairs={{0,16},{4,20},{8,24},{12,28},{16,0},{20,4},{24,8},{28,12},{1,17},{... | collective-permute-start | bytes 301064 | tf_op jit(solution)/shard_map/ppermute | solution.py:659
  276.2 10.8 %copy-start.23 = (f32[32,256]{1,0:T(8,128)}, f32[32,256]{1,0:T(8,128)S(1)}, u32[]{:S(2)}) copy-start(f32[32,256]{1,0:T(8,128)S(1)} %reshape.270.refs_1_) | copy-start | bytes 98308
  (36 other events, 204.7 us)

commit v2 on v1

v2 whole, which is shorter than its diff:
```python
import functools
import math

import jax
import jax.numpy as jnp
from jax import lax
from jax.experimental import pallas as pl
from jax.experimental.pallas import tpu as pltpu
from jax.sharding import PartitionSpec as P

STEP = 10
GAMMA = 0.99
LAMBDA = 0.95
CLIP = 0.1
ENTROPY_COEF = 0.01
VALUE_COEF = 0.5
BETA = 0.5
EPSILON = 1e-08
RATE = 1.0
BIAS_RATE = 0.1
HIGH = lax.Precision.HIGHEST
ROOT = math.sqrt(2.0 / math.pi)
CUBE = 0.044715
BF = jnp.bfloat16
F32 = jnp.float32
MIB = 2**20

NN = (((1,), (0,)), ((), ()))
NT = (((1,), (1,)), ((), ()))
TN = (((0,), (0,)), ((), ()))


def dot(a, b, dims=NN, precision=None):
    return lax.dot_general(a, b, dims, precision=precision, preferred_element_type=F32)


def params(limit=16, **more):
    return pltpu.CompilerParams(vmem_limit_bytes=limit * MIB, **more)


def cost(us):
    return pl.CostEstimate(flops=int(us * 1e9), bytes_accessed=0, transcendentals=0)


def near(shape, dtype):
    return pltpu.VMEM(shape, dtype)


def held(x):
    return pltpu.with_memory_space_constraint(x, pltpu.VMEM)


def far(x):
    return pltpu.with_memory_space_constraint(x, pltpu.HBM)


def vmem():
    return pl.BlockSpec(memory_space=pltpu.VMEM)


def smem():
    return pl.BlockSpec(memory_space=pltpu.SMEM)


def anywhere():
    return pl.BlockSpec(memory_space=pl.ANY)


def start_rows(source, target, sems):
    for r in range(source.shape[0]):
        pltpu.make_async_copy(source.at[r], target.at[r], sems.at[r]).start()


def start_row(source, target, sems, r):
    pltpu.make_async_copy(source.at[r], target.at[r], sems.at[r]).start()


def wait_row(source, target, sems, r):
    pltpu.make_async_copy(source.at[r], target.at[r], sems.at[r]).wait()


def wait_rows(source, target, sems):
    for r in range(source.shape[0]):
        wait_row(source, target, sems, r)


def dma(count):
    return pltpu.SemaphoreType.DMA((count,))


def gelu_both(x):
    x2 = x * x
    t = jnp.tanh(x * (ROOT + (ROOT * CUBE) * x2))
    h = 0.5 * x
    act = h + h * t
    slope = (0.5 + 0.5 * t) + h * (1.0 - t * t) * (ROOT + (3.0 * ROOT * CUBE) * x2)
    return act, slope


def wide(column, rows, n):
    k = column.shape[0]
    tall = jnp.concatenate([column] * (rows // k), axis=0) if rows > k else column
    return jnp.concatenate([tall] * (n // 128), axis=1)


def lanes(parts):
    return jnp.concatenate([p for p in parts if p.shape[1] > 0], axis=1)


def band_forward(w, kernel, feats, count):
    ch = w.shape[0]
    run = kernel * feats
    rows = []
    for j in range(count):
        parts = []
        for a in range(kernel):
            parts.append(jnp.zeros((ch, j * feats), F32))
            parts.append(w[:, a * run : (a + 1) * run])
            parts.append(jnp.zeros((ch, (count - 1 - j) * feats), F32))
        rows.append(lanes(parts))
    return jnp.concatenate(rows, axis=0).astype(BF)


def band_square(w, feats):
    ch = w.shape[0]
    rows = []
    for dy in range(2):
        for dx in range(2):
            lead = (dy * 3 + dx) * feats
            rows.append(
                lanes(
                    [
                        jnp.zeros((ch, lead), F32),
                        w[:, : 2 * feats],
                        jnp.zeros((ch, feats), F32),
                        w[:, 2 * feats :],
                        jnp.zeros((ch, 4 * feats - lead), F32),
                    ]
                )
            )
    return jnp.concatenate(rows, axis=0).astype(BF)


def band_back(w, kernel, feats, count):
    ch = w.shape[0]
    turned = w.T
    zero = jnp.zeros((feats, ch), F32)
    rows = []
    for i in range(count):
        parts = []
        for a in range(kernel):
            for j in range(kernel + count - 1):
                b = j - i
                if 0 <= b < kernel:
                    spot = ((kernel - 1 - a) * kernel + (kernel - 1 - b)) * feats
                    parts.append(turned[spot : spot + feats])
                else:
                    parts.append(zero)
        rows.append(lanes(parts))
    return jnp.concatenate(rows, axis=0).astype(BF)


def first_kernel(
    lengths_ref, dones_ref, rewards_ref, values_ref, weight_ref, bias_ref, adv_ref, piece_ref, bias_out_ref
):
    n = rewards_ref.shape[1]
    length = lengths_ref[0]
    position = lax.broadcasted_iota(jnp.int32, (8, n), 1)
    live = position < length
    mask = jnp.where(live, 1.0, 0.0)
    next_live = jnp.where(position + 1 < length, 1.0, 0.0)
    values = jnp.broadcast_to(values_ref[...], (8, n))
    rewards = jnp.broadcast_to(rewards_ref[...], (8, n))
    going = 1.0 - jnp.broadcast_to(dones_ref[...], (8, n)).astype(F32)

    def ahead(v, k, fill):
        return jnp.concatenate([v[:, k:], jnp.full((8, k), fill, F32)], axis=1)

    delta = rewards + GAMMA * going * ahead(values, 1, 0.0) * next_live - values
    total = mask * delta
    carry = mask * (GAMMA * LAMBDA) * going
    k = 1
    while k < n:
        total = total + carry * ahead(total, k, 0.0)
        carry = carry * ahead(carry, k, 0.0)
        k *= 2
    adv_ref[...] = total[0:1]
    count = jnp.sum(mask, axis=1, keepdims=True)
    mean = jnp.sum(mask * total, axis=1, keepdims=True) / count
    spread = jnp.sum(mask * (total - mean) ** 2, axis=1, keepdims=True)
    lane = lax.broadcasted_iota(jnp.int32, (8, 128), 1)
    stat = jnp.where(lane == 0, count, jnp.where(lane == 1, mean, jnp.where(lane == 2, spread, 0.0)))
    top = stat.astype(BF).astype(F32)
    mid = (stat - top).astype(BF).astype(F32)
    low = ((stat - top) - mid).astype(BF).astype(F32)
    line = lax.broadcasted_iota(jnp.int32, (8, 128), 0)
    terms = jnp.where(line == 0, top, jnp.where(line == 1, mid, jnp.where(line == 2, low, 0.0)))
    rows = weight_ref.shape[0]
    tail = piece_ref.shape[0] - 16
    piece_ref[...] = jnp.zeros_like(piece_ref)
    piece_ref[0:rows, :] = weight_ref[...].astype(BF)
    piece_ref[tail:, :] = jnp.concatenate([terms, jnp.zeros((8, 128), F32)], axis=0).astype(BF)
    size = bias_ref.shape[1]
    padded = bias_out_ref.shape[0]
    line = jnp.concatenate([bias_ref[...], jnp.zeros((1, padded - size), F32)], axis=1)
    bias_out_ref[...] = jnp.broadcast_to(line, (128, padded)).T


def first(lengths, dones, rewards, old_values, weight, bias):
    n = rewards.shape[1]
    rows = -(-weight.shape[0] // 16) * 16 + 16
    return pl.pallas_call(
        first_kernel,
        out_shape=(
            jax.ShapeDtypeStruct((1, n), F32),
            jax.ShapeDtypeStruct((rows, 128), BF),
            jax.ShapeDtypeStruct((-(-bias.shape[1] // 128) * 128, 128), F32),
        ),
        in_specs=[smem()] + [vmem()] * 5,
        out_specs=(vmem(),) * 3,
        cost_estimate=cost(3),
        name="first",
    )(lengths, dones, rewards, old_values, weight, bias)


def conv_one_kernel(
    frames_ref, weight_ref, bias_ref, act_ref, act_far_ref, slope_far_ref,
    band_ref, cells_ref, slope_ref, in_sems, act_sems, slope_sems,
):
    n = act_ref.shape[-1]
    half = act_ref.shape[0]
    step = pl.program_id(0)

    @pl.when(step == 0)
    def _():
        start_rows(frames_ref, cells_ref, in_sems)
        band_ref[...] = band_square(weight_ref[...], 64)
        wait_row(frames_ref, cells_ref, in_sems, 0)

    wait_row(frames_ref, cells_ref, in_sems, 2 * step + 1)
    wait_row(frames_ref, cells_ref, in_sems, 2 * step + 2)
    bias = wide(bias_ref[0:32, :], 128, n)
    for col in range(half):
        span = slice(col * 128, col * 128 + 192)
        patch = jnp.concatenate([cells_ref[2 * step + a, span, :] for a in range(3)], axis=0)
        act, slope = gelu_both(dot(band_ref[...], patch) + bias)
        act_ref[step, col] = act.astype(BF)
        slope_ref[step, col] = slope.astype(BF)
    start_row(act_ref, act_far_ref, act_sems, step)
    start_row(slope_ref, slope_far_ref, slope_sems, step)

    @pl.when(step == half - 1)
    def _():
        wait_rows(act_ref, act_far_ref, act_sems)
        wait_rows(slope_ref, slope_far_ref, slope_sems)


def conv_one(frames, weight, bias):
    grid, _, n = frames.shape
    half = grid // 2
    shape = (half, half, 128, n)
    return pl.pallas_call(
        conv_one_kernel,
        out_shape=(near(shape, BF), pltpu.HBM(shape, BF), pltpu.HBM(shape, BF)),
        grid=(half,),
        in_specs=[anywhere(), vmem(), vmem()],
        out_specs=(vmem(), anywhere(), anywhere()),
        scratch_shapes=[
            pltpu.VMEM((128, 576), BF),
            pltpu.VMEM(frames.shape, BF),
            pltpu.VMEM(shape, BF),
            dma(grid),
            dma(half),
            dma(half),
        ],
        compiler_params=params(36),
        cost_estimate=cost(12),
        name="conv_one",
    )(far(frames), weight, bias)


def conv_two_kernel(
    one_ref, weight_ref, bias_ref, act_ref, act_far_ref, slope_far_ref,
    band_ref, slope_ref, act_sems, slope_sems,
):
    n = act_ref.shape[-1]
    step = pl.program_id(0)

    @pl.when(step == 0)
    def _():
        band_ref[...] = band_forward(weight_ref[...], 2, 128, 3)

    bias = wide(bias_ref[32:96, :], 192, n)
    for part in range(3):
        span = slice(3 * part, 3 * part + 4)
        patch = jnp.concatenate(
            [one_ref[step + a, span].reshape(512, n) for a in range(2)], axis=0
        )
        act, slope = gelu_both(dot(band_ref[...], patch) + bias)
        rows = slice(part * 192, part * 192 + 192)
        act_ref[step, rows, :] = act.astype(BF)
        slope_ref[step, rows, :] = slope.astype(BF)
    start_row(act_ref, act_far_ref, act_sems, step)
    start_row(slope_ref, slope_far_ref, slope_sems, step)

    @pl.when(step == 8)
    def _():
        wait_rows(act_ref, act_far_ref, act_sems)
        wait_rows(slope_ref, slope_far_ref, slope_sems)


def conv_two(act_one, weight, bias):
    n = act_one.shape[-1]
    shape = (9, 576, n)
    return pl.pallas_call(
        conv_two_kernel,
        out_shape=(near(shape, BF), pltpu.HBM(shape, BF), pltpu.HBM(shape, BF)),
        grid=(9,),
        in_specs=[vmem()] * 3,
        out_specs=(vmem(), anywhere(), anywhere()),
        scratch_shapes=[pltpu.VMEM((192, 1024), BF), pltpu.VMEM(shape, BF), dma(9), dma(9)],
        compiler_params=params(24),
        cost_estimate=cost(7),
        name="conv_two",
    )(held(act_one), weight, bias)


def conv_three_kernel(two_ref, weight_ref, bias_ref, flat_ref, slope_ref, band_ref):
    n = flat_ref.shape[-1]
    step = pl.program_id(0)

    @pl.when(step == 0)
    def _():
        band_ref[...] = band_forward(weight_ref[...], 3, 64, 4)

    bias = wide(bias_ref[96:160, :], 256, n)
    for drop, start in ((0, 0), (1, 3)):
        patch = jnp.concatenate(
            [two_ref[step + a, start * 64 : start * 64 + 384, :] for a in range(3)], axis=0
        )
        pre = dot(band_ref[drop * 64 :, :], patch) + bias[drop * 64 :]
        act, slope = gelu_both(pre)
        rows = pl.ds(pl.multiple_of(step * 448, 64) + (start + drop) * 64, 256 - drop * 64)
        flat_ref[rows, :] = act.astype(BF)
        slope_ref[rows, :] = slope.astype(BF)


def conv_three(act_two, weight, bias):
    n = act_two.shape[-1]
    shape = near((3136, n), BF)
    return pl.pallas_call(
        conv_three_kernel,
        out_shape=(shape, shape),
        grid=(7,),
        in_specs=[vmem()] * 3,
        out_specs=(vmem(), vmem()),
        scratch_shapes=[pltpu.VMEM((256, 1152), BF)],
        compiler_params=params(),
        cost_estimate=cost(5),
        name="conv_three",
    )(held(act_two), weight, bias)


def head_gradient(heads, actions, adv, values, old_logp, mask, count, centre, var):
    rows, n = heads.shape
    acts = rows - 1
    norm_adv = (adv - centre) * lax.rsqrt(var + 1e-05)
    returns = adv + values
    index = lax.broadcasted_iota(jnp.int32, (rows, n), 0)
    is_logit = index < acts
    top = jnp.max(jnp.where(is_logit, heads, -jnp.inf), axis=0, keepdims=True)
    shifted = heads - top
    grown = jnp.where(is_logit, jnp.exp(jnp.where(is_logit, shifted, 0.0)), 0.0)
    total = jnp.sum(grown, axis=0, keepdims=True)
    logp_all = jnp.where(is_logit, shifted - jnp.log(total), 0.0)
    prob = jnp.where(is_logit, jnp.exp(logp_all), 0.0)
    chosen = jnp.where(index == actions, 1.0, 0.0)
    logp = jnp.sum(logp_all * chosen, axis=0, keepdims=True)
    plogp = jnp.sum(prob * logp_all, axis=0, keepdims=True)
    value = jnp.sum(jnp.where(index == acts, heads, 0.0), axis=0, keepdims=True)
    ratio = jnp.exp(logp - old_logp)
    bent = jnp.tanh((ratio - 1.0) / CLIP)
    soft = 1.0 + CLIP * bent
    plain = ratio * norm_adv
    clipped = soft * norm_adv
    share = jnp.where(plain < clipped, 1.0, jnp.where(plain > clipped, 0.0, 0.5))
    by_ratio = -norm_adv * (share + (1.0 - share) * (1.0 - bent * bent))
    scale = mask / count
    by_logp = by_ratio * ratio
    by_logit = by_logp * (chosen - prob) + ENTROPY_COEF * prob * (logp_all - plogp)
    by_value = VALUE_COEF * (value - returns)
    return jnp.where(is_logit, by_logit, by_value) * scale


def dense_kernel(*refs, places, n_dp, n_own, rows):
    place_ref, lengths_ref, flat_ref, slope_three_ref, heads_ref, bias_ref = refs[:6]
    actions_ref, adv_ref, values_ref, logp_ref = refs[6:10]
    piece_refs = refs[10 : 10 + len(places)]
    d_three_ref, keep_ref, send_ref, grad_heads_ref, sums_ref, sum_heads_ref = refs[10 + len(places) : -4]
    blocks_ref, weight_ref, d_dense_ref, sems = refs[-4:]
    n = flat_ref.shape[-1]
    cols = 128
    dp, own = place_ref[0], place_ref[1]
    stats = []
    copies = []
    for ref, spots in zip(piece_refs, places):
        for k, (i, j) in enumerate(spots):
            copies.append(
                pltpu.make_async_copy(ref.at[k], blocks_ref.at[i ^ dp, j ^ own], sems.at[len(copies)])
            )
    for copy in copies:
        copy.start()
    for copy in copies:
        copy.wait()
    for i in range(n_dp):
        for j in range(n_own):
            tail = blocks_ref[i, j, blocks_ref.shape[2] - 16 :].astype(F32)
            stats.append((tail[0:1] + tail[1:2]) + tail[2:3])
    stats = jnp.concatenate(stats, axis=0)
    each = stats[:, 0:1]
    count = jnp.sum(each, axis=0, keepdims=True)
    centre = jnp.sum(each * stats[:, 1:2], axis=0, keepdims=True) / count
    gap = stats[:, 1:2] - centre
    var = jnp.sum(stats[:, 2:3] + each * gap * gap, axis=0, keepdims=True) / count
    for i in range(n_dp):
        for j in range(n_own):
            weight_ref[i * rows : (i + 1) * rows, j * cols : (j + 1) * cols] = blocks_ref[i, j, 0:rows]
    hid = n_own * cols
    bias_dense = wide(bias_ref[160 : 160 + hid, :], hid, n)
    bias_heads = wide(bias_ref[160 + hid : 160 + hid + 19, :], 19, n)
    pre = dot(weight_ref[...], flat_ref[...], TN) + bias_dense
    hidden, slope = gelu_both(pre)
    hidden = hidden.astype(BF)
    head_weight = heads_ref[...].astype(BF)
    heads = dot(head_weight, hidden) + bias_heads
    position = lax.broadcasted_iota(jnp.int32, (1, n), 1)
    mask = jnp.where(position < lengths_ref[0], 1.0, 0.0)
    d_heads = head_gradient(
        heads, actions_ref[...], adv_ref[...], values_ref[...], logp_ref[...], mask, count, centre, var
    ).astype(BF)
    ones = jnp.ones((8, n), BF)
    grad_heads_ref[...] = dot(d_heads, hidden, NT)
    sum_heads_ref[...] = dot(ones, d_heads, NT)[0:1]
    d_dense = (dot(head_weight, d_heads, TN) * slope).astype(BF)
    sums_ref[0:1, 128 : 128 + hid] = dot(ones, d_dense, NT)[0:1]
    for j in range(n_own):
        d_dense_ref[j] = d_dense[j * cols : (j + 1) * cols]
    for half, ref in ((0, keep_ref), (1, send_ref)):
        for k in range(n_own // 4):
            both = [d_dense_ref[own ^ (4 * k + half)], d_dense_ref[own ^ (4 * k + 2 + half)]]
            block = dot(flat_ref[...], jnp.concatenate(both, axis=0), NT).astype(BF)
            for i in range(n_dp):
                rel = i ^ dp
                spot = (rel % 2) * (n_dp // 2) + rel // 2
                for m in range(2):
                    ref[2 * k + m, spot] = block[i * rows : (i + 1) * rows, m * cols : (m + 1) * cols]
    total = jnp.zeros((64, n), F32)
    for part in range(7):
        span = slice(part * 448, part * 448 + 448)
        d_three = (dot(weight_ref[span, :], d_dense) * slope_three_ref[span, :].astype(F32)).astype(BF)
        d_three_ref[span, :] = d_three
        back = d_three.astype(F32)
        for c in range(7):
            total = total + back[c * 64 : c * 64 + 64]
    sums_ref[0:1, 0:64] = dot(jnp.ones((8, n), F32), total, NT, HIGH)[0:1]
    sums_ref[0:1, 64:128] = jnp.zeros((1, 64), F32)


def dense(place, lengths, flat, slope_three, heads, bias, actions, adv, values, logp, pieces, n_dp, n_own, rows):
    n = flat.shape[-1]
    hid = n_own * 128
    full = n_dp * rows
    part = jax.ShapeDtypeStruct((n_own // 2, n_dp, rows, 128), BF)
    arrays = [p[0] for p in pieces]
    body = functools.partial(
        dense_kernel, places=[p[1] for p in pieces], n_dp=n_dp, n_own=n_own, rows=rows
    )
    return pl.pallas_call(
        body,
        out_shape=(
            near((full, n), BF),
            part,
            part,
            jax.ShapeDtypeStruct(heads.shape, F32),
            jax.ShapeDtypeStruct((1, 128 + hid), F32),
            jax.ShapeDtypeStruct((1, heads.shape[0]), F32),
        ),
        in_specs=[smem(), smem()] + [vmem()] * 8 + [anywhere()] * len(arrays),
        out_specs=(vmem(),) * 6,
        scratch_shapes=[
            pltpu.VMEM((n_dp, n_own) + arrays[0].shape[1:], BF),
            pltpu.VMEM((full, hid), BF),
            pltpu.VMEM((n_own, 128, n), BF),
            dma(n_dp * n_own),
        ],
        compiler_params=params(32),
        cost_estimate=cost(8),
        name="dense",
    )(place, lengths, held(flat), held(slope_three), heads, bias, actions, adv, values, logp, *arrays)


def conv_three_back_kernel(
    d_three_ref, act_far_ref, slope_far_ref, weight_ref, heads_ref,
    d_two_ref, pack_ref, sum_ref,
    band_ref, pad_ref, acc_ref, tot_ref, act_ref, slope_ref, act_sems, slope_sems,
):
    n = d_three_ref.shape[-1]
    step = pl.program_id(0)

    @pl.when(step == 0)
    def _():
        for r in range(9):
            start_row(slope_far_ref, slope_ref, slope_sems, r)
            start_row(act_far_ref, act_ref, act_sems, r)
        band_ref[...] = band_back(weight_ref[...], 3, 64, 3)
        pad_ref[...] = jnp.zeros_like(pad_ref)
        acc_ref[...] = jnp.zeros_like(acc_ref)
        tot_ref[...] = jnp.zeros_like(tot_ref)
        for r in range(7):
            pad_ref[r + 2, 128 : 128 + 448, :] = d_three_ref[r * 448 : r * 448 + 448, :]
        wait_row(act_far_ref, act_ref, act_sems, 0)
        wait_row(act_far_ref, act_ref, act_sems, 1)

    wait_row(slope_far_ref, slope_ref, slope_sems, step)
    total = tot_ref[...]
    for part in range(3):
        patch = jnp.concatenate(
            [pad_ref[step + a, part * 192 : part * 192 + 320, :] for a in range(3)], axis=0
        )
        rows = slice(part * 192, part * 192 + 192)
        d_two = (dot(band_ref[...], patch) * slope_ref[step, rows, :].astype(F32)).astype(BF)
        d_two_ref[step, rows, :] = d_two
        back = d_two.astype(F32)
        total = total + (back[0:64] + back[64:128]) + back[128:192]
    tot_ref[...] = total

    @pl.when(step < 7)
    def _():
        wait_row(act_far_ref, act_ref, act_sems, step + 2)
        row = pad_ref[step + 2, 128 : 128 + 448, :]
        second = jnp.concatenate([jnp.zeros((64, n), BF), row[256:448]], axis=0)
        for d_rows, start in ((row[0:256], 0), (second, 3)):
            span = slice(start * 64, start * 64 + 384)
            cells = jnp.concatenate([act_ref[step + a, span, :] for a in range(3)], axis=0)
            acc_ref[...] += dot(d_rows, cells, NT)

    @pl.when(step == 8)
    def _():
        for a in range(3):
            out = None
            for c in range(4):
                piece = acc_ref[c * 64 : c * 64 + 64, a * 384 + c * 64 : a * 384 + c * 64 + 192]
                out = piece if out is None else out + piece
            pack_ref[0:64, a * 192 : a * 192 + 192] = out.astype(BF)
        pack_ref[0:64, 576:640] = jnp.zeros((64, 64), BF)
        pack_ref[64:80, 0:512] = heads_ref[0:16, :].astype(BF)
        pack_ref[80:96, 0:512] = jnp.concatenate(
            [heads_ref[16:19, :], jnp.zeros((13, 512), F32)], axis=0
        ).astype(BF)
        pack_ref[64:96, 512:640] = jnp.zeros((32, 128), BF)
        sum_ref[...] = dot(jnp.ones((8, n), F32), tot_ref[...], NT, HIGH)[0:1]


def conv_three_back(d_three, act_two, slope_two, weight, heads):
    n = act_two.shape[-1]
    return pl.pallas_call(
        conv_three_back_kernel,
        out_shape=(
            near(act_two.shape, BF),
            jax.ShapeDtypeStruct((96, 640), BF),
            jax.ShapeDtypeStruct((1, 64), F32),
        ),
        grid=(9,),
        in_specs=[vmem(), anywhere(), anywhere(), vmem(), vmem()],
        out_specs=(vmem(),) * 3,
        scratch_shapes=[
            pltpu.VMEM((192, 960), BF),
            pltpu.VMEM((11, 704, n), BF),
            pltpu.VMEM((256, 1152), F32),
            pltpu.VMEM((64, n), F32),
            pltpu.VMEM(act_two.shape, BF),
            pltpu.VMEM(act_two.shape, BF),
            dma(9),
            dma(9),
        ],
        compiler_params=params(24),
        cost_estimate=cost(9),
        name="conv_three_back",
    )(held(d_three), act_two, slope_two, weight, heads)


def conv_two_back_kernel(
    d_two_ref, act_far_ref, slope_far_ref, weight_ref, d_one_ref, d_far_ref, grad_ref, sum_ref,
    band_ref, pad_ref, acc_ref, tot_ref, act_ref, slope_ref, act_sems, slope_sems, out_sems,
):
    n = d_one_ref.shape[-1]
    step = pl.program_id(0)

    @pl.when(step == 0)
    def _():
        for r in range(10):
            start_row(slope_far_ref, slope_ref, slope_sems, r)
            start_row(act_far_ref, act_ref, act_sems, r)
        band_ref[...] = band_back(weight_ref[...], 2, 128, 1)
        pad_ref[...] = jnp.zeros_like(pad_ref)
        acc_ref[...] = jnp.zeros_like(acc_ref)
        tot_ref[...] = jnp.zeros_like(tot_ref)
        for r in range(9):
            pad_ref[r + 1, 64 : 64 + 576, :] = d_two_ref[r]
        wait_row(act_far_ref, act_ref, act_sems, 0)

    wait_row(slope_far_ref, slope_ref, slope_sems, step)
    total = tot_ref[...]
    for col in range(10):
        patch = jnp.concatenate(
            [pad_ref[step + a, col * 64 : col * 64 + 128, :] for a in range(2)], axis=0
        )
        d_one = (dot(band_ref[...], patch) * slope_ref[step, col].astype(F32)).astype(BF)
        d_one_ref[step, col] = d_one
        total = total + d_one.astype(F32)
    tot_ref[...] = total
    start_row(d_one_ref, d_far_ref, out_sems, step)

    @pl.when(step < 9)
    def _():
        wait_row(act_far_ref, act_ref, act_sems, step + 1)
        for part in range(3):
            span = slice(3 * part, 3 * part + 4)
            cells = jnp.concatenate(
                [act_ref[step + a, span].reshape(512, n) for a in range(2)], axis=0
            )
            rows = pad_ref[step + 1, 64 + part * 192 : 64 + part * 192 + 192, :]
            acc_ref[...] += dot(rows, cells, NT)

    @pl.when(step == 9)
    def _():
        wait_rows(d_one_ref, d_far_ref, out_sems)
        for a in range(2):
            out = None
            for c in range(3):
                piece = acc_ref[c * 64 : c * 64 + 64, a * 512 + c * 128 : a * 512 + c * 128 + 256]
                out = piece if out is None else out + piece
            grad_ref[:, a * 256 : a * 256 + 256] = out.astype(BF)
        sums = dot(jnp.ones((8, n), F32), tot_ref[...], NT, HIGH)[0:1]
        sum_ref[...] = (sums[:, 0:32] + sums[:, 32:64]) + (sums[:, 64:96] + sums[:, 96:128])


def conv_two_back(d_two, act_one, slope_one, weight):
    n = act_one.shape[-1]
    shape = act_one.shape
    return pl.pallas_call(
        conv_two_back_kernel,
        out_shape=(
            near(shape, BF),
            pltpu.HBM(shape, BF),
            jax.ShapeDtypeStruct((64, 512), BF),
            jax.ShapeDtypeStruct((1, 32), F32),
        ),
        grid=(10,),
        in_specs=[vmem(), anywhere(), anywhere(), vmem()],
        out_specs=(vmem(), anywhere(), vmem(), vmem()),
        scratch_shapes=[
            pltpu.VMEM((128, 256), BF),
            pltpu.VMEM((11, 704, n), BF),
            pltpu.VMEM((192, 1024), F32),
            pltpu.VMEM((128, n), F32),
            pltpu.VMEM(shape, BF),
            pltpu.VMEM(shape, BF),
            dma(10),
            dma(10),
            dma(10),
        ],
        compiler_params=params(32),
        cost_estimate=cost(11),
        name="conv_two_back",
    )(held(d_two), act_one, slope_one, weight)


def conv_one_grad_kernel(
    frames_ref, d_one_ref, dense_ref, heads_ref, one_ref, two_ref, grad_ref, acc_ref, cells_ref, sems
):
    n = d_one_ref.shape[-1]
    step = pl.program_id(0)

    @pl.when(step == 0)
    def _():
        start_rows(frames_ref, cells_ref, sems)
        acc_ref[...] = jnp.zeros_like(acc_ref)
        wait_row(frames_ref, cells_ref, sems, 0)

    wait_row(frames_ref, cells_ref, sems, 2 * step + 1)
    wait_row(frames_ref, cells_ref, sems, 2 * step + 2)
    for pair in range(d_one_ref.shape[1] // 2):
        span = slice(pair * 256, pair * 256 + 320)
        cells = jnp.concatenate([cells_ref[2 * step + a, span, :] for a in range(3)], axis=0)
        rows = d_one_ref[step, 2 * pair : 2 * pair + 2].reshape(256, n)
        acc_ref[...] += dot(rows, cells, NT)

    @pl.when(step == pl.num_programs(0) - 1)
    def _():
        for a in range(2):
            out = None
            for k in range(2):
                for dy in range(2):
                    for dx in range(2):
                        row = ((k * 2 + dy) * 2 + dx) * 32
                        lane = (dy + a) * 320 + (2 * k + dx) * 64
                        piece = acc_ref[row : row + 32, lane : lane + 128]
                        out = piece if out is None else out + piece
            grad_ref[0:32, a * 128 : a * 128 + 128] = out
        grad_ref[32:40, :] = jnp.zeros((8, 256), F32)
        grad_ref[32:33, :] = dense_ref[0:1, 128:384]
        grad_ref[33:34, :] = dense_ref[0:1, 384:640]
        grad_ref[34:35, 0:64] = dense_ref[0:1, 0:64]
        grad_ref[35:36, 0:64] = two_ref[...]
        grad_ref[36:37, 0:32] = one_ref[...]
        grad_ref[37:38, 0:19] = heads_ref[...]


def conv_one_grad(frames, d_one, sums, sum_heads, sum_one, sum_two):
    return pl.pallas_call(
        conv_one_grad_kernel,
        out_shape=jax.ShapeDtypeStruct((40, 256), F32),
        grid=(d_one.shape[0],),
        in_specs=[anywhere()] + [vmem()] * 5,
        out_specs=vmem(),
        scratch_shapes=[
            pltpu.VMEM((256, 960), F32),
            pltpu.VMEM(frames.shape, BF),
            dma(frames.shape[0]),
        ],
        compiler_params=params(24),
        cost_estimate=cost(10),
        name="conv_one_grad",
    )(far(frames), held(d_one), sums, sum_heads, sum_one, sum_two)


def frames_back_kernel(*refs, begin, end, total):
    d_one_ref, weight_ref = refs[:2]
    out_ref, band_ref, here_ref, rows_ref, in_sems, out_sems = refs[-6:]
    n = rows_ref.shape[-1]
    step = pl.program_id(0)
    cells = here_ref.shape[1]
    zero = jnp.zeros((32, n), BF)
    lead = begin - 1
    kept = range(max(lead, 0), min(end, total - 1))

    def fetch(r):
        return pltpu.make_async_copy(d_one_ref.at[r], here_ref.at[r - lead], in_sems.at[r - lead])

    @pl.when(step == 0)
    def _():
        for r in kept:
            fetch(r).start()
        band_ref[...] = band_back(weight_ref[...], 2, 64, 3)
        if begin == 0:
            here_ref[0] = jnp.zeros_like(here_ref[0])
        else:
            fetch(lead).wait()
        if end == total:
            here_ref[end - 1 - lead] = jnp.zeros_like(here_ref[0])

    @pl.when(step + begin < total - 1)
    def _():
        fetch(step + begin).wait()

    def slab(at, dy, first):
        parts = []
        for c in range(first, first + 4):
            if c < 0 or c >= 2 * cells:
                parts.append(zero)
            else:
                spot = (dy * 2 + c % 2) * 32
                parts.append(here_ref[at, c // 2, spot : spot + 32, :])
        return jnp.concatenate(parts, axis=0)

    def row(up, low, at):
        for block in range(7):
            first = 3 * block - 1
            patch = jnp.concatenate([slab(*up, first), slab(*low, first)], axis=0)
            rows_ref[at, block * 192 : block * 192 + 192, :] = dot(band_ref[...], patch).astype(BF)

    def send(at):
        return pltpu.make_async_copy(rows_ref.at[at], out_ref.at[at + 2 * begin], out_sems.at[at])

    row((step, 1), (step + 1, 0), 2 * step)
    send(2 * step).start()

    @pl.when(step + begin < total - 1)
    def _():
        row((step + 1, 0), (step + 1, 1), 2 * step + 1)
        send(2 * step + 1).start()

    @pl.when(step == end - begin - 1)
    def _():
        for at in range(min(2 * end, 2 * total - 1) - 2 * begin):
            send(at).wait()


def frames_back(d_one, weight, shape, begin, end, so_far=None):
    total = d_one.shape[0] + 1
    old = [] if so_far is None else [so_far]
    count = end - begin
    return pl.pallas_call(
        functools.partial(frames_back_kernel, begin=begin, end=end, total=total),
        out_shape=pltpu.HBM(shape, BF),
        grid=(count,),
        in_specs=[anywhere(), vmem()] + [anywhere()] * len(old),
        out_specs=anywhere(),
        scratch_shapes=[
            pltpu.VMEM((192, 256), BF),
            pltpu.VMEM((count + 1,) + d_one.shape[1:], BF),
            pltpu.VMEM((2 * count,) + shape[1:], BF),
            dma(count + 1),
            dma(2 * count),
        ],
        input_output_aliases={2: 0} if old else {},
        compiler_params=params(24),
        cost_estimate=cost(count),
        name="frames_back",
    )(far(d_one), weight, *old)


def adam_terms(grad, mean, square):
    momentum = BETA * mean + (1.0 - BETA) * grad
    variance = BETA * square + (1.0 - BETA) * grad * grad
    fix = 1.0 - BETA**STEP
    direction = momentum / fix / (jnp.sqrt(variance / fix) + EPSILON)
    return (momentum, variance, direction)


def split(x):
    top = x.astype(BF)
    return top, (x - top.astype(F32)).astype(BF)


def dot3(a, b, dims=NN):
    a_top, a_low = split(a)
    b_top, b_low = split(b)
    return dot(a_top, b_top, dims) + (dot(a_top, b_low, dims) + dot(a_low, b_top, dims))


def turned_step(weight, grad, mean, square, left, right):
    rate = RATE / math.sqrt(weight.shape[1])
    turned = dot3(dot3(right, grad, TN), left)
    momentum, variance, direction = adam_terms(turned, mean, square)
    back = dot3(dot3(right, direction), left, NT)
    return momentum, variance, weight - rate * back


def steps_kernel(*refs, spots):
    count = len(spots)
    packs = 1 + max(spot[0] for spot in spots)
    ins, outs = refs[packs : packs + 5 * count], refs[packs + 5 * count :]
    for w, (pack, row, rows, cols) in enumerate(spots):
        grad = refs[pack][row : row + rows, 0:cols]
        weight, mean, square, left, right = [ref[...] for ref in ins[5 * w : 5 * w + 5]]
        results = (grad,) + turned_step(weight, grad, mean, square, left, right)
        for ref, value in zip(outs[4 * w : 4 * w + 4], results):
            ref[...] = value


def steps(packs, spots, groups):
    arrays = []
    shapes = []
    for weight, mean, square, left, right in groups:
        arrays += [weight.T, mean.T, square.T, left, right]
        shapes += [jax.ShapeDtypeStruct(weight.shape[::-1], F32)] * 4
    return pl.pallas_call(
        functools.partial(steps_kernel, spots=spots),
        out_shape=tuple(shapes),
        in_specs=[vmem()] * (len(packs) + len(arrays)),
        out_specs=(vmem(),) * len(shapes),
        compiler_params=params(24),
        cost_estimate=cost(5),
        name="steps",
    )(*packs, *arrays)


def dense_step_kernel(*refs, rate):
    weight_ref, mean_ref, square_ref, block_ref = refs[:4]
    grad_ref, mom_ref, var_ref, new_ref = refs[-4:]
    grad = None
    for ref in refs[4:-4]:
        part = ref[...].astype(F32)
        grad = part if grad is None else grad + part
    grad_ref[...] = grad
    turned = dot3(grad, block_ref[0])
    momentum, variance, direction = adam_terms(turned, mean_ref[...], square_ref[...])
    mom_ref[...] = momentum
    var_ref[...] = variance
    new_ref[...] = weight_ref[...] - rate * dot3(direction, block_ref[0], NT)


def dense_step(weight, mean, square, block, parts, rate):
    shape = jax.ShapeDtypeStruct(weight.shape, F32)
    return pl.pallas_call(
        functools.partial(dense_step_kernel, rate=rate),
        out_shape=(shape,) * 4,
        in_specs=[vmem()] * (4 + len(parts)),
        out_specs=(vmem(),) * 4,
        compiler_params=params(),
        cost_estimate=cost(3),
        name="dense_step",
    )(weight, mean, square, block, *parts)


def swap(x, axis, bit, size):
    return lax.ppermute(x, axis, [(i, i ^ bit) for i in range(size)])


def bits_of(size):
    return [1 << b for b in range(size.bit_length() - 1)]


def after(x, *others):
    return lax.optimization_barrier((x,) + others)[0]


def stage(x, axis, bits, size):
    if len(bits) == 1:
        return [swap(x, axis, bits[0], size)]
    one, two = bits
    return [swap(x, axis, bit, size) for bit in (one, two, one | two)]


def stage_sum(x, came):
    up = [v.astype(F32) for v in [x] + came]
    if len(up) == 2:
        return up[0] + up[1]
    return (up[0] + up[1]) + (up[2] + up[3])


def sum_stages(n_dp, n_own):
    bits = bits_of(n_dp)
    plan = [("own", tuple(bits_of(n_own)), n_own)]
    if len(bits) % 2:
        plan += [("dp", tuple(bits[k : k + 2]), n_dp) for k in range(1, len(bits), 2)]
        plan.append(("dp", (bits[0],), n_dp))
    else:
        plan += [("dp", tuple(bits[k : k + 2]), n_dp) for k in range(0, len(bits), 2)]
    return plan


def add_low(*terms):
    total = terms[0].astype(F32)
    for term in terms[1:]:
        total = total + term.astype(F32)
    return total.astype(BF)


def plain_gather(piece, n_dp, n_own):
    pieces = piece[None]
    spots = [(0, 0)]
    for bit in bits_of(n_dp):
        pieces = jnp.concatenate([pieces, swap(pieces, "dp", bit, n_dp)], axis=0)
        spots = spots + [(i ^ bit, j) for i, j in spots]
    for bit in bits_of(n_own):
        pieces = jnp.concatenate([pieces, swap(pieces, "own", bit, n_own)], axis=0)
        spots = spots + [(i, j ^ bit) for i, j in spots]
    return [(pieces, spots)]


def plain_scatter(keep, send, n_dp, n_own):
    block = add_low(keep, swap(send, "own", 1, n_own))
    bit = n_own // 2
    while bit > 1:
        half = block.shape[0] // 2
        block = add_low(block[:half], swap(block[half:], "own", bit, n_own))
        bit //= 2
    block = block[0]
    for bit in [1] + bits_of(n_dp)[:0:-1]:
        half = block.shape[0] // 2
        block = add_low(block[:half], swap(block[half:], "dp", bit, n_dp))
    return [block[0]]


def shards(
    frames, actions, dones, lengths, rewards, old_values, old_logp,
    conv_first, conv_second, conv_third, dense_hidden, dense_heads, bias_all,
    mean_first, mean_second, mean_third, mean_dense, mean_heads, mean_bias,
    square_first, square_second, square_third, square_dense, square_heads, square_bias,
    left_first, right_first, left_second, right_second, left_third, right_third,
    right_dense, left_heads, right_heads, *, n_dp, n_own,
):
    tokens, grid = frames.shape[0], frames.shape[1]
    planes = frames.shape[3]
    rows = dense_hidden.shape[0]
    tuned = (n_dp, n_own) == (8, 4)
    own_swap = lambda x, bit: swap(x, "own", bit, n_own)
    dp_swap = lambda x, bit: swap(x, "dp", bit, n_dp)
    place = jnp.stack([lax.axis_index("dp"), lax.axis_index("own")]).astype(jnp.int32)
    bias_row = bias_all.reshape(1, -1)
    adv, piece, bias = first(lengths, dones, rewards, old_values, dense_hidden, bias_row)
    cells = frames.transpose(1, 2, 3, 0).reshape(grid, grid * planes, tokens)

    if tuned:
        along_z = [dp_swap(piece, 2 * k) for k in (1, 2, 3)]
    act_one, act_one_far, slope_one = conv_one(cells, conv_first.T, bias)
    if tuned:
        z_spots = [[(0, 0), (2, 0)], [(4, 0), (6, 0)]]
        piece = after(piece, act_one_far)
        z_parts = [jnp.stack([piece, along_z[0]]), jnp.stack([along_z[1], along_z[2]])]
        act_one = after(act_one, *z_parts)
        x_parts = [dp_swap(z, 1) for z in z_parts]
        y_parts = [own_swap(z, 2) for z in z_parts]
        pieces = list(zip(z_parts, z_spots))
        pieces += [(own_swap(z, 1), [(i, j ^ 1) for i, j in sp]) for z, sp in pieces]
    else:
        pieces = plain_gather(piece, n_dp, n_own)
    act_two, act_two_far, slope_two = conv_two(act_one, conv_second.T, bias)
    if tuned:
        act_two, *arrived = lax.optimization_barrier((act_two, *x_parts, *y_parts))
        x_parts, y_parts = arrived[:2], arrived[2:]
        corner = [own_swap(x_parts[0], 2), dp_swap(y_parts[1], 1)]
        for parts, flip in ((x_parts, (1, 0)), (y_parts, (0, 2))):
            for part, spots in zip(parts, z_spots):
                spots = [(i ^ flip[0], j ^ flip[1]) for i, j in spots]
                pieces.append((part, spots))
                pieces.append((own_swap(part, 1), [(i, j ^ 1) for i, j in spots]))
    flat, slope_three = conv_three(act_two, conv_third.T, bias)
    if tuned:
        flat, *corner = lax.optimization_barrier((flat, *corner))
        for part, spots in zip(corner, z_spots):
            spots = [(i ^ 1, j ^ 2) for i, j in spots]
            pieces.append((part, spots))
            pieces.append((own_swap(part, 1), [(i, j ^ 1) for i, j in spots]))
    d_three, keep, send, here_heads, sums, sum_heads = dense(
        place, lengths, flat, slope_three, dense_heads.T, bias,
        actions, adv, old_values, old_logp, pieces, n_dp, n_own, rows,
    )

    plan = sum_stages(n_dp, n_own)

    def send_on(x, at, low):
        axis, bits, size = plan[at]
        x = x.astype(BF) if low else x
        return x, stage(x, axis, bits, size)

    def gather_up(state, other):
        x, came = state
        x, other = lax.optimization_barrier((x, other))
        return stage_sum(x, came)

    if tuned:
        came = own_swap(send, 1)
    d_two, pack_three, sum_two = conv_three_back(d_three, act_two_far, slope_two, conv_third.T, here_heads)
    if tuned:
        block = add_low(after(keep, d_two), came)
        by_y, by_x = own_swap(block[1, 4:6], 2), dp_swap(block[1, 6:8], 1)
        d_two = after(d_two, block)
    three = send_on(pack_three, 0, True)
    d_one, d_one_far, pack_two, sum_one = conv_two_back(d_two, act_one_far, slope_one, conv_second.T)
    if tuned:
        block = after(block, d_one)
        side_x = jnp.concatenate([add_low(block[0, 4:6], by_y), block[0, 6:8]])
        side_y = jnp.concatenate([block[1, 0:2], add_low(block[1, 2:4], by_x)])
        by_x, by_y = dp_swap(side_x, 1), own_swap(side_y, 2)
        d_one = after(d_one, side_x, side_y)
    three = send_on(gather_up(three, d_one_far), 1, True)
    d_one = after(d_one, three[0])
    two = send_on(pack_two, 0, True)
    pack_one = conv_one_grad(cells, d_one, sums, sum_heads, sum_one, sum_two)
    if tuned:
        column = add_low(after(block[0, 0:4], pack_one), by_x, by_y)
        parts = [column[0]] + [dp_swap(column[k], 2 * k) for k in (1, 2, 3)]
        d_one_far = after(d_one_far, column)
    else:
        parts = plain_scatter(keep, send, n_dp, n_own)
    three = send_on(gather_up(three, pack_one), 2, True)
    two = send_on(gather_up(two, pack_one), 1, True)
    one = send_on(pack_one, 0, False)
    d_one_far = after(d_one_far, three[0], two[0], one[0])
    shape = cells.shape
    back = frames_back(d_one_far, conv_first.T, shape, 0, 4)
    two = send_on(gather_up(two, back), 2, True)
    one = send_on(gather_up(one, back), 1, False)
    d_one_far = after(d_one_far, two[0], one[0])
    back = frames_back(d_one_far, conv_first.T, shape, 4, 8, back)
    one = send_on(gather_up(one, back), 2, False)
    d_one_far = after(d_one_far, one[0])
    back = frames_back(d_one_far, conv_first.T, shape, 8, grid // 2 + 1, back)

    def finish(state, low):
        for at in range(3, len(plan)):
            state = send_on(gather_up(state, back), at, low)
        return gather_up(state, back)

    frames_grad = back.reshape(grid, grid, planes, tokens).transpose(3, 0, 1, 2)
    grad_dense, *wide_step = dense_step(
        dense_hidden, mean_dense, square_dense, right_dense, parts, RATE / math.sqrt(rows * n_dp)
    )
    late = steps(
        [finish(three, True), finish(two, True)],
        [(0, 0, 64, 576), (0, 64, 19, 512), (1, 0, 64, 512)],
        [
            (conv_third, mean_third, square_third, left_third, right_third),
            (dense_heads, mean_heads, square_heads, left_heads, right_heads),
            (conv_second, mean_second, square_second, left_second, right_second),
        ],
    )
    third, top, second = late[0:4], late[4:8], late[8:12]
    pack_one = finish(one, False)
    first_step = steps(
        [pack_one], [(0, 0, 32, 256)], [(conv_first, mean_first, square_first, left_first, right_first)]
    )
    grad_bias = jnp.concatenate(
        [pack_one[36, 0:32], pack_one[35, 0:64], pack_one[34, 0:64], pack_one[32], pack_one[33], pack_one[37, 0:19]]
    )
    mom_bias, var_bias, bias_dir = adam_terms(grad_bias, mean_bias, square_bias)
    new_bias = bias_all - BIAS_RATE * bias_dir
    outs = [frames_grad]
    wide_step = [grad_dense] + list(wide_step)
    for index, bias_part in enumerate((grad_bias, mom_bias, var_bias, new_bias)):
        outs += [first_step[index].T, second[index].T, third[index].T, wide_step[index], top[index].T, bias_part]
    return tuple(outs)


def solution(mesh):
    n_dp, n_own = mesh.shape["dp"], mesh.shape["own"]
    both = ("dp", "own")
    rep = P()
    in_specs = (
        (P(both, None, None, None), P(both, None), P(both, None), P(both))
        + (P(both, None),) * 3
        + (rep, rep, rep, P("dp", "own"), rep, rep) * 3
        + (rep,) * 6
        + (P("own", None, None), rep, rep)
    )
    out_specs = (P(both, None, None, None),) + (rep, rep, rep, P("dp", "own"), rep, rep) * 4
    body = functools.partial(shards, n_dp=n_dp, n_own=n_own)
    return jax.shard_map(body, mesh=mesh, in_specs=in_specs, out_specs=out_specs, check_vma=False)
```

time: 294 us -> 175 us (0.60)
  waiting for transfers between devices: 66 us -> 16.4 us
  between operations: 41.5 us -> 2.18 us
  starting transfers between devices: 21.7 us -> 44 us
  local copies, waits for them, and re-layouts: 27.9 us -> 8.83 us
  Pallas kernels: 118 us -> 101 us
  other arithmetic: 16.9 us -> 1.83 us
    ppermute x20 -> x46, waiting for transfers between devices: 66 us -> 16.4 us  [swap(): return lax.ppermute(x, axis, [(i, i ^ bit) for i in range(size)])]
    ppermute x20 -> x46, starting transfers between devices: 21.7 us -> 44 us  [swap(): return lax.ppermute(x, axis, [(i, i ^ bit) for i in range(size)])]
    pallas_call x12 -> x13, Pallas kernels: 116 us -> 99.7 us  [the longest x1 16.3 us: conv_two_back(): pl.pallas_call(conv_two_back_kernel, out_shape=(near(shape, BF), pltpu.HB...]
    reshape x18 -> x1, local copies, waits for them, and re-layouts: 11.7 us -> 1.27 us  [shards(): bias_row = bias_all.reshape(1, -1)]
    slice x15 -> x1, local copies, waits for them, and re-layouts: 8.7 us -> 0.01 us  [shards(): pack_one[33]]
    concatenate x6 -> x2, other arithmetic: 5.83 us -> 0.08 us  [the longest x1 0.04 us: shards(): side_x = jnp.concatenate([add_low(block[0, 4:6], by_y), block[0, 6:8]])]
    another operation x5 -> x2, other arithmetic: 3.16 us -> 0.04 us  [the longest x1 0.02 us: shards(): jnp.stack([piece, along_z[0]])]
    unnamed x103 -> x94, local copies, waits for them, and re-layouts: 4.46 us -> 7.35 us
  transfers between devices with their start and end apart: 20 -> 46, of which waited for: 11 -> 9; matrix products, arithmetic and copies ran while one was open for 11% -> 1% of each run, Pallas kernels for 36% -> 49%
where the time goes in v2:
time: 175 us
  Pallas kernels  101 us (58%)
  starting transfers between devices  44 us (25%)
  waiting for transfers between devices  16.4 us (9%)
  local copies, waits for them, and re-layouts  8.83 us (5%)
  between operations  2.18 us (1%)
  other arithmetic  1.83 us (1%)
    ppermute x46, starting transfers between devices, swap(): return lax.ppermute(x, axis, [(i, i ^ bit) for i in range(size)])  44 us
    ppermute x46, waiting for transfers between devices, swap(): return lax.ppermute(x, axis, [(i, i ^ bit) for i in range(size)])  16.4 us
    pallas_call x1, Pallas kernels, conv_two_back(): pl.pallas_call(conv_two_back_kernel, out_shape=(near(shape, BF), pltpu.HB...  16.3 us
    pallas_call x1, Pallas kernels, conv_one(): pl.pallas_call(conv_one_kernel, out_shape=(near(shape, BF), pltpu.HBM(sha...  14.8 us
    pallas_call x3, Pallas kernels, frames_back(): pl.pallas_call(functools.partial(frames_back_kernel, begin=begin, end=end...  14 us
    pallas_call x1, Pallas kernels, dense(): pl.pallas_call(body, out_shape=(near((full, n), BF), part, part, jax.Shap...  11.5 us
    pallas_call x1, Pallas kernels, conv_one_grad(): pl.pallas_call(conv_one_grad_kernel, out_shape=jax.ShapeDtypeStruct((40,...  10.8 us
    pallas_call x1, Pallas kernels, conv_three_back(): pl.pallas_call(conv_three_back_kernel, out_shape=(near(act_two.shape, BF)...  10.4 us
  transfers between devices with their start and end apart: 46, of which 9 were waited for; matrix products, arithmetic and copies ran while one was open for 1% of the time, Pallas kernels for 49%

profile of v2, /device:TPU:0, one launch (start us, length us, event | category | flops | bytes accessed | tf_op | source)
XLA Modules:
  0.0 174.5 jit_solution(17299315189531319571)
XLA Ops:
  2.6 2.6 %first.1 = (f32[1,256]{1,0:T(1,128)}, bf16[416,128]{1,0:T(8,128)(2,1)}, f32[768,128]{1,0:T(8,128)}) custom-call(s32[1]{0:T(128)S(6)} %copy.63.lengths_ref.refs_1_, s32[1,256]{1,0:T(1,128)} %dones_ref.1, f32[1,256]{1,0:T(1,128)} %rewards_ref.1, f32[1,256]{1,0:T(1,128)} %refs_8_.1, f32[392,128]{1,0:T(8,128)} %refs_0_.1, f32[1,691]{1,0:T(1,128)} %reshape.64.bias_ref), custom_call_target="tpu_custom_call" | custom-call | flops 3000000000 | tf_op jit(solution)/shard_map/first/pallas_call | solution.py:212
  5.2 3.0 %collective-permute-start = (bf16[416,128]{1,0:T(8,128)(2,1)}, bf16[416,128]{1,0:T(8,128)(2,1)S(1)}, u32[]{:S(2)}, u32[]{:S(2)}) collective-permute-start(bf16[416,128]{1,0:T(8,128)(2,1)} %get-tuple-element.102), channel_id=1, source_target_pairs={{0,8},{4,12},{8,0},{12,4},{16,24},{20,28},{24,16},{28,20},{1,9},{5... | collective-permute-start | bytes 319496 | tf_op jit(solution)/shard_map/ppermute | solution.py:909
  8.2 2.6 %collective-permute-start.1 = (bf16[416,128]{1,0:T(8,128)(2,1)}, bf16[416,128]{1,0:T(8,128)(2,1)S(1)}, u32[]{:S(2)}, u32[]{:S(2)}) collective-permute-start(bf16[416,128]{1,0:T(8,128)(2,1)} %get-tuple-element.102), channel_id=1, source_target_pairs={{0,16},{4,20},{8,24},{12,28},{16,0},{20,4},{24,8},{28,12},{1,17},{... | collective-permute-start | bytes 319496 | tf_op jit(solution)/shard_map/ppermute | solution.py:909
  11.8 14.8 %conv_one.1 = (bf16[10,10,128,256]{3,2,1,0:T(8,128)(2,1)S(1)}, bf16[10,10,128,256]{3,2,1,0:T(8,128)(2,1)}, bf16[10,10,128,256]{3,2,1,0:T(8,128)(2,1)}) custom-call(bf16[21,1344,256]{2,1,0:T(8,128)(2,1)} %bitcast.106, f32[32,256]{1,0:T(8,128)S(1)} %bitcast.74, f32[768,128]{1,0:T(8,128)S(1)} %copy-done.35), custom_call_target="tpu_custom_call" | custom-call | flops 12000000000 | tf_op jit(solution)/shard_map/conv_one/pallas_call | solution.py:262
  26.6 1.8 %collective-permute-start.3 = (bf16[2,416,128]{2,1,0:T(8,128)(2,1)S(1)}, bf16[2,416,128]{2,1,0:T(8,128)(2,1)S(1)}, u32[]{:S(2)}, u32[]{:S(2)}) collective-permute-start(bf16[2,416,128]{2,1,0:T(8,128)(2,1)S(1)} %pad_maximum_fusion.2.refs_10_), channel_id=1, source_target_pairs={{0,4},{4,0},{8,12},{12,8},{16,20},{20,16},{24,28},{28,24},{1,5},{5... | collective-permute-start | bytes 638984 | tf_op jit(solution)/shard_map/ppermute | solution.py:909
  28.4 1.5 collective-permute-start.5
  30.9 8.3 %conv_two.1 = (bf16[9,576,256]{2,1,0:T(8,128)(2,1)S(1)}, bf16[9,576,256]{2,1,0:T(8,128)(2,1)}, bf16[9,576,256]{2,1,0:T(8,128)(2,1)}) custom-call(bf16[10,10,128,256]{3,2,1,0:T(8,128)(2,1)S(1)} %get-tuple-element.103.one_ref, f32[64,512]{1,0:T(8,128)S(1)} %bitcast.84, f32[768,128]{1,0:T(8,128)S(1)} %copy-done.35), custom_call_target="tpu_custom_call" | custom-call | flops 7000000000 | tf_op jit(solution)/shard_map/conv_two/pallas_call | solution.py:315
  39.8 1.8 %collective-permute-start.7 = (bf16[2,416,128]{2,1,0:T(8,128)(2,1)S(1)}, bf16[2,416,128]{2,1,0:T(8,128)(2,1)S(1)}, u32[]{:S(2)}, u32[]{:S(2)}) collective-permute-start(bf16[2,416,128]{2,1,0:T(8,128)(2,1)S(1)} %collective-permute-done.3.refs_14_), channel_id=1, source_target_pairs={{0,2},{1,3},{2,0},{3,1},{4,6},{5,7},{6,4},{7,5},{8,10},{9,11},{10,... | collective-permute-start | bytes 638984 | tf_op jit(solution)/shard_map/ppermute | solution.py:909
  41.6 1.5 collective-permute-start.8
  43.1 5.0 %conv_three.1 = (bf16[3136,256]{1,0:T(8,128)(2,1)S(1)}, bf16[3136,256]{1,0:T(8,128)(2,1)S(1)}) custom-call(bf16[9,576,256]{2,1,0:T(8,128)(2,1)S(1)} %get-tuple-element.105.two_ref, f32[64,576]{1,0:T(8,128)S(1)} %bitcast.79, f32[768,128]{1,0:T(8,128)S(1)} %copy-done.35), custom_call_target="tpu_custom_call" | custom-call | flops 5000000000 | tf_op jit(solution)/shard_map/conv_three/pallas_call | solution.py:351
  53.1 1.4 copy-done.32
  54.6 1.4 copy-done.34
  57.0 11.5 %dense.1 = (bf16[3136,256]{1,0:T(8,128)(2,1)S(1)}, bf16[2,8,392,128]{3,2,1,0:T(8,128)(2,1)S(1)}, bf16[2,8,392,128]{3,2,1,0:T(8,128)(2,1)S(1)}, f32[19,512]{1,0:T...) custom-call(s32[2]{0:T(128)S(1)} %pad_add_fusion.refs_0_, s32[1]{0:T(128)S(6)} %copy.63.lengths_ref.refs_1_, ...), custom_call_target="tpu_custom_call" | custom-call | flops 8000000000 | tf_op jit(solution)/shard_map/dense/pallas_call | solution.py:478
  68.8 10.4 %conv_three_back.1 = (bf16[9,576,256]{2,1,0:T(8,128)(2,1)S(1)}, bf16[96,640]{1,0:T(8,128)(2,1)S(1)}, f32[1,64]{1,0:T(1,128)S(1)}) custom-call(bf16[3136,256]{1,0:T(8,128)(2,1)S(1)} %get-tuple-element.116.d_three_ref, bf16[9,576,256]{2,1,0:T(8,128)(2,1)S(1)} %copy-done.29, bf16[9,576,256]{2,1,0:T(8,128)(2,1)S(1)} %copy-done.30, f32[64,576]{1,0:T(8,128)S(1)} %bitcast.80, ...), custom_call_target="tpu_custom_call" | custom-call | flops 8999999488 | tf_op jit(solution)/shard_map/conv_three_back/pallas_call | solution.py:566
  81.6 16.3 %conv_two_back.1 = (bf16[10,10,128,256]{3,2,1,0:T(8,128)(2,1)S(1)}, bf16[10,10,128,256]{3,2,1,0:T(8,128)(2,1)}, bf16[64,512]{1,0:T(8,128)(2,1)S(1)}, f32[1,32]{1,0:T(1,128)S(1)}) custom-call(bf16[9,576,256]{2,1,0:T(8,128)(2,1)S(1)} %get-tuple-element.124.d_two_ref, bf16[10,10,128,256]{3,2,1,0:T(8,128)(2,1)S(1)} %bitcast.96, ...), custom_call_target="tpu_custom_call" | custom-call | flops 11000000512 | tf_op jit(solution)/shard_map/conv_two_back/pallas_call | solution.py:651
  101.5 7.0 %collective-permute-done.18 = bf16[2,392,128]{2,1,0:T(8,128)(2,1)S(1)} collective-permute-done((bf16[2,392,128]{2,1,0:T(8,128)(2,1)S(1)}, bf16[2,392,128]{2,1,0:T(8,128)(2,1)S(1)}, u32[]{:S(2)}, u32[]{:S(2)}) %collective-permute-start.18) | collective-permute-done | bytes 200736 | tf_op jit(solution)/shard_map/ppermute | solution.py:909
  109.2 3.5 %collective-permute-start.26 = (bf16[96,640]{1,0:T(8,128)(2,1)S(1)}, bf16[96,640]{1,0:T(8,128)(2,1)S(1)}, u32[]{:S(2)}, u32[]{:S(2)}) collective-permute-start(bf16[96,640]{1,0:T(8,128)(2,1)S(1)} %add_convert_fusion.3), channel_id=1, source_target_pairs={{0,16},{4,20},{8,24},{12,28},{16,0},{20,4},{24,8},{28,12},{1,17},{... | collective-permute-start | bytes 368648 | tf_op jit(solution)/shard_map/ppermute | solution.py:909
  112.9 10.8 %conv_one_grad.1 = f32[40,256]{1,0:T(8,128)S(1)} custom-call(bf16[21,1344,256]{2,1,0:T(8,128)(2,1)} %bitcast.107, bf16[10,10,128,256]{3,2,1,0:T(8,128)(2,1)S(1)} %get-tuple-element.132.d_one_ref, f32[1,640]{1,0:T(1,128)S(1)} %get-tuple-element.133.dense_ref, f32[1,19]{1,0:T(1,128)S(1)} %get-tuple-element.134.heads_ref, ...), custom_call_target="tpu_custom_call" | custom-call | flops 10000000000 | tf_op jit(solution)/shard_map/conv_one_grad/pallas_call | solution.py:721
  126.7 3.9 %collective-permute-done.27 = bf16[96,640]{1,0:T(8,128)(2,1)S(1)} collective-permute-done((bf16[96,640]{1,0:T(8,128)(2,1)S(1)}, bf16[96,640]{1,0:T(8,128)(2,1)S(1)}, u32[]{:S(2)}, u32[]{:S(2)}) %collective-permute-start.27) | collective-permute-done | bytes 122912 | tf_op jit(solution)/shard_map/ppermute | solution.py:909
  130.6 3.3 %collective-permute-done.23 = bf16[4,392,128]{2,1,0:T(8,128)(2,1)S(1)} collective-permute-done((bf16[4,392,128]{2,1,0:T(8,128)(2,1)S(1)}, bf16[4,392,128]{2,1,0:T(8,128)(2,1)S(1)}, u32[]{:S(2)}, u32[]{:S(2)}) %collective-permute-start.23) | collective-permute-done | bytes 401440 | tf_op jit(solution)/shard_map/ppermute | solution.py:909
  135.1 2.8 %collective-permute-start.32 = (bf16[64,512]{1,0:T(8,128)(2,1)S(1)}, bf16[64,512]{1,0:T(8,128)(2,1)S(1)}, u32[]{:S(2)}, u32[]{:S(2)}) collective-permute-start(bf16[64,512]{1,0:T(8,128)(2,1)S(1)} %add_convert_fusion.5), channel_id=1, source_target_pairs={{0,16},{4,20},{8,24},{12,28},{16,0},{20,4},{24,8},{28,12},{1,17},{... | collective-permute-start | bytes 196616 | tf_op jit(solution)/shard_map/ppermute | solution.py:909
  138.2 4.8 %frames_back.3.refs_2_ = bf16[21,1344,256]{2,1,0:T(8,128)(2,1)} custom-call(bf16[10,10,128,256]{3,2,1,0:T(8,128)(2,1)} %get-tuple-element.147.refs_0_, f32[32,256]{1,0:T(8,128)S(1)} %bitcast.75), custom_call_target="tpu_custom_call" | custom-call | flops 4000000000 | tf_op jit(solution)/shard_map/frames_back/pallas_call | solution.py:804
  143.7 1.5 collective-permute-start.41
  145.9 2.3 %collective-permute-start.38 = (f32[40,256]{1,0:T(8,128)S(1)}, f32[40,256]{1,0:T(8,128)S(1)}, u32[]{:S(2)}, u32[]{:S(2)}) collective-permute-start(f32[40,256]{1,0:T(8,128)S(1)} %add_add_fusion.1), channel_id=1, source_target_pairs={{0,16},{4,20},{8,24},{12,28},{16,0},{20,4},{24,8},{28,12},{1,17},{... | collective-permute-start | bytes 122888 | tf_op jit(solution)/shard_map/ppermute | solution.py:909
  148.2 1.5 collective-permute-start.39
  150.4 5.0 %frames_back.4.refs_2_ = bf16[21,1344,256]{2,1,0:T(8,128)(2,1)} custom-call(bf16[10,10,128,256]{3,2,1,0:T(8,128)(2,1)} %get-tuple-element.147.refs_0_, f32[32,256]{1,0:T(8,128)S(1)} %bitcast.76, bf16[21,1344,256]{2,1,0:T(8,128)(2,1)} %frames_back.3.refs_2_), custom_call_target="tpu_custom_call", output_to_operand_aliasing={{}: (2, {})} | custom-call | flops 4000000000 | tf_op jit(solution)/shard_map/frames_back/pallas_call | solution.py:804
  156.4 2.9 %collective-permute-start.44 = (bf16[392,128]{1,0:T(8,128)(2,1)S(1)}, bf16[392,128]{1,0:T(8,128)(2,1)S(1)}, u32[]{:S(2)}, u32[]{:S(2)}) collective-permute-start(bf16[392,128]{1,0:T(8,128)(2,1)S(1)} %get-tuple-element.181), channel_id=1, source_target_pairs={{0,16},{4,20},{8,24},{12,28},{16,0},{20,4},{24,8},{28,12},{1,17},{... | collective-permute-start | bytes 301064 | tf_op jit(solution)/shard_map/ppermute | solution.py:909
  160.0 4.1 %frames_back.5 = bf16[21,1344,256]{2,1,0:T(8,128)(2,1)} custom-call(bf16[10,10,128,256]{3,2,1,0:T(8,128)(2,1)} %get-tuple-element.147.refs_0_, f32[32,256]{1,0:T(8,128)S(1)} %bitcast.77, bf16[21,1344,256]{2,1,0:T(8,128)(2,1)} %frames_back.4.refs_2_), custom_call_target="tpu_custom_call", output_to_operand_aliasing={{}: (2, {})} | custom-call | flops 3000000000 | tf_op jit(solution)/shard_map/frames_back/pallas_call | solution.py:804
  164.2 1.5 collective-permute-start.40
  165.9 4.7 %steps.3 = (f32[64,576]{1,0:T(8,128)}, f32[64,576]{1,0:T(8,128)}, f32[64,576]{1,0:T(8,128)}, f32[64,576]{1,0:T(8,128)}, f32[19,512]{1,0:T(8,128)}, /*index=5*/f3...) custom-call(f32[96,640]{1,0:T(8,128)S(1)} %convert_add_fusion.2.refs, ...), custom_call_target="tpu_custom_call" | custom-call | flops 5000000000 | tf_op jit(solution)/shard_map/steps/pallas_call | solution.py:869
  170.9 1.3 steps.2
  173.0 1.5 dense_step.1
  (198 shorter events, 25.9 us)
Async XLA Ops:
  5.2 21.4 %collective-permute-start = (bf16[416,128]{1,0:T(8,128)(2,1)}, bf16[416,128]{1,0:T(8,128)(2,1)S(1)}, u32[]{:S(2)}, u32[]{:S(2)}) collective-permute-start(bf16[416,128]{1,0:T(8,128)(2,1)} %get-tuple-element.102), channel_id=1, source_target_pairs={{0,8},{4,12},{8,0},{12,4},{16,24},{20,28},{24,16},{28,20},{1,9},{5... | collective-permute-start | bytes 319496 | tf_op jit(solution)/shard_map/ppermute | solution.py:909
  8.2 21.7 %collective-permute-start.1 = (bf16[416,128]{1,0:T(8,128)(2,1)}, bf16[416,128]{1,0:T(8,128)(2,1)S(1)}, u32[]{:S(2)}, u32[]{:S(2)}) collective-permute-start(bf16[416,128]{1,0:T(8,128)(2,1)} %get-tuple-element.102), channel_id=1, source_target_pairs={{0,16},{4,20},{8,24},{12,28},{16,0},{20,4},{24,8},{28,12},{1,17},{... | collective-permute-start | bytes 319496 | tf_op jit(solution)/shard_map/ppermute | solution.py:909
  10.8 19.1 %collective-permute-start.2 = (bf16[416,128]{1,0:T(8,128)(2,1)}, bf16[416,128]{1,0:T(8,128)(2,1)S(1)}, u32[]{:S(2)}, u32[]{:S(2)}) collective-permute-start(bf16[416,128]{1,0:T(8,128)(2,1)} %get-tuple-element.102), channel_id=1, source_target_pairs={{0,24},{4,28},{8,16},{12,20},{16,8},{20,12},{24,0},{28,4},{1,25},{... | collective-permute-start | bytes 319496 | tf_op jit(solution)/shard_map/ppermute | solution.py:909
  26.6 12.5 %collective-permute-start.3 = (bf16[2,416,128]{2,1,0:T(8,128)(2,1)S(1)}, bf16[2,416,128]{2,1,0:T(8,128)(2,1)S(1)}, u32[]{:S(2)}, u32[]{:S(2)}) collective-permute-start(bf16[2,416,128]{2,1,0:T(8,128)(2,1)S(1)} %pad_maximum_fusion.2.refs_10_), channel_id=1, source_target_pairs={{0,4},{4,0},{8,12},{12,8},{16,20},{20,16},{24,28},{28,24},{1,5},{5... | collective-permute-start | bytes 638984 | tf_op jit(solution)/shard_map/ppermute | solution.py:909
  28.4 11.3 %collective-permute-start.5 = (bf16[2,416,128]{2,1,0:T(8,128)(2,1)S(1)}, bf16[2,416,128]{2,1,0:T(8,128)(2,1)S(1)}, u32[]{:S(2)}, u32[]{:S(2)}) collective-permute-start(bf16[2,416,128]{2,1,0:T(8,128)(2,1)S(1)} %pad_maximum_fusion.2.refs_10_), channel_id=1, source_target_pairs={{0,2},{1,3},{2,0},{3,1},{4,6},{5,7},{6,4},{7,5},{8,10},{9,11},{10,... | collective-permute-start | bytes 638984 | tf_op jit(solution)/shard_map/ppermute | solution.py:909
  30.9 20.1 %collective-permute-start.9 = (bf16[2,416,128]{2,1,0:T(8,128)(2,1)S(1)}, bf16[2,416,128]{2,1,0:T(8,128)(2,1)S(1)}, u32[]{:S(2)}, u32[]{:S(2)}) collective-permute-start(bf16[2,416,128]{2,1,0:T(8,128)(2,1)S(1)} %pad_maximum_fusion.2.refs_10_), channel_id=1, source_target_pairs={{0,1},{1,0},{2,3},{3,2},{4,5},{5,4},{6,7},{7,6},{8,9},{9,8},{10,11... | collective-permute-start | bytes 638984 | tf_op jit(solution)/shard_map/ppermute | solution.py:909
  39.2 12.0 %collective-permute-start.10 = (bf16[2,416,128]{2,1,0:T(8,128)(2,1)S(1)}, bf16[2,416,128]{2,1,0:T(8,128)(2,1)S(1)}, u32[]{:S(2)}, u32[]{:S(2)}) collective-permute-start(bf16[2,416,128]{2,1,0:T(8,128)(2,1)S(1)} %pad_maximum_fusion.3.refs_11_), channel_id=1, source_target_pairs={{0,1},{1,0},{2,3},{3,2},{4,5},{5,4},{6,7},{7,6},{8,9},{9,8},{10,11... | collective-permute-start | bytes 638984 | tf_op jit(solution)/shard_map/ppermute | solution.py:909
  39.8 10.7 %collective-permute-start.7 = (bf16[2,416,128]{2,1,0:T(8,128)(2,1)S(1)}, bf16[2,416,128]{2,1,0:T(8,128)(2,1)S(1)}, u32[]{:S(2)}, u32[]{:S(2)}) collective-permute-start(bf16[2,416,128]{2,1,0:T(8,128)(2,1)S(1)} %collective-permute-done.3.refs_14_), channel_id=1, source_target_pairs={{0,2},{1,3},{2,0},{3,1},{4,6},{5,7},{6,4},{7,5},{8,10},{9,11},{10,... | collective-permute-start | bytes 638984 | tf_op jit(solution)/shard_map/ppermute | solution.py:909
  68.5 12.6 %collective-permute-start.17 = (bf16[2,8,392,128]{3,2,1,0:T(8,128)(2,1)S(1)}, bf16[2,8,392,128]{3,2,1,0:T(8,128)(2,1)S(1)}, u32[]{:S(2)}, u32[]{:S(2)}) collective-permute-start(bf16[2,8,392,128]{3,2,1,0:T(8,128)(2,1)S(1)} %get-tuple-element.123), channel_id=1, source_target_pairs={{0,1},{1,0},{2,3},{3,2},{4,5},{5,4},{6,7},{7,6},{8,9},{9,8},{10,11... | collective-permute-start | bytes 4816904 | tf_op jit(solution)/shard_map/ppermute | solution.py:909
  79.2 20.0 %collective-permute-start.20 = (bf16[96,640]{1,0:T(8,128)(2,1)S(1)}, bf16[96,640]{1,0:T(8,128)(2,1)S(1)}, u32[]{:S(2)}, u32[]{:S(2)}) collective-permute-start(bf16[96,640]{1,0:T(8,128)(2,1)S(1)} %get-tuple-element.131), channel_id=1, source_target_pairs={{0,1},{1,0},{2,3},{3,2},{4,5},{5,4},{6,7},{7,6},{8,9},{9,8},{10,11... | collective-permute-start | bytes 368648 | tf_op jit(solution)/shard_map/ppermute | solution.py:909
  79.5 20.6 %collective-permute-start.21 = (bf16[96,640]{1,0:T(8,128)(2,1)S(1)}, bf16[96,640]{1,0:T(8,128)(2,1)S(1)}, u32[]{:S(2)}, u32[]{:S(2)}) collective-permute-start(bf16[96,640]{1,0:T(8,128)(2,1)S(1)} %get-tuple-element.131), channel_id=1, source_target_pairs={{0,2},{1,3},{2,0},{3,1},{4,6},{5,7},{6,4},{7,5},{8,10},{9,11},{10,... | collective-permute-start | bytes 368648 | tf_op jit(solution)/shard_map/ppermute | solution.py:909
  80.1 20.7 %collective-permute-start.22 = (bf16[96,640]{1,0:T(8,128)(2,1)S(1)}, bf16[96,640]{1,0:T(8,128)(2,1)S(1)}, u32[]{:S(2)}, u32[]{:S(2)}) collective-permute-start(bf16[96,640]{1,0:T(8,128)(2,1)S(1)} %get-tuple-element.131), channel_id=1, source_target_pairs={{0,3},{1,2},{2,1},{3,0},{4,7},{5,6},{6,5},{7,4},{8,11},{9,10},{10,... | collective-permute-start | bytes 368648 | tf_op jit(solution)/shard_map/ppermute | solution.py:909
  97.9 25.8 %collective-permute-start.28 = (bf16[64,512]{1,0:T(8,128)(2,1)S(1)}, bf16[64,512]{1,0:T(8,128)(2,1)S(1)}, u32[]{:S(2)}, u32[]{:S(2)}) collective-permute-start(bf16[64,512]{1,0:T(8,128)(2,1)S(1)} %get-tuple-element.141), channel_id=1, source_target_pairs={{0,1},{1,0},{2,3},{3,2},{4,5},{5,4},{6,7},{7,6},{8,9},{9,8},{10,11... | collective-permute-start | bytes 196616 | tf_op jit(solution)/shard_map/ppermute | solution.py:909
  98.5 25.5 %collective-permute-start.29 = (bf16[64,512]{1,0:T(8,128)(2,1)S(1)}, bf16[64,512]{1,0:T(8,128)(2,1)S(1)}, u32[]{:S(2)}, u32[]{:S(2)}) collective-permute-start(bf16[64,512]{1,0:T(8,128)(2,1)S(1)} %get-tuple-element.141), channel_id=1, source_target_pairs={{0,2},{1,3},{2,0},{3,1},{4,6},{5,7},{6,4},{7,5},{8,10},{9,11},{10,... | collective-permute-start | bytes 196616 | tf_op jit(solution)/shard_map/ppermute | solution.py:909
  99.2 25.3 %collective-permute-start.30 = (bf16[64,512]{1,0:T(8,128)(2,1)S(1)}, bf16[64,512]{1,0:T(8,128)(2,1)S(1)}, u32[]{:S(2)}, u32[]{:S(2)}) collective-permute-start(bf16[64,512]{1,0:T(8,128)(2,1)S(1)} %get-tuple-element.141), channel_id=1, source_target_pairs={{0,3},{1,2},{2,1},{3,0},{4,7},{5,6},{6,5},{7,4},{8,11},{9,10},{10,... | collective-permute-start | bytes 196616 | tf_op jit(solution)/shard_map/ppermute | solution.py:909
  108.5 17.0 %collective-permute-start.25 = (bf16[96,640]{1,0:T(8,128)(2,1)S(1)}, bf16[96,640]{1,0:T(8,128)(2,1)S(1)}, u32[]{:S(2)}, u32[]{:S(2)}) collective-permute-start(bf16[96,640]{1,0:T(8,128)(2,1)S(1)} %add_convert_fusion.3), channel_id=1, source_target_pairs={{0,8},{4,12},{8,0},{12,4},{16,24},{20,28},{24,16},{28,20},{1,9},{5... | collective-permute-start | bytes 368648 | tf_op jit(solution)/shard_map/ppermute | solution.py:909
  109.2 16.4 %collective-permute-start.26 = (bf16[96,640]{1,0:T(8,128)(2,1)S(1)}, bf16[96,640]{1,0:T(8,128)(2,1)S(1)}, u32[]{:S(2)}, u32[]{:S(2)}) collective-permute-start(bf16[96,640]{1,0:T(8,128)(2,1)S(1)} %add_convert_fusion.3), channel_id=1, source_target_pairs={{0,16},{4,20},{8,24},{12,28},{16,0},{20,4},{24,8},{28,12},{1,17},{... | collective-permute-start | bytes 368648 | tf_op jit(solution)/shard_map/ppermute | solution.py:909
  124.0 10.0 %collective-permute-start.23 = (bf16[4,392,128]{2,1,0:T(8,128)(2,1)S(1)}, bf16[4,392,128]{2,1,0:T(8,128)(2,1)S(1)}, u32[]{:S(2)}, u32[]{:S(2)}) collective-permute-start(bf16[4,392,128]{2,1,0:T(8,128)(2,1)S(1)} %pad_maximum_fusion), channel_id=1, source_target_pairs={{0,4},{4,0},{8,12},{12,8},{16,20},{20,16},{24,28},{28,24},{1,5},{5... | collective-permute-start | bytes 1204232 | tf_op jit(solution)/shard_map/ppermute | solution.py:909
  124.4 10.7 %collective-permute-start.24 = (bf16[4,392,128]{2,1,0:T(8,128)(2,1)S(1)}, bf16[4,392,128]{2,1,0:T(8,128)(2,1)S(1)}, u32[]{:S(2)}, u32[]{:S(2)}) collective-permute-start(bf16[4,392,128]{2,1,0:T(8,128)(2,1)S(1)} %pad_maximum_fusion.1), channel_id=1, source_target_pairs={{0,2},{1,3},{2,0},{3,1},{4,6},{5,7},{6,4},{7,5},{8,10},{9,11},{10,... | collective-permute-start | bytes 1204232 | tf_op jit(solution)/shard_map/ppermute | solution.py:909
  125.5 17.6 %collective-permute-start.34 = (f32[40,256]{1,0:T(8,128)S(1)}, f32[40,256]{1,0:T(8,128)S(1)}, u32[]{:S(2)}, u32[]{:S(2)}) collective-permute-start(f32[40,256]{1,0:T(8,128)S(1)} %conv_one_grad.1), channel_id=1, source_target_pairs={{0,1},{1,0},{2,3},{3,2},{4,5},{5,4},{6,7},{7,6},{8,9},{9,8},{10,11... | collective-permute-start | bytes 122888 | tf_op jit(solution)/shard_map/ppermute | solution.py:909
  125.5 18.2 %collective-permute-start.35 = (f32[40,256]{1,0:T(8,128)S(1)}, f32[40,256]{1,0:T(8,128)S(1)}, u32[]{:S(2)}, u32[]{:S(2)}) collective-permute-start(f32[40,256]{1,0:T(8,128)S(1)} %conv_one_grad.1), channel_id=1, source_target_pairs={{0,2},{1,3},{2,0},{3,1},{4,6},{5,7},{6,4},{7,5},{8,10},{9,11},{10,... | collective-permute-start | bytes 122888 | tf_op jit(solution)/shard_map/ppermute | solution.py:909
  130.6 14.6 %collective-permute-start.36 = (f32[40,256]{1,0:T(8,128)S(1)}, f32[40,256]{1,0:T(8,128)S(1)}, u32[]{:S(2)}, u32[]{:S(2)}) collective-permute-start(f32[40,256]{1,0:T(8,128)S(1)} %conv_one_grad.1), channel_id=1, source_target_pairs={{0,3},{1,2},{2,1},{3,0},{4,7},{5,6},{6,5},{7,4},{8,11},{9,10},{10,... | collective-permute-start | bytes 122888 | tf_op jit(solution)/shard_map/ppermute | solution.py:909
  134.0 12.0 %collective-permute-start.31 = (bf16[64,512]{1,0:T(8,128)(2,1)S(1)}, bf16[64,512]{1,0:T(8,128)(2,1)S(1)}, u32[]{:S(2)}, u32[]{:S(2)}) collective-permute-start(bf16[64,512]{1,0:T(8,128)(2,1)S(1)} %add_convert_fusion.5), channel_id=1, source_target_pairs={{0,8},{4,12},{8,0},{12,4},{16,24},{20,28},{24,16},{28,20},{1,9},{5... | collective-permute-start | bytes 196616 | tf_op jit(solution)/shard_map/ppermute | solution.py:909
  135.1 13.0 %collective-permute-start.32 = (bf16[64,512]{1,0:T(8,128)(2,1)S(1)}, bf16[64,512]{1,0:T(8,128)(2,1)S(1)}, u32[]{:S(2)}, u32[]{:S(2)}) collective-permute-start(bf16[64,512]{1,0:T(8,128)(2,1)S(1)} %add_convert_fusion.5), channel_id=1, source_target_pairs={{0,16},{4,20},{8,24},{12,28},{16,0},{20,4},{24,8},{28,12},{1,17},{... | collective-permute-start | bytes 196616 | tf_op jit(solution)/shard_map/ppermute | solution.py:909
  143.7 20.4 %collective-permute-start.41 = (bf16[96,640]{1,0:T(8,128)(2,1)S(1)}, bf16[96,640]{1,0:T(8,128)(2,1)S(1)}, u32[]{:S(2)}, u32[]{:S(2)}) collective-permute-start(bf16[96,640]{1,0:T(8,128)(2,1)S(1)} %add_convert_fusion.2), channel_id=1, source_target_pairs={{0,4},{4,0},{8,12},{12,8},{16,20},{20,16},{24,28},{28,24},{1,5},{5... | collective-permute-start | bytes 368648 | tf_op jit(solution)/shard_map/ppermute | solution.py:909
  145.2 10.2 %collective-permute-start.37 = (f32[40,256]{1,0:T(8,128)S(1)}, f32[40,256]{1,0:T(8,128)S(1)}, u32[]{:S(2)}, u32[]{:S(2)}) collective-permute-start(f32[40,256]{1,0:T(8,128)S(1)} %add_add_fusion.1), channel_id=1, source_target_pairs={{0,8},{4,12},{8,0},{12,4},{16,24},{20,28},{24,16},{28,20},{1,9},{5... | collective-permute-start | bytes 122888 | tf_op jit(solution)/shard_map/ppermute | solution.py:909
  145.9 10.5 %collective-permute-start.38 = (f32[40,256]{1,0:T(8,128)S(1)}, f32[40,256]{1,0:T(8,128)S(1)}, u32[]{:S(2)}, u32[]{:S(2)}) collective-permute-start(f32[40,256]{1,0:T(8,128)S(1)} %add_add_fusion.1), channel_id=1, source_target_pairs={{0,16},{4,20},{8,24},{12,28},{16,0},{20,4},{24,8},{28,12},{1,17},{... | collective-permute-start | bytes 122888 | tf_op jit(solution)/shard_map/ppermute | solution.py:909
  148.2 11.1 %collective-permute-start.39 = (f32[40,256]{1,0:T(8,128)S(1)}, f32[40,256]{1,0:T(8,128)S(1)}, u32[]{:S(2)}, u32[]{:S(2)}) collective-permute-start(f32[40,256]{1,0:T(8,128)S(1)} %add_add_fusion.1), channel_id=1, source_target_pairs={{0,24},{4,28},{8,16},{12,20},{16,8},{20,12},{24,0},{28,4},{1,25},{... | collective-permute-start | bytes 122888 | tf_op jit(solution)/shard_map/ppermute | solution.py:909
  149.8 16.0 %collective-permute-start.42 = (bf16[64,512]{1,0:T(8,128)(2,1)S(1)}, bf16[64,512]{1,0:T(8,128)(2,1)S(1)}, u32[]{:S(2)}, u32[]{:S(2)}) collective-permute-start(bf16[64,512]{1,0:T(8,128)(2,1)S(1)} %add_convert_fusion.4), channel_id=1, source_target_pairs={{0,4},{4,0},{8,12},{12,8},{16,20},{20,16},{24,28},{28,24},{1,5},{5... | collective-permute-start | bytes 196616 | tf_op jit(solution)/shard_map/ppermute | solution.py:909
  155.4 17.5 %collective-permute-start.43 = (bf16[392,128]{1,0:T(8,128)(2,1)S(1)}, bf16[392,128]{1,0:T(8,128)(2,1)S(1)}, u32[]{:S(2)}, u32[]{:S(2)}) collective-permute-start(bf16[392,128]{1,0:T(8,128)(2,1)S(1)} %get-tuple-element.182), channel_id=1, source_target_pairs={{0,8},{4,12},{8,0},{12,4},{16,24},{20,28},{24,16},{28,20},{1,9},{5... | collective-permute-start | bytes 301064 | tf_op jit(solution)/shard_map/ppermute | solution.py:909
  156.4 16.6 %collective-permute-start.44 = (bf16[392,128]{1,0:T(8,128)(2,1)S(1)}, bf16[392,128]{1,0:T(8,128)(2,1)S(1)}, u32[]{:S(2)}, u32[]{:S(2)}) collective-permute-start(bf16[392,128]{1,0:T(8,128)(2,1)S(1)} %get-tuple-element.181), channel_id=1, source_target_pairs={{0,16},{4,20},{8,24},{12,28},{16,0},{20,4},{24,8},{28,12},{1,17},{... | collective-permute-start | bytes 301064 | tf_op jit(solution)/shard_map/ppermute | solution.py:909
  159.2 13.7 %collective-permute-start.45 = (bf16[392,128]{1,0:T(8,128)(2,1)S(1)}, bf16[392,128]{1,0:T(8,128)(2,1)S(1)}, u32[]{:S(2)}, u32[]{:S(2)}) collective-permute-start(bf16[392,128]{1,0:T(8,128)(2,1)S(1)} %get-tuple-element.180), channel_id=1, source_target_pairs={{0,24},{4,28},{8,16},{12,20},{16,8},{20,12},{24,0},{28,4},{1,25},{... | collective-permute-start | bytes 301064 | tf_op jit(solution)/shard_map/ppermute | solution.py:909
  (61 other events, 388.6 us)

commit v3 on v2

--- a/solution.py
+++ b/solution.py
@@ -97,8 +97,9 @@
     return act, slope
 
 
-def wide(column, rows, n):
-    k = column.shape[0]
+def wide(line, rows, n):
+    k = line.shape[1]
+    column = jnp.broadcast_to(line, (128, k)).T
     tall = jnp.concatenate([column] * (rows // k), axis=0) if rows > k else column
     return jnp.concatenate([tall] * (n // 128), axis=1)
 
@@ -161,7 +162,7 @@
 
 
 def first_kernel(
-    lengths_ref, dones_ref, rewards_ref, values_ref, weight_ref, bias_ref, adv_ref, piece_ref, bias_out_ref
+    lengths_ref, dones_ref, rewards_ref, values_ref, weight_ref, adv_ref, piece_ref
 ):
     n = rewards_ref.shape[1]
     length = lengths_ref[0]
@@ -200,13 +201,9 @@
     piece_ref[...] = jnp.zeros_like(piece_ref)
     piece_ref[0:rows, :] = weight_ref[...].astype(BF)
     piece_ref[tail:, :] = jnp.concatenate([terms, jnp.zeros((8, 128), F32)], axis=0).astype(BF)
-    size = bias_ref.shape[1]
-    padded = bias_out_ref.shape[0]
-    line = jnp.concatenate([bias_ref[...], jnp.zeros((1, padded - size), F32)], axis=1)
-    bias_out_ref[...] = jnp.broadcast_to(line, (128, padded)).T
-
-
-def first(lengths, dones, rewards, old_values, weight, bias):
+
+
+def first(lengths, dones, rewards, old_values, weight):
     n = rewards.shape[1]
     rows = -(-weight.shape[0] // 16) * 16 + 16
     return pl.pallas_call(
@@ -214,18 +211,17 @@
         out_shape=(
             jax.ShapeDtypeStruct((1, n), F32),
             jax.ShapeDtypeStruct((rows, 128), BF),
-            jax.ShapeDtypeStruct((-(-bias.shape[1] // 128) * 128, 128), F32),
         ),
-        in_specs=[smem()] + [vmem()] * 5,
-        out_specs=(vmem(),) * 3,
+        in_specs=[smem()] + [vmem()] * 4,
+        out_specs=(vmem(),) * 2,
         cost_estimate=cost(3),
         name="first",
-    )(lengths, dones, rewards, old_values, weight, bias)
+    )(lengths, dones, rewards, old_values, weight)
 
 
 def conv_one_kernel(
-    frames_ref, weight_ref, bias_ref, act_ref, act_far_ref, slope_far_ref,
-    band_ref, cells_ref, slope_ref, in_sems, act_sems, slope_sems,
+    frames_ref, weight_ref, bias_ref, act_ref, slope_far_ref,
+    band_ref, wide_ref, cells_ref, slope_ref, in_sems, slope_sems,
 ):
     n = act_ref.shape[-1]
     half = act_ref.shape[0]
@@ -235,23 +231,21 @@
     def _():
         start_rows(frames_ref, cells_ref, in_sems)
         band_ref[...] = band_square(weight_ref[...], 64)
+        wide_ref[...] = wide(bias_ref[:, 0:32], 128, n)
         wait_row(frames_ref, cells_ref, in_sems, 0)
 
     wait_row(frames_ref, cells_ref, in_sems, 2 * step + 1)
     wait_row(frames_ref, cells_ref, in_sems, 2 * step + 2)
-    bias = wide(bias_ref[0:32, :], 128, n)
     for col in range(half):
         span = slice(col * 128, col * 128 + 192)
         patch = jnp.concatenate([cells_ref[2 * step + a, span, :] for a in range(3)], axis=0)
-        act, slope = gelu_both(dot(band_ref[...], patch) + bias)
+        act, slope = gelu_both(dot(band_ref[...], patch) + wide_ref[...])
         act_ref[step, col] = act.astype(BF)
         slope_ref[step, col] = slope.astype(BF)
-    start_row(act_ref, act_far_ref, act_sems, step)
     start_row(slope_ref, slope_far_ref, slope_sems, step)
 
     @pl.when(step == half - 1)
     def _():
-        wait_rows(act_ref, act_far_ref, act_sems)
         wait_rows(slope_ref, slope_far_ref, slope_sems)
 
 
@@ -261,52 +255,49 @@
     shape = (half, half, 128, n)
     return pl.pallas_call(
         conv_one_kernel,
-        out_shape=(near(shape, BF), pltpu.HBM(shape, BF), pltpu.HBM(shape, BF)),
+        out_shape=(near(shape, BF), pltpu.HBM(shape, BF)),
         grid=(half,),
         in_specs=[anywhere(), vmem(), vmem()],
-        out_specs=(vmem(), anywhere(), anywhere()),
+        out_specs=(vmem(), anywhere()),
         scratch_shapes=[
             pltpu.VMEM((128, 576), BF),
+            pltpu.VMEM((128, n), F32),
             pltpu.VMEM(frames.shape, BF),
             pltpu.VMEM(shape, BF),
             dma(grid),
             dma(half),
-            dma(half),
         ],
-        compiler_params=params(36),
+        compiler_params=params(30),
         cost_estimate=cost(12),
         name="conv_one",
     )(far(frames), weight, bias)
 
 
 def conv_two_kernel(
-    one_ref, weight_ref, bias_ref, act_ref, act_far_ref, slope_far_ref,
-    band_ref, slope_ref, act_sems, slope_sems,
+    one_ref, weight_ref, bias_ref, act_ref, slope_ref, one_far_ref, band_ref, wide_ref, sems
 ):
     n = act_ref.shape[-1]
     step = pl.program_id(0)
 
     @pl.when(step == 0)
     def _():
+        start_rows(one_ref, one_far_ref, sems)
         band_ref[...] = band_forward(weight_ref[...], 2, 128, 3)
-
-    bias = wide(bias_ref[32:96, :], 192, n)
+        wide_ref[...] = wide(bias_ref[:, 32:96], 192, n)
+
     for part in range(3):
         span = slice(3 * part, 3 * part + 4)
         patch = jnp.concatenate(
             [one_ref[step + a, span].reshape(512, n) for a in range(2)], axis=0
         )
-        act, slope = gelu_both(dot(band_ref[...], patch) + bias)
+        act, slope = gelu_both(dot(band_ref[...], patch) + wide_ref[...])
         rows = slice(part * 192, part * 192 + 192)
         act_ref[step, rows, :] = act.astype(BF)
         slope_ref[step, rows, :] = slope.astype(BF)
-    start_row(act_ref, act_far_ref, act_sems, step)
-    start_row(slope_ref, slope_far_ref, slope_sems, step)
 
     @pl.when(step == 8)
     def _():
-        wait_rows(act_ref, act_far_ref, act_sems)
-        wait_rows(slope_ref, slope_far_ref, slope_sems)
+        wait_rows(one_ref, one_far_ref, sems)
 
 
 def conv_two(act_one, weight, bias):
@@ -314,51 +305,77 @@
     shape = (9, 576, n)
     return pl.pallas_call(
         conv_two_kernel,
-        out_shape=(near(shape, BF), pltpu.HBM(shape, BF), pltpu.HBM(shape, BF)),
+        out_shape=(near(shape, BF), near(shape, BF), pltpu.HBM(act_one.shape, BF)),
         grid=(9,),
         in_specs=[vmem()] * 3,
-        out_specs=(vmem(), anywhere(), anywhere()),
-        scratch_shapes=[pltpu.VMEM((192, 1024), BF), pltpu.VMEM(shape, BF), dma(9), dma(9)],
-        compiler_params=params(24),
+        out_specs=(vmem(), vmem(), anywhere()),
+        scratch_shapes=[pltpu.VMEM((192, 1024), BF), pltpu.VMEM((192, n), F32), dma(10)],
+        compiler_params=params(),
         cost_estimate=cost(7),
         name="conv_two",
     )(held(act_one), weight, bias)
 
 
-def conv_three_kernel(two_ref, weight_ref, bias_ref, flat_ref, slope_ref, band_ref):
-    n = flat_ref.shape[-1]
+def conv_three_kernel(
+    two_ref, slope_two_ref, weight_ref, bias_ref,
+    flat_far_ref, slope_far_ref, two_far_ref, slope_two_far_ref,
+    band_ref, wide_ref, flat_ref, slope_ref, two_sems, slope_two_sems, flat_sems, slope_sems,
+):
+    n = two_ref.shape[-1]
     step = pl.program_id(0)
 
     @pl.when(step == 0)
     def _():
+        start_rows(two_ref, two_far_ref, two_sems)
+        start_rows(slope_two_ref, slope_two_far_ref, slope_two_sems)
         band_ref[...] = band_forward(weight_ref[...], 3, 64, 4)
-
-    bias = wide(bias_ref[96:160, :], 256, n)
+        wide_ref[...] = wide(bias_ref[:, 96:160], 256, n)
+
     for drop, start in ((0, 0), (1, 3)):
         patch = jnp.concatenate(
             [two_ref[step + a, start * 64 : start * 64 + 384, :] for a in range(3)], axis=0
         )
-        pre = dot(band_ref[drop * 64 :, :], patch) + bias[drop * 64 :]
+        pre = dot(band_ref[drop * 64 :, :], patch) + wide_ref[drop * 64 :, :]
         act, slope = gelu_both(pre)
-        rows = pl.ds(pl.multiple_of(step * 448, 64) + (start + drop) * 64, 256 - drop * 64)
-        flat_ref[rows, :] = act.astype(BF)
-        slope_ref[rows, :] = slope.astype(BF)
-
-
-def conv_three(act_two, weight, bias):
+        rows = slice((start + drop) * 64, (start + 4) * 64)
+        flat_ref[step, rows, :] = act.astype(BF)
+        slope_ref[step, rows, :] = slope.astype(BF)
+    start_row(flat_ref, flat_far_ref, flat_sems, step)
+    start_row(slope_ref, slope_far_ref, slope_sems, step)
+
+    @pl.when(step == 6)
+    def _():
+        wait_rows(two_ref, two_far_ref, two_sems)
+        wait_rows(slope_two_ref, slope_two_far_ref, slope_two_sems)
+        wait_rows(flat_ref, flat_far_ref, flat_sems)
+        wait_rows(slope_ref, slope_far_ref, slope_sems)
+
+
+def conv_three(act_two, slope_two, weight, bias):
     n = act_two.shape[-1]
-    shape = near((3136, n), BF)
+    shape = (7, 448, n)
+    out = pltpu.HBM(shape, BF)
+    two = pltpu.HBM(act_two.shape, BF)
     return pl.pallas_call(
         conv_three_kernel,
-        out_shape=(shape, shape),
+        out_shape=(out, out, two, two),
         grid=(7,),
-        in_specs=[vmem()] * 3,
-        out_specs=(vmem(), vmem()),
-        scratch_shapes=[pltpu.VMEM((256, 1152), BF)],
+        in_specs=[vmem()] * 4,
+        out_specs=(anywhere(),) * 4,
+        scratch_shapes=[
+            pltpu.VMEM((256, 1152), BF),
+            pltpu.VMEM((256, n), F32),
+            pltpu.VMEM(shape, BF),
+            pltpu.VMEM(shape, BF),
+            dma(9),
+            dma(9),
+            dma(7),
+            dma(7),
+        ],
         compiler_params=params(),
         cost_estimate=cost(5),
         name="conv_three",
-    )(held(act_two), weight, bias)
+    )(held(act_two), held(slope_two), weight, bias)
 
 
 def head_gradient(heads, actions, adv, values, old_logp, mask, count, centre, var):
@@ -393,12 +410,15 @@
 
 
 def dense_kernel(*refs, places, n_dp, n_own, rows):
-    place_ref, lengths_ref, flat_ref, slope_three_ref, heads_ref, bias_ref = refs[:6]
-    actions_ref, adv_ref, values_ref, logp_ref = refs[6:10]
-    piece_refs = refs[10 : 10 + len(places)]
-    d_three_ref, keep_ref, send_ref, grad_heads_ref, sums_ref, sum_heads_ref = refs[10 + len(places) : -4]
-    blocks_ref, weight_ref, d_dense_ref, sems = refs[-4:]
-    n = flat_ref.shape[-1]
+    place_ref, lengths_ref, flat_far_ref, slope_far_ref, two_far_ref, slope_two_far_ref = refs[:6]
+    heads_ref, bias_ref, actions_ref, adv_ref, values_ref, logp_ref = refs[6:12]
+    piece_refs = refs[12 : 12 + len(places)]
+    (
+        d_three_ref, two_ref, slope_two_ref, keep_ref, send_ref, grad_heads_ref, sums_ref, sum_heads_ref,
+        blocks_ref, weight_ref, d_dense_ref, flat_rows_ref, slope_ref,
+        sems, two_sems, slope_two_sems, flat_sems, slope_sems,
+    ) = refs[12 + len(places) :]
+    n = flat_rows_ref.shape[-1]
     cols = 128
     dp, own = place_ref[0], place_ref[1]
     stats = []
@@ -410,6 +430,10 @@
             )
     for copy in copies:
         copy.start()
+    start_rows(flat_far_ref, flat_rows_ref, flat_sems)
+    start_rows(slope_far_ref, slope_ref, slope_sems)
+    start_rows(two_far_ref, two_ref, two_sems)
+    start_rows(slope_two_far_ref, slope_two_ref, slope_two_sems)
     for copy in copies:
         copy.wait()
     for i in range(n_dp):
@@ -426,9 +450,11 @@
         for j in range(n_own):
             weight_ref[i * rows : (i + 1) * rows, j * cols : (j + 1) * cols] = blocks_ref[i, j, 0:rows]
     hid = n_own * cols
-    bias_dense = wide(bias_ref[160 : 160 + hid, :], hid, n)
-    bias_heads = wide(bias_ref[160 + hid : 160 + hid + 19, :], 19, n)
-    pre = dot(weight_ref[...], flat_ref[...], TN) + bias_dense
+    bias_dense = wide(bias_ref[:, 160 : 160 + hid], hid, n)
+    bias_heads = wide(bias_ref[:, 160 + hid : 160 + hid + 19], 19, n)
+    wait_rows(flat_far_ref, flat_rows_ref, flat_sems)
+    flat = flat_rows_ref[...].reshape(n_dp * rows, n)
+    pre = dot(weight_ref[...], flat, TN) + bias_dense
     hidden, slope = gelu_both(pre)
     hidden = hidden.astype(BF)
     head_weight = heads_ref[...].astype(BF)
@@ -448,28 +474,33 @@
     for half, ref in ((0, keep_ref), (1, send_ref)):
         for k in range(n_own // 4):
             both = [d_dense_ref[own ^ (4 * k + half)], d_dense_ref[own ^ (4 * k + 2 + half)]]
-            block = dot(flat_ref[...], jnp.concatenate(both, axis=0), NT).astype(BF)
+            block = dot(flat, jnp.concatenate(both, axis=0), NT).astype(BF)
             for i in range(n_dp):
                 rel = i ^ dp
                 spot = (rel % 2) * (n_dp // 2) + rel // 2
                 for m in range(2):
                     ref[2 * k + m, spot] = block[i * rows : (i + 1) * rows, m * cols : (m + 1) * cols]
+    wait_rows(slope_far_ref, slope_ref, slope_sems)
     total = jnp.zeros((64, n), F32)
     for part in range(7):
         span = slice(part * 448, part * 448 + 448)
-        d_three = (dot(weight_ref[span, :], d_dense) * slope_three_ref[span, :].astype(F32)).astype(BF)
-        d_three_ref[span, :] = d_three
+        d_three = (dot(weight_ref[span, :], d_dense) * slope_ref[part].astype(F32)).astype(BF)
+        d_three_ref[part] = d_three
         back = d_three.astype(F32)
         for c in range(7):
             total = total + back[c * 64 : c * 64 + 64]
     sums_ref[0:1, 0:64] = dot(jnp.ones((8, n), F32), total, NT, HIGH)[0:1]
     sums_ref[0:1, 64:128] = jnp.zeros((1, 64), F32)
-
-
-def dense(place, lengths, flat, slope_three, heads, bias, actions, adv, values, logp, pieces, n_dp, n_own, rows):
+    wait_rows(two_far_ref, two_ref, two_sems)
+    wait_rows(slope_two_far_ref, slope_two_ref, slope_two_sems)
+
+
+def dense(
+    place, lengths, flat, slope_three, act_two, slope_two, heads, bias, actions, adv, values, logp,
+    pieces, n_dp, n_own, rows,
+):
     n = flat.shape[-1]
     hid = n_own * 128
-    full = n_dp * rows
     part = jax.ShapeDtypeStruct((n_own // 2, n_dp, rows, 128), BF)
     arrays = [p[0] for p in pieces]
     body = functools.partial(
@@ -478,50 +509,57 @@
     return pl.pallas_call(
         body,
         out_shape=(
-            near((full, n), BF),
+            near(flat.shape, BF),
+            near(act_two.shape, BF),
+            near(act_two.shape, BF),
             part,
             part,
             jax.ShapeDtypeStruct(heads.shape, F32),
             jax.ShapeDtypeStruct((1, 128 + hid), F32),
             jax.ShapeDtypeStruct((1, heads.shape[0]), F32),
         ),
-        in_specs=[smem(), smem()] + [vmem()] * 8 + [anywhere()] * len(arrays),
-        out_specs=(vmem(),) * 6,
+        in_specs=[smem(), smem()] + [anywhere()] * 4 + [vmem()] * 6 + [anywhere()] * len(arrays),
+        out_specs=(vmem(),) * 8,
         scratch_shapes=[
             pltpu.VMEM((n_dp, n_own) + arrays[0].shape[1:], BF),
-            pltpu.VMEM((full, hid), BF),
+            pltpu.VMEM((n_dp * rows, hid), BF),
             pltpu.VMEM((n_own, 128, n), BF),
+            pltpu.VMEM(flat.shape, BF),
+            pltpu.VMEM(flat.shape, BF),
             dma(n_dp * n_own),
+            dma(9),
+            dma(9),
+            dma(7),
+            dma(7),
         ],
         compiler_params=params(32),
         cost_estimate=cost(8),
         name="dense",
-    )(place, lengths, held(flat), held(slope_three), heads, bias, actions, adv, values, logp, *arrays)
+    )(
+        place, lengths, far(flat), far(slope_three), far(act_two), far(slope_two), heads, bias,
+        actions, adv, values, logp, *[far(a) for a in arrays],
+    )
 
 
 def conv_three_back_kernel(
-    d_three_ref, act_far_ref, slope_far_ref, weight_ref, heads_ref,
-    d_two_ref, pack_ref, sum_ref,
-    band_ref, pad_ref, acc_ref, tot_ref, act_ref, slope_ref, act_sems, slope_sems,
+    d_three_ref, act_ref, slope_ref, one_far_ref, slope_one_far_ref, weight_ref, heads_ref,
+    d_two_ref, one_ref, slope_one_ref, pack_ref, sum_ref,
+    band_ref, pad_ref, acc_ref, tot_ref, one_sems, slope_one_sems,
 ):
     n = d_three_ref.shape[-1]
     step = pl.program_id(0)
 
     @pl.when(step == 0)
     def _():
-        for r in range(9):
-            start_row(slope_far_ref, slope_ref, slope_sems, r)
-            start_row(act_far_ref, act_ref, act_sems, r)
+        start_rows(one_far_ref, one_ref, one_sems)
+        start_rows(slope_one_far_ref, slope_one_ref, slope_one_sems)
         band_ref[...] = band_back(weight_ref[...], 3, 64, 3)
         pad_ref[...] = jnp.zeros_like(pad_ref)
         acc_ref[...] = jnp.zeros_like(acc_ref)
         tot_ref[...] = jnp.zeros_like(tot_ref)
         for r in range(7):
-            pad_ref[r + 2, 128 : 128 + 448, :] = d_three_ref[r * 448 : r * 448 + 448, :]
-        wait_row(act_far_ref, act_ref, act_sems, 0)
-        wait_row(act_far_ref, act_ref, act_sems, 1)
-
-    wait_row(slope_far_ref, slope_ref, slope_sems, step)
+            pad_ref[r + 2, 128 : 128 + 448, :] = d_three_ref[r]
+
     total = tot_ref[...]
     for part in range(3):
         patch = jnp.concatenate(
@@ -536,7 +574,6 @@
 
     @pl.when(step < 7)
     def _():
-        wait_row(act_far_ref, act_ref, act_sems, step + 2)
         row = pad_ref[step + 2, 128 : 128 + 448, :]
         second = jnp.concatenate([jnp.zeros((64, n), BF), row[256:448]], axis=0)
         for d_rows, start in ((row[0:256], 0), (second, 3)):
@@ -546,6 +583,8 @@
 
     @pl.when(step == 8)
     def _():
+        wait_rows(one_far_ref, one_ref, one_sems)
+        wait_rows(slope_one_far_ref, slope_one_ref, slope_one_sems)
         for a in range(3):
             out = None
             for c in range(4):
@@ -561,55 +600,50 @@
         sum_ref[...] = dot(jnp.ones((8, n), F32), tot_ref[...], NT, HIGH)[0:1]
 
 
-def conv_three_back(d_three, act_two, slope_two, weight, heads):
+def conv_three_back(d_three, act_two, slope_two, act_one, slope_one, weight, heads):
     n = act_two.shape[-1]
     return pl.pallas_call(
         conv_three_back_kernel,
         out_shape=(
             near(act_two.shape, BF),
+            near(act_one.shape, BF),
+            near(act_one.shape, BF),
             jax.ShapeDtypeStruct((96, 640), BF),
             jax.ShapeDtypeStruct((1, 64), F32),
         ),
         grid=(9,),
-        in_specs=[vmem(), anywhere(), anywhere(), vmem(), vmem()],
-        out_specs=(vmem(),) * 3,
+        in_specs=[vmem()] * 3 + [anywhere()] * 2 + [vmem()] * 2,
+        out_specs=(vmem(),) * 5,
         scratch_shapes=[
             pltpu.VMEM((192, 960), BF),
             pltpu.VMEM((11, 704, n), BF),
             pltpu.VMEM((256, 1152), F32),
             pltpu.VMEM((64, n), F32),
-            pltpu.VMEM(act_two.shape, BF),
-            pltpu.VMEM(act_two.shape, BF),
-            dma(9),
-            dma(9),
+            dma(10),
+            dma(10),
         ],
-        compiler_params=params(24),
+        compiler_params=params(),
         cost_estimate=cost(9),
         name="conv_three_back",
-    )(held(d_three), act_two, slope_two, weight, heads)
+    )(held(d_three), held(act_two), held(slope_two), far(act_one), far(slope_one), weight, heads)
 
 
 def conv_two_back_kernel(
-    d_two_ref, act_far_ref, slope_far_ref, weight_ref, d_one_ref, d_far_ref, grad_ref, sum_ref,
-    band_ref, pad_ref, acc_ref, tot_ref, act_ref, slope_ref, act_sems, slope_sems, out_sems,
+    d_two_ref, act_ref, slope_ref, weight_ref, pack_ref, d_one_ref, d_far_ref, grad_ref, sum_ref,
+    band_ref, pad_ref, acc_ref, tot_ref, out_sems,
 ):
     n = d_one_ref.shape[-1]
     step = pl.program_id(0)
 
     @pl.when(step == 0)
     def _():
-        for r in range(10):
-            start_row(slope_far_ref, slope_ref, slope_sems, r)
-            start_row(act_far_ref, act_ref, act_sems, r)
         band_ref[...] = band_back(weight_ref[...], 2, 128, 1)
         pad_ref[...] = jnp.zeros_like(pad_ref)
         acc_ref[...] = jnp.zeros_like(acc_ref)
         tot_ref[...] = jnp.zeros_like(tot_ref)
         for r in range(9):
             pad_ref[r + 1, 64 : 64 + 576, :] = d_two_ref[r]
-        wait_row(act_far_ref, act_ref, act_sems, 0)
-
-    wait_row(slope_far_ref, slope_ref, slope_sems, step)
+
     total = tot_ref[...]
     for col in range(10):
         patch = jnp.concatenate(
@@ -623,7 +657,6 @@
 
     @pl.when(step < 9)
     def _():
-        wait_row(act_far_ref, act_ref, act_sems, step + 1)
         for part in range(3):
             span = slice(3 * part, 3 * part + 4)
             cells = jnp.concatenate(
@@ -640,12 +673,14 @@
             for c in range(3):
                 piece = acc_ref[c * 64 : c * 64 + 64, a * 512 + c * 128 : a * 512 + c * 128 + 256]
                 out = piece if out is None else out + piece
-            grad_ref[:, a * 256 : a * 256 + 256] = out.astype(BF)
+            grad_ref[96:160, a * 256 : a * 256 + 256] = out.astype(BF)
+        grad_ref[0:96, :] = pack_ref[...]
+        grad_ref[96:160, 512:640] = jnp.zeros((64, 128), BF)
         sums = dot(jnp.ones((8, n), F32), tot_ref[...], NT, HIGH)[0:1]
         sum_ref[...] = (sums[:, 0:32] + sums[:, 32:64]) + (sums[:, 64:96] + sums[:, 96:128])
 
 
-def conv_two_back(d_two, act_one, slope_one, weight):
+def conv_two_back(d_two, act_one, slope_one, weight, pack):
     n = act_one.shape[-1]
     shape = act_one.shape
     return pl.pallas_call(
@@ -653,27 +688,23 @@
         out_shape=(
             near(shape, BF),
             pltpu.HBM(shape, BF),
-            jax.ShapeDtypeStruct((64, 512), BF),
+            jax.ShapeDtypeStruct((160, 640), BF),
             jax.ShapeDtypeStruct((1, 32), F32),
         ),
         grid=(10,),
-        in_specs=[vmem(), anywhere(), anywhere(), vmem()],
+        in_specs=[vmem()] * 5,
         out_specs=(vmem(), anywhere(), vmem(), vmem()),
         scratch_shapes=[
             pltpu.VMEM((128, 256), BF),
             pltpu.VMEM((11, 704, n), BF),
             pltpu.VMEM((192, 1024), F32),
             pltpu.VMEM((128, n), F32),
-            pltpu.VMEM(shape, BF),
-            pltpu.VMEM(shape, BF),
-            dma(10),
-            dma(10),
             dma(10),
         ],
-        compiler_params=params(32),
+        compiler_params=params(),
         cost_estimate=cost(11),
         name="conv_two_back",
-    )(held(d_two), act_one, slope_one, weight)
+    )(held(d_two), held(act_one), held(slope_one), weight, pack)
 
 
 def conv_one_grad_kernel(
@@ -913,8 +944,9 @@
     return [1 << b for b in range(size.bit_length() - 1)]
 
 
-def after(x, *others):
-    return lax.optimization_barrier((x,) + others)[0]
+def fence(*values):
+    leaves, tree = jax.tree.flatten(values)
+    return jax.tree.unflatten(tree, lax.optimization_barrier(tuple(leaves)))
 
 
 def stage(x, axis, bits, size):
@@ -931,15 +963,20 @@
     return (up[0] + up[1]) + (up[2] + up[3])
 
 
-def sum_stages(n_dp, n_own):
-    bits = bits_of(n_dp)
-    plan = [("own", tuple(bits_of(n_own)), n_own)]
-    if len(bits) % 2:
-        plan += [("dp", tuple(bits[k : k + 2]), n_dp) for k in range(1, len(bits), 2)]
-        plan.append(("dp", (bits[0],), n_dp))
-    else:
-        plan += [("dp", tuple(bits[k : k + 2]), n_dp) for k in range(0, len(bits), 2)]
-    return plan
+def bit_pairs(bits):
+    odd = len(bits) % 2
+    return [tuple(bits[k : k + 2]) for k in range(odd, len(bits), 2)] + [(b,) for b in bits[:odd]]
+
+
+def few_stages(n_dp, n_own):
+    plan = [("own", bits, n_own) for bits in bit_pairs(bits_of(n_own))]
+    return plan + [("dp", bits, n_dp) for bits in bit_pairs(bits_of(n_dp))]
+
+
+def light_stages(n_dp, n_own):
+    far_first = bits_of(n_dp)[::-1]
+    plan = [("dp", (bit,), n_dp) for bit in far_first] + [("own", (bit,), n_own) for bit in bits_of(n_own)[::-1]]
+    return plan[:1] + plan[len(far_first) : -1] + plan[1 : len(far_first)] + plan[-1:]
 
 
 def add_low(*terms):
@@ -991,108 +1028,118 @@
     dp_swap = lambda x, bit: swap(x, "dp", bit, n_dp)
     place = jnp.stack([lax.axis_index("dp"), lax.axis_index("own")]).astype(jnp.int32)
     bias_row = bias_all.reshape(1, -1)
-    adv, piece, bias = first(lengths, dones, rewards, old_values, dense_hidden, bias_row)
+    adv, piece = first(lengths, dones, rewards, old_values, dense_hidden)
     cells = frames.transpose(1, 2, 3, 0).reshape(grid, grid * planes, tokens)
 
     if tuned:
         along_z = [dp_swap(piece, 2 * k) for k in (1, 2, 3)]
-    act_one, act_one_far, slope_one = conv_one(cells, conv_first.T, bias)
+    act_one, slope_one_far = conv_one(cells, conv_first.T, bias_row)
     if tuned:
-        z_spots = [[(0, 0), (2, 0)], [(4, 0), (6, 0)]]
-        piece = after(piece, act_one_far)
-        z_parts = [jnp.stack([piece, along_z[0]]), jnp.stack([along_z[1], along_z[2]])]
-        act_one = after(act_one, *z_parts)
-        x_parts = [dp_swap(z, 1) for z in z_parts]
-        y_parts = [own_swap(z, 2) for z in z_parts]
-        pieces = list(zip(z_parts, z_spots))
-        pieces += [(own_swap(z, 1), [(i, j ^ 1) for i, j in sp]) for z, sp in pieces]
+        spots = [(2 * k, 0) for k in range(4)]
+        act_one, piece, along_z = fence(act_one, piece, along_z)
+        column = jnp.stack([piece] + along_z)
+        act_one, column = fence(act_one, column)
+        by_x, by_y = dp_swap(column, 1), own_swap(column, 2)
     else:
         pieces = plain_gather(piece, n_dp, n_own)
-    act_two, act_two_far, slope_two = conv_two(act_one, conv_second.T, bias)
+    act_two, slope_two, act_one_far = conv_two(act_one, conv_second.T, bias_row)
     if tuned:
-        act_two, *arrived = lax.optimization_barrier((act_two, *x_parts, *y_parts))
-        x_parts, y_parts = arrived[:2], arrived[2:]
-        corner = [own_swap(x_parts[0], 2), dp_swap(y_parts[1], 1)]
-        for parts, flip in ((x_parts, (1, 0)), (y_parts, (0, 2))):
-            for part, spots in zip(parts, z_spots):
-                spots = [(i ^ flip[0], j ^ flip[1]) for i, j in spots]
-                pieces.append((part, spots))
-                pieces.append((own_swap(part, 1), [(i, j ^ 1) for i, j in spots]))
-    flat, slope_three = conv_three(act_two, conv_third.T, bias)
+        act_two, column, by_x, by_y = fence(act_two, column, by_x, by_y)
+        halves = (by_x[0:2], by_y[2:4])
+        plane = jnp.concatenate([column, by_x, by_y])
+        act_two, halves, plane = fence(act_two, halves, plane)
+        corner = [own_swap(halves[0], 2), dp_swap(halves[1], 1)]
+        other = own_swap(plane, 1)
+    flat, slope_three, act_two_far, slope_two_far = conv_three(act_two, slope_two, conv_third.T, bias_row)
     if tuned:
-        flat, *corner = lax.optimization_barrier((flat, *corner))
-        for part, spots in zip(corner, z_spots):
-            spots = [(i ^ 1, j ^ 2) for i, j in spots]
-            pieces.append((part, spots))
-            pieces.append((own_swap(part, 1), [(i, j ^ 1) for i, j in spots]))
-    d_three, keep, send, here_heads, sums, sum_heads = dense(
-        place, lengths, flat, slope_three, dense_heads.T, bias,
+        flat, corner = fence(flat, corner)
+        corner = jnp.concatenate(corner)
+        plane_spots = [(i ^ x, j ^ y) for x, y in ((0, 0), (1, 0), (0, 2)) for i, j in spots]
+        corner_spots = [(i ^ 1, j ^ 2) for i, j in spots]
+        pieces = [(plane, plane_spots), (corner, corner_spots)]
+        pieces += [
+            (other, [(i, j ^ 1) for i, j in plane_spots]),
+            (own_swap(corner, 1), [(i, j ^ 1) for i, j in corner_spots]),
+        ]
+    d_three, act_two, slope_two, keep, send, here_heads, sums, sum_heads = dense(
+        place, lengths, flat, slope_three, act_two_far, slope_two_far, dense_heads.T, bias_row,
         actions, adv, old_values, old_logp, pieces, n_dp, n_own, rows,
     )
 
-    plan = sum_stages(n_dp, n_own)
-
-    def send_on(x, at, low):
+    many_plan, one_plan = light_stages(n_dp, n_own), few_stages(n_dp, n_own)
+
+    def leave(x, plan, at):
         axis, bits, size = plan[at]
-        x = x.astype(BF) if low else x
-        return x, stage(x, axis, bits, size)
-
-    def gather_up(state, other):
-        x, came = state
-        x, other = lax.optimization_barrier((x, other))
-        return stage_sum(x, came)
-
+        return stage(x, axis, bits, size)
+
+    def rest(x, plan, at, low):
+        for k in range(at, len(plan)):
+            total = stage_sum(x, leave(x, plan, k))
+            x = total.astype(BF) if low and k < len(plan) - 1 else total
+        return x
+
+    d_three, act_two, slope_two, keep, send = fence(d_three, act_two, slope_two, keep, send)
+    came = own_swap(send, 1) if tuned else None
+    d_two, act_one, slope_one, pack, sum_two = conv_three_back(
+        d_three, act_two, slope_two, act_one_far, slope_one_far, conv_third.T, here_heads
+    )
     if tuned:
-        came = own_swap(send, 1)
-    d_two, pack_three, sum_two = conv_three_back(d_three, act_two_far, slope_two, conv_third.T, here_heads)
+        d_two, keep, came = fence(d_two, keep, came)
+        block = add_low(keep, came)
+        ends = (block[1, 4:6], block[1, 6:8])
+        d_two, block, ends = fence(d_two, block, ends)
+        by_y, by_x = own_swap(ends[0], 2), dp_swap(ends[1], 1)
+    d_one, d_one_far, pack, sum_one = conv_two_back(d_two, act_one, slope_one, conv_second.T, pack)
     if tuned:
-        block = add_low(after(keep, d_two), came)
-        by_y, by_x = own_swap(block[1, 4:6], 2), dp_swap(block[1, 6:8], 1)
-        d_two = after(d_two, block)
-    three = send_on(pack_three, 0, True)
-    d_one, d_one_far, pack_two, sum_one = conv_two_back(d_two, act_one_far, slope_one, conv_second.T)
-    if tuned:
-        block = after(block, d_one)
+        d_one, d_one_far, pack, block, by_x, by_y = fence(d_one, d_one_far, pack, block, by_x, by_y)
         side_x = jnp.concatenate([add_low(block[0, 4:6], by_y), block[0, 6:8]])
         side_y = jnp.concatenate([block[1, 0:2], add_low(block[1, 2:4], by_x)])
+        d_one, d_one_far, pack, block, side_x, side_y = fence(d_one, d_one_far, pack, block[0, 0:4], side_x, side_y)
         by_x, by_y = dp_swap(side_x, 1), own_swap(side_y, 2)
-        d_one = after(d_one, side_x, side_y)
-    three = send_on(gather_up(three, d_one_far), 1, True)
-    d_one = after(d_one, three[0])
-    two = send_on(pack_two, 0, True)
+    many = leave(pack, many_plan, 0)
     pack_one = conv_one_grad(cells, d_one, sums, sum_heads, sum_one, sum_two)
     if tuned:
-        column = add_low(after(block[0, 0:4], pack_one), by_x, by_y)
-        parts = [column[0]] + [dp_swap(column[k], 2 * k) for k in (1, 2, 3)]
-        d_one_far = after(d_one_far, column)
+        pack_one, block, by_x, by_y = fence(pack_one, block, by_x, by_y)
+        block = add_low(block, by_x, by_y)
+        parts = [block[k] for k in range(4)]
     else:
         parts = plain_scatter(keep, send, n_dp, n_own)
-    three = send_on(gather_up(three, pack_one), 2, True)
-    two = send_on(gather_up(two, pack_one), 1, True)
-    one = send_on(pack_one, 0, False)
-    d_one_far = after(d_one_far, three[0], two[0], one[0])
+    pack_one, d_one_far, pack, many = fence(pack_one, d_one_far, pack, many)
+    pack = stage_sum(pack, many).astype(BF)
+    pack_one, d_one_far, pack, parts = fence(pack_one, d_one_far, pack, parts)
+    if tuned:
+        parts = [parts[0]] + [dp_swap(parts[k], 2 * k) for k in (1, 2, 3)]
+    many = leave(pack, many_plan, 1)
+    one = leave(pack_one, one_plan, 0)
     shape = cells.shape
-    back = frames_back(d_one_far, conv_first.T, shape, 0, 4)
-    two = send_on(gather_up(two, back), 2, True)
-    one = send_on(gather_up(one, back), 1, False)
-    d_one_far = after(d_one_far, two[0], one[0])
-    back = frames_back(d_one_far, conv_first.T, shape, 4, 8, back)
-    one = send_on(gather_up(one, back), 2, False)
-    d_one_far = after(d_one_far, one[0])
-    back = frames_back(d_one_far, conv_first.T, shape, 8, grid // 2 + 1, back)
-
-    def finish(state, low):
-        for at in range(3, len(plan)):
-            state = send_on(gather_up(state, back), at, low)
-        return gather_up(state, back)
-
+    cuts = (0, 4, 8, grid // 2 + 1)
+    back = None
+    for k in range(3):
+        back = frames_back(d_one_far, conv_first.T, shape, cuts[k], cuts[k + 1], back)
+        back, d_one_far, parts, pack, many, pack_one, one = fence(
+            back, d_one_far, parts, pack, many, pack_one, one
+        )
+        pack = stage_sum(pack, many).astype(BF)
+        pack_one = stage_sum(pack_one, one)
+        back, d_one_far, parts, pack, pack_one = fence(back, d_one_far, parts, pack, pack_one)
+        many = leave(pack, many_plan, k + 2)
+        if k < 2:
+            one = leave(pack_one, one_plan, k + 1)
     frames_grad = back.reshape(grid, grid, planes, tokens).transpose(3, 0, 1, 2)
     grad_dense, *wide_step = dense_step(
         dense_hidden, mean_dense, square_dense, right_dense, parts, RATE / math.sqrt(rows * n_dp)
     )
+    pack_one = rest(pack_one, one_plan, 3, False)
+    first_step = steps(
+        [pack_one], [(0, 0, 32, 256)], [(conv_first, mean_first, square_first, left_first, right_first)]
+    )
+    grad_dense, first_step, pack, many = fence(grad_dense, first_step, pack, many)
+    pack = stage_sum(pack, many)
+    if len(many_plan) > 5:
+        pack = rest(pack.astype(BF), many_plan, 5, True)
     late = steps(
-        [finish(three, True), finish(two, True)],
-        [(0, 0, 64, 576), (0, 64, 19, 512), (1, 0, 64, 512)],
+        [pack],
+        [(0, 0, 64, 576), (0, 64, 19, 512), (0, 96, 64, 512)],
         [
             (conv_third, mean_third, square_third, left_third, right_third),
             (dense_heads, mean_heads, square_heads, left_heads, right_heads),
@@ -1100,10 +1147,6 @@
         ],
     )
     third, top, second = late[0:4], late[4:8], late[8:12]
-    pack_one = finish(one, False)
-    first_step = steps(
-        [pack_one], [(0, 0, 32, 256)], [(conv_first, mean_first, square_first, left_first, right_first)]
-    )
     grad_bias = jnp.concatenate(
         [pack_one[36, 0:32], pack_one[35, 0:64], pack_one[34, 0:64], pack_one[32], pack_one[33], pack_one[37, 0:19]]
     )

time: 175 us -> 142 us (0.81)
  waiting for transfers between devices: 16.4 us -> 5.9 us
  starting transfers between devices: 44 us -> 34 us
  local copies, waits for them, and re-layouts: 8.83 us -> 1.25 us
  Pallas kernels: 101 us -> 96.1 us
    ppermute x46 -> x29, waiting for transfers between devices: 16.4 us -> 5.9 us  [swap(): return lax.ppermute(x, axis, [(i, i ^ bit) for i in range(size)])]
    ppermute x46 -> x29, starting transfers between devices: 44 us -> 34 us  [swap(): return lax.ppermute(x, axis, [(i, i ^ bit) for i in range(size)])]
    unnamed x94 -> x73, local copies, waits for them, and re-layouts: 7.35 us -> 0.97 us
    pallas_call x1, Pallas kernels: 16.3 us -> 11.7 us  [conv_two_back(): pl.pallas_call(conv_two_back_kernel, out_shape=(near(shape, BF), pltpu.HB...]
  transfers between devices with their start and end apart: 46 -> 29, of which waited for: 9 -> 6; matrix products, arithmetic and copies ran while one was open for 1% -> 1% of each run, Pallas kernels for 49% -> 54%
where the time goes in v3:
time: 142 us; the launch traced here: 141 us
  Pallas kernels  96.1 us (68%)
  starting transfers between devices  34 us (24%)
  waiting for transfers between devices  5.9 us (4%)
  between operations  2.17 us (2%)
  other arithmetic  2 us (1%)
    ppermute x29, starting transfers between devices, swap(): return lax.ppermute(x, axis, [(i, i ^ bit) for i in range(size)])  34 us
    pallas_call x1, Pallas kernels, conv_one(): pl.pallas_call(conv_one_kernel, out_shape=(near(shape, BF), pltpu.HBM(sha...  14.5 us
    pallas_call x3, Pallas kernels, frames_back(): pl.pallas_call(functools.partial(frames_back_kernel, begin=begin, end=end...  13.8 us
    pallas_call x1, Pallas kernels, dense(): pl.pallas_call(body, out_shape=(near(flat.shape, BF), near(act_two.shape,...  12 us
    pallas_call x1, Pallas kernels, conv_two_back(): pl.pallas_call(conv_two_back_kernel, out_shape=(near(shape, BF), pltpu.HB...  11.7 us
    pallas_call x1, Pallas kernels, conv_one_grad(): pl.pallas_call(conv_one_grad_kernel, out_shape=jax.ShapeDtypeStruct((40,...  11 us
    pallas_call x1, Pallas kernels, conv_three_back(): pl.pallas_call(conv_three_back_kernel, out_shape=(near(act_two.shape, BF)...  9.39 us
    pallas_call x1, Pallas kernels, conv_two(): pl.pallas_call(conv_two_kernel, out_shape=(near(shape, BF), near(shape, B...  7.4 us
  transfers between devices with their start and end apart: 29, of which 6 were waited for; matrix products, arithmetic and copies ran while one was open for 1% of the time, Pallas kernels for 54%

profile of v3, /device:TPU:0, one launch (start us, length us, event | category | flops | bytes accessed | tf_op | source)
XLA Modules:
  0.0 141.5 jit_solution(17974568058989376172)
XLA Ops:
  1.3 2.4 %first.1 = (f32[1,256]{1,0:T(1,128)}, bf16[416,128]{1,0:T(8,128)(2,1)}) custom-call(s32[1]{0:T(128)S(6)} %copy.64.lengths_ref.refs_1_, s32[1,256]{1,0:T(1,128)} %dones_ref.1, f32[1,256]{1,0:T(1,128)} %rewards_ref.1, f32[1,256]{1,0:T(1,128)} %refs_10_.2, f32[392,128]{1,0:T(8,128)} %refs_0_.1), custom_call_target="tpu_custom_call" | custom-call | flops 3000000000 | tf_op jit(solution)/shard_map/first/pallas_call | solution.py:209
  3.7 5.0 %collective-permute-start.2 = (bf16[416,128]{1,0:T(8,128)(2,1)}, bf16[416,128]{1,0:T(8,128)(2,1)S(1)}, u32[]{:S(2)}, u32[]{:S(2)}) collective-permute-start(bf16[416,128]{1,0:T(8,128)(2,1)} %get-tuple-element.196), channel_id=1, source_target_pairs={{0,24},{4,28},{8,16},{12,20},{16,8},{20,12},{24,0},{28,4},{1,25},{... | collective-permute-start | bytes 319496 | tf_op jit(solution)/shard_map/ppermute | solution.py:940
  9.4 14.5 %conv_one.1 = (bf16[10,10,128,256]{3,2,1,0:T(8,128)(2,1)S(1)}, bf16[10,10,128,256]{3,2,1,0:T(8,128)(2,1)}) custom-call(bf16[21,1344,256]{2,1,0:T(8,128)(2,1)} %bitcast.102, f32[32,256]{1,0:T(8,128)S(1)} %bitcast.74, f32[1,691]{1,0:T(1,128)S(1)} %reshape.64.bias_ref.refs_7_), custom_call_target="tpu_custom_call" | custom-call | flops 12000000000 | tf_op jit(solution)/shard_map/conv_one/pallas_call | solution.py:256
  23.9 1.8 %collective-permute-start.4 = (bf16[4,416,128]{2,1,0:T(8,128)(2,1)S(1)}, bf16[4,416,128]{2,1,0:T(8,128)(2,1)S(1)}, u32[]{:S(2)}, u32[]{:S(2)}) collective-permute-start(bf16[4,416,128]{2,1,0:T(8,128)(2,1)S(1)} %pad_maximum_fusion.1), channel_id=1, source_target_pairs={{0,2},{1,3},{2,0},{3,1},{4,6},{5,7},{6,4},{7,5},{8,10},{9,11},{10,... | collective-permute-start | bytes 1277960 | tf_op jit(solution)/shard_map/ppermute | solution.py:940
  25.7 1.5 %collective-permute-start.3 = (bf16[4,416,128]{2,1,0:T(8,128)(2,1)S(1)}, bf16[4,416,128]{2,1,0:T(8,128)(2,1)S(1)}, u32[]{:S(2)}, u32[]{:S(2)}) collective-permute-start(bf16[4,416,128]{2,1,0:T(8,128)(2,1)S(1)} %pad_maximum_fusion.1), channel_id=1, source_target_pairs={{0,4},{4,0},{8,12},{12,8},{16,20},{20,16},{24,28},{28,24},{1,5},{5... | collective-permute-start | bytes 1277960 | tf_op jit(solution)/shard_map/ppermute | solution.py:940
  27.2 7.4 %conv_two.1 = (bf16[9,576,256]{2,1,0:T(8,128)(2,1)S(1)}, bf16[9,576,256]{2,1,0:T(8,128)(2,1)S(1)}, bf16[10,10,128,256]{3,2,1,0:T(8,128)(2,1)}) custom-call(bf16[10,10,128,256]{3,2,1,0:T(8,128)(2,1)S(1)} %get-tuple-element.200.one_ref, f32[64,512]{1,0:T(8,128)S(1)} %bitcast.84, f32[1,691]{1,0:T(1,128)S(1)} %reshape.64.bias_ref.refs_7_), custom_call_target="tpu_custom_call" | custom-call | flops 7000000000 | tf_op jit(solution)/shard_map/conv_two/pallas_call | solution.py:306
  35.0 1.2 collective-permute-done.3
  37.1 1.5 %collective-permute-start.6 = (bf16[2,416,128]{2,1,0:T(8,128)(2,1)S(1)}, bf16[2,416,128]{2,1,0:T(8,128)(2,1)S(1)}, u32[]{:S(2)}, u32[]{:S(2)}) collective-permute-start(bf16[2,416,128]{2,1,0:T(8,128)(2,1)S(1)} %slice.58), channel_id=1, source_target_pairs={{0,4},{4,0},{8,12},{12,8},{16,20},{20,16},{24,28},{28,24},{1,5},{5... | collective-permute-start | bytes 638984 | tf_op jit(solution)/shard_map/ppermute | solution.py:940
  38.6 6.3 %conv_three.1 = (bf16[7,448,256]{2,1,0:T(8,128)(2,1)}, bf16[7,448,256]{2,1,0:T(8,128)(2,1)}, bf16[9,576,256]{2,1,0:T(8,128)(2,1)}, bf16[9,576,256]{2,1,0:T(8,128)(2,1)}) custom-call(bf16[9,576,256]{2,1,0:T(8,128)(2,1)S(1)} %get-tuple-element.207.two_ref, bf16[9,576,256]{2,1,0:T(8,128)(2,1)S(1)} %get-tuple-element.208.slope_two_ref, f32[64,576]{1,0:T(8,128)S(1)} %bitcast.79, ...), custom_call_target="tpu_custom_call" | custom-call | flops 5000000000 | tf_op jit(solution)/shard_map/conv_three/pallas_call | solution.py:359
  45.2 1.7 %collective-permute-done.8.refs_15_ = bf16[4,416,128]{2,1,0:T(8,128)(2,1)S(1)} collective-permute-done((bf16[4,416,128]{2,1,0:T(8,128)(2,1)S(1)}, bf16[4,416,128]{2,1,0:T(8,128)(2,1)S(1)}, u32[]{:S(2)}, u32[]{:S(2)}) %collective-permute-start.8) | collective-permute-done | bytes 426016 | tf_op jit(solution)/shard_map/ppermute | solution.py:940
  47.7 12.0 %dense.1 = (bf16[7,448,256]{2,1,0:T(8,128)(2,1)S(1)}, bf16[9,576,256]{2,1,0:T(8,128)(2,1)S(1)}, bf16[9,576,256]{2,1,0:T(8,128)(2,1)S(1)}, bf16[2,8,392,128]{3,2,...) custom-call(s32[2]{0:T(128)S(1)} %pad_add_fusion.refs_0_, ...), custom_call_target="tpu_custom_call" | custom-call | flops 8000000000 | tf_op jit(solution)/shard_map/dense/pallas_call | solution.py:509
  59.9 9.4 %conv_three_back.1 = (bf16[9,576,256]{2,1,0:T(8,128)(2,1)S(1)}, bf16[10,10,128,256]{3,2,1,0:T(8,128)(2,1)S(1)}, bf16[10,10,128,256]{3,2,1,0:T(8,128)(2,1)S(1)}, bf16[96,640]{1,0:T(8,128)(2,1)S(1)}, f32[1,64]{1,0:T(1,128)S(1)}) custom-call(bf16[7,448,256]{2,1,0:T(8,128)(2,1)S(1)} %get-tuple-element.225.d_three_ref, ...), custom_call_target="tpu_custom_call" | custom-call | flops 8999999488 | tf_op jit(solution)/shard_map/conv_three_back/pallas_call | solution.py:605
  70.8 1.5 %collective-permute-start.11 = (bf16[2,392,128]{2,1,0:T(8,128)(2,1)S(1)}, bf16[2,392,128]{2,1,0:T(8,128)(2,1)S(1)}, u32[]{:S(2)}, u32[]{:S(2)}) collective-permute-start(bf16[2,392,128]{2,1,0:T(8,128)(2,1)S(1)} %get-tuple-element.246), channel_id=1, source_target_pairs={{0,2},{1,3},{2,0},{3,1},{4,6},{5,7},{6,4},{7,5},{8,10},{9,11},{10,... | collective-permute-start | bytes 602120 | tf_op jit(solution)/shard_map/ppermute | solution.py:940
  72.3 11.7 %conv_two_back.1 = (bf16[10,10,128,256]{3,2,1,0:T(8,128)(2,1)S(1)}, bf16[10,10,128,256]{3,2,1,0:T(8,128)(2,1)}, bf16[160,640]{1,0:T(8,128)(2,1)S(1)}, f32[1,32]{1,0:T(1,128)S(1)}) custom-call(bf16[9,576,256]{2,1,0:T(8,128)(2,1)S(1)} %get-tuple-element.237.d_two_ref, bf16[10,10,128,256]{3,2,1,0:T(8,128)(2,1)S(1)} %get-tuple-element.238.act_ref, ...), custom_call_target="tpu_custom_call" | custom-call | flops 11000000512 | tf_op jit(solution)/shard_map/conv_two_back/pallas_call | solution.py:686
  84.4 2.4 %collective-permute-start.14 = (bf16[160,640]{1,0:T(8,128)(2,1)S(1)}, bf16[160,640]{1,0:T(8,128)(2,1)S(1)}, u32[]{:S(2)}, u32[]{:S(2)}) collective-permute-start(bf16[160,640]{1,0:T(8,128)(2,1)S(1)} %get-tuple-element.266), channel_id=1, source_target_pairs={{0,16},{4,20},{8,24},{12,28},{16,0},{20,4},{24,8},{28,12},{1,17},{... | collective-permute-start | bytes 614408 | tf_op jit(solution)/shard_map/ppermute | solution.py:940
  86.8 1.1 collective-permute-start.12
  88.4 11.0 %conv_one_grad.1 = f32[40,256]{1,0:T(8,128)S(1)} custom-call(bf16[21,1344,256]{2,1,0:T(8,128)(2,1)} %bitcast.103, bf16[10,10,128,256]{3,2,1,0:T(8,128)(2,1)S(1)} %get-tuple-element.253.d_one_ref, f32[1,640]{1,0:T(1,128)S(1)} %get-tuple-element.254.dense_ref, f32[1,19]{1,0:T(1,128)S(1)} %get-tuple-element.255.heads_ref, ...), custom_call_target="tpu_custom_call" | custom-call | flops 10000000000 | tf_op jit(solution)/shard_map/conv_one_grad/pallas_call | solution.py:752
  99.8 1.5 %collective-permute-start.20 = (f32[40,256]{1,0:T(8,128)S(1)}, f32[40,256]{1,0:T(8,128)S(1)}, u32[]{:S(2)}, u32[]{:S(2)}) collective-permute-start(f32[40,256]{1,0:T(8,128)S(1)} %conv_one_grad.1), channel_id=1, source_target_pairs={{0,2},{1,3},{2,0},{3,1},{4,6},{5,7},{6,4},{7,5},{8,10},{9,11},{10,... | collective-permute-start | bytes 122888 | tf_op jit(solution)/shard_map/ppermute | solution.py:940
  101.6 1.7 %collective-permute-start.15 = (bf16[392,128]{1,0:T(8,128)(2,1)S(1)}, bf16[392,128]{1,0:T(8,128)(2,1)S(1)}, u32[]{:S(2)}, u32[]{:S(2)}) collective-permute-start(bf16[392,128]{1,0:T(8,128)(2,1)S(1)} %get-tuple-element.273), channel_id=1, source_target_pairs={{0,8},{4,12},{8,0},{12,4},{16,24},{20,28},{24,16},{28,20},{1,9},{5... | collective-permute-start | bytes 301064 | tf_op jit(solution)/shard_map/ppermute | solution.py:940
  103.7 2.4 %collective-permute-start.17 = (bf16[392,128]{1,0:T(8,128)(2,1)S(1)}, bf16[392,128]{1,0:T(8,128)(2,1)S(1)}, u32[]{:S(2)}, u32[]{:S(2)}) collective-permute-start(bf16[392,128]{1,0:T(8,128)(2,1)S(1)} %get-tuple-element.275), channel_id=1, source_target_pairs={{0,24},{4,28},{8,16},{12,20},{16,8},{20,12},{24,0},{28,4},{1,25},{... | collective-permute-start | bytes 301064 | tf_op jit(solution)/shard_map/ppermute | solution.py:940
  106.0 1.5 %collective-permute-start.18 = (bf16[160,640]{1,0:T(8,128)(2,1)S(1)}, bf16[160,640]{1,0:T(8,128)(2,1)S(1)}, u32[]{:S(2)}, u32[]{:S(2)}) collective-permute-start(bf16[160,640]{1,0:T(8,128)(2,1)S(1)} %add_convert_fusion.5), channel_id=1, source_target_pairs={{0,2},{1,3},{2,0},{3,1},{4,6},{5,7},{6,4},{7,5},{8,10},{9,11},{10,... | collective-permute-start | bytes 614408 | tf_op jit(solution)/shard_map/ppermute | solution.py:940
  107.5 4.8 %frames_back.3.refs_2_ = bf16[21,1344,256]{2,1,0:T(8,128)(2,1)} custom-call(bf16[10,10,128,256]{3,2,1,0:T(8,128)(2,1)} %get-tuple-element.310.refs_0_, f32[32,256]{1,0:T(8,128)S(1)} %bitcast.75), custom_call_target="tpu_custom_call" | custom-call | flops 4000000000 | tf_op jit(solution)/shard_map/frames_back/pallas_call | solution.py:835
  113.3 1.5 %collective-permute-start.25 = (f32[40,256]{1,0:T(8,128)S(1)}, f32[40,256]{1,0:T(8,128)S(1)}, u32[]{:S(2)}, u32[]{:S(2)}) collective-permute-start(f32[40,256]{1,0:T(8,128)S(1)} %add_add_fusion.1), channel_id=1, source_target_pairs={{0,24},{4,28},{8,16},{12,20},{16,8},{20,12},{24,0},{28,4},{1,25},{... | collective-permute-start | bytes 122888 | tf_op jit(solution)/shard_map/ppermute | solution.py:940
  114.7 2.7 %collective-permute-start.24 = (f32[40,256]{1,0:T(8,128)S(1)}, f32[40,256]{1,0:T(8,128)S(1)}, u32[]{:S(2)}, u32[]{:S(2)}) collective-permute-start(f32[40,256]{1,0:T(8,128)S(1)} %add_add_fusion.1), channel_id=1, source_target_pairs={{0,16},{4,20},{8,24},{12,28},{16,0},{20,4},{24,8},{28,12},{1,17},{... | collective-permute-start | bytes 122888 | tf_op jit(solution)/shard_map/ppermute | solution.py:940
  117.7 1.7 %collective-permute-start.22 = (bf16[160,640]{1,0:T(8,128)(2,1)S(1)}, bf16[160,640]{1,0:T(8,128)(2,1)S(1)}, u32[]{:S(2)}, u32[]{:S(2)}) collective-permute-start(bf16[160,640]{1,0:T(8,128)(2,1)S(1)} %add_convert_fusion.4), channel_id=1, source_target_pairs={{0,8},{4,12},{8,0},{12,4},{16,24},{20,28},{24,16},{28,20},{1,9},{5... | collective-permute-start | bytes 614408 | tf_op jit(solution)/shard_map/ppermute | solution.py:940
  119.4 5.0 %frames_back.4.refs_2_ = bf16[21,1344,256]{2,1,0:T(8,128)(2,1)} custom-call(bf16[10,10,128,256]{3,2,1,0:T(8,128)(2,1)} %get-tuple-element.310.refs_0_, f32[32,256]{1,0:T(8,128)S(1)} %bitcast.76, bf16[21,1344,256]{2,1,0:T(8,128)(2,1)} %frames_back.3.refs_2_), custom_call_target="tpu_custom_call", output_to_operand_aliasing={{}: (2, {})} | custom-call | flops 4000000000 | tf_op jit(solution)/shard_map/frames_back/pallas_call | solution.py:835
  125.4 1.0 collective-permute-start.27
  126.5 1.1 collective-permute-start.26
  127.5 4.0 %frames_back.5 = bf16[21,1344,256]{2,1,0:T(8,128)(2,1)} custom-call(bf16[10,10,128,256]{3,2,1,0:T(8,128)(2,1)} %get-tuple-element.310.refs_0_, f32[32,256]{1,0:T(8,128)S(1)} %bitcast.77, bf16[21,1344,256]{2,1,0:T(8,128)(2,1)} %frames_back.4.refs_2_), custom_call_target="tpu_custom_call", output_to_operand_aliasing={{}: (2, {})} | custom-call | flops 3000000000 | tf_op jit(solution)/shard_map/frames_back/pallas_call | solution.py:835
  132.8 1.3 steps.2
  134.4 1.5 %dense_step.1 = (f32[392,128]{1,0:T(8,128)}, f32[392,128]{1,0:T(8,128)}, f32[392,128]{1,0:T(8,128)}, f32[392,128]{1,0:T(8,128)}) custom-call(f32[392,128]{1,0:T(8,128)S(1)} %copy-done.5, f32[392,128]{1,0:T(8,128)S(1)} %copy-done.6, f32[392,128]{1,0:T(8,128)S(1)} %copy-done.7, f32[1,128,128]{2,1,0:T(8,128)S(1)} %copy-done.14, ...), custom_call_target="tpu_custom_call" | custom-call | flops 3000000000 | tf_op jit(solution)/shard_map/dense_step/pallas_call | solution.py:928
  136.7 4.7 %steps.3 = (f32[64,576]{1,0:T(8,128)}, f32[64,576]{1,0:T(8,128)}, f32[64,576]{1,0:T(8,128)}, f32[64,576]{1,0:T(8,128)}, f32[19,512]{1,0:T(8,128)}, /*index=5*/f3...) custom-call(f32[160,640]{1,0:T(8,128)S(1)} %convert_add_fusion.refs_, ...), custom_call_target="tpu_custom_call" | custom-call | flops 5000000000 | tf_op jit(solution)/shard_map/steps/pallas_call | solution.py:900
  (142 shorter events, 10.3 us)
Async XLA Ops:
  3.7 20.1 %collective-permute-start.2 = (bf16[416,128]{1,0:T(8,128)(2,1)}, bf16[416,128]{1,0:T(8,128)(2,1)S(1)}, u32[]{:S(2)}, u32[]{:S(2)}) collective-permute-start(bf16[416,128]{1,0:T(8,128)(2,1)} %get-tuple-element.196), channel_id=1, source_target_pairs={{0,24},{4,28},{8,16},{12,20},{16,8},{20,12},{24,0},{28,4},{1,25},{... | collective-permute-start | bytes 319496 | tf_op jit(solution)/shard_map/ppermute | solution.py:940
  8.8 15.1 %collective-permute-start.1 = (bf16[416,128]{1,0:T(8,128)(2,1)}, bf16[416,128]{1,0:T(8,128)(2,1)S(1)}, u32[]{:S(2)}, u32[]{:S(2)}) collective-permute-start(bf16[416,128]{1,0:T(8,128)(2,1)} %get-tuple-element.196), channel_id=1, source_target_pairs={{0,16},{4,20},{8,24},{12,28},{16,0},{20,4},{24,8},{28,12},{1,17},{... | collective-permute-start | bytes 319496 | tf_op jit(solution)/shard_map/ppermute | solution.py:940
  8.8 15.1 %collective-permute-start = (bf16[416,128]{1,0:T(8,128)(2,1)}, bf16[416,128]{1,0:T(8,128)(2,1)S(1)}, u32[]{:S(2)}, u32[]{:S(2)}) collective-permute-start(bf16[416,128]{1,0:T(8,128)(2,1)} %get-tuple-element.196), channel_id=1, source_target_pairs={{0,8},{4,12},{8,0},{12,4},{16,24},{20,28},{24,16},{28,20},{1,9},{5... | collective-permute-start | bytes 319496 | tf_op jit(solution)/shard_map/ppermute | solution.py:940
  9.3 14.5 %copy-start.30 = (bf16[416,128]{1,0:T(8,128)(2,1)S(1)}, bf16[416,128]{1,0:T(8,128)(2,1)}, u32[]{:S(2)}) copy-start(bf16[416,128]{1,0:T(8,128)(2,1)} %get-tuple-element.196) | copy-start | bytes 319492
  9.3 17.9 %copy-start.11 = (f32[512,64]{0,1:T(8,128)S(1)}, f32[512,64]{0,1:T(8,128)}, u32[]{:S(2)}) copy-start(f32[512,64]{0,1:T(8,128)} %param.42) | copy-start | bytes 393220
  23.9 11.1 %collective-permute-start.4 = (bf16[4,416,128]{2,1,0:T(8,128)(2,1)S(1)}, bf16[4,416,128]{2,1,0:T(8,128)(2,1)S(1)}, u32[]{:S(2)}, u32[]{:S(2)}) collective-permute-start(bf16[4,416,128]{2,1,0:T(8,128)(2,1)S(1)} %pad_maximum_fusion.1), channel_id=1, source_target_pairs={{0,2},{1,3},{2,0},{3,1},{4,6},{5,7},{6,4},{7,5},{8,10},{9,11},{10,... | collective-permute-start | bytes 1277960 | tf_op jit(solution)/shard_map/ppermute | solution.py:940
  25.7 10.5 %collective-permute-start.3 = (bf16[4,416,128]{2,1,0:T(8,128)(2,1)S(1)}, bf16[4,416,128]{2,1,0:T(8,128)(2,1)S(1)}, u32[]{:S(2)}, u32[]{:S(2)}) collective-permute-start(bf16[4,416,128]{2,1,0:T(8,128)(2,1)S(1)} %pad_maximum_fusion.1), channel_id=1, source_target_pairs={{0,4},{4,0},{8,12},{12,8},{16,20},{20,16},{24,28},{28,24},{1,5},{5... | collective-permute-start | bytes 1277960 | tf_op jit(solution)/shard_map/ppermute | solution.py:940
  36.5 10.4 %collective-permute-start.7 = (bf16[12,416,128]{2,1,0:T(8,128)(2,1)S(1)}, bf16[12,416,128]{2,1,0:T(8,128)(2,1)}, u32[]{:S(2)}, u32[]{:S(2)}) collective-permute-start(bf16[12,416,128]{2,1,0:T(8,128)(2,1)S(1)} %pad_maximum_fusion.refs_12_), channel_id=1, source_target_pairs={{0,1},{1,0},{2,3},{3,2},{4,5},{5,4},{6,7},{7,6},{8,9},{9,8},{10,11... | collective-permute-start | bytes 3833864 | tf_op jit(solution)/shard_map/ppermute | solution.py:940
  36.5 8.4 %collective-permute-start.5 = (bf16[2,416,128]{2,1,0:T(8,128)(2,1)S(1)}, bf16[2,416,128]{2,1,0:T(8,128)(2,1)S(1)}, u32[]{:S(2)}, u32[]{:S(2)}) collective-permute-start(bf16[2,416,128]{2,1,0:T(8,128)(2,1)S(1)} %slice.57), channel_id=1, source_target_pairs={{0,2},{1,3},{2,0},{3,1},{4,6},{5,7},{6,4},{7,5},{8,10},{9,11},{10,... | collective-permute-start | bytes 638984 | tf_op jit(solution)/shard_map/ppermute | solution.py:940
  37.1 7.9 %collective-permute-start.6 = (bf16[2,416,128]{2,1,0:T(8,128)(2,1)S(1)}, bf16[2,416,128]{2,1,0:T(8,128)(2,1)S(1)}, u32[]{:S(2)}, u32[]{:S(2)}) collective-permute-start(bf16[2,416,128]{2,1,0:T(8,128)(2,1)S(1)} %slice.58), channel_id=1, source_target_pairs={{0,4},{4,0},{8,12},{12,8},{16,20},{20,16},{24,28},{28,24},{1,5},{5... | collective-permute-start | bytes 638984 | tf_op jit(solution)/shard_map/ppermute | solution.py:940
  38.6 9.1 %copy-start.25 = (f32[1,256]{1,0:T(1,128)S(1)}, f32[1,256]{1,0:T(1,128)}, u32[]{:S(2)}) copy-start(f32[1,256]{1,0:T(1,128)} %refs_10_.2) | copy-start | bytes 3076
  45.1 1.8 %collective-permute-start.8 = (bf16[4,416,128]{2,1,0:T(8,128)(2,1)S(1)}, bf16[4,416,128]{2,1,0:T(8,128)(2,1)S(1)}, u32[]{:S(2)}, u32[]{:S(2)}) collective-permute-start(bf16[4,416,128]{2,1,0:T(8,128)(2,1)S(1)} %constant_dynamic-update-slice_fusion.refs_13_), channel_id=1, source_target_pairs={{0,1},{1,0},{2,3},{3,2},{4,5},{5,4},{6,7},{7,6},{8,9},{9,8},{10,11... | collective-permute-start | bytes 1277960 | tf_op jit(solution)/shard_map/ppermute | solution.py:940
  59.7 9.6 %collective-permute-start.9 = (bf16[2,8,392,128]{3,2,1,0:T(8,128)(2,1)S(1)}, bf16[2,8,392,128]{3,2,1,0:T(8,128)(2,1)S(1)}, u32[]{:S(2)}, u32[]{:S(2)}) collective-permute-start(bf16[2,8,392,128]{3,2,1,0:T(8,128)(2,1)S(1)} %get-tuple-element.233), channel_id=1, source_target_pairs={{0,1},{1,0},{2,3},{3,2},{4,5},{5,4},{6,7},{7,6},{8,9},{9,8},{10,11... | collective-permute-start | bytes 4816904 | tf_op jit(solution)/shard_map/ppermute | solution.py:940
  69.8 14.3 %collective-permute-start.10 = (bf16[2,392,128]{2,1,0:T(8,128)(2,1)S(1)}, bf16[2,392,128]{2,1,0:T(8,128)(2,1)S(1)}, u32[]{:S(2)}, u32[]{:S(2)}) collective-permute-start(bf16[2,392,128]{2,1,0:T(8,128)(2,1)S(1)} %get-tuple-element.245), channel_id=1, source_target_pairs={{0,4},{4,0},{8,12},{12,8},{16,20},{20,16},{24,28},{28,24},{1,5},{5... | collective-permute-start | bytes 602120 | tf_op jit(solution)/shard_map/ppermute | solution.py:940
  70.8 13.3 %collective-permute-start.11 = (bf16[2,392,128]{2,1,0:T(8,128)(2,1)S(1)}, bf16[2,392,128]{2,1,0:T(8,128)(2,1)S(1)}, u32[]{:S(2)}, u32[]{:S(2)}) collective-permute-start(bf16[2,392,128]{2,1,0:T(8,128)(2,1)S(1)} %get-tuple-element.246), channel_id=1, source_target_pairs={{0,2},{1,3},{2,0},{3,1},{4,6},{5,7},{6,4},{7,5},{8,10},{9,11},{10,... | collective-permute-start | bytes 602120 | tf_op jit(solution)/shard_map/ppermute | solution.py:940
  84.4 15.1 %collective-permute-start.14 = (bf16[160,640]{1,0:T(8,128)(2,1)S(1)}, bf16[160,640]{1,0:T(8,128)(2,1)S(1)}, u32[]{:S(2)}, u32[]{:S(2)}) collective-permute-start(bf16[160,640]{1,0:T(8,128)(2,1)S(1)} %get-tuple-element.266), channel_id=1, source_target_pairs={{0,16},{4,20},{8,24},{12,28},{16,0},{20,4},{24,8},{28,12},{1,17},{... | collective-permute-start | bytes 614408 | tf_op jit(solution)/shard_map/ppermute | solution.py:940
  86.8 12.6 %collective-permute-start.12 = (bf16[4,392,128]{2,1,0:T(8,128)(2,1)S(1)}, bf16[4,392,128]{2,1,0:T(8,128)(2,1)S(1)}, u32[]{:S(2)}, u32[]{:S(2)}) collective-permute-start(bf16[4,392,128]{2,1,0:T(8,128)(2,1)S(1)} %get-tuple-element.259), channel_id=1, source_target_pairs={{0,4},{4,0},{8,12},{12,8},{16,20},{20,16},{24,28},{28,24},{1,5},{5... | collective-permute-start | bytes 1204232 | tf_op jit(solution)/shard_map/ppermute | solution.py:940
  87.9 11.6 %collective-permute-start.13 = (bf16[4,392,128]{2,1,0:T(8,128)(2,1)S(1)}, bf16[4,392,128]{2,1,0:T(8,128)(2,1)S(1)}, u32[]{:S(2)}, u32[]{:S(2)}) collective-permute-start(bf16[4,392,128]{2,1,0:T(8,128)(2,1)S(1)} %get-tuple-element.260), channel_id=1, source_target_pairs={{0,2},{1,3},{2,0},{3,1},{4,6},{5,7},{6,4},{7,5},{8,10},{9,11},{10,... | collective-permute-start | bytes 1204232 | tf_op jit(solution)/shard_map/ppermute | solution.py:940
  99.7 3.9 %collective-permute-start.21 = (f32[40,256]{1,0:T(8,128)S(1)}, f32[40,256]{1,0:T(8,128)S(1)}, u32[]{:S(2)}, u32[]{:S(2)}) collective-permute-start(f32[40,256]{1,0:T(8,128)S(1)} %conv_one_grad.1), channel_id=1, source_target_pairs={{0,3},{1,2},{2,1},{3,0},{4,7},{5,6},{6,5},{7,4},{8,11},{9,10},{10,... | collective-permute-start | bytes 122888 | tf_op jit(solution)/shard_map/ppermute | solution.py:940
  99.8 6.2 %collective-permute-start.20 = (f32[40,256]{1,0:T(8,128)S(1)}, f32[40,256]{1,0:T(8,128)S(1)}, u32[]{:S(2)}, u32[]{:S(2)}) collective-permute-start(f32[40,256]{1,0:T(8,128)S(1)} %conv_one_grad.1), channel_id=1, source_target_pairs={{0,2},{1,3},{2,0},{3,1},{4,6},{5,7},{6,4},{7,5},{8,10},{9,11},{10,... | collective-permute-start | bytes 122888 | tf_op jit(solution)/shard_map/ppermute | solution.py:940
  101.4 11.0 %collective-permute-start.19 = (f32[40,256]{1,0:T(8,128)S(1)}, f32[40,256]{1,0:T(8,128)S(1)}, u32[]{:S(2)}, u32[]{:S(2)}) collective-permute-start(f32[40,256]{1,0:T(8,128)S(1)} %conv_one_grad.1), channel_id=1, source_target_pairs={{0,1},{1,0},{2,3},{3,2},{4,5},{5,4},{6,7},{7,6},{8,9},{9,8},{10,11... | collective-permute-start | bytes 122888 | tf_op jit(solution)/shard_map/ppermute | solution.py:940
  101.6 10.7 %collective-permute-start.15 = (bf16[392,128]{1,0:T(8,128)(2,1)S(1)}, bf16[392,128]{1,0:T(8,128)(2,1)S(1)}, u32[]{:S(2)}, u32[]{:S(2)}) collective-permute-start(bf16[392,128]{1,0:T(8,128)(2,1)S(1)} %get-tuple-element.273), channel_id=1, source_target_pairs={{0,8},{4,12},{8,0},{12,4},{16,24},{20,28},{24,16},{28,20},{1,9},{5... | collective-permute-start | bytes 301064 | tf_op jit(solution)/shard_map/ppermute | solution.py:940
  103.4 9.8 %collective-permute-start.16 = (bf16[392,128]{1,0:T(8,128)(2,1)S(1)}, bf16[392,128]{1,0:T(8,128)(2,1)S(1)}, u32[]{:S(2)}, u32[]{:S(2)}) collective-permute-start(bf16[392,128]{1,0:T(8,128)(2,1)S(1)} %get-tuple-element.274), channel_id=1, source_target_pairs={{0,16},{4,20},{8,24},{12,28},{16,0},{20,4},{24,8},{28,12},{1,17},{... | collective-permute-start | bytes 301064 | tf_op jit(solution)/shard_map/ppermute | solution.py:940
  103.7 9.5 %collective-permute-start.17 = (bf16[392,128]{1,0:T(8,128)(2,1)S(1)}, bf16[392,128]{1,0:T(8,128)(2,1)S(1)}, u32[]{:S(2)}, u32[]{:S(2)}) collective-permute-start(bf16[392,128]{1,0:T(8,128)(2,1)S(1)} %get-tuple-element.275), channel_id=1, source_target_pairs={{0,24},{4,28},{8,16},{12,20},{16,8},{20,12},{24,0},{28,4},{1,25},{... | collective-permute-start | bytes 301064 | tf_op jit(solution)/shard_map/ppermute | solution.py:940
  106.0 7.1 %collective-permute-start.18 = (bf16[160,640]{1,0:T(8,128)(2,1)S(1)}, bf16[160,640]{1,0:T(8,128)(2,1)S(1)}, u32[]{:S(2)}, u32[]{:S(2)}) collective-permute-start(bf16[160,640]{1,0:T(8,128)(2,1)S(1)} %add_convert_fusion.5), channel_id=1, source_target_pairs={{0,2},{1,3},{2,0},{3,1},{4,6},{5,7},{6,4},{7,5},{8,10},{9,11},{10,... | collective-permute-start | bytes 614408 | tf_op jit(solution)/shard_map/ppermute | solution.py:940
  113.3 11.2 %collective-permute-start.25 = (f32[40,256]{1,0:T(8,128)S(1)}, f32[40,256]{1,0:T(8,128)S(1)}, u32[]{:S(2)}, u32[]{:S(2)}) collective-permute-start(f32[40,256]{1,0:T(8,128)S(1)} %add_add_fusion.1), channel_id=1, source_target_pairs={{0,24},{4,28},{8,16},{12,20},{16,8},{20,12},{24,0},{28,4},{1,25},{... | collective-permute-start | bytes 122888 | tf_op jit(solution)/shard_map/ppermute | solution.py:940
  114.7 9.7 %collective-permute-start.24 = (f32[40,256]{1,0:T(8,128)S(1)}, f32[40,256]{1,0:T(8,128)S(1)}, u32[]{:S(2)}, u32[]{:S(2)}) collective-permute-start(f32[40,256]{1,0:T(8,128)S(1)} %add_add_fusion.1), channel_id=1, source_target_pairs={{0,16},{4,20},{8,24},{12,28},{16,0},{20,4},{24,8},{28,12},{1,17},{... | collective-permute-start | bytes 122888 | tf_op jit(solution)/shard_map/ppermute | solution.py:940
  117.4 7.1 %collective-permute-start.23 = (f32[40,256]{1,0:T(8,128)S(1)}, f32[40,256]{1,0:T(8,128)S(1)}, u32[]{:S(2)}, u32[]{:S(2)}) collective-permute-start(f32[40,256]{1,0:T(8,128)S(1)} %add_add_fusion.1), channel_id=1, source_target_pairs={{0,8},{4,12},{8,0},{12,4},{16,24},{20,28},{24,16},{28,20},{1,9},{5... | collective-permute-start | bytes 122888 | tf_op jit(solution)/shard_map/ppermute | solution.py:940
  117.7 7.6 %collective-permute-start.22 = (bf16[160,640]{1,0:T(8,128)(2,1)S(1)}, bf16[160,640]{1,0:T(8,128)(2,1)S(1)}, u32[]{:S(2)}, u32[]{:S(2)}) collective-permute-start(bf16[160,640]{1,0:T(8,128)(2,1)S(1)} %add_convert_fusion.4), channel_id=1, source_target_pairs={{0,8},{4,12},{8,0},{12,4},{16,24},{20,28},{24,16},{28,20},{1,9},{5... | collective-permute-start | bytes 614408 | tf_op jit(solution)/shard_map/ppermute | solution.py:940
  125.4 6.1 %collective-permute-start.27 = (f32[40,256]{1,0:T(8,128)S(1)}, f32[40,256]{1,0:T(8,128)S(1)}, u32[]{:S(2)}, u32[]{:S(2)}) collective-permute-start(f32[40,256]{1,0:T(8,128)S(1)} %add_add_fusion), channel_id=1, source_target_pairs={{0,4},{4,0},{8,12},{12,8},{16,20},{20,16},{24,28},{28,24},{1,5},{5... | collective-permute-start | bytes 122888 | tf_op jit(solution)/shard_map/ppermute | solution.py:940
  126.5 6.0 %collective-permute-start.26 = (bf16[160,640]{1,0:T(8,128)(2,1)S(1)}, bf16[160,640]{1,0:T(8,128)(2,1)S(1)}, u32[]{:S(2)}, u32[]{:S(2)}) collective-permute-start(bf16[160,640]{1,0:T(8,128)(2,1)S(1)} %add_convert_fusion.3), channel_id=1, source_target_pairs={{0,4},{4,0},{8,12},{12,8},{16,20},{20,16},{24,28},{28,24},{1,5},{5... | collective-permute-start | bytes 614408 | tf_op jit(solution)/shard_map/ppermute | solution.py:940
  132.6 4.0 %collective-permute-start.28 = (bf16[160,640]{1,0:T(8,128)(2,1)S(1)}, bf16[160,640]{1,0:T(8,128)(2,1)S(1)}, u32[]{:S(2)}, u32[]{:S(2)}) collective-permute-start(bf16[160,640]{1,0:T(8,128)(2,1)S(1)} %add_convert_fusion.2), channel_id=1, source_target_pairs={{0,1},{1,0},{2,3},{3,2},{4,5},{5,4},{6,7},{7,6},{8,9},{9,8},{10,11... | collective-permute-start | bytes 614408 | tf_op jit(solution)/shard_map/ppermute | solution.py:940
  (33 other events, 134.1 us)

commit v4 on v3

--- a/solution.py
+++ b/solution.py
@@ -34,7 +34,7 @@
     return lax.dot_general(a, b, dims, precision=precision, preferred_element_type=F32)
 
 
-def params(limit=16, **more):
+def params(limit=32, **more):
     return pltpu.CompilerParams(vmem_limit_bytes=limit * MIB, **more)
 
 
@@ -66,22 +66,34 @@
     return pl.BlockSpec(memory_space=pl.ANY)
 
 
+def row_copy(source, target, sems, r):
+    return pltpu.make_async_copy(source.at[r], target.at[r], sems.at[r])
+
+
 def start_rows(source, target, sems):
     for r in range(source.shape[0]):
-        pltpu.make_async_copy(source.at[r], target.at[r], sems.at[r]).start()
-
-
-def start_row(source, target, sems, r):
-    pltpu.make_async_copy(source.at[r], target.at[r], sems.at[r]).start()
-
-
-def wait_row(source, target, sems, r):
-    pltpu.make_async_copy(source.at[r], target.at[r], sems.at[r]).wait()
+        row_copy(source, target, sems, r).start()
 
 
 def wait_rows(source, target, sems):
     for r in range(source.shape[0]):
-        wait_row(source, target, sems, r)
+        row_copy(source, target, sems, r).wait()
+
+
+def call(body, ins, outs, in_specs=None, out_specs=None, scratch=(), grid=None, us=5, name=None, aliases=None, limit=24):
+    more = {} if grid is None else {"grid": (grid,)}
+    return pl.pallas_call(
+        body,
+        out_shape=tuple(outs),
+        in_specs=list(in_specs or [vmem()] * len(ins)),
+        out_specs=tuple(out_specs or [vmem()] * len(outs)),
+        scratch_shapes=list(scratch),
+        input_output_aliases=aliases or {},
+        compiler_params=params(limit),
+        cost_estimate=cost(us),
+        name=name,
+        **more,
+    )(*ins)
 
 
 def dma(count):
@@ -90,11 +102,10 @@
 
 def gelu_both(x):
     x2 = x * x
-    t = jnp.tanh(x * (ROOT + (ROOT * CUBE) * x2))
+    up = 1.0 + jnp.tanh(x * (ROOT + (ROOT * CUBE) * x2))
     h = 0.5 * x
-    act = h + h * t
-    slope = (0.5 + 0.5 * t) + h * (1.0 - t * t) * (ROOT + (3.0 * ROOT * CUBE) * x2)
-    return act, slope
+    bend = h * (ROOT + (3.0 * ROOT * CUBE) * x2)
+    return h * up, up * (0.5 + bend * (2.0 - up))
 
 
 def wide(line, rows, n):
@@ -162,8 +173,18 @@
 
 
 def first_kernel(
-    lengths_ref, dones_ref, rewards_ref, values_ref, weight_ref, adv_ref, piece_ref
+    lengths_ref, dones_far_ref, rewards_far_ref, values_far_ref, weight_far_ref, frames_ref,
+    adv_ref, piece_ref, cells_ref, dones_ref, rewards_ref, values_ref, weight_ref, sems, small_sems,
 ):
+    near_refs = (dones_ref, rewards_ref, values_ref, weight_ref)
+    far_refs = (dones_far_ref, rewards_far_ref, values_far_ref, weight_far_ref)
+    small = [pltpu.make_async_copy(a, b, small_sems.at[k]) for k, (a, b) in enumerate(zip(far_refs, near_refs))]
+    for copy in small:
+        copy.start()
+    for r in range(5):
+        ring_copy(frames_ref, cells_ref, sems, r).start()
+    for copy in small:
+        copy.wait()
     n = rewards_ref.shape[1]
     length = lengths_ref[0]
     position = lax.broadcasted_iota(jnp.int32, (8, n), 1)
@@ -201,80 +222,95 @@
     piece_ref[...] = jnp.zeros_like(piece_ref)
     piece_ref[0:rows, :] = weight_ref[...].astype(BF)
     piece_ref[tail:, :] = jnp.concatenate([terms, jnp.zeros((8, 128), F32)], axis=0).astype(BF)
-
-
-def first(lengths, dones, rewards, old_values, weight):
+    for r in range(5):
+        ring_copy(frames_ref, cells_ref, sems, r).wait()
+
+
+def first(lengths, dones, rewards, old_values, weight, frames):
     n = rewards.shape[1]
     rows = -(-weight.shape[0] // 16) * 16 + 16
+    small = [dones, rewards, old_values, weight]
     return pl.pallas_call(
         first_kernel,
         out_shape=(
             jax.ShapeDtypeStruct((1, n), F32),
             jax.ShapeDtypeStruct((rows, 128), BF),
+            near((RING,) + frames.shape[1:], BF),
         ),
-        in_specs=[smem()] + [vmem()] * 4,
-        out_specs=(vmem(),) * 2,
+        in_specs=[smem()] + [anywhere()] * 5,
+        out_specs=(vmem(),) * 3,
+        scratch_shapes=[pltpu.VMEM(a.shape, a.dtype) for a in small] + [dma(5), dma(4)],
+        compiler_params=params(16),
         cost_estimate=cost(3),
         name="first",
-    )(lengths, dones, rewards, old_values, weight)
+    )(lengths, *[far(a) for a in small], far(frames))
+
+
+RING = 8
+
+
+def ring_copy(frames_ref, cells_ref, sems, r):
+    slot = r % RING if isinstance(r, int) else lax.rem(r, RING)
+    return pltpu.make_async_copy(frames_ref.at[r], cells_ref.at[slot], sems.at[slot])
+
+
+def fetch_rows(frames_ref, cells_ref, sems, step, last):
+    @pl.when(step < last - 1)
+    def _():
+        ring_copy(frames_ref, cells_ref, sems, 2 * step + 5).start()
+        ring_copy(frames_ref, cells_ref, sems, 2 * step + 6).start()
+
+    @pl.when(step >= 2)
+    def _():
+        ring_copy(frames_ref, cells_ref, sems, 2 * step + 1).wait()
+        ring_copy(frames_ref, cells_ref, sems, 2 * step + 2).wait()
+
+    return [lax.rem(2 * step + a, RING) for a in range(3)]
 
 
 def conv_one_kernel(
-    frames_ref, weight_ref, bias_ref, act_ref, slope_far_ref,
-    band_ref, wide_ref, cells_ref, slope_ref, in_sems, slope_sems,
+    frames_ref, weight_ref, bias_ref, cells_in_ref, act_ref, slope_ref, cells_ref, band_ref, wide_ref, sems
 ):
     n = act_ref.shape[-1]
     half = act_ref.shape[0]
     step = pl.program_id(0)
 
+    slots = fetch_rows(frames_ref, cells_ref, sems, step, half - 1)
+
     @pl.when(step == 0)
     def _():
-        start_rows(frames_ref, cells_ref, in_sems)
         band_ref[...] = band_square(weight_ref[...], 64)
         wide_ref[...] = wide(bias_ref[:, 0:32], 128, n)
-        wait_row(frames_ref, cells_ref, in_sems, 0)
-
-    wait_row(frames_ref, cells_ref, in_sems, 2 * step + 1)
-    wait_row(frames_ref, cells_ref, in_sems, 2 * step + 2)
+
     for col in range(half):
         span = slice(col * 128, col * 128 + 192)
-        patch = jnp.concatenate([cells_ref[2 * step + a, span, :] for a in range(3)], axis=0)
+        patch = jnp.concatenate([cells_ref[slot, span, :] for slot in slots], axis=0)
         act, slope = gelu_both(dot(band_ref[...], patch) + wide_ref[...])
         act_ref[step, col] = act.astype(BF)
         slope_ref[step, col] = slope.astype(BF)
-    start_row(slope_ref, slope_far_ref, slope_sems, step)
-
-    @pl.when(step == half - 1)
-    def _():
-        wait_rows(slope_ref, slope_far_ref, slope_sems)
-
-
-def conv_one(frames, weight, bias):
+
+
+def conv_one(frames, weight, bias, cells):
     grid, _, n = frames.shape
     half = grid // 2
     shape = (half, half, 128, n)
-    return pl.pallas_call(
+    return call(
         conv_one_kernel,
-        out_shape=(near(shape, BF), pltpu.HBM(shape, BF)),
-        grid=(half,),
-        in_specs=[anywhere(), vmem(), vmem()],
-        out_specs=(vmem(), anywhere()),
-        scratch_shapes=[
-            pltpu.VMEM((128, 576), BF),
-            pltpu.VMEM((128, n), F32),
-            pltpu.VMEM(frames.shape, BF),
-            pltpu.VMEM(shape, BF),
-            dma(grid),
-            dma(half),
-        ],
-        compiler_params=params(30),
-        cost_estimate=cost(12),
+        [far(frames), weight, bias, held(cells)],
+        [near(shape, BF), near(shape, BF), near(cells.shape, BF)],
+        in_specs=[anywhere()] + [vmem()] * 3,
+        scratch=[pltpu.VMEM((128, 576), BF), pltpu.VMEM((128, n), F32), dma(RING)],
+        grid=half,
+        us=12,
         name="conv_one",
-    )(far(frames), weight, bias)
+        aliases={3: 2},
+        limit=16,
+    )
 
 
 def conv_two_kernel(
-    one_ref, weight_ref, bias_ref, act_ref, slope_ref, one_far_ref, band_ref, wide_ref, sems
+    one_ref, slope_one_ref, weight_ref, bias_ref, act_ref, slope_ref, one_far_ref, slope_one_far_ref,
+    band_ref, wide_ref, sems, slope_sems,
 ):
     n = act_ref.shape[-1]
     step = pl.program_id(0)
@@ -282,6 +318,7 @@
     @pl.when(step == 0)
     def _():
         start_rows(one_ref, one_far_ref, sems)
+        start_rows(slope_one_ref, slope_one_far_ref, slope_sems)
         band_ref[...] = band_forward(weight_ref[...], 2, 128, 3)
         wide_ref[...] = wide(bias_ref[:, 32:96], 192, n)
 
@@ -298,22 +335,23 @@
     @pl.when(step == 8)
     def _():
         wait_rows(one_ref, one_far_ref, sems)
-
-
-def conv_two(act_one, weight, bias):
+        wait_rows(slope_one_ref, slope_one_far_ref, slope_sems)
+
+
+def conv_two(act_one, slope_one, weight, bias):
     n = act_one.shape[-1]
     shape = (9, 576, n)
-    return pl.pallas_call(
+    return call(
         conv_two_kernel,
-        out_shape=(near(shape, BF), near(shape, BF), pltpu.HBM(act_one.shape, BF)),
-        grid=(9,),
-        in_specs=[vmem()] * 3,
-        out_specs=(vmem(), vmem(), anywhere()),
-        scratch_shapes=[pltpu.VMEM((192, 1024), BF), pltpu.VMEM((192, n), F32), dma(10)],
-        compiler_params=params(),
-        cost_estimate=cost(7),
+        [held(act_one), held(slope_one), weight, bias],
+        [near(shape, BF)] * 2 + [pltpu.HBM(act_one.shape, BF)] * 2,
+        out_specs=[vmem(), vmem(), anywhere(), anywhere()],
+        scratch=[pltpu.VMEM((192, 1024), BF), pltpu.VMEM((192, n), F32), dma(10), dma(10)],
+        grid=9,
+        us=7,
         name="conv_two",
-    )(held(act_one), weight, bias)
+        limit=16,
+    )
 
 
 def conv_three_kernel(
@@ -340,8 +378,8 @@
         rows = slice((start + drop) * 64, (start + 4) * 64)
         flat_ref[step, rows, :] = act.astype(BF)
         slope_ref[step, rows, :] = slope.astype(BF)
-    start_row(flat_ref, flat_far_ref, flat_sems, step)
-    start_row(slope_ref, slope_far_ref, slope_sems, step)
+    row_copy(flat_ref, flat_far_ref, flat_sems, step).start()
+    row_copy(slope_ref, slope_far_ref, slope_sems, step).start()
 
     @pl.when(step == 6)
     def _():
@@ -354,15 +392,13 @@
 def conv_three(act_two, slope_two, weight, bias):
     n = act_two.shape[-1]
     shape = (7, 448, n)
-    out = pltpu.HBM(shape, BF)
-    two = pltpu.HBM(act_two.shape, BF)
-    return pl.pallas_call(
+    out, two = pltpu.HBM(shape, BF), pltpu.HBM(act_two.shape, BF)
+    return call(
         conv_three_kernel,
-        out_shape=(out, out, two, two),
-        grid=(7,),
-        in_specs=[vmem()] * 4,
-        out_specs=(anywhere(),) * 4,
-        scratch_shapes=[
+        [held(act_two), held(slope_two), weight, bias],
+        [out, out, two, two],
+        out_specs=[anywhere()] * 4,
+        scratch=[
             pltpu.VMEM((256, 1152), BF),
             pltpu.VMEM((256, n), F32),
             pltpu.VMEM(shape, BF),
@@ -372,10 +408,11 @@
             dma(7),
             dma(7),
         ],
-        compiler_params=params(),
-        cost_estimate=cost(5),
+        grid=7,
+        us=6,
         name="conv_three",
-    )(held(act_two), held(slope_two), weight, bias)
+        limit=16,
+    )
 
 
 def head_gradient(heads, actions, adv, values, old_logp, mask, count, centre, var):
@@ -410,15 +447,16 @@
 
 
 def dense_kernel(*refs, places, n_dp, n_own, rows):
-    place_ref, lengths_ref, flat_far_ref, slope_far_ref, two_far_ref, slope_two_far_ref = refs[:6]
-    heads_ref, bias_ref, actions_ref, adv_ref, values_ref, logp_ref = refs[6:12]
-    piece_refs = refs[12 : 12 + len(places)]
+    place_ref, lengths_ref = refs[:2]
+    small_far_refs, (flat_far_ref, slope_far_ref, two_far_ref) = refs[2:8], refs[8:11]
+    piece_refs = refs[11 : 11 + len(places)]
     (
-        d_three_ref, two_ref, slope_two_ref, keep_ref, send_ref, grad_heads_ref, sums_ref, sum_heads_ref,
-        blocks_ref, weight_ref, d_dense_ref, flat_rows_ref, slope_ref,
-        sems, two_sems, slope_two_sems, flat_sems, slope_sems,
-    ) = refs[12 + len(places) :]
-    n = flat_rows_ref.shape[-1]
+        d_three_far_ref, two_ref, keep_ref, send_ref, grad_heads_ref, sums_ref, sum_heads_ref,
+        blocks_ref, weight_ref, d_dense_ref, flat_ref, slope_ref, *small_refs,
+        sems, two_sems, flat_sems, slope_sems, small_sems,
+    ) = refs[11 + len(places) :]
+    heads_ref, bias_ref, actions_ref, adv_ref, values_ref, logp_ref = small_refs
+    n = flat_ref.shape[-1]
     cols = 128
     dp, own = place_ref[0], place_ref[1]
     stats = []
@@ -428,14 +466,15 @@
             copies.append(
                 pltpu.make_async_copy(ref.at[k], blocks_ref.at[i ^ dp, j ^ own], sems.at[len(copies)])
             )
+    for k in range(6):
+        copies.append(pltpu.make_async_copy(small_far_refs[k], small_refs[k], small_sems.at[k]))
     for copy in copies:
         copy.start()
-    start_rows(flat_far_ref, flat_rows_ref, flat_sems)
+    start_rows(flat_far_ref, flat_ref, flat_sems)
+    for copy in copies:
+        copy.wait()
     start_rows(slope_far_ref, slope_ref, slope_sems)
     start_rows(two_far_ref, two_ref, two_sems)
-    start_rows(slope_two_far_ref, slope_two_ref, slope_two_sems)
-    for copy in copies:
-        copy.wait()
     for i in range(n_dp):
         for j in range(n_own):
             tail = blocks_ref[i, j, blocks_ref.shape[2] - 16 :].astype(F32)
@@ -452,8 +491,8 @@
     hid = n_own * cols
     bias_dense = wide(bias_ref[:, 160 : 160 + hid], hid, n)
     bias_heads = wide(bias_ref[:, 160 + hid : 160 + hid + 19], 19, n)
-    wait_rows(flat_far_ref, flat_rows_ref, flat_sems)
-    flat = flat_rows_ref[...].reshape(n_dp * rows, n)
+    wait_rows(flat_far_ref, flat_ref, flat_sems)
+    flat = flat_ref[...].reshape(n_dp * rows, n)
     pre = dot(weight_ref[...], flat, TN) + bias_dense
     hidden, slope = gelu_both(pre)
     hidden = hidden.astype(BF)
@@ -485,81 +524,90 @@
     for part in range(7):
         span = slice(part * 448, part * 448 + 448)
         d_three = (dot(weight_ref[span, :], d_dense) * slope_ref[part].astype(F32)).astype(BF)
-        d_three_ref[part] = d_three
+        slope_ref[part] = d_three
+        row_copy(slope_ref, d_three_far_ref, slope_sems, part).start()
         back = d_three.astype(F32)
         for c in range(7):
             total = total + back[c * 64 : c * 64 + 64]
     sums_ref[0:1, 0:64] = dot(jnp.ones((8, n), F32), total, NT, HIGH)[0:1]
     sums_ref[0:1, 64:128] = jnp.zeros((1, 64), F32)
     wait_rows(two_far_ref, two_ref, two_sems)
-    wait_rows(slope_two_far_ref, slope_two_ref, slope_two_sems)
+    wait_rows(slope_ref, d_three_far_ref, slope_sems)
 
 
 def dense(
-    place, lengths, flat, slope_three, act_two, slope_two, heads, bias, actions, adv, values, logp,
+    place, lengths, heads, bias, actions, adv, values, logp, flat, slope_three, act_two,
     pieces, n_dp, n_own, rows,
 ):
     n = flat.shape[-1]
     hid = n_own * 128
-    part = jax.ShapeDtypeStruct((n_own // 2, n_dp, rows, 128), BF)
-    arrays = [p[0] for p in pieces]
+    part = pltpu.HBM((n_own // 2, n_dp, rows, 128), BF)
+    arrays = [far(p[0]) for p in pieces]
+    small = [heads, bias, actions, adv, values, logp]
     body = functools.partial(
         dense_kernel, places=[p[1] for p in pieces], n_dp=n_dp, n_own=n_own, rows=rows
     )
-    return pl.pallas_call(
+    return call(
         body,
-        out_shape=(
-            near(flat.shape, BF),
-            near(act_two.shape, BF),
+        [place, lengths] + [far(a) for a in small + [flat, slope_three, act_two]] + arrays,
+        [
+            pltpu.HBM(flat.shape, BF),
             near(act_two.shape, BF),
             part,
             part,
             jax.ShapeDtypeStruct(heads.shape, F32),
             jax.ShapeDtypeStruct((1, 128 + hid), F32),
             jax.ShapeDtypeStruct((1, heads.shape[0]), F32),
-        ),
-        in_specs=[smem(), smem()] + [anywhere()] * 4 + [vmem()] * 6 + [anywhere()] * len(arrays),
-        out_specs=(vmem(),) * 8,
-        scratch_shapes=[
+        ],
+        in_specs=[smem(), smem()] + [anywhere()] * (9 + len(arrays)),
+        out_specs=[anywhere()] + [vmem()] * 6,
+        scratch=[
             pltpu.VMEM((n_dp, n_own) + arrays[0].shape[1:], BF),
             pltpu.VMEM((n_dp * rows, hid), BF),
             pltpu.VMEM((n_own, 128, n), BF),
             pltpu.VMEM(flat.shape, BF),
             pltpu.VMEM(flat.shape, BF),
-            dma(n_dp * n_own),
-            dma(9),
-            dma(9),
-            dma(7),
-            dma(7),
-        ],
-        compiler_params=params(32),
-        cost_estimate=cost(8),
+        ]
+        + [pltpu.VMEM(a.shape, a.dtype) for a in small]
+        + [dma(n_dp * n_own), dma(9), dma(7), dma(7), dma(6)],
+        us=10,
         name="dense",
-    )(
-        place, lengths, far(flat), far(slope_three), far(act_two), far(slope_two), heads, bias,
-        actions, adv, values, logp, *[far(a) for a in arrays],
+        limit=32,
     )
 
 
 def conv_three_back_kernel(
-    d_three_ref, act_ref, slope_ref, one_far_ref, slope_one_far_ref, weight_ref, heads_ref,
+    act_ref, d_three_ref, slope_far_ref, one_far_ref, slope_one_far_ref, weight_ref, heads_ref,
     d_two_ref, one_ref, slope_one_ref, pack_ref, sum_ref,
-    band_ref, pad_ref, acc_ref, tot_ref, one_sems, slope_one_sems,
+    band_ref, pad_ref, acc_ref, tot_ref, slope_ref, one_sems, slope_one_sems, slope_sems, d_sems,
 ):
-    n = d_three_ref.shape[-1]
+    n = act_ref.shape[-1]
     step = pl.program_id(0)
 
+    def three_row(r):
+        inner = pad_ref.at[r + 2, pl.ds(128, 448), :]
+        return pltpu.make_async_copy(d_three_ref.at[r], inner, d_sems.at[r])
+
     @pl.when(step == 0)
     def _():
-        start_rows(one_far_ref, one_ref, one_sems)
-        start_rows(slope_one_far_ref, slope_one_ref, slope_one_sems)
+        for r in range(7):
+            three_row(r).start()
+        for r in range(11):
+            if 2 <= r < 9:
+                pad_ref[r, 0:128, :] = jnp.zeros((128, n), BF)
+                pad_ref[r, 576:704, :] = jnp.zeros((128, n), BF)
+            else:
+                pad_ref[r] = jnp.zeros((704, n), BF)
+        start_rows(slope_far_ref, slope_ref, slope_sems)
         band_ref[...] = band_back(weight_ref[...], 3, 64, 3)
-        pad_ref[...] = jnp.zeros_like(pad_ref)
         acc_ref[...] = jnp.zeros_like(acc_ref)
         tot_ref[...] = jnp.zeros_like(tot_ref)
         for r in range(7):
-            pad_ref[r + 2, 128 : 128 + 448, :] = d_three_ref[r]
-
+            three_row(r).wait()
+        start_rows(one_far_ref, one_ref, one_sems)
+        start_rows(slope_one_far_ref, slope_one_ref, slope_one_sems)
+
+    row_copy(slope_far_ref, slope_ref, slope_sems, step).wait()
     total = tot_ref[...]
     for part in range(3):
         patch = jnp.concatenate(
@@ -602,35 +650,38 @@
 
 def conv_three_back(d_three, act_two, slope_two, act_one, slope_one, weight, heads):
     n = act_two.shape[-1]
-    return pl.pallas_call(
+    return call(
         conv_three_back_kernel,
-        out_shape=(
+        [held(act_two)] + [far(a) for a in (d_three, slope_two, act_one, slope_one)] + [weight, heads],
+        [
             near(act_two.shape, BF),
             near(act_one.shape, BF),
             near(act_one.shape, BF),
             jax.ShapeDtypeStruct((96, 640), BF),
             jax.ShapeDtypeStruct((1, 64), F32),
-        ),
-        grid=(9,),
-        in_specs=[vmem()] * 3 + [anywhere()] * 2 + [vmem()] * 2,
-        out_specs=(vmem(),) * 5,
-        scratch_shapes=[
+        ],
+        in_specs=[vmem()] + [anywhere()] * 4 + [vmem()] * 2,
+        scratch=[
             pltpu.VMEM((192, 960), BF),
             pltpu.VMEM((11, 704, n), BF),
             pltpu.VMEM((256, 1152), F32),
             pltpu.VMEM((64, n), F32),
+            pltpu.VMEM(act_two.shape, BF),
             dma(10),
             dma(10),
+            dma(9),
+            dma(7),
         ],
-        compiler_params=params(),
-        cost_estimate=cost(9),
+        grid=9,
+        us=9,
         name="conv_three_back",
-    )(held(d_three), held(act_two), held(slope_two), far(act_one), far(slope_one), weight, heads)
+        limit=16,
+    )
 
 
 def conv_two_back_kernel(
-    d_two_ref, act_ref, slope_ref, weight_ref, pack_ref, d_one_ref, d_far_ref, grad_ref, sum_ref,
-    band_ref, pad_ref, acc_ref, tot_ref, out_sems,
+    d_two_ref, act_ref, slope_ref, weight_ref, pack_ref, d_one_ref, grad_ref, sum_ref,
+    band_ref, pad_ref, acc_ref, tot_ref,
 ):
     n = d_one_ref.shape[-1]
     step = pl.program_id(0)
@@ -653,7 +704,6 @@
         d_one_ref[step, col] = d_one
         total = total + d_one.astype(F32)
     tot_ref[...] = total
-    start_row(d_one_ref, d_far_ref, out_sems, step)
 
     @pl.when(step < 9)
     def _():
@@ -667,7 +717,6 @@
 
     @pl.when(step == 9)
     def _():
-        wait_rows(d_one_ref, d_far_ref, out_sems)
         for a in range(2):
             out = None
             for c in range(3):
@@ -682,52 +731,48 @@
 
 def conv_two_back(d_two, act_one, slope_one, weight, pack):
     n = act_one.shape[-1]
-    shape = act_one.shape
-    return pl.pallas_call(
+    return call(
         conv_two_back_kernel,
-        out_shape=(
-            near(shape, BF),
-            pltpu.HBM(shape, BF),
+        [held(d_two), held(act_one), held(slope_one), weight, pack],
+        [
+            near(act_one.shape, BF),
             jax.ShapeDtypeStruct((160, 640), BF),
             jax.ShapeDtypeStruct((1, 32), F32),
-        ),
-        grid=(10,),
-        in_specs=[vmem()] * 5,
-        out_specs=(vmem(), anywhere(), vmem(), vmem()),
-        scratch_shapes=[
+        ],
+        scratch=[
             pltpu.VMEM((128, 256), BF),
             pltpu.VMEM((11, 704, n), BF),
             pltpu.VMEM((192, 1024), F32),
             pltpu.VMEM((128, n), F32),
-            dma(10),
         ],
-        compiler_params=params(),
-        cost_estimate=cost(11),
+        grid=10,
+        us=11,
         name="conv_two_back",
-    )(held(d_two), held(act_one), held(slope_one), weight, pack)
+        limit=16,
+    )
 
 
 def conv_one_grad_kernel(
-    frames_ref, d_one_ref, dense_ref, heads_ref, one_ref, two_ref, grad_ref, acc_ref, cells_ref, sems
+    frames_ref, d_one_ref, cells_in_ref, dense_ref, heads_ref, one_ref, two_ref,
+    grad_ref, d_out_ref, cells_ref, acc_ref, sems,
 ):
     n = d_one_ref.shape[-1]
     step = pl.program_id(0)
+    half = pl.num_programs(0)
+
+    slots = fetch_rows(frames_ref, cells_ref, sems, step, half - 1)
 
     @pl.when(step == 0)
     def _():
-        start_rows(frames_ref, cells_ref, sems)
         acc_ref[...] = jnp.zeros_like(acc_ref)
-        wait_row(frames_ref, cells_ref, sems, 0)
-
-    wait_row(frames_ref, cells_ref, sems, 2 * step + 1)
-    wait_row(frames_ref, cells_ref, sems, 2 * step + 2)
+
     for pair in range(d_one_ref.shape[1] // 2):
         span = slice(pair * 256, pair * 256 + 320)
-        cells = jnp.concatenate([cells_ref[2 * step + a, span, :] for a in range(3)], axis=0)
+        cells = jnp.concatenate([cells_ref[slot, span, :] for slot in slots], axis=0)
         rows = d_one_ref[step, 2 * pair : 2 * pair + 2].reshape(256, n)
         acc_ref[...] += dot(rows, cells, NT)
 
-    @pl.when(step == pl.num_programs(0) - 1)
+    @pl.when(step == half - 1)
     def _():
         for a in range(2):
             out = None
@@ -738,118 +783,123 @@
                         lane = (dy + a) * 320 + (2 * k + dx) * 64
                         piece = acc_ref[row : row + 32, lane : lane + 128]
                         out = piece if out is None else out + piece
-            grad_ref[0:32, a * 128 : a * 128 + 128] = out
-        grad_ref[32:40, :] = jnp.zeros((8, 256), F32)
-        grad_ref[32:33, :] = dense_ref[0:1, 128:384]
-        grad_ref[33:34, :] = dense_ref[0:1, 384:640]
-        grad_ref[34:35, 0:64] = dense_ref[0:1, 0:64]
-        grad_ref[35:36, 0:64] = two_ref[...]
-        grad_ref[36:37, 0:32] = one_ref[...]
-        grad_ref[37:38, 0:19] = heads_ref[...]
-
-
-def conv_one_grad(frames, d_one, sums, sum_heads, sum_one, sum_two):
+            grad_ref[:, a * 128 : a * 128 + 128] = out[0:16]
+            grad_ref[:, 256 + a * 128 : 384 + a * 128] = out[16:32]
+        grad_ref[:, 512:640] = jnp.zeros((16, 128), F32)
+        for k in range(4):
+            grad_ref[k : k + 1, 512:640] = dense_ref[0:1, 128 + k * 128 : 256 + k * 128]
+        grad_ref[4:5, 512:576] = dense_ref[0:1, 0:64]
+        grad_ref[5:6, 512:576] = two_ref[...]
+        grad_ref[6:7, 512:544] = one_ref[...]
+        grad_ref[7:8, 512:531] = heads_ref[...]
+
+
+def conv_one_grad(frames, d_one, cells, sums, sum_heads, sum_one, sum_two):
     return pl.pallas_call(
         conv_one_grad_kernel,
-        out_shape=jax.ShapeDtypeStruct((40, 256), F32),
+        out_shape=(
+            jax.ShapeDtypeStruct((16, 640), F32),
+            near(d_one.shape, BF),
+            near(cells.shape, BF),
+        ),
         grid=(d_one.shape[0],),
-        in_specs=[anywhere()] + [vmem()] * 5,
-        out_specs=vmem(),
-        scratch_shapes=[
-            pltpu.VMEM((256, 960), F32),
-            pltpu.VMEM(frames.shape, BF),
-            dma(frames.shape[0]),
-        ],
-        compiler_params=params(24),
+        in_specs=[anywhere()] + [vmem()] * 6,
+        out_specs=(vmem(),) * 3,
+        scratch_shapes=[pltpu.VMEM((256, 960), F32), dma(RING)],
+        input_output_aliases={1: 1, 2: 2},
+        compiler_params=params(16),
         cost_estimate=cost(10),
         name="conv_one_grad",
-    )(far(frames), held(d_one), sums, sum_heads, sum_one, sum_two)
-
-
-def frames_back_kernel(*refs, begin, end, total):
+    )(far(frames), held(d_one), held(cells), sums, sum_heads, sum_one, sum_two)
+
+
+def frames_back_kernel(*refs, begin, end, total, ahead):
     d_one_ref, weight_ref = refs[:2]
-    out_ref, band_ref, here_ref, rows_ref, in_sems, out_sems = refs[-6:]
+    if ahead:
+        frames_ref = refs[2]
+        out_ref, d_out_ref, cells_ref, band_ref, rows_ref, sems, cell_sems = refs[-7:]
+    else:
+        out_ref, d_out_ref, band_ref, rows_ref, sems = refs[-5:]
     n = rows_ref.shape[-1]
     step = pl.program_id(0)
-    cells = here_ref.shape[1]
+    row = step + begin
+    cells = d_one_ref.shape[1]
     zero = jnp.zeros((32, n), BF)
-    lead = begin - 1
-    kept = range(max(lead, 0), min(end, total - 1))
-
-    def fetch(r):
-        return pltpu.make_async_copy(d_one_ref.at[r], here_ref.at[r - lead], in_sems.at[r - lead])
 
     @pl.when(step == 0)
     def _():
-        for r in kept:
-            fetch(r).start()
+        if ahead:
+            for r in range(5):
+                ring_copy(frames_ref, cells_ref, cell_sems, r).start()
         band_ref[...] = band_back(weight_ref[...], 2, 64, 3)
-        if begin == 0:
-            here_ref[0] = jnp.zeros_like(here_ref[0])
-        else:
-            fetch(lead).wait()
-        if end == total:
-            here_ref[end - 1 - lead] = jnp.zeros_like(here_ref[0])
-
-    @pl.when(step + begin < total - 1)
-    def _():
-        fetch(step + begin).wait()
-
-    def slab(at, dy, first):
+
+    def slab(at, dy, first, alive):
         parts = []
         for c in range(first, first + 4):
             if c < 0 or c >= 2 * cells:
                 parts.append(zero)
             else:
                 spot = (dy * 2 + c % 2) * 32
-                parts.append(here_ref[at, c // 2, spot : spot + 32, :])
-        return jnp.concatenate(parts, axis=0)
-
-    def row(up, low, at):
+                parts.append(d_one_ref[at, c // 2, spot : spot + 32, :])
+        whole = jnp.concatenate(parts, axis=0)
+        return whole if alive is None else jnp.where(alive, whole, jnp.zeros_like(whole))
+
+    def make(up, low, at):
         for block in range(7):
             first = 3 * block - 1
-            patch = jnp.concatenate([slab(*up, first), slab(*low, first)], axis=0)
+            patch = jnp.concatenate([slab(*up[:2], first, up[2]), slab(*low[:2], first, low[2])], axis=0)
             rows_ref[at, block * 192 : block * 192 + 192, :] = dot(band_ref[...], patch).astype(BF)
 
     def send(at):
-        return pltpu.make_async_copy(rows_ref.at[at], out_ref.at[at + 2 * begin], out_sems.at[at])
-
-    row((step, 1), (step + 1, 0), 2 * step)
+        return pltpu.make_async_copy(rows_ref.at[at], out_ref.at[at + 2 * begin], sems.at[at])
+
+    here = row if end < total else jnp.minimum(row, total - 2)
+    above = row - 1 if begin > 0 else jnp.maximum(row - 1, 0)
+    make(
+        (above, 1, None if begin > 0 else row > 0),
+        (here, 0, None if end < total else row < total - 1),
+        2 * step,
+    )
     send(2 * step).start()
 
-    @pl.when(step + begin < total - 1)
-    def _():
-        row((step + 1, 0), (step + 1, 1), 2 * step + 1)
+    @pl.when(row < total - 1)
+    def _():
+        make((here, 0, None), (here, 1, None), 2 * step + 1)
         send(2 * step + 1).start()
 
     @pl.when(step == end - begin - 1)
     def _():
         for at in range(min(2 * end, 2 * total - 1) - 2 * begin):
             send(at).wait()
-
-
-def frames_back(d_one, weight, shape, begin, end, so_far=None):
+        if ahead:
+            for r in range(5):
+                ring_copy(frames_ref, cells_ref, cell_sems, r).wait()
+
+
+def frames_back(d_one, weight, shape, begin, end, so_far=None, frames=None):
     total = d_one.shape[0] + 1
-    old = [] if so_far is None else [so_far]
+    ahead = frames is not None
+    more = [far(frames)] if ahead else [] if so_far is None else [so_far]
     count = end - begin
-    return pl.pallas_call(
-        functools.partial(frames_back_kernel, begin=begin, end=end, total=total),
-        out_shape=pltpu.HBM(shape, BF),
-        grid=(count,),
-        in_specs=[anywhere(), vmem()] + [anywhere()] * len(old),
-        out_specs=anywhere(),
-        scratch_shapes=[
+    cells = [near((RING,) + shape[1:], BF)] if ahead else []
+    return call(
+        functools.partial(frames_back_kernel, begin=begin, end=end, total=total, ahead=ahead),
+        [held(d_one), weight] + more,
+        [pltpu.HBM(shape, BF), near(d_one.shape, BF)] + cells,
+        in_specs=[vmem(), vmem()] + [anywhere()] * len(more),
+        out_specs=[anywhere(), vmem()] + [vmem()] * len(cells),
+        scratch=[
             pltpu.VMEM((192, 256), BF),
-            pltpu.VMEM((count + 1,) + d_one.shape[1:], BF),
             pltpu.VMEM((2 * count,) + shape[1:], BF),
-            dma(count + 1),
             dma(2 * count),
-        ],
-        input_output_aliases={2: 0} if old else {},
-        compiler_params=params(24),
-        cost_estimate=cost(count),
+        ]
+        + [dma(5)] * len(cells),
+        grid=count,
+        us=count,
         name="frames_back",
-    )(far(d_one), weight, *old)
+        aliases={0: 1, 2: 0} if so_far is not None else {0: 1},
+        limit=16,
+    )
 
 
 def adam_terms(grad, mean, square):
@@ -868,7 +918,11 @@
 def dot3(a, b, dims=NN):
     a_top, a_low = split(a)
     b_top, b_low = split(b)
-    return dot(a_top, b_top, dims) + (dot(a_top, b_low, dims) + dot(a_low, b_top, dims))
+    if dims == TN:
+        return dot(a_top, b_top, dims) + (dot(a_top, b_low, dims) + dot(a_low, b_top, dims))
+    rows = a.shape[0]
+    both = dot(jnp.concatenate([a_top, a_low], axis=0), b_top, dims)
+    return both[:rows] + (both[rows:] + dot(a_top, b_low, dims))
 
 
 def turned_step(weight, grad, mean, square, left, right):
@@ -884,7 +938,9 @@
     packs = 1 + max(spot[0] for spot in spots)
     ins, outs = refs[packs : packs + 5 * count], refs[packs + 5 * count :]
     for w, (pack, row, rows, cols) in enumerate(spots):
-        grad = refs[pack][row : row + rows, 0:cols]
+        grad = refs[pack][row : row + rows, 0:cols].astype(F32)
+        if rows == 16:
+            grad = jnp.concatenate([grad, refs[pack][row : row + rows, cols : 2 * cols]], axis=0)
         weight, mean, square, left, right = [ref[...] for ref in ins[5 * w : 5 * w + 5]]
         results = (grad,) + turned_step(weight, grad, mean, square, left, right)
         for ref, value in zip(outs[4 * w : 4 * w + 4], results):
@@ -902,7 +958,7 @@
         out_shape=tuple(shapes),
         in_specs=[vmem()] * (len(packs) + len(arrays)),
         out_specs=(vmem(),) * len(shapes),
-        compiler_params=params(24),
+        compiler_params=params(32),
         cost_estimate=cost(5),
         name="steps",
     )(*packs, *arrays)
@@ -947,36 +1003,6 @@
 def fence(*values):
     leaves, tree = jax.tree.flatten(values)
     return jax.tree.unflatten(tree, lax.optimization_barrier(tuple(leaves)))
-
-
-def stage(x, axis, bits, size):
-    if len(bits) == 1:
-        return [swap(x, axis, bits[0], size)]
-    one, two = bits
-    return [swap(x, axis, bit, size) for bit in (one, two, one | two)]
-
-
-def stage_sum(x, came):
-    up = [v.astype(F32) for v in [x] + came]
-    if len(up) == 2:
-        return up[0] + up[1]
-    return (up[0] + up[1]) + (up[2] + up[3])
-
-
-def bit_pairs(bits):
-    odd = len(bits) % 2
-    return [tuple(bits[k : k + 2]) for k in range(odd, len(bits), 2)] + [(b,) for b in bits[:odd]]
-
-
-def few_stages(n_dp, n_own):
-    plan = [("own", bits, n_own) for bits in bit_pairs(bits_of(n_own))]
-    return plan + [("dp", bits, n_dp) for bits in bit_pairs(bits_of(n_dp))]
-
-
-def light_stages(n_dp, n_own):
-    far_first = bits_of(n_dp)[::-1]
-    plan = [("dp", (bit,), n_dp) for bit in far_first] + [("own", (bit,), n_own) for bit in bits_of(n_own)[::-1]]
-    return plan[:1] + plan[len(far_first) : -1] + plan[1 : len(far_first)] + plan[-1:]
 
 
 def add_low(*terms):
@@ -1028,26 +1054,26 @@
     dp_swap = lambda x, bit: swap(x, "dp", bit, n_dp)
     place = jnp.stack([lax.axis_index("dp"), lax.axis_index("own")]).astype(jnp.int32)
     bias_row = bias_all.reshape(1, -1)
-    adv, piece = first(lengths, dones, rewards, old_values, dense_hidden)
     cells = frames.transpose(1, 2, 3, 0).reshape(grid, grid * planes, tokens)
+    adv, piece, ring = first(lengths, dones, rewards, old_values, dense_hidden, cells)
 
     if tuned:
         along_z = [dp_swap(piece, 2 * k) for k in (1, 2, 3)]
-    act_one, slope_one_far = conv_one(cells, conv_first.T, bias_row)
+    act_one, slope_one, _ = conv_one(cells, conv_first.T, bias_row, ring)
     if tuned:
         spots = [(2 * k, 0) for k in range(4)]
-        act_one, piece, along_z = fence(act_one, piece, along_z)
+        act_one, slope_one, piece, along_z = fence(act_one, slope_one, piece, along_z)
         column = jnp.stack([piece] + along_z)
-        act_one, column = fence(act_one, column)
+        act_one, slope_one, column = fence(act_one, slope_one, column)
         by_x, by_y = dp_swap(column, 1), own_swap(column, 2)
     else:
         pieces = plain_gather(piece, n_dp, n_own)
-    act_two, slope_two, act_one_far = conv_two(act_one, conv_second.T, bias_row)
+    act_two, slope_two, act_one_far, slope_one_far = conv_two(act_one, slope_one, conv_second.T, bias_row)
     if tuned:
-        act_two, column, by_x, by_y = fence(act_two, column, by_x, by_y)
+        act_two, slope_two, column, by_x, by_y = fence(act_two, slope_two, column, by_x, by_y)
         halves = (by_x[0:2], by_y[2:4])
         plane = jnp.concatenate([column, by_x, by_y])
-        act_two, halves, plane = fence(act_two, halves, plane)
+        act_two, slope_two, halves, plane = fence(act_two, slope_two, halves, plane)
         corner = [own_swap(halves[0], 2), dp_swap(halves[1], 1)]
         other = own_swap(plane, 1)
     flat, slope_three, act_two_far, slope_two_far = conv_three(act_two, slope_two, conv_third.T, bias_row)
@@ -1061,82 +1087,102 @@
             (other, [(i, j ^ 1) for i, j in plane_spots]),
             (own_swap(corner, 1), [(i, j ^ 1) for i, j in corner_spots]),
         ]
-    d_three, act_two, slope_two, keep, send, here_heads, sums, sum_heads = dense(
-        place, lengths, flat, slope_three, act_two_far, slope_two_far, dense_heads.T, bias_row,
-        actions, adv, old_values, old_logp, pieces, n_dp, n_own, rows,
-    )
-
-    many_plan, one_plan = light_stages(n_dp, n_own), few_stages(n_dp, n_own)
-
-    def leave(x, plan, at):
-        axis, bits, size = plan[at]
-        return stage(x, axis, bits, size)
-
-    def rest(x, plan, at, low):
-        for k in range(at, len(plan)):
-            total = stage_sum(x, leave(x, plan, k))
-            x = total.astype(BF) if low and k < len(plan) - 1 else total
-        return x
-
-    d_three, act_two, slope_two, keep, send = fence(d_three, act_two, slope_two, keep, send)
+    d_three, act_two, keep, send, here_heads, sums, sum_heads = dense(
+        place, lengths, dense_heads.T, bias_row, actions, adv, old_values, old_logp,
+        flat, slope_three, act_two_far, pieces, n_dp, n_own, rows,
+    )
+
     came = own_swap(send, 1) if tuned else None
     d_two, act_one, slope_one, pack, sum_two = conv_three_back(
-        d_three, act_two, slope_two, act_one_far, slope_one_far, conv_third.T, here_heads
+        d_three, act_two, slope_two_far, act_one_far, slope_one_far, conv_third.T, here_heads
     )
     if tuned:
-        d_two, keep, came = fence(d_two, keep, came)
+        d_two, act_one, slope_one, keep, came = fence(d_two, act_one, slope_one, keep, came)
         block = add_low(keep, came)
         ends = (block[1, 4:6], block[1, 6:8])
-        d_two, block, ends = fence(d_two, block, ends)
+        d_two, act_one, slope_one, block, ends = fence(d_two, act_one, slope_one, block, ends)
         by_y, by_x = own_swap(ends[0], 2), dp_swap(ends[1], 1)
-    d_one, d_one_far, pack, sum_one = conv_two_back(d_two, act_one, slope_one, conv_second.T, pack)
+    d_one, pack, sum_one = conv_two_back(d_two, act_one, slope_one, conv_second.T, pack)
+
+    shape = cells.shape
+    side = lax.axis_index("own") % 2
+    rows_half = pack.shape[0] // 2
     if tuned:
-        d_one, d_one_far, pack, block, by_x, by_y = fence(d_one, d_one_far, pack, block, by_x, by_y)
+        d_one, pack, block, by_x, by_y = fence(d_one, pack, block, by_x, by_y)
         side_x = jnp.concatenate([add_low(block[0, 4:6], by_y), block[0, 6:8]])
         side_y = jnp.concatenate([block[1, 0:2], add_low(block[1, 2:4], by_x)])
-        d_one, d_one_far, pack, block, side_x, side_y = fence(d_one, d_one_far, pack, block[0, 0:4], side_x, side_y)
+        block = block[0, 0:4]
+    else:
+        side_x = side_y = block = jnp.zeros((8, 128), BF)
+    half = lax.dynamic_slice_in_dim(pack, side * rows_half, rows_half)
+    gone = lax.dynamic_slice_in_dim(pack, (1 - side) * rows_half, rows_half)
+    d_one, half, gone, block, side_x, side_y = fence(d_one, half, gone, block, side_x, side_y)
+    if tuned:
         by_x, by_y = dp_swap(side_x, 1), own_swap(side_y, 2)
-    many = leave(pack, many_plan, 0)
-    pack_one = conv_one_grad(cells, d_one, sums, sum_heads, sum_one, sum_two)
+    came = own_swap(gone, 1)
+    cuts = (0, 2, 5, 8, grid // 2 + 1)
+    back, d_one, ring = frames_back(d_one, conv_first.T, shape, cuts[0], cuts[1], frames=cells)
+    back, d_one, ring, half, came = fence(back, d_one, ring, half, came)
+    half = add_low(half, came)
+    back, d_one, ring, half = fence(back, d_one, ring, half)
+    far_bits = bits_of(n_dp)[:0:-1]
+    came = dp_swap(half, far_bits[0])
+    pack_one, d_one, _ = conv_one_grad(cells, d_one, ring, sums, sum_heads, sum_one, sum_two)
     if tuned:
-        pack_one, block, by_x, by_y = fence(pack_one, block, by_x, by_y)
+        pack_one, d_one, block, by_x, by_y = fence(pack_one, d_one, block, by_x, by_y)
         block = add_low(block, by_x, by_y)
-        parts = [block[k] for k in range(4)]
+    pack_one, d_one, half, came = fence(pack_one, d_one, half, came)
+
+    half = add_low(half, came)
+    pack_one, d_one, half, block = fence(pack_one, d_one, half, block)
+    came_one = dp_swap(pack_one, far_bits[0])
+    came = own_swap(half, 2)
+    if tuned:
+        parts = [block[0]] + [dp_swap(block[k], 2 * k) for k in (1, 2, 3)]
     else:
         parts = plain_scatter(keep, send, n_dp, n_own)
-    pack_one, d_one_far, pack, many = fence(pack_one, d_one_far, pack, many)
-    pack = stage_sum(pack, many).astype(BF)
-    pack_one, d_one_far, pack, parts = fence(pack_one, d_one_far, pack, parts)
-    if tuned:
-        parts = [parts[0]] + [dp_swap(parts[k], 2 * k) for k in (1, 2, 3)]
-    many = leave(pack, many_plan, 1)
-    one = leave(pack_one, one_plan, 0)
-    shape = cells.shape
-    cuts = (0, 4, 8, grid // 2 + 1)
-    back = None
-    for k in range(3):
-        back = frames_back(d_one_far, conv_first.T, shape, cuts[k], cuts[k + 1], back)
-        back, d_one_far, parts, pack, many, pack_one, one = fence(
-            back, d_one_far, parts, pack, many, pack_one, one
-        )
-        pack = stage_sum(pack, many).astype(BF)
-        pack_one = stage_sum(pack_one, one)
-        back, d_one_far, parts, pack, pack_one = fence(back, d_one_far, parts, pack, pack_one)
-        many = leave(pack, many_plan, k + 2)
-        if k < 2:
-            one = leave(pack_one, one_plan, k + 1)
+    back, d_one = frames_back(d_one, conv_first.T, shape, cuts[1], cuts[2], back)
+    back, d_one, half, came, pack_one, came_one = fence(back, d_one, half, came, pack_one, came_one)
+
+    def join(pack, pack_one):
+        return jnp.concatenate([pack.astype(BF), *split(pack_one)])
+
+    def part(both):
+        count = pack_one.shape[0]
+        low = both[rows_half:].astype(F32)
+        return both[:rows_half].astype(F32), low[:count] + low[count:]
+
+    def add_up(both, came):
+        a, b = part(both), part(came)
+        return a[0] + b[0], a[1] + b[1]
+
+    both = join(add_low(half, came), pack_one + came_one)
+    back, d_one, both = fence(back, d_one, both)
+    more = [1] + far_bits[1:]
+    came = dp_swap(both, more[0])
+    back, d_one = frames_back(d_one, conv_first.T, shape, cuts[2], cuts[3], back)
+    back, d_one, both, came = fence(back, d_one, both, came)
+    both = join(*add_up(both, came))
+    back, d_one, both = fence(back, d_one, both)
+    came = dp_swap(both, more[1])
+    back, d_one = frames_back(d_one, conv_first.T, shape, cuts[3], cuts[4], back)
+    for bit in more[2:]:
+        both = join(*add_up(both, came))
+        came = dp_swap(both, bit)
+    back, parts, both, came = fence(back, parts, both, came)
+    both = join(*add_up(both, came))
+    parts, both = fence(parts, both)
+    came = own_swap(both, 1)
     frames_grad = back.reshape(grid, grid, planes, tokens).transpose(3, 0, 1, 2)
     grad_dense, *wide_step = dense_step(
         dense_hidden, mean_dense, square_dense, right_dense, parts, RATE / math.sqrt(rows * n_dp)
     )
-    pack_one = rest(pack_one, one_plan, 3, False)
-    first_step = steps(
-        [pack_one], [(0, 0, 32, 256)], [(conv_first, mean_first, square_first, left_first, right_first)]
-    )
-    grad_dense, first_step, pack, many = fence(grad_dense, first_step, pack, many)
-    pack = stage_sum(pack, many)
-    if len(many_plan) > 5:
-        pack = rest(pack.astype(BF), many_plan, 5, True)
+    grad_dense, both, came = fence(grad_dense, both, came)
+    pack_one = add_up(both, came)[1]
+    halves = (both[:rows_half], came[:rows_half])
+    pack = jnp.concatenate([jnp.where(side == 0, *halves), jnp.where(side == 0, *halves[::-1])])
+    pack_one, pack = fence(pack_one, pack)
+    one = own_swap(pack_one, 2)
     late = steps(
         [pack],
         [(0, 0, 64, 576), (0, 64, 19, 512), (0, 96, 64, 512)],
@@ -1146,9 +1192,17 @@
             (conv_second, mean_second, square_second, left_second, right_second),
         ],
     )
+    late, pack_one, one = fence(late, pack_one, one)
+    pack_one = pack_one + one
     third, top, second = late[0:4], late[4:8], late[8:12]
+    first_step = steps(
+        [pack_one],
+        [(0, 0, 16, 256)],
+        [(conv_first, mean_first, square_first, left_first, right_first)],
+    )
+    line = pack_one[:, 512:]
     grad_bias = jnp.concatenate(
-        [pack_one[36, 0:32], pack_one[35, 0:64], pack_one[34, 0:64], pack_one[32], pack_one[33], pack_one[37, 0:19]]
+        [line[6, 0:32], line[5, 0:64], line[4, 0:64], line[0], line[1], line[2], line[3], line[7, 0:19]]
     )
     mom_bias, var_bias, bias_dir = adam_terms(grad_bias, mean_bias, square_bias)
     new_bias = bias_all - BIAS_RATE * bias_dir

time: 142 us -> 132 us (0.930)
  Pallas kernels: 96.1 us -> 90.1 us
  starting transfers between devices: 34 us -> 28.8 us
  other arithmetic: 2 us -> 3.43 us
    pallas_call x10 -> x11, Pallas kernels: 86.2 us -> 80.9 us  [the longest x10 70.8 us: call(): pl.pallas_call(body, out_shape=tuple(outs), in_specs=list(in_specs or [vm...]
    ppermute x29 -> x25, starting transfers between devices: 34 us -> 28.8 us  [swap(): return lax.ppermute(x, axis, [(i, i ^ bit) for i in range(size)])]
    convert_element_type x3 -> x6, other arithmetic: 0.7 us -> 2.2 us  [add_low(): return total.astype(BF)]
    ppermute x29 -> x25, waiting for transfers between devices: 5.9 us -> 5.57 us  [swap(): return lax.ppermute(x, axis, [(i, i ^ bit) for i in range(size)])]
  transfers between devices with their start and end apart: 29 -> 25, of which waited for: 6 -> 5; matrix products, arithmetic and copies ran while one was open for 1% -> 0% of each run, Pallas kernels for 54% -> 56%
where the time goes in v4:
time: 132 us; the launch traced here: 131 us
  Pallas kernels  90.1 us (68%)
  starting transfers between devices  28.8 us (22%)
  waiting for transfers between devices  5.57 us (4%)
  other arithmetic  3.43 us (3%)
  between operations  2.25 us (2%)
    pallas_call x10, Pallas kernels, call(): pl.pallas_call(body, out_shape=tuple(outs), in_specs=list(in_specs or [vm...  70.8 us
    ppermute x25, starting transfers between devices, swap(): return lax.ppermute(x, axis, [(i, i ^ bit) for i in range(size)])  28.8 us
    pallas_call x1, Pallas kernels, conv_one_grad(): pl.pallas_call(conv_one_grad_kernel, out_shape=(jax.ShapeDtypeStruct((16,...  10.1 us
    ppermute x25, waiting for transfers between devices, swap(): return lax.ppermute(x, axis, [(i, i ^ bit) for i in range(size)])  5.57 us
    pallas_call x2, Pallas kernels, steps(): pl.pallas_call(functools.partial(steps_kernel, spots=spots), out_shape=tu...  5.21 us
  transfers between devices with their start and end apart: 25, of which 5 were waited for; matrix products, arithmetic and copies ran while one was open for 0% of the time, Pallas kernels for 56%

profile of v4, /device:TPU:0, one launch (start us, length us, event | category | flops | bytes accessed | tf_op | source)
XLA Modules:
  0.0 131.4 jit_solution(15276248884788044347)
XLA Ops:
  1.3 2.6 %first.1 = (f32[1,256]{1,0:T(1,128)S(1)}, bf16[416,128]{1,0:T(8,128)(2,1)S(1)}, bf16[8,1344,256]{2,1,0:T(8,128)(2,1)S(1)}) custom-call(s32[1]{0:T(128)S(6)} %copy.80.lengths_ref.refs_1_, s32[1,256]{1,0:T(1,128)} %dones_far_ref.1, f32[1,256]{1,0:T(1,128)} %rewards_far_ref.1, f32[1,256]{1,0:T(1,128)} %refs_6_.1, f32[392,128]{1,0:T(8,128)} %refs_0_.1, ...), custom_call_target="tpu_custom_call" | custom-call | flops 3000000000 | tf_op jit(solution)/shard_map/first/pallas_call | solution.py:233
  4.0 5.1 %collective-permute-start.2 = (bf16[416,128]{1,0:T(8,128)(2,1)S(1)}, bf16[416,128]{1,0:T(8,128)(2,1)S(1)}, u32[]{:S(2)}, u32[]{:S(2)}) collective-permute-start(bf16[416,128]{1,0:T(8,128)(2,1)S(1)} %get-tuple-element.203), channel_id=1, source_target_pairs={{0,24},{4,28},{8,16},{12,20},{16,8},{20,12},{24,0},{28,4},{1,25},{... | collective-permute-start | bytes 319496 | tf_op jit(solution)/shard_map/ppermute | solution.py:996
  9.8 11.0 %conv_one.1 = (bf16[10,10,128,256]{3,2,1,0:T(8,128)(2,1)S(1)}, bf16[10,10,128,256]{3,2,1,0:T(8,128)(2,1)S(1)}, bf16[8,1344,256]{2,1,0:T(8,128)(2,1)S(1)}) custom-call(bf16[21,1344,256]{2,1,0:T(8,128)(2,1)} %bitcast.105, f32[32,256]{1,0:T(8,128)S(1)} %bitcast.80, f32[1,691]{1,0:T(1,128)S(1)} %reshape.64.bias_ref.refs_3_, ...), custom_call_target="tpu_custom_call", output_to_operand_aliasing={{2}: (3, {})} | custom-call | flops 12000000000 | tf_op jit(solution)/shard_map/conv_one/pallas_call | solution.py:85
  20.9 1.7 %collective-permute-start.4 = (bf16[4,416,128]{2,1,0:T(8,128)(2,1)S(1)}, bf16[4,416,128]{2,1,0:T(8,128)(2,1)S(1)}, u32[]{:S(2)}, u32[]{:S(2)}) collective-permute-start(bf16[4,416,128]{2,1,0:T(8,128)(2,1)S(1)} %pad_maximum_fusion.1), channel_id=1, source_target_pairs={{0,2},{1,3},{2,0},{3,1},{4,6},{5,7},{6,4},{7,5},{8,10},{9,11},{10,... | collective-permute-start | bytes 1277960 | tf_op jit(solution)/shard_map/ppermute | solution.py:996
  22.6 1.5 %collective-permute-start.3 = (bf16[4,416,128]{2,1,0:T(8,128)(2,1)S(1)}, bf16[4,416,128]{2,1,0:T(8,128)(2,1)S(1)}, u32[]{:S(2)}, u32[]{:S(2)}) collective-permute-start(bf16[4,416,128]{2,1,0:T(8,128)(2,1)S(1)} %pad_maximum_fusion.1), channel_id=1, source_target_pairs={{0,4},{4,0},{8,12},{12,8},{16,20},{20,16},{24,28},{28,24},{1,5},{5... | collective-permute-start | bytes 1277960 | tf_op jit(solution)/shard_map/ppermute | solution.py:996
  24.1 7.3 %conv_two.1 = (bf16[9,576,256]{2,1,0:T(8,128)(2,1)S(1)}, bf16[9,576,256]{2,1,0:T(8,128)(2,1)S(1)}, bf16[10,10,128,256]{3,2,1,0:T(8,128)(2,1)}, bf16[10,10,128,256]{3,2,1,0:T(8,128)(2,1)}) custom-call(bf16[10,10,128,256]{3,2,1,0:T(8,128)(2,1)S(1)} %get-tuple-element.207.one_ref, bf16[10,10,128,256]{3,2,1,0:T(8,128)(2,1)S(1)} %get-tuple-element.208.slope_one_ref, ...), custom_call_target="tpu_custom_call" | custom-call | flops 7000000000 | tf_op jit(solution)/shard_map/conv_two/pallas_call | solution.py:85
  31.9 1.2 collective-permute-done.3
  34.0 1.5 %collective-permute-start.6 = (bf16[2,416,128]{2,1,0:T(8,128)(2,1)S(1)}, bf16[2,416,128]{2,1,0:T(8,128)(2,1)S(1)}, u32[]{:S(2)}, u32[]{:S(2)}) collective-permute-start(bf16[2,416,128]{2,1,0:T(8,128)(2,1)S(1)} %slice.145), channel_id=1, source_target_pairs={{0,4},{4,0},{8,12},{12,8},{16,20},{20,16},{24,28},{28,24},{1,5},{5... | collective-permute-start | bytes 638984 | tf_op jit(solution)/shard_map/ppermute | solution.py:996
  35.5 6.1 %conv_three.1 = (bf16[7,448,256]{2,1,0:T(8,128)(2,1)}, bf16[7,448,256]{2,1,0:T(8,128)(2,1)}, bf16[9,576,256]{2,1,0:T(8,128)(2,1)}, bf16[9,576,256]{2,1,0:T(8,128)(2,1)}) custom-call(bf16[9,576,256]{2,1,0:T(8,128)(2,1)S(1)} %get-tuple-element.217.two_ref, bf16[9,576,256]{2,1,0:T(8,128)(2,1)S(1)} %get-tuple-element.218.slope_two_ref, f32[64,576]{1,0:T(8,128)S(1)} %bitcast.87, ...), custom_call_target="tpu_custom_call" | custom-call | flops 6000000000 | tf_op jit(solution)/shard_map/conv_three/pallas_call | solution.py:85
  41.9 1.7 %collective-permute-done.8.refs_14_ = bf16[4,416,128]{2,1,0:T(8,128)(2,1)S(1)} collective-permute-done((bf16[4,416,128]{2,1,0:T(8,128)(2,1)S(1)}, bf16[4,416,128]{2,1,0:T(8,128)(2,1)S(1)}, u32[]{:S(2)}, u32[]{:S(2)}) %collective-permute-start.8) | collective-permute-done | bytes 426016 | tf_op jit(solution)/shard_map/ppermute | solution.py:996
  44.3 12.5 %dense.1 = (bf16[7,448,256]{2,1,0:T(8,128)(2,1)}, bf16[9,576,256]{2,1,0:T(8,128)(2,1)S(1)}, bf16[2,8,392,128]{3,2,1,0:T(8,128)(2,1)}, bf16[2,8,392,128]{3,2,1,0:...) custom-call(s32[2]{0:T(128)S(1)} %pad_add_fusion.refs_0_, ...), custom_call_target="tpu_custom_call" | custom-call | flops 10000000000 | tf_op jit(solution)/shard_map/dense/pallas_call | solution.py:85
  57.1 11.2 %conv_three_back.1 = (bf16[9,576,256]{2,1,0:T(8,128)(2,1)S(1)}, bf16[10,10,128,256]{3,2,1,0:T(8,128)(2,1)S(1)}, bf16[10,10,128,256]{3,2,1,0:T(8,128)(2,1)S(1)}, bf16[96,640]{1,0:T(8,128)(2,1)S(1)}, f32[1,64]{1,0:T(1,128)S(1)}) custom-call(bf16[9,576,256]{2,1,0:T(8,128)(2,1)S(1)} %get-tuple-element.228.act_ref, ...), custom_call_target="tpu_custom_call" | custom-call | flops 8999999488 | tf_op jit(solution)/shard_map/conv_three_back/pallas_call | solution.py:85
  68.2 1.8 %add_convert_fusion = bf16[2,8,392,128]{3,2,1,0:T(8,128)(2,1)S(1)} fusion(bf16[2,8,392,128]{3,2,1,0:T(8,128)(2,1)} %collective-permute-done.9, bf16[2,8,392,128]{3,2,1,0:T(8,128)(2,1)S(1)} %copy-done.26), kind=kLoop, calls=%fused_computation | loop fusion | flops 3211264 | bytes 4816896 | tf_op jit(solution)/shard_map/convert_element_type | solution.py:1012
  70.1 1.2 collective-permute-start.10
  71.4 1.5 %collective-permute-start.11 = (bf16[2,392,128]{2,1,0:T(8,128)(2,1)S(1)}, bf16[2,392,128]{2,1,0:T(8,128)(2,1)S(1)}, u32[]{:S(2)}, u32[]{:S(2)}) collective-permute-start(bf16[2,392,128]{2,1,0:T(8,128)(2,1)S(1)} %get-tuple-element.252), channel_id=1, source_target_pairs={{0,2},{1,3},{2,0},{3,1},{4,6},{5,7},{6,4},{7,5},{8,10},{9,11},{10,... | collective-permute-start | bytes 602120 | tf_op jit(solution)/shard_map/ppermute | solution.py:996
  72.9 10.5 %conv_two_back.1 = (bf16[10,10,128,256]{3,2,1,0:T(8,128)(2,1)S(1)}, bf16[160,640]{1,0:T(8,128)(2,1)S(1)}, f32[1,32]{1,0:T(1,128)S(1)}) custom-call(bf16[9,576,256]{2,1,0:T(8,128)(2,1)S(1)} %get-tuple-element.244.d_two_ref, bf16[10,10,128,256]{3,2,1,0:T(8,128)(2,1)S(1)} %get-tuple-element.245.act_ref, ...), custom_call_target="tpu_custom_call" | custom-call | flops 11000000512 | tf_op jit(solution)/shard_map/conv_two_back/pallas_call | solution.py:85
  83.8 1.1 collective-permute-start.13
  85.4 3.0 %frames_back.4 = (bf16[21,1344,256]{2,1,0:T(8,128)(2,1)}, bf16[10,10,128,256]{3,2,1,0:T(8,128)(2,1)S(1)}, bf16[8,1344,256]{2,1,0:T(8,128)(2,1)S(1)}) custom-call(bf16[10,10,128,256]{3,2,1,0:T(8,128)(2,1)S(1)} %get-tuple-element.258.refs_0_, f32[32,256]{1,0:T(8,128)S(1)} %bitcast.81, bf16[21,1344,256]{2,1,0:T(8,128)(2,1)} %bitcast.106), custom_call_target="tpu_custom_call", output_to_operand_aliasing={{1}: (0, {})} | custom-call | flops 2000000000 | tf_op jit(solution)/shard_map/frames_back/pallas_call | solution.py:85
  88.5 2.4 %collective-permute-start.15 = (bf16[80,640]{1,0:T(8,128)(2,1)S(1)}, bf16[80,640]{1,0:T(8,128)(2,1)S(1)}, u32[]{:S(2)}, u32[]{:S(2)}) collective-permute-start(bf16[80,640]{1,0:T(8,128)(2,1)S(1)} %add_convert_fusion.6), channel_id=1, source_target_pairs={{0,16},{4,20},{8,24},{12,28},{16,0},{20,4},{24,8},{28,12},{1,17},{... | collective-permute-start | bytes 307208 | tf_op jit(solution)/shard_map/ppermute | solution.py:996
  90.9 10.1 %conv_one_grad.1 = (f32[16,640]{1,0:T(8,128)S(1)}, bf16[10,10,128,256]{3,2,1,0:T(8,128)(2,1)S(1)}, bf16[8,1344,256]{2,1,0:T(8,128)(2,1)S(1)}) custom-call(bf16[21,1344,256]{2,1,0:T(8,128)(2,1)} %bitcast.107, bf16[10,10,128,256]{3,2,1,0:T(8,128)(2,1)S(1)} %get-tuple-element.269.d_one_ref, ...), custom_call_target="tpu_custom_call", output_to_operand_aliasing={{1}: (1, {}), {2}: (2, {})} | custom-call | flops 10000000000 | tf_op jit(solution)/shard_map/conv_one_grad/pallas_call | solution.py:798
  101.9 1.5 %collective-permute-start.16 = (bf16[80,640]{1,0:T(8,128)(2,1)S(1)}, bf16[80,640]{1,0:T(8,128)(2,1)S(1)}, u32[]{:S(2)}, u32[]{:S(2)}) collective-permute-start(bf16[80,640]{1,0:T(8,128)(2,1)S(1)} %add_convert_fusion.5), channel_id=1, source_target_pairs={{0,2},{1,3},{2,0},{3,1},{4,6},{5,7},{6,4},{7,5},{8,10},{9,11},{10,... | collective-permute-start | bytes 307208 | tf_op jit(solution)/shard_map/ppermute | solution.py:996
  103.4 3.5 %collective-permute-start.21 = (bf16[392,128]{1,0:T(8,128)(2,1)S(1)}, bf16[392,128]{1,0:T(8,128)(2,1)S(1)}, u32[]{:S(2)}, u32[]{:S(2)}) collective-permute-start(bf16[392,128]{1,0:T(8,128)(2,1)S(1)} %get-tuple-element.380), channel_id=1, source_target_pairs={{0,24},{4,28},{8,16},{12,20},{16,8},{20,12},{24,0},{28,4},{1,25},{... | collective-permute-start | bytes 301064 | tf_op jit(solution)/shard_map/ppermute | solution.py:996
  107.9 3.2 %frames_back.5 = (bf16[21,1344,256]{2,1,0:T(8,128)(2,1)}, bf16[10,10,128,256]{3,2,1,0:T(8,128)(2,1)S(1)}) custom-call(bf16[10,10,128,256]{3,2,1,0:T(8,128)(2,1)S(1)} %get-tuple-element.290.refs_0_, f32[32,256]{1,0:T(8,128)S(1)} %bitcast.82, bf16[21,1344,256]{2,1,0:T(8,128)(2,1)} %get-tuple-element.291.refs_2_), custom_call_target="tpu_custom_call", output_to_operand_aliasing={{1}: (0, {}), {0}: (2, {})} | custom-call | flops 3000000000 | tf_op jit(solution)/shard_map/frames_back/pallas_call | solution.py:85
  111.2 1.0 collective-permute-start.18
  112.2 3.2 %frames_back.6 = (bf16[21,1344,256]{2,1,0:T(8,128)(2,1)}, bf16[10,10,128,256]{3,2,1,0:T(8,128)(2,1)S(1)}) custom-call(bf16[10,10,128,256]{3,2,1,0:T(8,128)(2,1)S(1)} %get-tuple-element.302.refs_0_, f32[32,256]{1,0:T(8,128)S(1)} %bitcast.83, bf16[21,1344,256]{2,1,0:T(8,128)(2,1)} %get-tuple-element.303.refs_2_), custom_call_target="tpu_custom_call", output_to_operand_aliasing={{1}: (0, {}), {0}: (2, {})} | custom-call | flops 3000000000 | tf_op jit(solution)/shard_map/frames_back/pallas_call | solution.py:85
  116.5 1.2 collective-permute-start.22
  117.7 2.8 %frames_back.7 = (bf16[21,1344,256]{2,1,0:T(8,128)(2,1)}, bf16[10,10,128,256]{3,2,1,0:T(8,128)(2,1)S(1)}) custom-call(bf16[10,10,128,256]{3,2,1,0:T(8,128)(2,1)S(1)} %get-tuple-element.311.refs_0_, f32[32,256]{1,0:T(8,128)S(1)} %bitcast.84, bf16[21,1344,256]{2,1,0:T(8,128)(2,1)} %get-tuple-element.312.refs_2_), custom_call_target="tpu_custom_call", output_to_operand_aliasing={{1}: (0, {}), {0}: (2, {})} | custom-call | flops 3000000000 | tf_op jit(solution)/shard_map/frames_back/pallas_call | solution.py:85
  120.6 1.1 collective-permute-done.22
  122.1 1.4 %dense_step.1 = (f32[392,128]{1,0:T(8,128)}, f32[392,128]{1,0:T(8,128)}, f32[392,128]{1,0:T(8,128)}, f32[392,128]{1,0:T(8,128)}) custom-call(f32[392,128]{1,0:T(8,128)S(1)} %copy-done.1, f32[392,128]{1,0:T(8,128)S(1)} %copy-done.7, f32[392,128]{1,0:T(8,128)S(1)} %copy-done.8, f32[1,128,128]{2,1,0:T(8,128)S(1)} %copy-done.15, ...), custom_call_target="tpu_custom_call" | custom-call | flops 3000000000 | tf_op jit(solution)/shard_map/dense_step/pallas_call | solution.py:984
  123.5 1.7 %collective-permute-start.24 = (f32[16,640]{1,0:T(8,128)S(1)}, f32[16,640]{1,0:T(8,128)S(1)}, u32[]{:S(2)}, u32[]{:S(2)}) collective-permute-start(f32[16,640]{1,0:T(8,128)S(1)} %fusion.2), channel_id=1, source_target_pairs={{0,2},{1,3},{2,0},{3,1},{4,6},{5,7},{6,4},{7,5},{8,10},{9,11},{10,... | collective-permute-start | bytes 122888 | tf_op jit(solution)/shard_map/ppermute | solution.py:996
  125.4 3.9 %steps.2 = (f32[64,576]{1,0:T(8,128)}, f32[64,576]{1,0:T(8,128)}, f32[64,576]{1,0:T(8,128)}, f32[64,576]{1,0:T(8,128)}, f32[19,512]{1,0:T(8,128)}, /*index=5*/f3...) custom-call(bf16[160,640]{1,0:T(8,128)(2,1)S(1)} %pad_maximum_fusion, ...), custom_call_target="tpu_custom_call" | custom-call | flops 5000000000 | tf_op jit(solution)/shard_map/steps/pallas_call | solution.py:956
  130.2 1.3 steps.3
  (145 shorter events, 8.2 us)
Async XLA Ops:
  1.3 8.4 %copy-start.29 = (f32[691]{0:T(1024)S(1)}, f32[691]{0:T(1024)}, u32[]{:S(2)}) copy-start(f32[691]{0:T(1024)} %param.46) | copy-start | bytes 8296
  1.3 8.4 %copy-start = (f32[256,32]{0,1:T(8,128)S(1)}, f32[256,32]{0,1:T(8,128)}, u32[]{:S(2)}) copy-start(f32[256,32]{0,1:T(8,128)} %param.41) | copy-start | bytes 98308
  4.0 16.8 %copy-start.25 = (f32[1,256]{1,0:T(1,128)}, f32[1,256]{1,0:T(1,128)S(1)}, u32[]{:S(2)}) copy-start(f32[1,256]{1,0:T(1,128)S(1)} %get-tuple-element.196.refs_5_) | copy-start | bytes 3076
  4.0 16.8 %collective-permute-start.2 = (bf16[416,128]{1,0:T(8,128)(2,1)S(1)}, bf16[416,128]{1,0:T(8,128)(2,1)S(1)}, u32[]{:S(2)}, u32[]{:S(2)}) collective-permute-start(bf16[416,128]{1,0:T(8,128)(2,1)S(1)} %get-tuple-element.203), channel_id=1, source_target_pairs={{0,24},{4,28},{8,16},{12,20},{16,8},{20,12},{24,0},{28,4},{1,25},{... | collective-permute-start | bytes 319496 | tf_op jit(solution)/shard_map/ppermute | solution.py:996
  9.1 11.7 %collective-permute-start.1 = (bf16[416,128]{1,0:T(8,128)(2,1)S(1)}, bf16[416,128]{1,0:T(8,128)(2,1)S(1)}, u32[]{:S(2)}, u32[]{:S(2)}) collective-permute-start(bf16[416,128]{1,0:T(8,128)(2,1)S(1)} %get-tuple-element.203), channel_id=1, source_target_pairs={{0,16},{4,20},{8,24},{12,28},{16,0},{20,4},{24,8},{28,12},{1,17},{... | collective-permute-start | bytes 319496 | tf_op jit(solution)/shard_map/ppermute | solution.py:996
  9.1 11.7 %collective-permute-start = (bf16[416,128]{1,0:T(8,128)(2,1)S(1)}, bf16[416,128]{1,0:T(8,128)(2,1)S(1)}, u32[]{:S(2)}, u32[]{:S(2)}) collective-permute-start(bf16[416,128]{1,0:T(8,128)(2,1)S(1)} %get-tuple-element.203), channel_id=1, source_target_pairs={{0,8},{4,12},{8,0},{12,4},{16,24},{20,28},{24,16},{28,20},{1,9},{5... | collective-permute-start | bytes 319496 | tf_op jit(solution)/shard_map/ppermute | solution.py:996
  9.8 25.8 %copy-start.2 = (f32[1,691]{1,0:T(1,128)}, f32[1,691]{1,0:T(1,128)S(1)}, u32[]{:S(2)}) copy-start(f32[1,691]{1,0:T(1,128)S(1)} %reshape.64.bias_ref.refs_3_) | copy-start | bytes 8296
  9.8 14.3 %copy-start.12 = (f32[512,64]{0,1:T(8,128)S(1)}, f32[512,64]{0,1:T(8,128)}, u32[]{:S(2)}) copy-start(f32[512,64]{0,1:T(8,128)} %param.42) | copy-start | bytes 393220
  20.9 11.1 %collective-permute-start.4 = (bf16[4,416,128]{2,1,0:T(8,128)(2,1)S(1)}, bf16[4,416,128]{2,1,0:T(8,128)(2,1)S(1)}, u32[]{:S(2)}, u32[]{:S(2)}) collective-permute-start(bf16[4,416,128]{2,1,0:T(8,128)(2,1)S(1)} %pad_maximum_fusion.1), channel_id=1, source_target_pairs={{0,2},{1,3},{2,0},{3,1},{4,6},{5,7},{6,4},{7,5},{8,10},{9,11},{10,... | collective-permute-start | bytes 1277960 | tf_op jit(solution)/shard_map/ppermute | solution.py:996
  22.6 10.6 %collective-permute-start.3 = (bf16[4,416,128]{2,1,0:T(8,128)(2,1)S(1)}, bf16[4,416,128]{2,1,0:T(8,128)(2,1)S(1)}, u32[]{:S(2)}, u32[]{:S(2)}) collective-permute-start(bf16[4,416,128]{2,1,0:T(8,128)(2,1)S(1)} %pad_maximum_fusion.1), channel_id=1, source_target_pairs={{0,4},{4,0},{8,12},{12,8},{16,20},{20,16},{24,28},{28,24},{1,5},{5... | collective-permute-start | bytes 1277960 | tf_op jit(solution)/shard_map/ppermute | solution.py:996
  33.4 8.3 %copy-start.27 = (bf16[12,416,128]{2,1,0:T(8,128)(2,1)}, bf16[12,416,128]{2,1,0:T(8,128)(2,1)S(1)}, u32[]{:S(2)}) copy-start(bf16[12,416,128]{2,1,0:T(8,128)(2,1)S(1)} %pad_maximum_fusion.refs_11_) | copy-start | bytes 3833860
  33.4 10.2 %collective-permute-start.7 = (bf16[12,416,128]{2,1,0:T(8,128)(2,1)S(1)}, bf16[12,416,128]{2,1,0:T(8,128)(2,1)}, u32[]{:S(2)}, u32[]{:S(2)}) collective-permute-start(bf16[12,416,128]{2,1,0:T(8,128)(2,1)S(1)} %pad_maximum_fusion.refs_11_), channel_id=1, source_target_pairs={{0,1},{1,0},{2,3},{3,2},{4,5},{5,4},{6,7},{7,6},{8,9},{9,8},{10,11... | collective-permute-start | bytes 3833864 | tf_op jit(solution)/shard_map/ppermute | solution.py:996
  33.5 8.2 %collective-permute-start.5 = (bf16[2,416,128]{2,1,0:T(8,128)(2,1)S(1)}, bf16[2,416,128]{2,1,0:T(8,128)(2,1)S(1)}, u32[]{:S(2)}, u32[]{:S(2)}) collective-permute-start(bf16[2,416,128]{2,1,0:T(8,128)(2,1)S(1)} %slice.144), channel_id=1, source_target_pairs={{0,2},{1,3},{2,0},{3,1},{4,6},{5,7},{6,4},{7,5},{8,10},{9,11},{10,... | collective-permute-start | bytes 638984 | tf_op jit(solution)/shard_map/ppermute | solution.py:996
  34.0 7.7 %collective-permute-start.6 = (bf16[2,416,128]{2,1,0:T(8,128)(2,1)S(1)}, bf16[2,416,128]{2,1,0:T(8,128)(2,1)S(1)}, u32[]{:S(2)}, u32[]{:S(2)}) collective-permute-start(bf16[2,416,128]{2,1,0:T(8,128)(2,1)S(1)} %slice.145), channel_id=1, source_target_pairs={{0,4},{4,0},{8,12},{12,8},{16,20},{20,16},{24,28},{28,24},{1,5},{5... | collective-permute-start | bytes 638984 | tf_op jit(solution)/shard_map/ppermute | solution.py:996
  41.8 1.8 %collective-permute-start.8 = (bf16[4,416,128]{2,1,0:T(8,128)(2,1)S(1)}, bf16[4,416,128]{2,1,0:T(8,128)(2,1)S(1)}, u32[]{:S(2)}, u32[]{:S(2)}) collective-permute-start(bf16[4,416,128]{2,1,0:T(8,128)(2,1)S(1)} %constant_dynamic-update-slice_fusion.refs_12_), channel_id=1, source_target_pairs={{0,1},{1,0},{2,3},{3,2},{4,5},{5,4},{6,7},{7,6},{8,9},{9,8},{10,11... | collective-permute-start | bytes 1277960 | tf_op jit(solution)/shard_map/ppermute | solution.py:996
  56.9 11.4 %collective-permute-start.9 = (bf16[2,8,392,128]{3,2,1,0:T(8,128)(2,1)}, bf16[2,8,392,128]{3,2,1,0:T(8,128)(2,1)}, u32[]{:S(2)}, u32[]{:S(2)}) collective-permute-start(bf16[2,8,392,128]{3,2,1,0:T(8,128)(2,1)} %get-tuple-element.238), channel_id=1, source_target_pairs={{0,1},{1,0},{2,3},{3,2},{4,5},{5,4},{6,7},{7,6},{8,9},{9,8},{10,11... | collective-permute-start | bytes 4816904 | tf_op jit(solution)/shard_map/ppermute | solution.py:996
  57.1 11.2 %copy-start.26 = (bf16[2,8,392,128]{3,2,1,0:T(8,128)(2,1)S(1)}, bf16[2,8,392,128]{3,2,1,0:T(8,128)(2,1)}, u32[]{:S(2)}) copy-start(bf16[2,8,392,128]{3,2,1,0:T(8,128)(2,1)} %get-tuple-element.242) | copy-start | bytes 4816900
  70.1 13.2 %collective-permute-start.10 = (bf16[2,392,128]{2,1,0:T(8,128)(2,1)S(1)}, bf16[2,392,128]{2,1,0:T(8,128)(2,1)S(1)}, u32[]{:S(2)}, u32[]{:S(2)}) collective-permute-start(bf16[2,392,128]{2,1,0:T(8,128)(2,1)S(1)} %get-tuple-element.251), channel_id=1, source_target_pairs={{0,4},{4,0},{8,12},{12,8},{16,20},{20,16},{24,28},{28,24},{1,5},{5... | collective-permute-start | bytes 602120 | tf_op jit(solution)/shard_map/ppermute | solution.py:996
  71.4 12.0 %collective-permute-start.11 = (bf16[2,392,128]{2,1,0:T(8,128)(2,1)S(1)}, bf16[2,392,128]{2,1,0:T(8,128)(2,1)S(1)}, u32[]{:S(2)}, u32[]{:S(2)}) collective-permute-start(bf16[2,392,128]{2,1,0:T(8,128)(2,1)S(1)} %get-tuple-element.252), channel_id=1, source_target_pairs={{0,2},{1,3},{2,0},{3,1},{4,6},{5,7},{6,4},{7,5},{8,10},{9,11},{10,... | collective-permute-start | bytes 602120 | tf_op jit(solution)/shard_map/ppermute | solution.py:996
  83.7 4.8 %collective-permute-start.12 = (bf16[80,640]{1,0:T(8,128)(2,1)S(1)}, bf16[80,640]{1,0:T(8,128)(2,1)S(1)}, u32[]{:S(2)}, u32[]{:S(2)}) collective-permute-start(bf16[80,640]{1,0:T(8,128)(2,1)S(1)} %get-tuple-element.263), channel_id=1, source_target_pairs={{0,1},{1,0},{2,3},{3,2},{4,5},{5,4},{6,7},{7,6},{8,9},{9,8},{10,11... | collective-permute-start | bytes 307208 | tf_op jit(solution)/shard_map/ppermute | solution.py:996
  83.8 17.2 %collective-permute-start.13 = (bf16[4,392,128]{2,1,0:T(8,128)(2,1)S(1)}, bf16[4,392,128]{2,1,0:T(8,128)(2,1)S(1)}, u32[]{:S(2)}, u32[]{:S(2)}) collective-permute-start(bf16[4,392,128]{2,1,0:T(8,128)(2,1)S(1)} %get-tuple-element.278), channel_id=1, source_target_pairs={{0,4},{4,0},{8,12},{12,8},{16,20},{20,16},{24,28},{28,24},{1,5},{5... | collective-permute-start | bytes 1204232 | tf_op jit(solution)/shard_map/ppermute | solution.py:996
  84.9 16.1 %collective-permute-start.14 = (bf16[4,392,128]{2,1,0:T(8,128)(2,1)S(1)}, bf16[4,392,128]{2,1,0:T(8,128)(2,1)S(1)}, u32[]{:S(2)}, u32[]{:S(2)}) collective-permute-start(bf16[4,392,128]{2,1,0:T(8,128)(2,1)S(1)} %get-tuple-element.279), channel_id=1, source_target_pairs={{0,2},{1,3},{2,0},{3,1},{4,6},{5,7},{6,4},{7,5},{8,10},{9,11},{10,... | collective-permute-start | bytes 1204232 | tf_op jit(solution)/shard_map/ppermute | solution.py:996
  88.5 12.5 %collective-permute-start.15 = (bf16[80,640]{1,0:T(8,128)(2,1)S(1)}, bf16[80,640]{1,0:T(8,128)(2,1)S(1)}, u32[]{:S(2)}, u32[]{:S(2)}) collective-permute-start(bf16[80,640]{1,0:T(8,128)(2,1)S(1)} %add_convert_fusion.6), channel_id=1, source_target_pairs={{0,16},{4,20},{8,24},{12,28},{16,0},{20,4},{24,8},{28,12},{1,17},{... | collective-permute-start | bytes 307208 | tf_op jit(solution)/shard_map/ppermute | solution.py:996
  101.2 9.9 %collective-permute-start.17 = (f32[16,640]{1,0:T(8,128)S(1)}, f32[16,640]{1,0:T(8,128)S(1)}, u32[]{:S(2)}, u32[]{:S(2)}) collective-permute-start(f32[16,640]{1,0:T(8,128)S(1)} %get-tuple-element.300), channel_id=1, source_target_pairs={{0,16},{4,20},{8,24},{12,28},{16,0},{20,4},{24,8},{28,12},{1,17},{... | collective-permute-start | bytes 122888 | tf_op jit(solution)/shard_map/ppermute | solution.py:996
  101.9 9.2 %collective-permute-start.16 = (bf16[80,640]{1,0:T(8,128)(2,1)S(1)}, bf16[80,640]{1,0:T(8,128)(2,1)S(1)}, u32[]{:S(2)}, u32[]{:S(2)}) collective-permute-start(bf16[80,640]{1,0:T(8,128)(2,1)S(1)} %add_convert_fusion.5), channel_id=1, source_target_pairs={{0,2},{1,3},{2,0},{3,1},{4,6},{5,7},{6,4},{7,5},{8,10},{9,11},{10,... | collective-permute-start | bytes 307208 | tf_op jit(solution)/shard_map/ppermute | solution.py:996
  103.4 17.1 %collective-permute-start.21 = (bf16[392,128]{1,0:T(8,128)(2,1)S(1)}, bf16[392,128]{1,0:T(8,128)(2,1)S(1)}, u32[]{:S(2)}, u32[]{:S(2)}) collective-permute-start(bf16[392,128]{1,0:T(8,128)(2,1)S(1)} %get-tuple-element.380), channel_id=1, source_target_pairs={{0,24},{4,28},{8,16},{12,20},{16,8},{20,12},{24,0},{28,4},{1,25},{... | collective-permute-start | bytes 301064 | tf_op jit(solution)/shard_map/ppermute | solution.py:996
  107.0 13.6 %collective-permute-start.20 = (bf16[392,128]{1,0:T(8,128)(2,1)S(1)}, bf16[392,128]{1,0:T(8,128)(2,1)S(1)}, u32[]{:S(2)}, u32[]{:S(2)}) collective-permute-start(bf16[392,128]{1,0:T(8,128)(2,1)S(1)} %get-tuple-element.381), channel_id=1, source_target_pairs={{0,16},{4,20},{8,24},{12,28},{16,0},{20,4},{24,8},{28,12},{1,17},{... | collective-permute-start | bytes 301064 | tf_op jit(solution)/shard_map/ppermute | solution.py:996
  107.0 13.6 %collective-permute-start.19 = (bf16[392,128]{1,0:T(8,128)(2,1)S(1)}, bf16[392,128]{1,0:T(8,128)(2,1)S(1)}, u32[]{:S(2)}, u32[]{:S(2)}) collective-permute-start(bf16[392,128]{1,0:T(8,128)(2,1)S(1)} %get-tuple-element.382), channel_id=1, source_target_pairs={{0,8},{4,12},{8,0},{12,4},{16,24},{20,28},{24,16},{28,20},{1,9},{5... | collective-permute-start | bytes 301064 | tf_op jit(solution)/shard_map/ppermute | solution.py:996
  111.2 5.2 %collective-permute-start.18 = (bf16[112,640]{1,0:T(8,128)(2,1)S(1)}, bf16[112,640]{1,0:T(8,128)(2,1)S(1)}, u32[]{:S(2)}, u32[]{:S(2)}) collective-permute-start(bf16[112,640]{1,0:T(8,128)(2,1)S(1)} %pad_maximum_fusion.5), channel_id=1, source_target_pairs={{0,4},{4,0},{8,12},{12,8},{16,20},{20,16},{24,28},{28,24},{1,5},{5... | collective-permute-start | bytes 430088 | tf_op jit(solution)/shard_map/ppermute | solution.py:996
  116.5 5.2 %collective-permute-start.22 = (bf16[112,640]{1,0:T(8,128)(2,1)S(1)}, bf16[112,640]{1,0:T(8,128)(2,1)S(1)}, u32[]{:S(2)}, u32[]{:S(2)}) collective-permute-start(bf16[112,640]{1,0:T(8,128)(2,1)S(1)} %pad_maximum_fusion.6), channel_id=1, source_target_pairs={{0,8},{4,12},{8,0},{12,4},{16,24},{20,28},{24,16},{28,20},{1,9},{5... | collective-permute-start | bytes 430088 | tf_op jit(solution)/shard_map/ppermute | solution.py:996
  121.9 1.5 %collective-permute-start.23 = (bf16[112,640]{1,0:T(8,128)(2,1)S(1)}, bf16[112,640]{1,0:T(8,128)(2,1)S(1)}, u32[]{:S(2)}, u32[]{:S(2)}) collective-permute-start(bf16[112,640]{1,0:T(8,128)(2,1)S(1)} %pad_maximum_fusion.7), channel_id=1, source_target_pairs={{0,1},{1,0},{2,3},{3,2},{4,5},{5,4},{6,7},{7,6},{8,9},{9,8},{10,11... | collective-permute-start | bytes 430088 | tf_op jit(solution)/shard_map/ppermute | solution.py:996
  123.5 5.8 %collective-permute-start.24 = (f32[16,640]{1,0:T(8,128)S(1)}, f32[16,640]{1,0:T(8,128)S(1)}, u32[]{:S(2)}, u32[]{:S(2)}) collective-permute-start(f32[16,640]{1,0:T(8,128)S(1)} %fusion.2), channel_id=1, source_target_pairs={{0,2},{1,3},{2,0},{3,1},{4,6},{5,7},{6,4},{7,5},{8,10},{9,11},{10,... | collective-permute-start | bytes 122888 | tf_op jit(solution)/shard_map/ppermute | solution.py:996
  (27 other events, 102.8 us)

commit v5 on v4

--- a/solution.py
+++ b/solution.py
@@ -451,9 +451,9 @@
     small_far_refs, (flat_far_ref, slope_far_ref, two_far_ref) = refs[2:8], refs[8:11]
     piece_refs = refs[11 : 11 + len(places)]
     (
-        d_three_far_ref, two_ref, keep_ref, send_ref, grad_heads_ref, sums_ref, sum_heads_ref,
-        blocks_ref, weight_ref, d_dense_ref, flat_ref, slope_ref, *small_refs,
-        sems, two_sems, flat_sems, slope_sems, small_sems,
+        d_three_far_ref, two_ref, keep_far_ref, send_far_ref, grad_heads_ref, sums_ref, sum_heads_ref,
+        blocks_ref, weight_ref, d_dense_ref, flat_ref, slope_ref, keep_ref, send_ref, *small_refs,
+        sems, two_sems, flat_sems, slope_sems, small_sems, out_sems,
     ) = refs[11 + len(places) :]
     heads_ref, bias_ref, actions_ref, adv_ref, values_ref, logp_ref = small_refs
     n = flat_ref.shape[-1]
@@ -493,7 +493,7 @@
     bias_heads = wide(bias_ref[:, 160 + hid : 160 + hid + 19], 19, n)
     wait_rows(flat_far_ref, flat_ref, flat_sems)
     flat = flat_ref[...].reshape(n_dp * rows, n)
-    pre = dot(weight_ref[...], flat, TN) + bias_dense
+    pre = dot(flat, weight_ref[...], TN).T + bias_dense
     hidden, slope = gelu_both(pre)
     hidden = hidden.astype(BF)
     head_weight = heads_ref[...].astype(BF)
@@ -510,7 +510,8 @@
     sums_ref[0:1, 128 : 128 + hid] = dot(ones, d_dense, NT)[0:1]
     for j in range(n_own):
         d_dense_ref[j] = d_dense[j * cols : (j + 1) * cols]
-    for half, ref in ((0, keep_ref), (1, send_ref)):
+    outs = []
+    for half, ref, far_ref in ((1, send_ref, send_far_ref), (0, keep_ref, keep_far_ref)):
         for k in range(n_own // 4):
             both = [d_dense_ref[own ^ (4 * k + half)], d_dense_ref[own ^ (4 * k + 2 + half)]]
             block = dot(flat, jnp.concatenate(both, axis=0), NT).astype(BF)
@@ -519,6 +520,9 @@
                 spot = (rel % 2) * (n_dp // 2) + rel // 2
                 for m in range(2):
                     ref[2 * k + m, spot] = block[i * rows : (i + 1) * rows, m * cols : (m + 1) * cols]
+            for m in range(2 * k, 2 * k + 2):
+                outs.append(pltpu.make_async_copy(ref.at[m], far_ref.at[m], out_sems.at[len(outs)]))
+                outs[-1].start()
     wait_rows(slope_far_ref, slope_ref, slope_sems)
     total = jnp.zeros((64, n), F32)
     for part in range(7):
@@ -533,6 +537,8 @@
     sums_ref[0:1, 64:128] = jnp.zeros((1, 64), F32)
     wait_rows(two_far_ref, two_ref, two_sems)
     wait_rows(slope_ref, d_three_far_ref, slope_sems)
+    for copy in outs:
+        copy.wait()
 
 
 def dense(
@@ -560,16 +566,18 @@
             jax.ShapeDtypeStruct((1, heads.shape[0]), F32),
         ],
         in_specs=[smem(), smem()] + [anywhere()] * (9 + len(arrays)),
-        out_specs=[anywhere()] + [vmem()] * 6,
+        out_specs=[anywhere(), vmem(), anywhere(), anywhere()] + [vmem()] * 3,
         scratch=[
             pltpu.VMEM((n_dp, n_own) + arrays[0].shape[1:], BF),
             pltpu.VMEM((n_dp * rows, hid), BF),
             pltpu.VMEM((n_own, 128, n), BF),
             pltpu.VMEM(flat.shape, BF),
             pltpu.VMEM(flat.shape, BF),
+            pltpu.VMEM((n_own // 2, n_dp, rows, 128), BF),
+            pltpu.VMEM((n_own // 2, n_dp, rows, 128), BF),
         ]
         + [pltpu.VMEM(a.shape, a.dtype) for a in small]
-        + [dma(n_dp * n_own), dma(9), dma(7), dma(7), dma(6)],
+        + [dma(n_dp * n_own), dma(9), dma(7), dma(7), dma(6), dma(n_own)],
         us=10,
         name="dense",
         limit=32,
@@ -602,12 +610,18 @@
         band_ref[...] = band_back(weight_ref[...], 3, 64, 3)
         acc_ref[...] = jnp.zeros_like(acc_ref)
         tot_ref[...] = jnp.zeros_like(tot_ref)
-        for r in range(7):
-            three_row(r).wait()
+
+    @pl.when(step < 7)
+    def _():
+        three_row(step).wait()
+
+    row_copy(slope_far_ref, slope_ref, slope_sems, step).wait()
+
+    @pl.when(step == 1)
+    def _():
         start_rows(one_far_ref, one_ref, one_sems)
         start_rows(slope_one_far_ref, slope_one_ref, slope_one_sems)
 
-    row_copy(slope_far_ref, slope_ref, slope_sems, step).wait()
     total = tot_ref[...]
     for part in range(3):
         patch = jnp.concatenate(
@@ -689,11 +703,17 @@
     @pl.when(step == 0)
     def _():
         band_ref[...] = band_back(weight_ref[...], 2, 128, 1)
-        pad_ref[...] = jnp.zeros_like(pad_ref)
+        pad_ref[0] = jnp.zeros((704, n), BF)
+        pad_ref[10] = jnp.zeros((704, n), BF)
+        for r in range(1, 10):
+            pad_ref[r, 0:64, :] = jnp.zeros((64, n), BF)
+            pad_ref[r, 640:704, :] = jnp.zeros((64, n), BF)
         acc_ref[...] = jnp.zeros_like(acc_ref)
         tot_ref[...] = jnp.zeros_like(tot_ref)
-        for r in range(9):
-            pad_ref[r + 1, 64 : 64 + 576, :] = d_two_ref[r]
+
+    @pl.when(step < 9)
+    def _():
+        pad_ref[step + 1, 64 : 64 + 576, :] = d_two_ref[step]
 
     total = tot_ref[...]
     for col in range(10):
@@ -819,19 +839,21 @@
         frames_ref = refs[2]
         out_ref, d_out_ref, cells_ref, band_ref, rows_ref, sems, cell_sems = refs[-7:]
     else:
-        out_ref, d_out_ref, band_ref, rows_ref, sems = refs[-5:]
+        band_ref = weight_ref
+        out_ref, d_out_ref, rows_ref, sems = refs[-4:]
     n = rows_ref.shape[-1]
     step = pl.program_id(0)
     row = step + begin
     cells = d_one_ref.shape[1]
     zero = jnp.zeros((32, n), BF)
 
-    @pl.when(step == 0)
-    def _():
-        if ahead:
+    if ahead:
+
+        @pl.when(step == 0)
+        def _():
             for r in range(5):
                 ring_copy(frames_ref, cells_ref, cell_sems, r).start()
-        band_ref[...] = band_back(weight_ref[...], 2, 64, 3)
+            band_ref[...] = band_back(weight_ref[...], 2, 64, 3)
 
     def slab(at, dy, first, alive):
         parts = []
@@ -881,19 +903,14 @@
     ahead = frames is not None
     more = [far(frames)] if ahead else [] if so_far is None else [so_far]
     count = end - begin
-    cells = [near((RING,) + shape[1:], BF)] if ahead else []
+    cells = [near((RING,) + shape[1:], BF), jax.ShapeDtypeStruct((192, 256), BF)] if ahead else []
     return call(
         functools.partial(frames_back_kernel, begin=begin, end=end, total=total, ahead=ahead),
         [held(d_one), weight] + more,
         [pltpu.HBM(shape, BF), near(d_one.shape, BF)] + cells,
         in_specs=[vmem(), vmem()] + [anywhere()] * len(more),
         out_specs=[anywhere(), vmem()] + [vmem()] * len(cells),
-        scratch=[
-            pltpu.VMEM((192, 256), BF),
-            pltpu.VMEM((2 * count,) + shape[1:], BF),
-            dma(2 * count),
-        ]
-        + [dma(5)] * len(cells),
+        scratch=[pltpu.VMEM((2 * count,) + shape[1:], BF), dma(2 * count)] + [dma(5)] * ahead,
         grid=count,
         us=count,
         name="frames_back",
@@ -925,11 +942,18 @@
     return both[:rows] + (both[rows:] + dot(a_top, b_low, dims))
 
 
+def dot2(a, b, dims=NN):
+    rows = a.shape[0]
+    both = dot(jnp.concatenate(split(a), axis=0), b, dims)
+    return both[:rows] + both[rows:]
+
+
 def turned_step(weight, grad, mean, square, left, right):
     rate = RATE / math.sqrt(weight.shape[1])
-    turned = dot3(dot3(right, grad, TN), left)
+    left = left.astype(BF)
+    turned = dot2(dot3(right, grad, TN), left)
     momentum, variance, direction = adam_terms(turned, mean, square)
-    back = dot3(dot3(right, direction), left, NT)
+    back = dot2(dot3(right, direction), left, NT)
     return momentum, variance, weight - rate * back
 
 
@@ -1121,7 +1145,7 @@
         by_x, by_y = dp_swap(side_x, 1), own_swap(side_y, 2)
     came = own_swap(gone, 1)
     cuts = (0, 2, 5, 8, grid // 2 + 1)
-    back, d_one, ring = frames_back(d_one, conv_first.T, shape, cuts[0], cuts[1], frames=cells)
+    back, d_one, ring, band = frames_back(d_one, conv_first.T, shape, cuts[0], cuts[1], frames=cells)
     back, d_one, ring, half, came = fence(back, d_one, ring, half, came)
     half = add_low(half, came)
     back, d_one, ring, half = fence(back, d_one, ring, half)
@@ -1141,7 +1165,7 @@
         parts = [block[0]] + [dp_swap(block[k], 2 * k) for k in (1, 2, 3)]
     else:
         parts = plain_scatter(keep, send, n_dp, n_own)
-    back, d_one = frames_back(d_one, conv_first.T, shape, cuts[1], cuts[2], back)
+    back, d_one = frames_back(d_one, band, shape, cuts[1], cuts[2], back)
     back, d_one, half, came, pack_one, came_one = fence(back, d_one, half, came, pack_one, came_one)
 
     def join(pack, pack_one):
@@ -1160,12 +1184,12 @@
     back, d_one, both = fence(back, d_one, both)
     more = [1] + far_bits[1:]
     came = dp_swap(both, more[0])
-    back, d_one = frames_back(d_one, conv_first.T, shape, cuts[2], cuts[3], back)
+    back, d_one = frames_back(d_one, band, shape, cuts[2], cuts[3], back)
     back, d_one, both, came = fence(back, d_one, both, came)
     both = join(*add_up(both, came))
     back, d_one, both = fence(back, d_one, both)
     came = dp_swap(both, more[1])
-    back, d_one = frames_back(d_one, conv_first.T, shape, cuts[3], cuts[4], back)
+    back, d_one = frames_back(d_one, band, shape, cuts[3], cuts[4], back)
     for bit in more[2:]:
         both = join(*add_up(both, came))
         came = dp_swap(both, bit)

time: 132 us -> 126 us (0.955)
  Pallas kernels: 90.1 us -> 84.4 us
    pallas_call x10, Pallas kernels: 70.8 us -> 66.2 us  [call(): pl.pallas_call(body, out_shape=tuple(outs), in_specs=list(in_specs or [vm...]
where the time goes in v5:
time: 126 us
  Pallas kernels  84.4 us (67%)
  starting transfers between devices  29.1 us (23%)
  waiting for transfers between devices  5.8 us (5%)
  other arithmetic  3.45 us (3%)
  between operations  2.24 us (2%)
  local copies, waits for them, and re-layouts  1.28 us (1%)
    pallas_call x10, Pallas kernels, call(): pl.pallas_call(body, out_shape=tuple(outs), in_specs=list(in_specs or [vm...  66.2 us
    ppermute x25, starting transfers between devices, swap(): return lax.ppermute(x, axis, [(i, i ^ bit) for i in range(size)])  29.1 us
    pallas_call x1, Pallas kernels, conv_one_grad(): pl.pallas_call(conv_one_grad_kernel, out_shape=(jax.ShapeDtypeStruct((16,...  9.87 us
    ppermute x25, waiting for transfers between devices, swap(): return lax.ppermute(x, axis, [(i, i ^ bit) for i in range(size)])  5.8 us
    pallas_call x2, Pallas kernels, steps(): pl.pallas_call(functools.partial(steps_kernel, spots=spots), out_shape=tu...  4.32 us
    pallas_call x1, Pallas kernels, first(): pl.pallas_call(first_kernel, out_shape=(jax.ShapeDtypeStruct((1, n), F32)...  2.64 us
  transfers between devices with their start and end apart: 25, of which 5 were waited for; matrix products, arithmetic and copies ran while one was open for 0% of the time, Pallas kernels for 56%

profile of v5, /device:TPU:0, one launch (start us, length us, event | category | flops | bytes accessed | tf_op | source)
XLA Modules:
  0.0 126.3 jit_solution(10094168909688250030)
XLA Ops:
  1.3 2.6 %first.1 = (f32[1,256]{1,0:T(1,128)S(1)}, bf16[416,128]{1,0:T(8,128)(2,1)S(1)}, bf16[8,1344,256]{2,1,0:T(8,128)(2,1)S(1)}) custom-call(s32[1]{0:T(128)S(6)} %copy.80.lengths_ref.refs_1_, s32[1,256]{1,0:T(1,128)} %dones_far_ref.1, f32[1,256]{1,0:T(1,128)} %rewards_far_ref.1, f32[1,256]{1,0:T(1,128)} %refs_6_.1, f32[392,128]{1,0:T(8,128)} %refs_0_.1, ...), custom_call_target="tpu_custom_call" | custom-call | flops 3000000000 | tf_op jit(solution)/shard_map/first/pallas_call | solution.py:233
  4.0 5.1 %collective-permute-start.2 = (bf16[416,128]{1,0:T(8,128)(2,1)S(1)}, bf16[416,128]{1,0:T(8,128)(2,1)S(1)}, u32[]{:S(2)}, u32[]{:S(2)}) collective-permute-start(bf16[416,128]{1,0:T(8,128)(2,1)S(1)} %get-tuple-element.204), channel_id=1, source_target_pairs={{0,24},{4,28},{8,16},{12,20},{16,8},{20,12},{24,0},{28,4},{1,25},{... | collective-permute-start | bytes 319496 | tf_op jit(solution)/shard_map/ppermute | solution.py:1020
  9.8 11.0 %conv_one.1 = (bf16[10,10,128,256]{3,2,1,0:T(8,128)(2,1)S(1)}, bf16[10,10,128,256]{3,2,1,0:T(8,128)(2,1)S(1)}, bf16[8,1344,256]{2,1,0:T(8,128)(2,1)S(1)}) custom-call(bf16[21,1344,256]{2,1,0:T(8,128)(2,1)} %bitcast.102, f32[32,256]{1,0:T(8,128)S(1)} %bitcast.81, f32[1,691]{1,0:T(1,128)S(1)} %reshape.64.bias_ref.refs_3_, ...), custom_call_target="tpu_custom_call", output_to_operand_aliasing={{2}: (3, {})} | custom-call | flops 12000000000 | tf_op jit(solution)/shard_map/conv_one/pallas_call | solution.py:85
  20.9 1.7 %collective-permute-start.4 = (bf16[4,416,128]{2,1,0:T(8,128)(2,1)S(1)}, bf16[4,416,128]{2,1,0:T(8,128)(2,1)S(1)}, u32[]{:S(2)}, u32[]{:S(2)}) collective-permute-start(bf16[4,416,128]{2,1,0:T(8,128)(2,1)S(1)} %pad_maximum_fusion.1), channel_id=1, source_target_pairs={{0,2},{1,3},{2,0},{3,1},{4,6},{5,7},{6,4},{7,5},{8,10},{9,11},{10,... | collective-permute-start | bytes 1277960 | tf_op jit(solution)/shard_map/ppermute | solution.py:1020
  22.6 1.5 %collective-permute-start.3 = (bf16[4,416,128]{2,1,0:T(8,128)(2,1)S(1)}, bf16[4,416,128]{2,1,0:T(8,128)(2,1)S(1)}, u32[]{:S(2)}, u32[]{:S(2)}) collective-permute-start(bf16[4,416,128]{2,1,0:T(8,128)(2,1)S(1)} %pad_maximum_fusion.1), channel_id=1, source_target_pairs={{0,4},{4,0},{8,12},{12,8},{16,20},{20,16},{24,28},{28,24},{1,5},{5... | collective-permute-start | bytes 1277960 | tf_op jit(solution)/shard_map/ppermute | solution.py:1020
  24.1 7.3 %conv_two.1 = (bf16[9,576,256]{2,1,0:T(8,128)(2,1)S(1)}, bf16[9,576,256]{2,1,0:T(8,128)(2,1)S(1)}, bf16[10,10,128,256]{3,2,1,0:T(8,128)(2,1)}, bf16[10,10,128,256]{3,2,1,0:T(8,128)(2,1)}) custom-call(bf16[10,10,128,256]{3,2,1,0:T(8,128)(2,1)S(1)} %get-tuple-element.208.one_ref, bf16[10,10,128,256]{3,2,1,0:T(8,128)(2,1)S(1)} %get-tuple-element.209.slope_one_ref, ...), custom_call_target="tpu_custom_call" | custom-call | flops 7000000000 | tf_op jit(solution)/shard_map/conv_two/pallas_call | solution.py:85
  31.9 1.2 collective-permute-done.3
  34.0 1.5 %collective-permute-start.6 = (bf16[2,416,128]{2,1,0:T(8,128)(2,1)S(1)}, bf16[2,416,128]{2,1,0:T(8,128)(2,1)S(1)}, u32[]{:S(2)}, u32[]{:S(2)}) collective-permute-start(bf16[2,416,128]{2,1,0:T(8,128)(2,1)S(1)} %slice.145), channel_id=1, source_target_pairs={{0,4},{4,0},{8,12},{12,8},{16,20},{20,16},{24,28},{28,24},{1,5},{5... | collective-permute-start | bytes 638984 | tf_op jit(solution)/shard_map/ppermute | solution.py:1020
  35.5 6.1 %conv_three.1 = (bf16[7,448,256]{2,1,0:T(8,128)(2,1)}, bf16[7,448,256]{2,1,0:T(8,128)(2,1)}, bf16[9,576,256]{2,1,0:T(8,128)(2,1)}, bf16[9,576,256]{2,1,0:T(8,128)(2,1)}) custom-call(bf16[9,576,256]{2,1,0:T(8,128)(2,1)S(1)} %get-tuple-element.218.two_ref, bf16[9,576,256]{2,1,0:T(8,128)(2,1)S(1)} %get-tuple-element.219.slope_two_ref, f32[64,576]{1,0:T(8,128)S(1)} %bitcast.84, ...), custom_call_target="tpu_custom_call" | custom-call | flops 6000000000 | tf_op jit(solution)/shard_map/conv_three/pallas_call | solution.py:85
  41.9 1.7 %collective-permute-done.8.refs_14_ = bf16[4,416,128]{2,1,0:T(8,128)(2,1)S(1)} collective-permute-done((bf16[4,416,128]{2,1,0:T(8,128)(2,1)S(1)}, bf16[4,416,128]{2,1,0:T(8,128)(2,1)S(1)}, u32[]{:S(2)}, u32[]{:S(2)}) %collective-permute-start.8) | collective-permute-done | bytes 426016 | tf_op jit(solution)/shard_map/ppermute | solution.py:1020
  44.3 9.6 %dense.1 = (bf16[7,448,256]{2,1,0:T(8,128)(2,1)}, bf16[9,576,256]{2,1,0:T(8,128)(2,1)S(1)}, bf16[2,8,392,128]{3,2,1,0:T(8,128)(2,1)}, bf16[2,8,392,128]{3,2,1,0:...) custom-call(s32[2]{0:T(128)S(1)} %pad_add_fusion.refs_0_, ...), custom_call_target="tpu_custom_call" | custom-call | flops 10000000000 | tf_op jit(solution)/shard_map/dense/pallas_call | solution.py:85
  54.1 10.2 %conv_three_back.1 = (bf16[9,576,256]{2,1,0:T(8,128)(2,1)S(1)}, bf16[10,10,128,256]{3,2,1,0:T(8,128)(2,1)S(1)}, bf16[10,10,128,256]{3,2,1,0:T(8,128)(2,1)S(1)}, bf16[96,640]{1,0:T(8,128)(2,1)S(1)}, f32[1,64]{1,0:T(1,128)S(1)}) custom-call(bf16[9,576,256]{2,1,0:T(8,128)(2,1)S(1)} %get-tuple-element.229.act_ref, ...), custom_call_target="tpu_custom_call" | custom-call | flops 8999999488 | tf_op jit(solution)/shard_map/conv_three_back/pallas_call | solution.py:85
  64.3 1.8 %add_convert_fusion = bf16[2,8,392,128]{3,2,1,0:T(8,128)(2,1)S(1)} fusion(bf16[2,8,392,128]{3,2,1,0:T(8,128)(2,1)} %collective-permute-done.9, bf16[2,8,392,128]{3,2,1,0:T(8,128)(2,1)S(1)} %copy-done.26), kind=kLoop, calls=%fused_computation | loop fusion | flops 3211264 | bytes 4816896 | tf_op jit(solution)/shard_map/convert_element_type | solution.py:1036
  66.2 1.2 collective-permute-start.10
  67.4 1.5 %collective-permute-start.11 = (bf16[2,392,128]{2,1,0:T(8,128)(2,1)S(1)}, bf16[2,392,128]{2,1,0:T(8,128)(2,1)S(1)}, u32[]{:S(2)}, u32[]{:S(2)}) collective-permute-start(bf16[2,392,128]{2,1,0:T(8,128)(2,1)S(1)} %get-tuple-element.253), channel_id=1, source_target_pairs={{0,2},{1,3},{2,0},{3,1},{4,6},{5,7},{6,4},{7,5},{8,10},{9,11},{10,... | collective-permute-start | bytes 602120 | tf_op jit(solution)/shard_map/ppermute | solution.py:1020
  68.9 10.5 %conv_two_back.1 = (bf16[10,10,128,256]{3,2,1,0:T(8,128)(2,1)S(1)}, bf16[160,640]{1,0:T(8,128)(2,1)S(1)}, f32[1,32]{1,0:T(1,128)S(1)}) custom-call(bf16[9,576,256]{2,1,0:T(8,128)(2,1)S(1)} %get-tuple-element.245.d_two_ref, bf16[10,10,128,256]{3,2,1,0:T(8,128)(2,1)S(1)} %get-tuple-element.246.act_ref, ...), custom_call_target="tpu_custom_call" | custom-call | flops 11000000512 | tf_op jit(solution)/shard_map/conv_two_back/pallas_call | solution.py:85
  81.4 3.0 %frames_back.4 = (bf16[21,1344,256]{2,1,0:T(8,128)(2,1)}, bf16[10,10,128,256]{3,2,1,0:T(8,128)(2,1)S(1)}, bf16[8,1344,256]{2,1,0:T(8,128)(2,1)S(1)}, bf16[192,256]{1,0:T(8,128)(2,1)S(1)}) custom-call(bf16[10,10,128,256]{3,2,1,0:T(8,128)(2,1)S(1)} %get-tuple-element.259.refs_0_, f32[32,256]{1,0:T(8,128)S(1)} %bitcast.82, ...), custom_call_target="tpu_custom_call", output_to_operand_aliasing={{1}: (0, {})} | custom-call | flops 2000000000 | tf_op jit(solution)/shard_map/frames_back/pallas_call | solution.py:85
  84.5 2.4 %collective-permute-start.15 = (bf16[80,640]{1,0:T(8,128)(2,1)S(1)}, bf16[80,640]{1,0:T(8,128)(2,1)S(1)}, u32[]{:S(2)}, u32[]{:S(2)}) collective-permute-start(bf16[80,640]{1,0:T(8,128)(2,1)S(1)} %add_convert_fusion.6), channel_id=1, source_target_pairs={{0,16},{4,20},{8,24},{12,28},{16,0},{20,4},{24,8},{28,12},{1,17},{... | collective-permute-start | bytes 307208 | tf_op jit(solution)/shard_map/ppermute | solution.py:1020
  86.8 9.9 %conv_one_grad.1 = (f32[16,640]{1,0:T(8,128)S(1)}, bf16[10,10,128,256]{3,2,1,0:T(8,128)(2,1)S(1)}, bf16[8,1344,256]{2,1,0:T(8,128)(2,1)S(1)}) custom-call(bf16[21,1344,256]{2,1,0:T(8,128)(2,1)} %bitcast.104, bf16[10,10,128,256]{3,2,1,0:T(8,128)(2,1)S(1)} %get-tuple-element.270.d_one_ref, ...), custom_call_target="tpu_custom_call", output_to_operand_aliasing={{1}: (1, {}), {2}: (2, {})} | custom-call | flops 10000000000 | tf_op jit(solution)/shard_map/conv_one_grad/pallas_call | solution.py:818
  97.6 1.5 %collective-permute-start.16 = (bf16[80,640]{1,0:T(8,128)(2,1)S(1)}, bf16[80,640]{1,0:T(8,128)(2,1)S(1)}, u32[]{:S(2)}, u32[]{:S(2)}) collective-permute-start(bf16[80,640]{1,0:T(8,128)(2,1)S(1)} %add_convert_fusion.5), channel_id=1, source_target_pairs={{0,2},{1,3},{2,0},{3,1},{4,6},{5,7},{6,4},{7,5},{8,10},{9,11},{10,... | collective-permute-start | bytes 307208 | tf_op jit(solution)/shard_map/ppermute | solution.py:1020
  99.2 3.5 %collective-permute-start.21 = (bf16[392,128]{1,0:T(8,128)(2,1)S(1)}, bf16[392,128]{1,0:T(8,128)(2,1)S(1)}, u32[]{:S(2)}, u32[]{:S(2)}) collective-permute-start(bf16[392,128]{1,0:T(8,128)(2,1)S(1)} %get-tuple-element.382), channel_id=1, source_target_pairs={{0,24},{4,28},{8,16},{12,20},{16,8},{20,12},{24,0},{28,4},{1,25},{... | collective-permute-start | bytes 301064 | tf_op jit(solution)/shard_map/ppermute | solution.py:1020
  103.6 3.0 %frames_back.5 = (bf16[21,1344,256]{2,1,0:T(8,128)(2,1)}, bf16[10,10,128,256]{3,2,1,0:T(8,128)(2,1)S(1)}) custom-call(bf16[10,10,128,256]{3,2,1,0:T(8,128)(2,1)S(1)} %get-tuple-element.291.refs_0_, bf16[192,256]{1,0:T(8,128)(2,1)S(1)} %get-tuple-element.292.refs_1_, ...), custom_call_target="tpu_custom_call", output_to_operand_aliasing={{1}: (0, {}), {0}: (2, {})} | custom-call | flops 3000000000 | tf_op jit(solution)/shard_map/frames_back/pallas_call | solution.py:85
  106.7 1.2 collective-permute-start.18
  107.9 3.0 %frames_back.6 = (bf16[21,1344,256]{2,1,0:T(8,128)(2,1)}, bf16[10,10,128,256]{3,2,1,0:T(8,128)(2,1)S(1)}) custom-call(bf16[10,10,128,256]{3,2,1,0:T(8,128)(2,1)S(1)} %get-tuple-element.304.refs_0_, bf16[192,256]{1,0:T(8,128)(2,1)S(1)} %get-tuple-element.292.refs_1_, ...), custom_call_target="tpu_custom_call", output_to_operand_aliasing={{1}: (0, {}), {0}: (2, {})} | custom-call | flops 3000000000 | tf_op jit(solution)/shard_map/frames_back/pallas_call | solution.py:85
  110.9 1.0 collective-permute-done.18
  112.0 1.2 collective-permute-start.22
  113.2 2.6 %frames_back.7 = (bf16[21,1344,256]{2,1,0:T(8,128)(2,1)}, bf16[10,10,128,256]{3,2,1,0:T(8,128)(2,1)S(1)}) custom-call(bf16[10,10,128,256]{3,2,1,0:T(8,128)(2,1)S(1)} %get-tuple-element.313.refs_0_, bf16[192,256]{1,0:T(8,128)(2,1)S(1)} %get-tuple-element.292.refs_1_, ...), custom_call_target="tpu_custom_call", output_to_operand_aliasing={{1}: (0, {}), {0}: (2, {})} | custom-call | flops 3000000000 | tf_op jit(solution)/shard_map/frames_back/pallas_call | solution.py:85
  115.8 1.3 %collective-permute-done.22 = bf16[112,640]{1,0:T(8,128)(2,1)S(1)} collective-permute-done((bf16[112,640]{1,0:T(8,128)(2,1)S(1)}, bf16[112,640]{1,0:T(8,128)(2,1)S(1)}, u32[]{:S(2)}, u32[]{:S(2)}) %collective-permute-start.22) | collective-permute-done | bytes 143392 | tf_op jit(solution)/shard_map/ppermute | solution.py:1020
  117.6 1.4 %dense_step.1 = (f32[392,128]{1,0:T(8,128)}, f32[392,128]{1,0:T(8,128)}, f32[392,128]{1,0:T(8,128)}, f32[392,128]{1,0:T(8,128)}) custom-call(f32[392,128]{1,0:T(8,128)S(1)} %copy-done, f32[392,128]{1,0:T(8,128)S(1)} %copy-done.7, f32[392,128]{1,0:T(8,128)S(1)} %copy-done.8, f32[1,128,128]{2,1,0:T(8,128)S(1)} %copy-done.15, ...), custom_call_target="tpu_custom_call" | custom-call | flops 3000000000 | tf_op jit(solution)/shard_map/dense_step/pallas_call | solution.py:1008
  119.0 1.9 %collective-permute-start.24 = (f32[16,640]{1,0:T(8,128)S(1)}, f32[16,640]{1,0:T(8,128)S(1)}, u32[]{:S(2)}, u32[]{:S(2)}) collective-permute-start(f32[16,640]{1,0:T(8,128)S(1)} %fusion.2), channel_id=1, source_target_pairs={{0,2},{1,3},{2,0},{3,1},{4,6},{5,7},{6,4},{7,5},{8,10},{9,11},{10,... | collective-permute-start | bytes 122888 | tf_op jit(solution)/shard_map/ppermute | solution.py:1020
  121.2 3.1 %steps.2 = (f32[64,576]{1,0:T(8,128)}, f32[64,576]{1,0:T(8,128)}, f32[64,576]{1,0:T(8,128)}, f32[64,576]{1,0:T(8,128)}, f32[19,512]{1,0:T(8,128)}, /*index=5*/f3...) custom-call(bf16[160,640]{1,0:T(8,128)(2,1)S(1)} %pad_maximum_fusion, ...), custom_call_target="tpu_custom_call" | custom-call | flops 5000000000 | tf_op jit(solution)/shard_map/steps/pallas_call | solution.py:980
  125.1 1.2 steps.3
  (145 shorter events, 8.2 us)
Async XLA Ops:
  1.3 8.4 %copy-start.29 = (f32[691]{0:T(1024)S(1)}, f32[691]{0:T(1024)}, u32[]{:S(2)}) copy-start(f32[691]{0:T(1024)} %param.46) | copy-start | bytes 8296
  1.3 8.4 %copy-start.1 = (f32[256,32]{0,1:T(8,128)S(1)}, f32[256,32]{0,1:T(8,128)}, u32[]{:S(2)}) copy-start(f32[256,32]{0,1:T(8,128)} %param.41) | copy-start | bytes 98308
  4.0 16.8 %copy-start.25 = (f32[1,256]{1,0:T(1,128)}, f32[1,256]{1,0:T(1,128)S(1)}, u32[]{:S(2)}) copy-start(f32[1,256]{1,0:T(1,128)S(1)} %get-tuple-element.197.refs_5_) | copy-start | bytes 3076
  4.0 16.8 %collective-permute-start.2 = (bf16[416,128]{1,0:T(8,128)(2,1)S(1)}, bf16[416,128]{1,0:T(8,128)(2,1)S(1)}, u32[]{:S(2)}, u32[]{:S(2)}) collective-permute-start(bf16[416,128]{1,0:T(8,128)(2,1)S(1)} %get-tuple-element.204), channel_id=1, source_target_pairs={{0,24},{4,28},{8,16},{12,20},{16,8},{20,12},{24,0},{28,4},{1,25},{... | collective-permute-start | bytes 319496 | tf_op jit(solution)/shard_map/ppermute | solution.py:1020
  9.1 11.7 %collective-permute-start.1 = (bf16[416,128]{1,0:T(8,128)(2,1)S(1)}, bf16[416,128]{1,0:T(8,128)(2,1)S(1)}, u32[]{:S(2)}, u32[]{:S(2)}) collective-permute-start(bf16[416,128]{1,0:T(8,128)(2,1)S(1)} %get-tuple-element.204), channel_id=1, source_target_pairs={{0,16},{4,20},{8,24},{12,28},{16,0},{20,4},{24,8},{28,12},{1,17},{... | collective-permute-start | bytes 319496 | tf_op jit(solution)/shard_map/ppermute | solution.py:1020
  9.1 11.7 %collective-permute-start = (bf16[416,128]{1,0:T(8,128)(2,1)S(1)}, bf16[416,128]{1,0:T(8,128)(2,1)S(1)}, u32[]{:S(2)}, u32[]{:S(2)}) collective-permute-start(bf16[416,128]{1,0:T(8,128)(2,1)S(1)} %get-tuple-element.204), channel_id=1, source_target_pairs={{0,8},{4,12},{8,0},{12,4},{16,24},{20,28},{24,16},{28,20},{1,9},{5... | collective-permute-start | bytes 319496 | tf_op jit(solution)/shard_map/ppermute | solution.py:1020
  9.8 25.8 %copy-start.2 = (f32[1,691]{1,0:T(1,128)}, f32[1,691]{1,0:T(1,128)S(1)}, u32[]{:S(2)}) copy-start(f32[1,691]{1,0:T(1,128)S(1)} %reshape.64.bias_ref.refs_3_) | copy-start | bytes 8296
  9.8 14.3 %copy-start.12 = (f32[512,64]{0,1:T(8,128)S(1)}, f32[512,64]{0,1:T(8,128)}, u32[]{:S(2)}) copy-start(f32[512,64]{0,1:T(8,128)} %param.42) | copy-start | bytes 393220
  20.9 11.1 %collective-permute-start.4 = (bf16[4,416,128]{2,1,0:T(8,128)(2,1)S(1)}, bf16[4,416,128]{2,1,0:T(8,128)(2,1)S(1)}, u32[]{:S(2)}, u32[]{:S(2)}) collective-permute-start(bf16[4,416,128]{2,1,0:T(8,128)(2,1)S(1)} %pad_maximum_fusion.1), channel_id=1, source_target_pairs={{0,2},{1,3},{2,0},{3,1},{4,6},{5,7},{6,4},{7,5},{8,10},{9,11},{10,... | collective-permute-start | bytes 1277960 | tf_op jit(solution)/shard_map/ppermute | solution.py:1020
  22.6 10.6 %collective-permute-start.3 = (bf16[4,416,128]{2,1,0:T(8,128)(2,1)S(1)}, bf16[4,416,128]{2,1,0:T(8,128)(2,1)S(1)}, u32[]{:S(2)}, u32[]{:S(2)}) collective-permute-start(bf16[4,416,128]{2,1,0:T(8,128)(2,1)S(1)} %pad_maximum_fusion.1), channel_id=1, source_target_pairs={{0,4},{4,0},{8,12},{12,8},{16,20},{20,16},{24,28},{28,24},{1,5},{5... | collective-permute-start | bytes 1277960 | tf_op jit(solution)/shard_map/ppermute | solution.py:1020
  33.4 8.3 %copy-start.27 = (bf16[12,416,128]{2,1,0:T(8,128)(2,1)}, bf16[12,416,128]{2,1,0:T(8,128)(2,1)S(1)}, u32[]{:S(2)}) copy-start(bf16[12,416,128]{2,1,0:T(8,128)(2,1)S(1)} %pad_maximum_fusion.refs_11_) | copy-start | bytes 3833860
  33.4 10.2 %collective-permute-start.7 = (bf16[12,416,128]{2,1,0:T(8,128)(2,1)S(1)}, bf16[12,416,128]{2,1,0:T(8,128)(2,1)}, u32[]{:S(2)}, u32[]{:S(2)}) collective-permute-start(bf16[12,416,128]{2,1,0:T(8,128)(2,1)S(1)} %pad_maximum_fusion.refs_11_), channel_id=1, source_target_pairs={{0,1},{1,0},{2,3},{3,2},{4,5},{5,4},{6,7},{7,6},{8,9},{9,8},{10,11... | collective-permute-start | bytes 3833864 | tf_op jit(solution)/shard_map/ppermute | solution.py:1020
  33.5 8.2 %collective-permute-start.5 = (bf16[2,416,128]{2,1,0:T(8,128)(2,1)S(1)}, bf16[2,416,128]{2,1,0:T(8,128)(2,1)S(1)}, u32[]{:S(2)}, u32[]{:S(2)}) collective-permute-start(bf16[2,416,128]{2,1,0:T(8,128)(2,1)S(1)} %slice.144), channel_id=1, source_target_pairs={{0,2},{1,3},{2,0},{3,1},{4,6},{5,7},{6,4},{7,5},{8,10},{9,11},{10,... | collective-permute-start | bytes 638984 | tf_op jit(solution)/shard_map/ppermute | solution.py:1020
  34.0 7.7 %collective-permute-start.6 = (bf16[2,416,128]{2,1,0:T(8,128)(2,1)S(1)}, bf16[2,416,128]{2,1,0:T(8,128)(2,1)S(1)}, u32[]{:S(2)}, u32[]{:S(2)}) collective-permute-start(bf16[2,416,128]{2,1,0:T(8,128)(2,1)S(1)} %slice.145), channel_id=1, source_target_pairs={{0,4},{4,0},{8,12},{12,8},{16,20},{20,16},{24,28},{28,24},{1,5},{5... | collective-permute-start | bytes 638984 | tf_op jit(solution)/shard_map/ppermute | solution.py:1020
  41.8 1.8 %collective-permute-start.8 = (bf16[4,416,128]{2,1,0:T(8,128)(2,1)S(1)}, bf16[4,416,128]{2,1,0:T(8,128)(2,1)S(1)}, u32[]{:S(2)}, u32[]{:S(2)}) collective-permute-start(bf16[4,416,128]{2,1,0:T(8,128)(2,1)S(1)} %constant_dynamic-update-slice_fusion.refs_12_), channel_id=1, source_target_pairs={{0,1},{1,0},{2,3},{3,2},{4,5},{5,4},{6,7},{7,6},{8,9},{9,8},{10,11... | collective-permute-start | bytes 1277960 | tf_op jit(solution)/shard_map/ppermute | solution.py:1020
  53.9 10.4 %collective-permute-start.9 = (bf16[2,8,392,128]{3,2,1,0:T(8,128)(2,1)}, bf16[2,8,392,128]{3,2,1,0:T(8,128)(2,1)}, u32[]{:S(2)}, u32[]{:S(2)}) collective-permute-start(bf16[2,8,392,128]{3,2,1,0:T(8,128)(2,1)} %get-tuple-element.239), channel_id=1, source_target_pairs={{0,1},{1,0},{2,3},{3,2},{4,5},{5,4},{6,7},{7,6},{8,9},{9,8},{10,11... | collective-permute-start | bytes 4816904 | tf_op jit(solution)/shard_map/ppermute | solution.py:1020
  54.1 10.2 %copy-start.26 = (bf16[2,8,392,128]{3,2,1,0:T(8,128)(2,1)S(1)}, bf16[2,8,392,128]{3,2,1,0:T(8,128)(2,1)}, u32[]{:S(2)}) copy-start(bf16[2,8,392,128]{3,2,1,0:T(8,128)(2,1)} %get-tuple-element.243) | copy-start | bytes 4816900
  66.2 13.3 %collective-permute-start.10 = (bf16[2,392,128]{2,1,0:T(8,128)(2,1)S(1)}, bf16[2,392,128]{2,1,0:T(8,128)(2,1)S(1)}, u32[]{:S(2)}, u32[]{:S(2)}) collective-permute-start(bf16[2,392,128]{2,1,0:T(8,128)(2,1)S(1)} %get-tuple-element.252), channel_id=1, source_target_pairs={{0,4},{4,0},{8,12},{12,8},{16,20},{20,16},{24,28},{28,24},{1,5},{5... | collective-permute-start | bytes 602120 | tf_op jit(solution)/shard_map/ppermute | solution.py:1020
  67.4 12.1 %collective-permute-start.11 = (bf16[2,392,128]{2,1,0:T(8,128)(2,1)S(1)}, bf16[2,392,128]{2,1,0:T(8,128)(2,1)S(1)}, u32[]{:S(2)}, u32[]{:S(2)}) collective-permute-start(bf16[2,392,128]{2,1,0:T(8,128)(2,1)S(1)} %get-tuple-element.253), channel_id=1, source_target_pairs={{0,2},{1,3},{2,0},{3,1},{4,6},{5,7},{6,4},{7,5},{8,10},{9,11},{10,... | collective-permute-start | bytes 602120 | tf_op jit(solution)/shard_map/ppermute | solution.py:1020
  79.8 4.6 %collective-permute-start.12 = (bf16[80,640]{1,0:T(8,128)(2,1)S(1)}, bf16[80,640]{1,0:T(8,128)(2,1)S(1)}, u32[]{:S(2)}, u32[]{:S(2)}) collective-permute-start(bf16[80,640]{1,0:T(8,128)(2,1)S(1)} %get-tuple-element.264), channel_id=1, source_target_pairs={{0,1},{1,0},{2,3},{3,2},{4,5},{5,4},{6,7},{7,6},{8,9},{9,8},{10,11... | collective-permute-start | bytes 307208 | tf_op jit(solution)/shard_map/ppermute | solution.py:1020
  79.9 16.8 %collective-permute-start.13 = (bf16[4,392,128]{2,1,0:T(8,128)(2,1)S(1)}, bf16[4,392,128]{2,1,0:T(8,128)(2,1)S(1)}, u32[]{:S(2)}, u32[]{:S(2)}) collective-permute-start(bf16[4,392,128]{2,1,0:T(8,128)(2,1)S(1)} %get-tuple-element.279), channel_id=1, source_target_pairs={{0,4},{4,0},{8,12},{12,8},{16,20},{20,16},{24,28},{28,24},{1,5},{5... | collective-permute-start | bytes 1204232 | tf_op jit(solution)/shard_map/ppermute | solution.py:1020
  80.9 15.9 %collective-permute-start.14 = (bf16[4,392,128]{2,1,0:T(8,128)(2,1)S(1)}, bf16[4,392,128]{2,1,0:T(8,128)(2,1)S(1)}, u32[]{:S(2)}, u32[]{:S(2)}) collective-permute-start(bf16[4,392,128]{2,1,0:T(8,128)(2,1)S(1)} %get-tuple-element.280), channel_id=1, source_target_pairs={{0,2},{1,3},{2,0},{3,1},{4,6},{5,7},{6,4},{7,5},{8,10},{9,11},{10,... | collective-permute-start | bytes 1204232 | tf_op jit(solution)/shard_map/ppermute | solution.py:1020
  84.5 12.3 %collective-permute-start.15 = (bf16[80,640]{1,0:T(8,128)(2,1)S(1)}, bf16[80,640]{1,0:T(8,128)(2,1)S(1)}, u32[]{:S(2)}, u32[]{:S(2)}) collective-permute-start(bf16[80,640]{1,0:T(8,128)(2,1)S(1)} %add_convert_fusion.6), channel_id=1, source_target_pairs={{0,16},{4,20},{8,24},{12,28},{16,0},{20,4},{24,8},{28,12},{1,17},{... | collective-permute-start | bytes 307208 | tf_op jit(solution)/shard_map/ppermute | solution.py:1020
  96.9 9.7 %collective-permute-start.17 = (f32[16,640]{1,0:T(8,128)S(1)}, f32[16,640]{1,0:T(8,128)S(1)}, u32[]{:S(2)}, u32[]{:S(2)}) collective-permute-start(f32[16,640]{1,0:T(8,128)S(1)} %get-tuple-element.302), channel_id=1, source_target_pairs={{0,16},{4,20},{8,24},{12,28},{16,0},{20,4},{24,8},{28,12},{1,17},{... | collective-permute-start | bytes 122888 | tf_op jit(solution)/shard_map/ppermute | solution.py:1020
  97.6 9.0 %collective-permute-start.16 = (bf16[80,640]{1,0:T(8,128)(2,1)S(1)}, bf16[80,640]{1,0:T(8,128)(2,1)S(1)}, u32[]{:S(2)}, u32[]{:S(2)}) collective-permute-start(bf16[80,640]{1,0:T(8,128)(2,1)S(1)} %add_convert_fusion.5), channel_id=1, source_target_pairs={{0,2},{1,3},{2,0},{3,1},{4,6},{5,7},{6,4},{7,5},{8,10},{9,11},{10,... | collective-permute-start | bytes 307208 | tf_op jit(solution)/shard_map/ppermute | solution.py:1020
  99.2 16.6 %collective-permute-start.21 = (bf16[392,128]{1,0:T(8,128)(2,1)S(1)}, bf16[392,128]{1,0:T(8,128)(2,1)S(1)}, u32[]{:S(2)}, u32[]{:S(2)}) collective-permute-start(bf16[392,128]{1,0:T(8,128)(2,1)S(1)} %get-tuple-element.382), channel_id=1, source_target_pairs={{0,24},{4,28},{8,16},{12,20},{16,8},{20,12},{24,0},{28,4},{1,25},{... | collective-permute-start | bytes 301064 | tf_op jit(solution)/shard_map/ppermute | solution.py:1020
  102.7 13.1 %collective-permute-start.20 = (bf16[392,128]{1,0:T(8,128)(2,1)S(1)}, bf16[392,128]{1,0:T(8,128)(2,1)S(1)}, u32[]{:S(2)}, u32[]{:S(2)}) collective-permute-start(bf16[392,128]{1,0:T(8,128)(2,1)S(1)} %get-tuple-element.383), channel_id=1, source_target_pairs={{0,16},{4,20},{8,24},{12,28},{16,0},{20,4},{24,8},{28,12},{1,17},{... | collective-permute-start | bytes 301064 | tf_op jit(solution)/shard_map/ppermute | solution.py:1020
  102.7 13.1 %collective-permute-start.19 = (bf16[392,128]{1,0:T(8,128)(2,1)S(1)}, bf16[392,128]{1,0:T(8,128)(2,1)S(1)}, u32[]{:S(2)}, u32[]{:S(2)}) collective-permute-start(bf16[392,128]{1,0:T(8,128)(2,1)S(1)} %get-tuple-element.384), channel_id=1, source_target_pairs={{0,8},{4,12},{8,0},{12,4},{16,24},{20,28},{24,16},{28,20},{1,9},{5... | collective-permute-start | bytes 301064 | tf_op jit(solution)/shard_map/ppermute | solution.py:1020
  106.7 5.2 %collective-permute-start.18 = (bf16[112,640]{1,0:T(8,128)(2,1)S(1)}, bf16[112,640]{1,0:T(8,128)(2,1)S(1)}, u32[]{:S(2)}, u32[]{:S(2)}) collective-permute-start(bf16[112,640]{1,0:T(8,128)(2,1)S(1)} %pad_maximum_fusion.5), channel_id=1, source_target_pairs={{0,4},{4,0},{8,12},{12,8},{16,20},{20,16},{24,28},{28,24},{1,5},{5... | collective-permute-start | bytes 430088 | tf_op jit(solution)/shard_map/ppermute | solution.py:1020
  112.0 5.2 %collective-permute-start.22 = (bf16[112,640]{1,0:T(8,128)(2,1)S(1)}, bf16[112,640]{1,0:T(8,128)(2,1)S(1)}, u32[]{:S(2)}, u32[]{:S(2)}) collective-permute-start(bf16[112,640]{1,0:T(8,128)(2,1)S(1)} %pad_maximum_fusion.6), channel_id=1, source_target_pairs={{0,8},{4,12},{8,0},{12,4},{16,24},{20,28},{24,16},{28,20},{1,9},{5... | collective-permute-start | bytes 430088 | tf_op jit(solution)/shard_map/ppermute | solution.py:1020
  117.4 1.5 %collective-permute-start.23 = (bf16[112,640]{1,0:T(8,128)(2,1)S(1)}, bf16[112,640]{1,0:T(8,128)(2,1)S(1)}, u32[]{:S(2)}, u32[]{:S(2)}) collective-permute-start(bf16[112,640]{1,0:T(8,128)(2,1)S(1)} %pad_maximum_fusion.7), channel_id=1, source_target_pairs={{0,1},{1,0},{2,3},{3,2},{4,5},{5,4},{6,7},{7,6},{8,9},{9,8},{10,11... | collective-permute-start | bytes 430088 | tf_op jit(solution)/shard_map/ppermute | solution.py:1020
  119.0 5.2 %collective-permute-start.24 = (f32[16,640]{1,0:T(8,128)S(1)}, f32[16,640]{1,0:T(8,128)S(1)}, u32[]{:S(2)}, u32[]{:S(2)}) collective-permute-start(f32[16,640]{1,0:T(8,128)S(1)} %fusion.2), channel_id=1, source_target_pairs={{0,2},{1,3},{2,0},{3,1},{4,6},{5,7},{6,4},{7,5},{8,10},{9,11},{10,... | collective-permute-start | bytes 122888 | tf_op jit(solution)/shard_map/ppermute | solution.py:1020
  (27 other events, 100.7 us)

commit v6 on v5

--- a/solution.py
+++ b/solution.py
@@ -219,16 +219,21 @@
     terms = jnp.where(line == 0, top, jnp.where(line == 1, mid, jnp.where(line == 2, low, 0.0)))
     rows = weight_ref.shape[0]
     tail = piece_ref.shape[0] - 16
-    piece_ref[...] = jnp.zeros_like(piece_ref)
-    piece_ref[0:rows, :] = weight_ref[...].astype(BF)
-    piece_ref[tail:, :] = jnp.concatenate([terms, jnp.zeros((8, 128), F32)], axis=0).astype(BF)
+    lead = max(rows - tail, 0)
+    if tail > rows:
+        piece_ref[rows // 16 * 16 : tail, :] = jnp.zeros((tail - rows // 16 * 16, 128), BF)
+    piece_ref[0 : min(rows, tail), :] = weight_ref[0 : min(rows, tail), :].astype(BF)
+    last = [weight_ref[rows - lead :, :]] if lead else []
+    last += [jnp.zeros((8 - lead, 128), F32)] if lead < 8 else []
+    piece_ref[tail:, :] = jnp.concatenate(last + [terms], axis=0).astype(BF)
     for r in range(5):
         ring_copy(frames_ref, cells_ref, sems, r).wait()
 
 
 def first(lengths, dones, rewards, old_values, weight, frames):
     n = rewards.shape[1]
-    rows = -(-weight.shape[0] // 16) * 16 + 16
+    rows = -(-weight.shape[0] // 16) * 16
+    rows += 16 if weight.shape[0] - (rows - 16) > 8 else 0
     small = [dones, rewards, old_values, weight]
     return pl.pallas_call(
         first_kernel,
@@ -246,7 +251,7 @@
     )(lengths, *[far(a) for a in small], far(frames))
 
 
-RING = 8
+RING = 10
 
 
 def ring_copy(frames_ref, cells_ref, sems, r):
@@ -255,17 +260,17 @@
 
 
 def fetch_rows(frames_ref, cells_ref, sems, step, last):
-    @pl.when(step < last - 1)
-    def _():
-        ring_copy(frames_ref, cells_ref, sems, 2 * step + 5).start()
-        ring_copy(frames_ref, cells_ref, sems, 2 * step + 6).start()
-
-    @pl.when(step >= 2)
-    def _():
-        ring_copy(frames_ref, cells_ref, sems, 2 * step + 1).wait()
-        ring_copy(frames_ref, cells_ref, sems, 2 * step + 2).wait()
-
-    return [lax.rem(2 * step + a, RING) for a in range(3)]
+    @pl.when(step < last)
+    def _():
+        for a in range(5, 9):
+            ring_copy(frames_ref, cells_ref, sems, 4 * step + a).start()
+
+    @pl.when(step >= 1)
+    def _():
+        for a in range(1, 5):
+            ring_copy(frames_ref, cells_ref, sems, 4 * step + a).wait()
+
+    return [lax.rem(4 * step + a, RING) for a in range(5)]
 
 
 def conv_one_kernel(
@@ -275,19 +280,20 @@
     half = act_ref.shape[0]
     step = pl.program_id(0)
 
-    slots = fetch_rows(frames_ref, cells_ref, sems, step, half - 1)
+    slots = fetch_rows(frames_ref, cells_ref, sems, step, half // 2 - 1)
 
     @pl.when(step == 0)
     def _():
         band_ref[...] = band_square(weight_ref[...], 64)
         wide_ref[...] = wide(bias_ref[:, 0:32], 128, n)
 
-    for col in range(half):
-        span = slice(col * 128, col * 128 + 192)
-        patch = jnp.concatenate([cells_ref[slot, span, :] for slot in slots], axis=0)
-        act, slope = gelu_both(dot(band_ref[...], patch) + wide_ref[...])
-        act_ref[step, col] = act.astype(BF)
-        slope_ref[step, col] = slope.astype(BF)
+    for q in range(2):
+        for col in range(half):
+            span = slice(col * 128, col * 128 + 192)
+            patch = jnp.concatenate([cells_ref[slot, span, :] for slot in slots[2 * q : 2 * q + 3]], axis=0)
+            act, slope = gelu_both(dot(band_ref[...], patch) + wide_ref[...])
+            act_ref[2 * step + q, col] = act.astype(BF)
+            slope_ref[2 * step + q, col] = slope.astype(BF)
 
 
 def conv_one(frames, weight, bias, cells):
@@ -300,7 +306,7 @@
         [near(shape, BF), near(shape, BF), near(cells.shape, BF)],
         in_specs=[anywhere()] + [vmem()] * 3,
         scratch=[pltpu.VMEM((128, 576), BF), pltpu.VMEM((128, n), F32), dma(RING)],
-        grid=half,
+        grid=half // 2,
         us=12,
         name="conv_one",
         aliases={3: 2},
@@ -322,17 +328,18 @@
         band_ref[...] = band_forward(weight_ref[...], 2, 128, 3)
         wide_ref[...] = wide(bias_ref[:, 32:96], 192, n)
 
-    for part in range(3):
-        span = slice(3 * part, 3 * part + 4)
-        patch = jnp.concatenate(
-            [one_ref[step + a, span].reshape(512, n) for a in range(2)], axis=0
-        )
-        act, slope = gelu_both(dot(band_ref[...], patch) + wide_ref[...])
-        rows = slice(part * 192, part * 192 + 192)
-        act_ref[step, rows, :] = act.astype(BF)
-        slope_ref[step, rows, :] = slope.astype(BF)
-
-    @pl.when(step == 8)
+    for row in range(9):
+        for part in range(3):
+            span = slice(3 * part, 3 * part + 4)
+            patch = jnp.concatenate(
+                [one_ref[row + a, span].reshape(512, n) for a in range(2)], axis=0
+            )
+            act, slope = gelu_both(dot(band_ref[...], patch) + wide_ref[...])
+            rows = slice(part * 192, part * 192 + 192)
+            act_ref[row, rows, :] = act.astype(BF)
+            slope_ref[row, rows, :] = slope.astype(BF)
+
+    @pl.when(step == 0)
     def _():
         wait_rows(one_ref, one_far_ref, sems)
         wait_rows(slope_one_ref, slope_one_far_ref, slope_sems)
@@ -347,7 +354,7 @@
         [near(shape, BF)] * 2 + [pltpu.HBM(act_one.shape, BF)] * 2,
         out_specs=[vmem(), vmem(), anywhere(), anywhere()],
         scratch=[pltpu.VMEM((192, 1024), BF), pltpu.VMEM((192, n), F32), dma(10), dma(10)],
-        grid=9,
+        grid=1,
         us=7,
         name="conv_two",
         limit=16,
@@ -360,33 +367,26 @@
     band_ref, wide_ref, flat_ref, slope_ref, two_sems, slope_two_sems, flat_sems, slope_sems,
 ):
     n = two_ref.shape[-1]
-    step = pl.program_id(0)
-
-    @pl.when(step == 0)
-    def _():
-        start_rows(two_ref, two_far_ref, two_sems)
-        start_rows(slope_two_ref, slope_two_far_ref, slope_two_sems)
-        band_ref[...] = band_forward(weight_ref[...], 3, 64, 4)
-        wide_ref[...] = wide(bias_ref[:, 96:160], 256, n)
-
-    for drop, start in ((0, 0), (1, 3)):
-        patch = jnp.concatenate(
-            [two_ref[step + a, start * 64 : start * 64 + 384, :] for a in range(3)], axis=0
-        )
-        pre = dot(band_ref[drop * 64 :, :], patch) + wide_ref[drop * 64 :, :]
-        act, slope = gelu_both(pre)
-        rows = slice((start + drop) * 64, (start + 4) * 64)
-        flat_ref[step, rows, :] = act.astype(BF)
-        slope_ref[step, rows, :] = slope.astype(BF)
-    row_copy(flat_ref, flat_far_ref, flat_sems, step).start()
-    row_copy(slope_ref, slope_far_ref, slope_sems, step).start()
-
-    @pl.when(step == 6)
-    def _():
-        wait_rows(two_ref, two_far_ref, two_sems)
-        wait_rows(slope_two_ref, slope_two_far_ref, slope_two_sems)
-        wait_rows(flat_ref, flat_far_ref, flat_sems)
-        wait_rows(slope_ref, slope_far_ref, slope_sems)
+    start_rows(two_ref, two_far_ref, two_sems)
+    start_rows(slope_two_ref, slope_two_far_ref, slope_two_sems)
+    band_ref[...] = band_forward(weight_ref[...], 3, 64, 4)
+    wide_ref[...] = wide(bias_ref[:, 96:160], 256, n)
+    for row in range(7):
+        for drop, start in ((0, 0), (1, 3)):
+            patch = jnp.concatenate(
+                [two_ref[row + a, start * 64 : start * 64 + 384, :] for a in range(3)], axis=0
+            )
+            pre = dot(band_ref[drop * 64 :, :], patch) + wide_ref[drop * 64 :, :]
+            act, slope = gelu_both(pre)
+            rows = slice((start + drop) * 64, (start + 4) * 64)
+            flat_ref[row, rows, :] = act.astype(BF)
+            slope_ref[row, rows, :] = slope.astype(BF)
+        row_copy(flat_ref, flat_far_ref, flat_sems, row).start()
+        row_copy(slope_ref, slope_far_ref, slope_sems, row).start()
+    wait_rows(two_ref, two_far_ref, two_sems)
+    wait_rows(slope_two_ref, slope_two_far_ref, slope_two_sems)
+    wait_rows(flat_ref, flat_far_ref, flat_sems)
+    wait_rows(slope_ref, slope_far_ref, slope_sems)
 
 
 def conv_three(act_two, slope_two, weight, bias):
@@ -408,7 +408,6 @@
             dma(7),
             dma(7),
         ],
-        grid=7,
         us=6,
         name="conv_three",
         limit=16,
@@ -478,7 +477,7 @@
     for i in range(n_dp):
         for j in range(n_own):
             tail = blocks_ref[i, j, blocks_ref.shape[2] - 16 :].astype(F32)
-            stats.append((tail[0:1] + tail[1:2]) + tail[2:3])
+            stats.append((tail[8:9] + tail[9:10]) + tail[10:11])
     stats = jnp.concatenate(stats, axis=0)
     each = stats[:, 0:1]
     count = jnp.sum(each, axis=0, keepdims=True)
@@ -611,39 +610,49 @@
         acc_ref[...] = jnp.zeros_like(acc_ref)
         tot_ref[...] = jnp.zeros_like(tot_ref)
 
-    @pl.when(step < 7)
-    def _():
-        three_row(step).wait()
-
-    row_copy(slope_far_ref, slope_ref, slope_sems, step).wait()
-
-    @pl.when(step == 1)
+    lines = [3 * step + q for q in range(3)]
+    for line in lines:
+
+        @pl.when(line < 7)
+        def _(line=line):
+            three_row(line).wait()
+
+        row_copy(slope_far_ref, slope_ref, slope_sems, line).wait()
+
+    @pl.when(step == 0)
     def _():
         start_rows(one_far_ref, one_ref, one_sems)
         start_rows(slope_one_far_ref, slope_one_ref, slope_one_sems)
 
     total = tot_ref[...]
-    for part in range(3):
-        patch = jnp.concatenate(
-            [pad_ref[step + a, part * 192 : part * 192 + 320, :] for a in range(3)], axis=0
-        )
-        rows = slice(part * 192, part * 192 + 192)
-        d_two = (dot(band_ref[...], patch) * slope_ref[step, rows, :].astype(F32)).astype(BF)
-        d_two_ref[step, rows, :] = d_two
-        back = d_two.astype(F32)
-        total = total + (back[0:64] + back[64:128]) + back[128:192]
+    for line in lines:
+        for part in range(3):
+            patch = jnp.concatenate(
+                [pad_ref[line + a, part * 192 : part * 192 + 320, :] for a in range(3)], axis=0
+            )
+            rows = slice(part * 192, part * 192 + 192)
+            d_two = (dot(band_ref[...], patch) * slope_ref[line, rows, :].astype(F32)).astype(BF)
+            d_two_ref[line, rows, :] = d_two
+            back = d_two.astype(F32)
+            total = total + (back[0:64] + back[64:128]) + back[128:192]
     tot_ref[...] = total
 
-    @pl.when(step < 7)
-    def _():
-        row = pad_ref[step + 2, 128 : 128 + 448, :]
+    def grads(line):
+        row = pad_ref[line + 2, 128 : 128 + 448, :]
         second = jnp.concatenate([jnp.zeros((64, n), BF), row[256:448]], axis=0)
         for d_rows, start in ((row[0:256], 0), (second, 3)):
             span = slice(start * 64, start * 64 + 384)
-            cells = jnp.concatenate([act_ref[step + a, span, :] for a in range(3)], axis=0)
+            cells = jnp.concatenate([act_ref[line + a, span, :] for a in range(3)], axis=0)
             acc_ref[...] += dot(d_rows, cells, NT)
 
-    @pl.when(step == 8)
+    grads(lines[0])
+
+    @pl.when(step < 2)
+    def _():
+        grads(lines[1])
+        grads(lines[2])
+
+    @pl.when(step == 2)
     def _():
         wait_rows(one_far_ref, one_ref, one_sems)
         wait_rows(slope_one_far_ref, slope_one_ref, slope_one_sems)
@@ -686,7 +695,7 @@
             dma(9),
             dma(7),
         ],
-        grid=9,
+        grid=3,
         us=9,
         name="conv_three_back",
         limit=16,
@@ -711,31 +720,42 @@
         acc_ref[...] = jnp.zeros_like(acc_ref)
         tot_ref[...] = jnp.zeros_like(tot_ref)
 
-    @pl.when(step < 9)
-    def _():
-        pad_ref[step + 1, 64 : 64 + 576, :] = d_two_ref[step]
+    lines = [5 * step + q for q in range(5)]
+    for line in lines[:4]:
+        pad_ref[line + 1, 64 : 64 + 576, :] = d_two_ref[line]
+
+    @pl.when(step < 1)
+    def _():
+        pad_ref[lines[4] + 1, 64 : 64 + 576, :] = d_two_ref[lines[4]]
 
     total = tot_ref[...]
-    for col in range(10):
-        patch = jnp.concatenate(
-            [pad_ref[step + a, col * 64 : col * 64 + 128, :] for a in range(2)], axis=0
-        )
-        d_one = (dot(band_ref[...], patch) * slope_ref[step, col].astype(F32)).astype(BF)
-        d_one_ref[step, col] = d_one
-        total = total + d_one.astype(F32)
+    for line in lines:
+        for col in range(10):
+            patch = jnp.concatenate(
+                [pad_ref[line + a, col * 64 : col * 64 + 128, :] for a in range(2)], axis=0
+            )
+            d_one = (dot(band_ref[...], patch) * slope_ref[line, col].astype(F32)).astype(BF)
+            d_one_ref[line, col] = d_one
+            total = total + d_one.astype(F32)
     tot_ref[...] = total
 
-    @pl.when(step < 9)
-    def _():
+    def grads(line):
         for part in range(3):
             span = slice(3 * part, 3 * part + 4)
             cells = jnp.concatenate(
-                [act_ref[step + a, span].reshape(512, n) for a in range(2)], axis=0
+                [act_ref[line + a, span].reshape(512, n) for a in range(2)], axis=0
             )
-            rows = pad_ref[step + 1, 64 + part * 192 : 64 + part * 192 + 192, :]
+            rows = pad_ref[line + 1, 64 + part * 192 : 64 + part * 192 + 192, :]
             acc_ref[...] += dot(rows, cells, NT)
 
-    @pl.when(step == 9)
+    for line in lines[:4]:
+        grads(line)
+
+    @pl.when(step < 1)
+    def _():
+        grads(lines[4])
+
+    @pl.when(step == 1)
     def _():
         for a in range(2):
             out = None
@@ -765,7 +785,7 @@
             pltpu.VMEM((192, 1024), F32),
             pltpu.VMEM((128, n), F32),
         ],
-        grid=10,
+        grid=2,
         us=11,
         name="conv_two_back",
         limit=16,
@@ -786,11 +806,12 @@
     def _():
         acc_ref[...] = jnp.zeros_like(acc_ref)
 
-    for pair in range(d_one_ref.shape[1] // 2):
-        span = slice(pair * 256, pair * 256 + 320)
-        cells = jnp.concatenate([cells_ref[slot, span, :] for slot in slots], axis=0)
-        rows = d_one_ref[step, 2 * pair : 2 * pair + 2].reshape(256, n)
-        acc_ref[...] += dot(rows, cells, NT)
+    for q in range(2):
+        for pair in range(5):
+            span = slice(pair * 256, pair * 256 + 320)
+            cells = jnp.concatenate([cells_ref[slot, span, :] for slot in slots[2 * q : 2 * q + 3]], axis=0)
+            rows = d_one_ref[2 * step + q, 2 * pair : 2 * pair + 2].reshape(256, n)
+            acc_ref[...] += dot(rows, cells, NT)
 
     @pl.when(step == half - 1)
     def _():
@@ -822,7 +843,7 @@
             near(d_one.shape, BF),
             near(cells.shape, BF),
         ),
-        grid=(d_one.shape[0],),
+        grid=(d_one.shape[0] // 2,),
         in_specs=[anywhere()] + [vmem()] * 6,
         out_specs=(vmem(),) * 3,
         scratch_shapes=[pltpu.VMEM((256, 960), F32), dma(RING)],
@@ -842,60 +863,40 @@
         band_ref = weight_ref
         out_ref, d_out_ref, rows_ref, sems = refs[-4:]
     n = rows_ref.shape[-1]
-    step = pl.program_id(0)
-    row = step + begin
     cells = d_one_ref.shape[1]
     zero = jnp.zeros((32, n), BF)
-
     if ahead:
-
-        @pl.when(step == 0)
-        def _():
-            for r in range(5):
-                ring_copy(frames_ref, cells_ref, cell_sems, r).start()
-            band_ref[...] = band_back(weight_ref[...], 2, 64, 3)
-
-    def slab(at, dy, first, alive):
+        for r in range(5):
+            ring_copy(frames_ref, cells_ref, cell_sems, r).start()
+        band_ref[...] = band_back(weight_ref[...], 2, 64, 3)
+
+    def slab(line, first):
         parts = []
         for c in range(first, first + 4):
-            if c < 0 or c >= 2 * cells:
+            if c < 0 or c >= 2 * cells or line < 0 or line >= 2 * cells:
                 parts.append(zero)
             else:
-                spot = (dy * 2 + c % 2) * 32
-                parts.append(d_one_ref[at, c // 2, spot : spot + 32, :])
-        whole = jnp.concatenate(parts, axis=0)
-        return whole if alive is None else jnp.where(alive, whole, jnp.zeros_like(whole))
-
-    def make(up, low, at):
+                spot = (line % 2 * 2 + c % 2) * 32
+                parts.append(d_one_ref[line // 2, c // 2, spot : spot + 32, :])
+        return jnp.concatenate(parts, axis=0)
+
+    def send(line):
+        spot = line - 2 * begin
+        return pltpu.make_async_copy(rows_ref.at[spot], out_ref.at[line], sems.at[spot])
+
+    lines = range(2 * begin, min(2 * end, 2 * total - 1))
+    for line in lines:
         for block in range(7):
             first = 3 * block - 1
-            patch = jnp.concatenate([slab(*up[:2], first, up[2]), slab(*low[:2], first, low[2])], axis=0)
-            rows_ref[at, block * 192 : block * 192 + 192, :] = dot(band_ref[...], patch).astype(BF)
-
-    def send(at):
-        return pltpu.make_async_copy(rows_ref.at[at], out_ref.at[at + 2 * begin], sems.at[at])
-
-    here = row if end < total else jnp.minimum(row, total - 2)
-    above = row - 1 if begin > 0 else jnp.maximum(row - 1, 0)
-    make(
-        (above, 1, None if begin > 0 else row > 0),
-        (here, 0, None if end < total else row < total - 1),
-        2 * step,
-    )
-    send(2 * step).start()
-
-    @pl.when(row < total - 1)
-    def _():
-        make((here, 0, None), (here, 1, None), 2 * step + 1)
-        send(2 * step + 1).start()
-
-    @pl.when(step == end - begin - 1)
-    def _():
-        for at in range(min(2 * end, 2 * total - 1) - 2 * begin):
-            send(at).wait()
-        if ahead:
-            for r in range(5):
-                ring_copy(frames_ref, cells_ref, cell_sems, r).wait()
+            patch = jnp.concatenate([slab(line - 1, first), slab(line, first)], axis=0)
+            rows = slice(block * 192, block * 192 + 192)
+            rows_ref[line - 2 * begin, rows, :] = dot(band_ref[...], patch).astype(BF)
+        send(line).start()
+    for line in lines:
+        send(line).wait()
+    if ahead:
+        for r in range(5):
+            ring_copy(frames_ref, cells_ref, cell_sems, r).wait()
 
 
 def frames_back(d_one, weight, shape, begin, end, so_far=None, frames=None):
@@ -911,7 +912,6 @@
         in_specs=[vmem(), vmem()] + [anywhere()] * len(more),
         out_specs=[anywhere(), vmem()] + [vmem()] * len(cells),
         scratch=[pltpu.VMEM((2 * count,) + shape[1:], BF), dma(2 * count)] + [dma(5)] * ahead,
-        grid=count,
         us=count,
         name="frames_back",
         aliases={0: 1, 2: 0} if so_far is not None else {0: 1},

time: 126 us -> 120 us (0.952)
  Pallas kernels: 84.4 us -> 75.1 us
  waiting for transfers between devices: 5.8 us -> 7.95 us
    pallas_call x10, Pallas kernels: 66.2 us -> 57.7 us  [call(): pl.pallas_call(body, out_shape=tuple(outs), in_specs=list(in_specs or [vm...]
    ppermute x25, waiting for transfers between devices: 5.8 us -> 7.95 us  [swap(): return lax.ppermute(x, axis, [(i, i ^ bit) for i in range(size)])]
  transfers between devices with their start and end apart: 25 -> 25, of which waited for: 5 -> 6; matrix products, arithmetic and copies ran while one was open for 0% -> 0% of each run, Pallas kernels for 56% -> 51%
where the time goes in v6:
time: 120 us
  Pallas kernels  75.1 us (63%)
  starting transfers between devices  30 us (25%)
  waiting for transfers between devices  7.95 us (7%)
  other arithmetic  3.45 us (3%)
  between operations  2.23 us (2%)
  local copies, waits for them, and re-layouts  1.29 us (1%)
    pallas_call x10, Pallas kernels, call(): pl.pallas_call(body, out_shape=tuple(outs), in_specs=list(in_specs or [vm...  57.7 us
    ppermute x25, starting transfers between devices, swap(): return lax.ppermute(x, axis, [(i, i ^ bit) for i in range(size)])  30 us
    pallas_call x1, Pallas kernels, conv_one_grad(): pl.pallas_call(conv_one_grad_kernel, out_shape=(jax.ShapeDtypeStruct((16,...  9.11 us
    ppermute x25, waiting for transfers between devices, swap(): return lax.ppermute(x, axis, [(i, i ^ bit) for i in range(size)])  7.95 us
    pallas_call x2, Pallas kernels, steps(): pl.pallas_call(functools.partial(steps_kernel, spots=spots), out_shape=tu...  4.32 us
    pallas_call x1, Pallas kernels, first(): pl.pallas_call(first_kernel, out_shape=(jax.ShapeDtypeStruct((1, n), F32)...  2.65 us
  transfers between devices with their start and end apart: 25, of which 6 were waited for; matrix products, arithmetic and copies ran while one was open for 0% of the time, Pallas kernels for 51%

profile of v6, /device:TPU:0, one launch (start us, length us, event | category | flops | bytes accessed | tf_op | source)
XLA Modules:
  0.0 120.0 jit_solution(15642601367176321528)
XLA Ops:
  1.3 2.6 %first.1 = (f32[1,256]{1,0:T(1,128)S(1)}, bf16[400,128]{1,0:T(8,128)(2,1)S(1)}, bf16[10,1344,256]{2,1,0:T(8,128)(2,1)S(1)}) custom-call(s32[1]{0:T(128)S(6)} %copy.80.lengths_ref.refs_1_, s32[1,256]{1,0:T(1,128)} %dones_far_ref.1, f32[1,256]{1,0:T(1,128)} %rewards_far_ref.1, f32[1,256]{1,0:T(1,128)} %refs_6_.1, f32[392,128]{1,0:T(8,128)} %refs_0_.1, ...), custom_call_target="tpu_custom_call" | custom-call | flops 3000000000 | tf_op jit(solution)/shard_map/first/pallas_call | solution.py:238
  4.0 5.1 %collective-permute-start.2 = (bf16[400,128]{1,0:T(8,128)(2,1)S(1)}, bf16[400,128]{1,0:T(8,128)(2,1)S(1)}, u32[]{:S(2)}, u32[]{:S(2)}) collective-permute-start(bf16[400,128]{1,0:T(8,128)(2,1)S(1)} %get-tuple-element.204), channel_id=1, source_target_pairs={{0,24},{4,28},{8,16},{12,20},{16,8},{20,12},{24,0},{28,4},{1,25},{... | collective-permute-start | bytes 307208 | tf_op jit(solution)/shard_map/ppermute | solution.py:1020
  9.8 10.2 %conv_one.1 = (bf16[10,10,128,256]{3,2,1,0:T(8,128)(2,1)S(1)}, bf16[10,10,128,256]{3,2,1,0:T(8,128)(2,1)S(1)}, bf16[10,1344,256]{2,1,0:T(8,128)(2,1)S(1)}) custom-call(bf16[21,1344,256]{2,1,0:T(8,128)(2,1)} %bitcast.102, f32[32,256]{1,0:T(8,128)S(1)} %bitcast.81, f32[1,691]{1,0:T(1,128)S(1)} %reshape.64.bias_ref.refs_3_, ...), custom_call_target="tpu_custom_call", output_to_operand_aliasing={{2}: (3, {})} | custom-call | flops 12000000000 | tf_op jit(solution)/shard_map/conv_one/pallas_call | solution.py:85
  20.1 1.7 %collective-permute-start.4 = (bf16[4,400,128]{2,1,0:T(8,128)(2,1)S(1)}, bf16[4,400,128]{2,1,0:T(8,128)(2,1)S(1)}, u32[]{:S(2)}, u32[]{:S(2)}) collective-permute-start(bf16[4,400,128]{2,1,0:T(8,128)(2,1)S(1)} %pad_maximum_fusion.1), channel_id=1, source_target_pairs={{0,2},{1,3},{2,0},{3,1},{4,6},{5,7},{6,4},{7,5},{8,10},{9,11},{10,... | collective-permute-start | bytes 1228808 | tf_op jit(solution)/shard_map/ppermute | solution.py:1020
  21.9 1.5 %collective-permute-start.3 = (bf16[4,400,128]{2,1,0:T(8,128)(2,1)S(1)}, bf16[4,400,128]{2,1,0:T(8,128)(2,1)S(1)}, u32[]{:S(2)}, u32[]{:S(2)}) collective-permute-start(bf16[4,400,128]{2,1,0:T(8,128)(2,1)S(1)} %pad_maximum_fusion.1), channel_id=1, source_target_pairs={{0,4},{4,0},{8,12},{12,8},{16,20},{20,16},{24,28},{28,24},{1,5},{5... | collective-permute-start | bytes 1228808 | tf_op jit(solution)/shard_map/ppermute | solution.py:1020
  23.4 5.6 %conv_two.1 = (bf16[9,576,256]{2,1,0:T(8,128)(2,1)S(1)}, bf16[9,576,256]{2,1,0:T(8,128)(2,1)S(1)}, bf16[10,10,128,256]{3,2,1,0:T(8,128)(2,1)}, bf16[10,10,128,256]{3,2,1,0:T(8,128)(2,1)}) custom-call(bf16[10,10,128,256]{3,2,1,0:T(8,128)(2,1)S(1)} %get-tuple-element.208.one_ref, bf16[10,10,128,256]{3,2,1,0:T(8,128)(2,1)S(1)} %get-tuple-element.209.slope_one_ref, ...), custom_call_target="tpu_custom_call" | custom-call | flops 7000000000 | tf_op jit(solution)/shard_map/conv_two/pallas_call | solution.py:85
  29.0 1.9 %collective-permute-done.4 = bf16[4,400,128]{2,1,0:T(8,128)(2,1)S(1)} collective-permute-done((bf16[4,400,128]{2,1,0:T(8,128)(2,1)S(1)}, bf16[4,400,128]{2,1,0:T(8,128)(2,1)S(1)}, u32[]{:S(2)}, u32[]{:S(2)}) %collective-permute-start.4) | collective-permute-done | bytes 409632 | tf_op jit(solution)/shard_map/ppermute | solution.py:1020
  30.9 1.2 %collective-permute-done.3 = bf16[4,400,128]{2,1,0:T(8,128)(2,1)S(1)} collective-permute-done((bf16[4,400,128]{2,1,0:T(8,128)(2,1)S(1)}, bf16[4,400,128]{2,1,0:T(8,128)(2,1)S(1)}, u32[]{:S(2)}, u32[]{:S(2)}) %collective-permute-start.3) | collective-permute-done | bytes 409632 | tf_op jit(solution)/shard_map/ppermute | solution.py:1020
  32.9 1.5 %collective-permute-start.6 = (bf16[2,400,128]{2,1,0:T(8,128)(2,1)S(1)}, bf16[2,400,128]{2,1,0:T(8,128)(2,1)S(1)}, u32[]{:S(2)}, u32[]{:S(2)}) collective-permute-start(bf16[2,400,128]{2,1,0:T(8,128)(2,1)S(1)} %slice.145), channel_id=1, source_target_pairs={{0,4},{4,0},{8,12},{12,8},{16,20},{20,16},{24,28},{28,24},{1,5},{5... | collective-permute-start | bytes 614408 | tf_op jit(solution)/shard_map/ppermute | solution.py:1020
  34.4 5.4 %conv_three.1 = (bf16[7,448,256]{2,1,0:T(8,128)(2,1)}, bf16[7,448,256]{2,1,0:T(8,128)(2,1)}, bf16[9,576,256]{2,1,0:T(8,128)(2,1)}, bf16[9,576,256]{2,1,0:T(8,128)(2,1)}) custom-call(bf16[9,576,256]{2,1,0:T(8,128)(2,1)S(1)} %get-tuple-element.218.two_ref, bf16[9,576,256]{2,1,0:T(8,128)(2,1)S(1)} %get-tuple-element.219.slope_two_ref, f32[64,576]{1,0:T(8,128)S(1)} %bitcast.84, ...), custom_call_target="tpu_custom_call" | custom-call | flops 6000000000 | tf_op jit(solution)/shard_map/conv_three/pallas_call | solution.py:85
  40.3 1.6 %collective-permute-done.8.refs_14_ = bf16[4,400,128]{2,1,0:T(8,128)(2,1)S(1)} collective-permute-done((bf16[4,400,128]{2,1,0:T(8,128)(2,1)S(1)}, bf16[4,400,128]{2,1,0:T(8,128)(2,1)S(1)}, u32[]{:S(2)}, u32[]{:S(2)}) %collective-permute-start.8) | collective-permute-done | bytes 409632 | tf_op jit(solution)/shard_map/ppermute | solution.py:1020
  42.7 9.5 %dense.1 = (bf16[7,448,256]{2,1,0:T(8,128)(2,1)}, bf16[9,576,256]{2,1,0:T(8,128)(2,1)S(1)}, bf16[2,8,392,128]{3,2,1,0:T(8,128)(2,1)}, bf16[2,8,392,128]{3,2,1,0:...) custom-call(s32[2]{0:T(128)S(1)} %pad_add_fusion.refs_0_, ...), custom_call_target="tpu_custom_call" | custom-call | flops 10000000000 | tf_op jit(solution)/shard_map/dense/pallas_call | solution.py:85
  52.5 8.4 %conv_three_back.1 = (bf16[9,576,256]{2,1,0:T(8,128)(2,1)S(1)}, bf16[10,10,128,256]{3,2,1,0:T(8,128)(2,1)S(1)}, bf16[10,10,128,256]{3,2,1,0:T(8,128)(2,1)S(1)}, bf16[96,640]{1,0:T(8,128)(2,1)S(1)}, f32[1,64]{1,0:T(1,128)S(1)}) custom-call(bf16[9,576,256]{2,1,0:T(8,128)(2,1)S(1)} %get-tuple-element.229.act_ref, ...), custom_call_target="tpu_custom_call" | custom-call | flops 8999999488 | tf_op jit(solution)/shard_map/conv_three_back/pallas_call | solution.py:85
  60.9 1.8 %add_convert_fusion = bf16[2,8,392,128]{3,2,1,0:T(8,128)(2,1)S(1)} fusion(bf16[2,8,392,128]{3,2,1,0:T(8,128)(2,1)} %collective-permute-done.9, bf16[2,8,392,128]{3,2,1,0:T(8,128)(2,1)S(1)} %copy-done.26), kind=kLoop, calls=%fused_computation | loop fusion | flops 3211264 | bytes 4816896 | tf_op jit(solution)/shard_map/convert_element_type | solution.py:1036
  62.8 1.6 %collective-permute-start.10 = (bf16[2,392,128]{2,1,0:T(8,128)(2,1)S(1)}, bf16[2,392,128]{2,1,0:T(8,128)(2,1)S(1)}, u32[]{:S(2)}, u32[]{:S(2)}) collective-permute-start(bf16[2,392,128]{2,1,0:T(8,128)(2,1)S(1)} %get-tuple-element.252), channel_id=1, source_target_pairs={{0,4},{4,0},{8,12},{12,8},{16,20},{20,16},{24,28},{28,24},{1,5},{5... | collective-permute-start | bytes 602120 | tf_op jit(solution)/shard_map/ppermute | solution.py:1020
  64.4 1.5 %collective-permute-start.11 = (bf16[2,392,128]{2,1,0:T(8,128)(2,1)S(1)}, bf16[2,392,128]{2,1,0:T(8,128)(2,1)S(1)}, u32[]{:S(2)}, u32[]{:S(2)}) collective-permute-start(bf16[2,392,128]{2,1,0:T(8,128)(2,1)S(1)} %get-tuple-element.253), channel_id=1, source_target_pairs={{0,2},{1,3},{2,0},{3,1},{4,6},{5,7},{6,4},{7,5},{8,10},{9,11},{10,... | collective-permute-start | bytes 602120 | tf_op jit(solution)/shard_map/ppermute | solution.py:1020
  65.9 8.3 %conv_two_back.1 = (bf16[10,10,128,256]{3,2,1,0:T(8,128)(2,1)S(1)}, bf16[160,640]{1,0:T(8,128)(2,1)S(1)}, f32[1,32]{1,0:T(1,128)S(1)}) custom-call(bf16[9,576,256]{2,1,0:T(8,128)(2,1)S(1)} %get-tuple-element.245.d_two_ref, bf16[10,10,128,256]{3,2,1,0:T(8,128)(2,1)S(1)} %get-tuple-element.246.act_ref, ...), custom_call_target="tpu_custom_call" | custom-call | flops 11000000512 | tf_op jit(solution)/shard_map/conv_two_back/pallas_call | solution.py:85
  75.7 3.2 %frames_back.4 = (bf16[21,1344,256]{2,1,0:T(8,128)(2,1)}, bf16[10,10,128,256]{3,2,1,0:T(8,128)(2,1)S(1)}, bf16[10,1344,256]{2,1,0:T(8,128)(2,1)S(1)}, bf16[192,256]{1,0:T(8,128)(2,1)S(1)}) custom-call(bf16[10,10,128,256]{3,2,1,0:T(8,128)(2,1)S(1)} %get-tuple-element.259.refs_0_, f32[32,256]{1,0:T(8,128)S(1)} %bitcast.82, ...), custom_call_target="tpu_custom_call", output_to_operand_aliasing={{1}: (0, {})} | custom-call | flops 2000000000 | tf_op jit(solution)/shard_map/frames_back/pallas_call | solution.py:85
  78.9 2.4 %collective-permute-start.15 = (bf16[80,640]{1,0:T(8,128)(2,1)S(1)}, bf16[80,640]{1,0:T(8,128)(2,1)S(1)}, u32[]{:S(2)}, u32[]{:S(2)}) collective-permute-start(bf16[80,640]{1,0:T(8,128)(2,1)S(1)} %add_convert_fusion.6), channel_id=1, source_target_pairs={{0,16},{4,20},{8,24},{12,28},{16,0},{20,4},{24,8},{28,12},{1,17},{... | collective-permute-start | bytes 307208 | tf_op jit(solution)/shard_map/ppermute | solution.py:1020
  81.3 9.1 %conv_one_grad.1 = (f32[16,640]{1,0:T(8,128)S(1)}, bf16[10,10,128,256]{3,2,1,0:T(8,128)(2,1)S(1)}, bf16[10,1344,256]{2,1,0:T(8,128)(2,1)S(1)}) custom-call(bf16[21,1344,256]{2,1,0:T(8,128)(2,1)} %bitcast.104, bf16[10,10,128,256]{3,2,1,0:T(8,128)(2,1)S(1)} %get-tuple-element.270.d_one_ref, ...), custom_call_target="tpu_custom_call", output_to_operand_aliasing={{1}: (1, {}), {2}: (2, {})} | custom-call | flops 10000000000 | tf_op jit(solution)/shard_map/conv_one_grad/pallas_call | solution.py:839
  91.3 1.5 %collective-permute-start.16 = (bf16[80,640]{1,0:T(8,128)(2,1)S(1)}, bf16[80,640]{1,0:T(8,128)(2,1)S(1)}, u32[]{:S(2)}, u32[]{:S(2)}) collective-permute-start(bf16[80,640]{1,0:T(8,128)(2,1)S(1)} %add_convert_fusion.5), channel_id=1, source_target_pairs={{0,2},{1,3},{2,0},{3,1},{4,6},{5,7},{6,4},{7,5},{8,10},{9,11},{10,... | collective-permute-start | bytes 307208 | tf_op jit(solution)/shard_map/ppermute | solution.py:1020
  92.9 3.5 %collective-permute-start.21 = (bf16[392,128]{1,0:T(8,128)(2,1)S(1)}, bf16[392,128]{1,0:T(8,128)(2,1)S(1)}, u32[]{:S(2)}, u32[]{:S(2)}) collective-permute-start(bf16[392,128]{1,0:T(8,128)(2,1)S(1)} %get-tuple-element.382), channel_id=1, source_target_pairs={{0,24},{4,28},{8,16},{12,20},{16,8},{20,12},{24,0},{28,4},{1,25},{... | collective-permute-start | bytes 301064 | tf_op jit(solution)/shard_map/ppermute | solution.py:1020
  97.4 2.4 %frames_back.5 = (bf16[21,1344,256]{2,1,0:T(8,128)(2,1)}, bf16[10,10,128,256]{3,2,1,0:T(8,128)(2,1)S(1)}) custom-call(bf16[10,10,128,256]{3,2,1,0:T(8,128)(2,1)S(1)} %get-tuple-element.291.refs_0_, bf16[192,256]{1,0:T(8,128)(2,1)S(1)} %get-tuple-element.292.refs_1_, ...), custom_call_target="tpu_custom_call", output_to_operand_aliasing={{1}: (0, {}), {0}: (2, {})} | custom-call | flops 3000000000 | tf_op jit(solution)/shard_map/frames_back/pallas_call | solution.py:85
  99.9 1.6 %collective-permute-start.18 = (bf16[112,640]{1,0:T(8,128)(2,1)S(1)}, bf16[112,640]{1,0:T(8,128)(2,1)S(1)}, u32[]{:S(2)}, u32[]{:S(2)}) collective-permute-start(bf16[112,640]{1,0:T(8,128)(2,1)S(1)} %pad_maximum_fusion.5), channel_id=1, source_target_pairs={{0,4},{4,0},{8,12},{12,8},{16,20},{20,16},{24,28},{28,24},{1,5},{5... | collective-permute-start | bytes 430088 | tf_op jit(solution)/shard_map/ppermute | solution.py:1020
  101.4 2.4 %frames_back.6 = (bf16[21,1344,256]{2,1,0:T(8,128)(2,1)}, bf16[10,10,128,256]{3,2,1,0:T(8,128)(2,1)S(1)}) custom-call(bf16[10,10,128,256]{3,2,1,0:T(8,128)(2,1)S(1)} %get-tuple-element.304.refs_0_, bf16[192,256]{1,0:T(8,128)(2,1)S(1)} %get-tuple-element.292.refs_1_, ...), custom_call_target="tpu_custom_call", output_to_operand_aliasing={{1}: (0, {}), {0}: (2, {})} | custom-call | flops 3000000000 | tf_op jit(solution)/shard_map/frames_back/pallas_call | solution.py:85
  103.8 1.2 collective-permute-done.18
  106.4 2.2 %frames_back.7 = (bf16[21,1344,256]{2,1,0:T(8,128)(2,1)}, bf16[10,10,128,256]{3,2,1,0:T(8,128)(2,1)S(1)}) custom-call(bf16[10,10,128,256]{3,2,1,0:T(8,128)(2,1)S(1)} %get-tuple-element.313.refs_0_, bf16[192,256]{1,0:T(8,128)(2,1)S(1)} %get-tuple-element.292.refs_1_, ...), custom_call_target="tpu_custom_call", output_to_operand_aliasing={{1}: (0, {}), {0}: (2, {})} | custom-call | flops 3000000000 | tf_op jit(solution)/shard_map/frames_back/pallas_call | solution.py:85
  108.6 1.8 %collective-permute-done.22 = bf16[112,640]{1,0:T(8,128)(2,1)S(1)} collective-permute-done((bf16[112,640]{1,0:T(8,128)(2,1)S(1)}, bf16[112,640]{1,0:T(8,128)(2,1)S(1)}, u32[]{:S(2)}, u32[]{:S(2)}) %collective-permute-start.22) | collective-permute-done | bytes 143392 | tf_op jit(solution)/shard_map/ppermute | solution.py:1020
  110.7 1.4 %dense_step.1 = (f32[392,128]{1,0:T(8,128)}, f32[392,128]{1,0:T(8,128)}, f32[392,128]{1,0:T(8,128)}, f32[392,128]{1,0:T(8,128)}) custom-call(f32[392,128]{1,0:T(8,128)S(1)} %copy-done, f32[392,128]{1,0:T(8,128)S(1)} %copy-done.7, f32[392,128]{1,0:T(8,128)S(1)} %copy-done.8, f32[1,128,128]{2,1,0:T(8,128)S(1)} %copy-done.15, ...), custom_call_target="tpu_custom_call" | custom-call | flops 3000000000 | tf_op jit(solution)/shard_map/dense_step/pallas_call | solution.py:1008
  112.2 2.5 %collective-permute-start.24 = (f32[16,640]{1,0:T(8,128)S(1)}, f32[16,640]{1,0:T(8,128)S(1)}, u32[]{:S(2)}, u32[]{:S(2)}) collective-permute-start(f32[16,640]{1,0:T(8,128)S(1)} %fusion.2), channel_id=1, source_target_pairs={{0,2},{1,3},{2,0},{3,1},{4,6},{5,7},{6,4},{7,5},{8,10},{9,11},{10,... | collective-permute-start | bytes 122888 | tf_op jit(solution)/shard_map/ppermute | solution.py:1020
  114.9 3.1 %steps.2 = (f32[64,576]{1,0:T(8,128)}, f32[64,576]{1,0:T(8,128)}, f32[64,576]{1,0:T(8,128)}, f32[64,576]{1,0:T(8,128)}, f32[19,512]{1,0:T(8,128)}, /*index=5*/f3...) custom-call(bf16[160,640]{1,0:T(8,128)(2,1)S(1)} %pad_maximum_fusion, ...), custom_call_target="tpu_custom_call" | custom-call | flops 5000000000 | tf_op jit(solution)/shard_map/steps/pallas_call | solution.py:980
  118.8 1.2 %steps.3 = (f32[32,256]{1,0:T(8,128)}, f32[32,256]{1,0:T(8,128)}, f32[32,256]{1,0:T(8,128)}, f32[32,256]{1,0:T(8,128)}) custom-call(f32[16,640]{1,0:T(8,128)S(1)} %add.108.refs_0_, f32[32,256]{1,0:T(8,128)S(1)} %bitcast.83, f32[32,256]{1,0:T(8,128)S(1)} %bitcast.98, f32[32,256]{1,0:T(8,128)S(1)} %bitcast.99, f32[256,256]{1,0:T(8,128)S(1)} %copy-done.6, ...), custom_call_target="tpu_custom_call" | custom-call | flops 5000000000 | tf_op jit(solution)/shard_map/steps/pallas_call | solution.py:980
  (145 shorter events, 8.7 us)
Async XLA Ops:
  1.3 8.4 %copy-start.29 = (f32[691]{0:T(1024)S(1)}, f32[691]{0:T(1024)}, u32[]{:S(2)}) copy-start(f32[691]{0:T(1024)} %param.46) | copy-start | bytes 8296
  1.3 8.4 %copy-start.1 = (f32[256,32]{0,1:T(8,128)S(1)}, f32[256,32]{0,1:T(8,128)}, u32[]{:S(2)}) copy-start(f32[256,32]{0,1:T(8,128)} %param.41) | copy-start | bytes 98308
  4.0 16.0 %copy-start.25 = (f32[1,256]{1,0:T(1,128)}, f32[1,256]{1,0:T(1,128)S(1)}, u32[]{:S(2)}) copy-start(f32[1,256]{1,0:T(1,128)S(1)} %get-tuple-element.197.refs_5_) | copy-start | bytes 3076
  4.0 16.0 %collective-permute-start.2 = (bf16[400,128]{1,0:T(8,128)(2,1)S(1)}, bf16[400,128]{1,0:T(8,128)(2,1)S(1)}, u32[]{:S(2)}, u32[]{:S(2)}) collective-permute-start(bf16[400,128]{1,0:T(8,128)(2,1)S(1)} %get-tuple-element.204), channel_id=1, source_target_pairs={{0,24},{4,28},{8,16},{12,20},{16,8},{20,12},{24,0},{28,4},{1,25},{... | collective-permute-start | bytes 307208 | tf_op jit(solution)/shard_map/ppermute | solution.py:1020
  9.1 10.9 %collective-permute-start.1 = (bf16[400,128]{1,0:T(8,128)(2,1)S(1)}, bf16[400,128]{1,0:T(8,128)(2,1)S(1)}, u32[]{:S(2)}, u32[]{:S(2)}) collective-permute-start(bf16[400,128]{1,0:T(8,128)(2,1)S(1)} %get-tuple-element.204), channel_id=1, source_target_pairs={{0,16},{4,20},{8,24},{12,28},{16,0},{20,4},{24,8},{28,12},{1,17},{... | collective-permute-start | bytes 307208 | tf_op jit(solution)/shard_map/ppermute | solution.py:1020
  9.1 10.9 %collective-permute-start = (bf16[400,128]{1,0:T(8,128)(2,1)S(1)}, bf16[400,128]{1,0:T(8,128)(2,1)S(1)}, u32[]{:S(2)}, u32[]{:S(2)}) collective-permute-start(bf16[400,128]{1,0:T(8,128)(2,1)S(1)} %get-tuple-element.204), channel_id=1, source_target_pairs={{0,8},{4,12},{8,0},{12,4},{16,24},{20,28},{24,16},{28,20},{1,9},{5... | collective-permute-start | bytes 307208 | tf_op jit(solution)/shard_map/ppermute | solution.py:1020
  9.8 24.7 %copy-start.2 = (f32[1,691]{1,0:T(1,128)}, f32[1,691]{1,0:T(1,128)S(1)}, u32[]{:S(2)}) copy-start(f32[1,691]{1,0:T(1,128)S(1)} %reshape.64.bias_ref.refs_3_) | copy-start | bytes 8296
  9.8 13.6 %copy-start.12 = (f32[512,64]{0,1:T(8,128)S(1)}, f32[512,64]{0,1:T(8,128)}, u32[]{:S(2)}) copy-start(f32[512,64]{0,1:T(8,128)} %param.42) | copy-start | bytes 393220
  20.1 10.7 %collective-permute-start.4 = (bf16[4,400,128]{2,1,0:T(8,128)(2,1)S(1)}, bf16[4,400,128]{2,1,0:T(8,128)(2,1)S(1)}, u32[]{:S(2)}, u32[]{:S(2)}) collective-permute-start(bf16[4,400,128]{2,1,0:T(8,128)(2,1)S(1)} %pad_maximum_fusion.1), channel_id=1, source_target_pairs={{0,2},{1,3},{2,0},{3,1},{4,6},{5,7},{6,4},{7,5},{8,10},{9,11},{10,... | collective-permute-start | bytes 1228808 | tf_op jit(solution)/shard_map/ppermute | solution.py:1020
  21.9 10.2 %collective-permute-start.3 = (bf16[4,400,128]{2,1,0:T(8,128)(2,1)S(1)}, bf16[4,400,128]{2,1,0:T(8,128)(2,1)S(1)}, u32[]{:S(2)}, u32[]{:S(2)}) collective-permute-start(bf16[4,400,128]{2,1,0:T(8,128)(2,1)S(1)} %pad_maximum_fusion.1), channel_id=1, source_target_pairs={{0,4},{4,0},{8,12},{12,8},{16,20},{20,16},{24,28},{28,24},{1,5},{5... | collective-permute-start | bytes 1228808 | tf_op jit(solution)/shard_map/ppermute | solution.py:1020
  32.3 7.6 %copy-start.27 = (bf16[12,400,128]{2,1,0:T(8,128)(2,1)}, bf16[12,400,128]{2,1,0:T(8,128)(2,1)S(1)}, u32[]{:S(2)}) copy-start(bf16[12,400,128]{2,1,0:T(8,128)(2,1)S(1)} %pad_maximum_fusion.refs_11_) | copy-start | bytes 3686404
  32.3 9.7 %collective-permute-start.7 = (bf16[12,400,128]{2,1,0:T(8,128)(2,1)S(1)}, bf16[12,400,128]{2,1,0:T(8,128)(2,1)}, u32[]{:S(2)}, u32[]{:S(2)}) collective-permute-start(bf16[12,400,128]{2,1,0:T(8,128)(2,1)S(1)} %pad_maximum_fusion.refs_11_), channel_id=1, source_target_pairs={{0,1},{1,0},{2,3},{3,2},{4,5},{5,4},{6,7},{7,6},{8,9},{9,8},{10,11... | collective-permute-start | bytes 3686408 | tf_op jit(solution)/shard_map/ppermute | solution.py:1020
  32.4 7.5 %collective-permute-start.5 = (bf16[2,400,128]{2,1,0:T(8,128)(2,1)S(1)}, bf16[2,400,128]{2,1,0:T(8,128)(2,1)S(1)}, u32[]{:S(2)}, u32[]{:S(2)}) collective-permute-start(bf16[2,400,128]{2,1,0:T(8,128)(2,1)S(1)} %slice.144), channel_id=1, source_target_pairs={{0,2},{1,3},{2,0},{3,1},{4,6},{5,7},{6,4},{7,5},{8,10},{9,11},{10,... | collective-permute-start | bytes 614408 | tf_op jit(solution)/shard_map/ppermute | solution.py:1020
  32.9 7.1 %collective-permute-start.6 = (bf16[2,400,128]{2,1,0:T(8,128)(2,1)S(1)}, bf16[2,400,128]{2,1,0:T(8,128)(2,1)S(1)}, u32[]{:S(2)}, u32[]{:S(2)}) collective-permute-start(bf16[2,400,128]{2,1,0:T(8,128)(2,1)S(1)} %slice.145), channel_id=1, source_target_pairs={{0,4},{4,0},{8,12},{12,8},{16,20},{20,16},{24,28},{28,24},{1,5},{5... | collective-permute-start | bytes 614408 | tf_op jit(solution)/shard_map/ppermute | solution.py:1020
  40.1 1.8 %collective-permute-start.8 = (bf16[4,400,128]{2,1,0:T(8,128)(2,1)S(1)}, bf16[4,400,128]{2,1,0:T(8,128)(2,1)S(1)}, u32[]{:S(2)}, u32[]{:S(2)}) collective-permute-start(bf16[4,400,128]{2,1,0:T(8,128)(2,1)S(1)} %constant_dynamic-update-slice_fusion.refs_12_), channel_id=1, source_target_pairs={{0,1},{1,0},{2,3},{3,2},{4,5},{5,4},{6,7},{7,6},{8,9},{9,8},{10,11... | collective-permute-start | bytes 1228808 | tf_op jit(solution)/shard_map/ppermute | solution.py:1020
  52.3 8.6 %collective-permute-start.9 = (bf16[2,8,392,128]{3,2,1,0:T(8,128)(2,1)}, bf16[2,8,392,128]{3,2,1,0:T(8,128)(2,1)}, u32[]{:S(2)}, u32[]{:S(2)}) collective-permute-start(bf16[2,8,392,128]{3,2,1,0:T(8,128)(2,1)} %get-tuple-element.239), channel_id=1, source_target_pairs={{0,1},{1,0},{2,3},{3,2},{4,5},{5,4},{6,7},{7,6},{8,9},{9,8},{10,11... | collective-permute-start | bytes 4816904 | tf_op jit(solution)/shard_map/ppermute | solution.py:1020
  52.5 8.4 %copy-start.26 = (bf16[2,8,392,128]{3,2,1,0:T(8,128)(2,1)S(1)}, bf16[2,8,392,128]{3,2,1,0:T(8,128)(2,1)}, u32[]{:S(2)}) copy-start(bf16[2,8,392,128]{3,2,1,0:T(8,128)(2,1)} %get-tuple-element.243) | copy-start | bytes 4816900
  62.8 11.4 %collective-permute-start.10 = (bf16[2,392,128]{2,1,0:T(8,128)(2,1)S(1)}, bf16[2,392,128]{2,1,0:T(8,128)(2,1)S(1)}, u32[]{:S(2)}, u32[]{:S(2)}) collective-permute-start(bf16[2,392,128]{2,1,0:T(8,128)(2,1)S(1)} %get-tuple-element.252), channel_id=1, source_target_pairs={{0,4},{4,0},{8,12},{12,8},{16,20},{20,16},{24,28},{28,24},{1,5},{5... | collective-permute-start | bytes 602120 | tf_op jit(solution)/shard_map/ppermute | solution.py:1020
  64.4 9.8 %collective-permute-start.11 = (bf16[2,392,128]{2,1,0:T(8,128)(2,1)S(1)}, bf16[2,392,128]{2,1,0:T(8,128)(2,1)S(1)}, u32[]{:S(2)}, u32[]{:S(2)}) collective-permute-start(bf16[2,392,128]{2,1,0:T(8,128)(2,1)S(1)} %get-tuple-element.253), channel_id=1, source_target_pairs={{0,2},{1,3},{2,0},{3,1},{4,6},{5,7},{6,4},{7,5},{8,10},{9,11},{10,... | collective-permute-start | bytes 602120 | tf_op jit(solution)/shard_map/ppermute | solution.py:1020
  74.5 4.4 %collective-permute-start.12 = (bf16[80,640]{1,0:T(8,128)(2,1)S(1)}, bf16[80,640]{1,0:T(8,128)(2,1)S(1)}, u32[]{:S(2)}, u32[]{:S(2)}) collective-permute-start(bf16[80,640]{1,0:T(8,128)(2,1)S(1)} %get-tuple-element.264), channel_id=1, source_target_pairs={{0,1},{1,0},{2,3},{3,2},{4,5},{5,4},{6,7},{7,6},{8,9},{9,8},{10,11... | collective-permute-start | bytes 307208 | tf_op jit(solution)/shard_map/ppermute | solution.py:1020
  74.6 15.8 %collective-permute-start.13 = (bf16[4,392,128]{2,1,0:T(8,128)(2,1)S(1)}, bf16[4,392,128]{2,1,0:T(8,128)(2,1)S(1)}, u32[]{:S(2)}, u32[]{:S(2)}) collective-permute-start(bf16[4,392,128]{2,1,0:T(8,128)(2,1)S(1)} %get-tuple-element.279), channel_id=1, source_target_pairs={{0,4},{4,0},{8,12},{12,8},{16,20},{20,16},{24,28},{28,24},{1,5},{5... | collective-permute-start | bytes 1204232 | tf_op jit(solution)/shard_map/ppermute | solution.py:1020
  75.2 15.2 %collective-permute-start.14 = (bf16[4,392,128]{2,1,0:T(8,128)(2,1)S(1)}, bf16[4,392,128]{2,1,0:T(8,128)(2,1)S(1)}, u32[]{:S(2)}, u32[]{:S(2)}) collective-permute-start(bf16[4,392,128]{2,1,0:T(8,128)(2,1)S(1)} %get-tuple-element.280), channel_id=1, source_target_pairs={{0,2},{1,3},{2,0},{3,1},{4,6},{5,7},{6,4},{7,5},{8,10},{9,11},{10,... | collective-permute-start | bytes 1204232 | tf_op jit(solution)/shard_map/ppermute | solution.py:1020
  78.9 11.5 %collective-permute-start.15 = (bf16[80,640]{1,0:T(8,128)(2,1)S(1)}, bf16[80,640]{1,0:T(8,128)(2,1)S(1)}, u32[]{:S(2)}, u32[]{:S(2)}) collective-permute-start(bf16[80,640]{1,0:T(8,128)(2,1)S(1)} %add_convert_fusion.6), channel_id=1, source_target_pairs={{0,16},{4,20},{8,24},{12,28},{16,0},{20,4},{24,8},{28,12},{1,17},{... | collective-permute-start | bytes 307208 | tf_op jit(solution)/shard_map/ppermute | solution.py:1020
  90.6 9.1 %collective-permute-start.17 = (f32[16,640]{1,0:T(8,128)S(1)}, f32[16,640]{1,0:T(8,128)S(1)}, u32[]{:S(2)}, u32[]{:S(2)}) collective-permute-start(f32[16,640]{1,0:T(8,128)S(1)} %get-tuple-element.302), channel_id=1, source_target_pairs={{0,16},{4,20},{8,24},{12,28},{16,0},{20,4},{24,8},{28,12},{1,17},{... | collective-permute-start | bytes 122888 | tf_op jit(solution)/shard_map/ppermute | solution.py:1020
  91.3 8.4 %collective-permute-start.16 = (bf16[80,640]{1,0:T(8,128)(2,1)S(1)}, bf16[80,640]{1,0:T(8,128)(2,1)S(1)}, u32[]{:S(2)}, u32[]{:S(2)}) collective-permute-start(bf16[80,640]{1,0:T(8,128)(2,1)S(1)} %add_convert_fusion.5), channel_id=1, source_target_pairs={{0,2},{1,3},{2,0},{3,1},{4,6},{5,7},{6,4},{7,5},{8,10},{9,11},{10,... | collective-permute-start | bytes 307208 | tf_op jit(solution)/shard_map/ppermute | solution.py:1020
  92.9 15.7 %collective-permute-start.21 = (bf16[392,128]{1,0:T(8,128)(2,1)S(1)}, bf16[392,128]{1,0:T(8,128)(2,1)S(1)}, u32[]{:S(2)}, u32[]{:S(2)}) collective-permute-start(bf16[392,128]{1,0:T(8,128)(2,1)S(1)} %get-tuple-element.382), channel_id=1, source_target_pairs={{0,24},{4,28},{8,16},{12,20},{16,8},{20,12},{24,0},{28,4},{1,25},{... | collective-permute-start | bytes 301064 | tf_op jit(solution)/shard_map/ppermute | solution.py:1020
  96.4 12.1 %collective-permute-start.20 = (bf16[392,128]{1,0:T(8,128)(2,1)S(1)}, bf16[392,128]{1,0:T(8,128)(2,1)S(1)}, u32[]{:S(2)}, u32[]{:S(2)}) collective-permute-start(bf16[392,128]{1,0:T(8,128)(2,1)S(1)} %get-tuple-element.383), channel_id=1, source_target_pairs={{0,16},{4,20},{8,24},{12,28},{16,0},{20,4},{24,8},{28,12},{1,17},{... | collective-permute-start | bytes 301064 | tf_op jit(solution)/shard_map/ppermute | solution.py:1020
  96.4 12.1 %collective-permute-start.19 = (bf16[392,128]{1,0:T(8,128)(2,1)S(1)}, bf16[392,128]{1,0:T(8,128)(2,1)S(1)}, u32[]{:S(2)}, u32[]{:S(2)}) collective-permute-start(bf16[392,128]{1,0:T(8,128)(2,1)S(1)} %get-tuple-element.384), channel_id=1, source_target_pairs={{0,8},{4,12},{8,0},{12,4},{16,24},{20,28},{24,16},{28,20},{1,9},{5... | collective-permute-start | bytes 301064 | tf_op jit(solution)/shard_map/ppermute | solution.py:1020
  99.9 5.2 %collective-permute-start.18 = (bf16[112,640]{1,0:T(8,128)(2,1)S(1)}, bf16[112,640]{1,0:T(8,128)(2,1)S(1)}, u32[]{:S(2)}, u32[]{:S(2)}) collective-permute-start(bf16[112,640]{1,0:T(8,128)(2,1)S(1)} %pad_maximum_fusion.5), channel_id=1, source_target_pairs={{0,4},{4,0},{8,12},{12,8},{16,20},{20,16},{24,28},{28,24},{1,5},{5... | collective-permute-start | bytes 430088 | tf_op jit(solution)/shard_map/ppermute | solution.py:1020
  105.2 5.2 %collective-permute-start.22 = (bf16[112,640]{1,0:T(8,128)(2,1)S(1)}, bf16[112,640]{1,0:T(8,128)(2,1)S(1)}, u32[]{:S(2)}, u32[]{:S(2)}) collective-permute-start(bf16[112,640]{1,0:T(8,128)(2,1)S(1)} %pad_maximum_fusion.6), channel_id=1, source_target_pairs={{0,8},{4,12},{8,0},{12,4},{16,24},{20,28},{24,16},{28,20},{1,9},{5... | collective-permute-start | bytes 430088 | tf_op jit(solution)/shard_map/ppermute | solution.py:1020
  110.6 1.5 %collective-permute-start.23 = (bf16[112,640]{1,0:T(8,128)(2,1)S(1)}, bf16[112,640]{1,0:T(8,128)(2,1)S(1)}, u32[]{:S(2)}, u32[]{:S(2)}) collective-permute-start(bf16[112,640]{1,0:T(8,128)(2,1)S(1)} %pad_maximum_fusion.7), channel_id=1, source_target_pairs={{0,1},{1,0},{2,3},{3,2},{4,5},{5,4},{6,7},{7,6},{8,9},{9,8},{10,11... | collective-permute-start | bytes 430088 | tf_op jit(solution)/shard_map/ppermute | solution.py:1020
  112.2 5.7 %collective-permute-start.24 = (f32[16,640]{1,0:T(8,128)S(1)}, f32[16,640]{1,0:T(8,128)S(1)}, u32[]{:S(2)}, u32[]{:S(2)}) collective-permute-start(f32[16,640]{1,0:T(8,128)S(1)} %fusion.2), channel_id=1, source_target_pairs={{0,2},{1,3},{2,0},{3,1},{4,6},{5,7},{6,4},{7,5},{8,10},{9,11},{10,... | collective-permute-start | bytes 122888 | tf_op jit(solution)/shard_map/ppermute | solution.py:1020
  (27 other events, 108.9 us)

commit v7 on v6

--- a/solution.py
+++ b/solution.py
@@ -1144,7 +1144,7 @@
     if tuned:
         by_x, by_y = dp_swap(side_x, 1), own_swap(side_y, 2)
     came = own_swap(gone, 1)
-    cuts = (0, 2, 5, 8, grid // 2 + 1)
+    cuts = (0, 1, 4, 7, grid // 2 + 1)
     back, d_one, ring, band = frames_back(d_one, conv_first.T, shape, cuts[0], cuts[1], frames=cells)
     back, d_one, ring, half, came = fence(back, d_one, ring, half, came)
     half = add_low(half, came)

time: 120 us -> 135 us (1.12)
  local copies, waits for them, and re-layouts: 1.29 us -> 18 us
  starting transfers between devices: 30 us -> 28.1 us
    unnamed x69 -> x81, local copies, waits for them, and re-layouts: 0.95 us -> 17.7 us
    ppermute x25, starting transfers between devices: 30 us -> 28.1 us  [swap(): return lax.ppermute(x, axis, [(i, i ^ bit) for i in range(size)])]
  transfers between devices with their start and end apart: 25 -> 25, of which waited for: 6 -> 7; matrix products, arithmetic and copies ran while one was open for 0% -> 0% of each run, Pallas kernels for 51% -> 46%
where the time goes in v7:
time: 135 us
  Pallas kernels  75.5 us (56%)
  starting transfers between devices  28.1 us (21%)
  local copies, waits for them, and re-layouts  18 us (13%)
  waiting for transfers between devices  7.63 us (6%)
  other arithmetic  3.45 us (3%)
  between operations  2.16 us (2%)
    pallas_call x10, Pallas kernels, call(): pl.pallas_call(body, out_shape=tuple(outs), in_specs=list(in_specs or [vm...  57.8 us
    ppermute x25, starting transfers between devices, swap(): return lax.ppermute(x, axis, [(i, i ^ bit) for i in range(size)])  28.1 us
    unnamed x81, local copies, waits for them, and re-layouts  17.7 us
    pallas_call x1, Pallas kernels, conv_one_grad(): pl.pallas_call(conv_one_grad_kernel, out_shape=(jax.ShapeDtypeStruct((16,...  9.33 us
    ppermute x25, waiting for transfers between devices, swap(): return lax.ppermute(x, axis, [(i, i ^ bit) for i in range(size)])  7.63 us
    pallas_call x2, Pallas kernels, steps(): pl.pallas_call(functools.partial(steps_kernel, spots=spots), out_shape=tu...  4.33 us
  transfers between devices with their start and end apart: 25, of which 7 were waited for; matrix products, arithmetic and copies ran while one was open for 0% of the time, Pallas kernels for 46%

profile of v7, /device:TPU:0, one launch (start us, length us, event | category | flops | bytes accessed | tf_op | source)
XLA Modules:
  0.0 134.8 jit_solution(12022482032658391020)
XLA Ops:
  1.3 2.6 %first.1 = (f32[1,256]{1,0:T(1,128)S(1)}, bf16[400,128]{1,0:T(8,128)(2,1)S(1)}, bf16[10,1344,256]{2,1,0:T(8,128)(2,1)S(1)}) custom-call(s32[1]{0:T(128)S(6)} %copy.80.lengths_ref.refs_1_, s32[1,256]{1,0:T(1,128)} %dones_far_ref.1, f32[1,256]{1,0:T(1,128)} %rewards_far_ref.1, f32[1,256]{1,0:T(1,128)} %refs_6_.1, f32[392,128]{1,0:T(8,128)} %refs_0_.1, ...), custom_call_target="tpu_custom_call" | custom-call | flops 3000000000 | tf_op jit(solution)/shard_map/first/pallas_call | solution.py:238
  4.0 5.1 %collective-permute-start.2 = (bf16[400,128]{1,0:T(8,128)(2,1)S(1)}, bf16[400,128]{1,0:T(8,128)(2,1)S(1)}, u32[]{:S(2)}, u32[]{:S(2)}) collective-permute-start(bf16[400,128]{1,0:T(8,128)(2,1)S(1)} %get-tuple-element.204), channel_id=1, source_target_pairs={{0,24},{4,28},{8,16},{12,20},{16,8},{20,12},{24,0},{28,4},{1,25},{... | collective-permute-start | bytes 307208 | tf_op jit(solution)/shard_map/ppermute | solution.py:1020
  9.8 10.2 %conv_one.1 = (bf16[10,10,128,256]{3,2,1,0:T(8,128)(2,1)S(1)}, bf16[10,10,128,256]{3,2,1,0:T(8,128)(2,1)S(1)}, bf16[10,1344,256]{2,1,0:T(8,128)(2,1)S(1)}) custom-call(bf16[21,1344,256]{2,1,0:T(8,128)(2,1)} %bitcast.102, f32[32,256]{1,0:T(8,128)S(1)} %bitcast.81, f32[1,691]{1,0:T(1,128)S(1)} %reshape.64.bias_ref.refs_3_, ...), custom_call_target="tpu_custom_call", output_to_operand_aliasing={{2}: (3, {})} | custom-call | flops 12000000000 | tf_op jit(solution)/shard_map/conv_one/pallas_call | solution.py:85
  20.1 1.7 %collective-permute-start.4 = (bf16[4,400,128]{2,1,0:T(8,128)(2,1)S(1)}, bf16[4,400,128]{2,1,0:T(8,128)(2,1)S(1)}, u32[]{:S(2)}, u32[]{:S(2)}) collective-permute-start(bf16[4,400,128]{2,1,0:T(8,128)(2,1)S(1)} %pad_maximum_fusion.1), channel_id=1, source_target_pairs={{0,2},{1,3},{2,0},{3,1},{4,6},{5,7},{6,4},{7,5},{8,10},{9,11},{10,... | collective-permute-start | bytes 1228808 | tf_op jit(solution)/shard_map/ppermute | solution.py:1020
  21.9 1.5 %collective-permute-start.3 = (bf16[4,400,128]{2,1,0:T(8,128)(2,1)S(1)}, bf16[4,400,128]{2,1,0:T(8,128)(2,1)S(1)}, u32[]{:S(2)}, u32[]{:S(2)}) collective-permute-start(bf16[4,400,128]{2,1,0:T(8,128)(2,1)S(1)} %pad_maximum_fusion.1), channel_id=1, source_target_pairs={{0,4},{4,0},{8,12},{12,8},{16,20},{20,16},{24,28},{28,24},{1,5},{5... | collective-permute-start | bytes 1228808 | tf_op jit(solution)/shard_map/ppermute | solution.py:1020
  23.4 5.6 %conv_two.1 = (bf16[9,576,256]{2,1,0:T(8,128)(2,1)S(1)}, bf16[9,576,256]{2,1,0:T(8,128)(2,1)S(1)}, bf16[10,10,128,256]{3,2,1,0:T(8,128)(2,1)}, bf16[10,10,128,256]{3,2,1,0:T(8,128)(2,1)}) custom-call(bf16[10,10,128,256]{3,2,1,0:T(8,128)(2,1)S(1)} %get-tuple-element.208.one_ref, bf16[10,10,128,256]{3,2,1,0:T(8,128)(2,1)S(1)} %get-tuple-element.209.slope_one_ref, ...), custom_call_target="tpu_custom_call" | custom-call | flops 7000000000 | tf_op jit(solution)/shard_map/conv_two/pallas_call | solution.py:85
  29.0 1.9 %collective-permute-done.4 = bf16[4,400,128]{2,1,0:T(8,128)(2,1)S(1)} collective-permute-done((bf16[4,400,128]{2,1,0:T(8,128)(2,1)S(1)}, bf16[4,400,128]{2,1,0:T(8,128)(2,1)S(1)}, u32[]{:S(2)}, u32[]{:S(2)}) %collective-permute-start.4) | collective-permute-done | bytes 409632 | tf_op jit(solution)/shard_map/ppermute | solution.py:1020
  32.9 1.5 %collective-permute-start.6 = (bf16[2,400,128]{2,1,0:T(8,128)(2,1)S(1)}, bf16[2,400,128]{2,1,0:T(8,128)(2,1)S(1)}, u32[]{:S(2)}, u32[]{:S(2)}) collective-permute-start(bf16[2,400,128]{2,1,0:T(8,128)(2,1)S(1)} %slice.145), channel_id=1, source_target_pairs={{0,4},{4,0},{8,12},{12,8},{16,20},{20,16},{24,28},{28,24},{1,5},{5... | collective-permute-start | bytes 614408 | tf_op jit(solution)/shard_map/ppermute | solution.py:1020
  34.4 5.5 %conv_three.1 = (bf16[7,448,256]{2,1,0:T(8,128)(2,1)}, bf16[7,448,256]{2,1,0:T(8,128)(2,1)}, bf16[9,576,256]{2,1,0:T(8,128)(2,1)}, bf16[9,576,256]{2,1,0:T(8,128)(2,1)}) custom-call(bf16[9,576,256]{2,1,0:T(8,128)(2,1)S(1)} %get-tuple-element.218.two_ref, bf16[9,576,256]{2,1,0:T(8,128)(2,1)S(1)} %get-tuple-element.219.slope_two_ref, f32[64,576]{1,0:T(8,128)S(1)} %bitcast.84, ...), custom_call_target="tpu_custom_call" | custom-call | flops 6000000000 | tf_op jit(solution)/shard_map/conv_three/pallas_call | solution.py:85
  40.3 1.6 %collective-permute-done.8.refs_14_ = bf16[4,400,128]{2,1,0:T(8,128)(2,1)S(1)} collective-permute-done((bf16[4,400,128]{2,1,0:T(8,128)(2,1)S(1)}, bf16[4,400,128]{2,1,0:T(8,128)(2,1)S(1)}, u32[]{:S(2)}, u32[]{:S(2)}) %collective-permute-start.8) | collective-permute-done | bytes 409632 | tf_op jit(solution)/shard_map/ppermute | solution.py:1020
  42.7 9.5 %dense.1 = (bf16[7,448,256]{2,1,0:T(8,128)(2,1)}, bf16[9,576,256]{2,1,0:T(8,128)(2,1)S(1)}, bf16[2,8,392,128]{3,2,1,0:T(8,128)(2,1)}, bf16[2,8,392,128]{3,2,1,0:...) custom-call(s32[2]{0:T(128)S(1)} %pad_add_fusion.refs_0_, ...), custom_call_target="tpu_custom_call" | custom-call | flops 10000000000 | tf_op jit(solution)/shard_map/dense/pallas_call | solution.py:85
  52.4 8.4 %conv_three_back.1 = (bf16[9,576,256]{2,1,0:T(8,128)(2,1)S(1)}, bf16[10,10,128,256]{3,2,1,0:T(8,128)(2,1)S(1)}, bf16[10,10,128,256]{3,2,1,0:T(8,128)(2,1)S(1)}, bf16[96,640]{1,0:T(8,128)(2,1)S(1)}, f32[1,64]{1,0:T(1,128)S(1)}) custom-call(bf16[9,576,256]{2,1,0:T(8,128)(2,1)S(1)} %get-tuple-element.229.act_ref, ...), custom_call_target="tpu_custom_call" | custom-call | flops 8999999488 | tf_op jit(solution)/shard_map/conv_three_back/pallas_call | solution.py:85
  60.9 1.8 %add_convert_fusion = bf16[2,8,392,128]{3,2,1,0:T(8,128)(2,1)S(1)} fusion(bf16[2,8,392,128]{3,2,1,0:T(8,128)(2,1)} %collective-permute-done.9, bf16[2,8,392,128]{3,2,1,0:T(8,128)(2,1)S(1)} %copy-done.32), kind=kLoop, calls=%fused_computation | loop fusion | flops 3211264 | bytes 4816896 | tf_op jit(solution)/shard_map/convert_element_type | solution.py:1036
  62.8 1.6 %collective-permute-start.10 = (bf16[2,392,128]{2,1,0:T(8,128)(2,1)S(1)}, bf16[2,392,128]{2,1,0:T(8,128)(2,1)S(1)}, u32[]{:S(2)}, u32[]{:S(2)}) collective-permute-start(bf16[2,392,128]{2,1,0:T(8,128)(2,1)S(1)} %get-tuple-element.252), channel_id=1, source_target_pairs={{0,4},{4,0},{8,12},{12,8},{16,20},{20,16},{24,28},{28,24},{1,5},{5... | collective-permute-start | bytes 602120 | tf_op jit(solution)/shard_map/ppermute | solution.py:1020
  64.3 1.5 %collective-permute-start.11 = (bf16[2,392,128]{2,1,0:T(8,128)(2,1)S(1)}, bf16[2,392,128]{2,1,0:T(8,128)(2,1)S(1)}, u32[]{:S(2)}, u32[]{:S(2)}) collective-permute-start(bf16[2,392,128]{2,1,0:T(8,128)(2,1)S(1)} %get-tuple-element.253), channel_id=1, source_target_pairs={{0,2},{1,3},{2,0},{3,1},{4,6},{5,7},{6,4},{7,5},{8,10},{9,11},{10,... | collective-permute-start | bytes 602120 | tf_op jit(solution)/shard_map/ppermute | solution.py:1020
  65.8 8.3 %conv_two_back.1 = (bf16[10,10,128,256]{3,2,1,0:T(8,128)(2,1)S(1)}, bf16[160,640]{1,0:T(8,128)(2,1)S(1)}, f32[1,32]{1,0:T(1,128)S(1)}) custom-call(bf16[9,576,256]{2,1,0:T(8,128)(2,1)S(1)} %get-tuple-element.245.d_two_ref, bf16[10,10,128,256]{3,2,1,0:T(8,128)(2,1)S(1)} %get-tuple-element.246.act_ref, ...), custom_call_target="tpu_custom_call" | custom-call | flops 11000000512 | tf_op jit(solution)/shard_map/conv_two_back/pallas_call | solution.py:85
  74.1 2.8 %copy-done = bf16[10,10,128,256]{3,2,1,0:T(8,128)(2,1)} copy-done((bf16[10,10,128,256]{3,2,1,0:T(8,128)(2,1)}, bf16[10,10,128,256]{3,2,1,0:T(8,128)(2,1)S(1)}, u32[]{:S(2)}) %copy-start) | copy-done | bytes 6553624
  78.4 2.9 %copy-done.1 = bf16[10,10,128,256]{3,2,1,0:T(8,128)(2,1)S(1)} copy-done((bf16[10,10,128,256]{3,2,1,0:T(8,128)(2,1)S(1)}, bf16[10,10,128,256]{3,2,1,0:T(8,128)(2,1)}, u32[]{:S(2)}) %copy-start.1) | copy-done | bytes 6553624
  81.3 2.8 %frames_back.4 = (bf16[21,1344,256]{2,1,0:T(8,128)(2,1)}, bf16[10,10,128,256]{3,2,1,0:T(8,128)(2,1)S(1)}, bf16[10,1344,256]{2,1,0:T(8,128)(2,1)S(1)}, bf16[192,256]{1,0:T(8,128)(2,1)S(1)}) custom-call(bf16[10,10,128,256]{3,2,1,0:T(8,128)(2,1)S(1)} %copy-done.1, f32[32,256]{1,0:T(8,128)S(1)} %bitcast.82, ...), custom_call_target="tpu_custom_call", output_to_operand_aliasing={{1}: (0, {})} | custom-call | flops 1000000000 | tf_op jit(solution)/shard_map/frames_back/pallas_call | solution.py:85
  84.2 2.7 %copy-done.2 = bf16[10,10,128,256]{3,2,1,0:T(8,128)(2,1)} copy-done((bf16[10,10,128,256]{3,2,1,0:T(8,128)(2,1)}, bf16[10,10,128,256]{3,2,1,0:T(8,128)(2,1)S(1)}, u32[]{:S(2)}) %copy-start.2) | copy-done | bytes 6553624
  86.8 2.4 %collective-permute-start.15 = (bf16[80,640]{1,0:T(8,128)(2,1)S(1)}, bf16[80,640]{1,0:T(8,128)(2,1)S(1)}, u32[]{:S(2)}, u32[]{:S(2)}) collective-permute-start(bf16[80,640]{1,0:T(8,128)(2,1)S(1)} %add_convert_fusion.6), channel_id=1, source_target_pairs={{0,16},{4,20},{8,24},{12,28},{16,0},{20,4},{24,8},{28,12},{1,17},{... | collective-permute-start | bytes 307208 | tf_op jit(solution)/shard_map/ppermute | solution.py:1020
  89.2 2.9 %copy-done.3 = bf16[10,10,128,256]{3,2,1,0:T(8,128)(2,1)S(1)} copy-done((bf16[10,10,128,256]{3,2,1,0:T(8,128)(2,1)S(1)}, bf16[10,10,128,256]{3,2,1,0:T(8,128)(2,1)}, u32[]{:S(2)}) %copy-start.3) | copy-done | bytes 6553624
  92.1 9.3 %conv_one_grad.1 = (f32[16,640]{1,0:T(8,128)S(1)}, bf16[10,10,128,256]{3,2,1,0:T(8,128)(2,1)S(1)}, bf16[10,1344,256]{2,1,0:T(8,128)(2,1)S(1)}) custom-call(bf16[21,1344,256]{2,1,0:T(8,128)(2,1)} %bitcast.104, bf16[10,10,128,256]{3,2,1,0:T(8,128)(2,1)S(1)} %copy-done.3, ...), custom_call_target="tpu_custom_call", output_to_operand_aliasing={{1}: (1, {}), {2}: (2, {})} | custom-call | flops 10000000000 | tf_op jit(solution)/shard_map/conv_one_grad/pallas_call | solution.py:839
  101.4 2.7 %copy-done.4 = bf16[10,10,128,256]{3,2,1,0:T(8,128)(2,1)} copy-done((bf16[10,10,128,256]{3,2,1,0:T(8,128)(2,1)}, bf16[10,10,128,256]{3,2,1,0:T(8,128)(2,1)S(1)}, u32[]{:S(2)}) %copy-start.4) | copy-done | bytes 6553624
  105.0 1.5 %collective-permute-start.16 = (bf16[80,640]{1,0:T(8,128)(2,1)S(1)}, bf16[80,640]{1,0:T(8,128)(2,1)S(1)}, u32[]{:S(2)}, u32[]{:S(2)}) collective-permute-start(bf16[80,640]{1,0:T(8,128)(2,1)S(1)} %add_convert_fusion.5), channel_id=1, source_target_pairs={{0,2},{1,3},{2,0},{3,1},{4,6},{5,7},{6,4},{7,5},{8,10},{9,11},{10,... | collective-permute-start | bytes 307208 | tf_op jit(solution)/shard_map/ppermute | solution.py:1020
  106.5 3.5 %collective-permute-start.21 = (bf16[392,128]{1,0:T(8,128)(2,1)S(1)}, bf16[392,128]{1,0:T(8,128)(2,1)S(1)}, u32[]{:S(2)}, u32[]{:S(2)}) collective-permute-start(bf16[392,128]{1,0:T(8,128)(2,1)S(1)} %get-tuple-element.382), channel_id=1, source_target_pairs={{0,24},{4,28},{8,16},{12,20},{16,8},{20,12},{24,0},{28,4},{1,25},{... | collective-permute-start | bytes 301064 | tf_op jit(solution)/shard_map/ppermute | solution.py:1020
  111.0 2.9 %copy-done.5 = bf16[10,10,128,256]{3,2,1,0:T(8,128)(2,1)S(1)} copy-done((bf16[10,10,128,256]{3,2,1,0:T(8,128)(2,1)S(1)}, bf16[10,10,128,256]{3,2,1,0:T(8,128)(2,1)}, u32[]{:S(2)}) %copy-start.5) | copy-done | bytes 6553624
  113.9 2.4 %frames_back.5 = (bf16[21,1344,256]{2,1,0:T(8,128)(2,1)}, bf16[10,10,128,256]{3,2,1,0:T(8,128)(2,1)S(1)}) custom-call(bf16[10,10,128,256]{3,2,1,0:T(8,128)(2,1)S(1)} %copy-done.5, bf16[192,256]{1,0:T(8,128)(2,1)S(1)} %get-tuple-element.292.refs_1_, bf16[21,1344,256]{2,1,0:T(8,128)(2,1)} %get-tuple-element.293.refs_2_), custom_call_target="tpu_custom_call", output_to_operand_aliasing={{1}: (0, {}), {0}: (2, {})} | custom-call | flops 3000000000 | tf_op jit(solution)/shard_map/frames_back/pallas_call | solution.py:85
  116.4 1.6 %collective-permute-start.18 = (bf16[112,640]{1,0:T(8,128)(2,1)S(1)}, bf16[112,640]{1,0:T(8,128)(2,1)S(1)}, u32[]{:S(2)}, u32[]{:S(2)}) collective-permute-start(bf16[112,640]{1,0:T(8,128)(2,1)S(1)} %pad_maximum_fusion.5), channel_id=1, source_target_pairs={{0,4},{4,0},{8,12},{12,8},{16,20},{20,16},{24,28},{28,24},{1,5},{5... | collective-permute-start | bytes 430088 | tf_op jit(solution)/shard_map/ppermute | solution.py:1020
  117.9 2.4 %frames_back.6 = (bf16[21,1344,256]{2,1,0:T(8,128)(2,1)}, bf16[10,10,128,256]{3,2,1,0:T(8,128)(2,1)S(1)}) custom-call(bf16[10,10,128,256]{3,2,1,0:T(8,128)(2,1)S(1)} %get-tuple-element.304.refs_0_, bf16[192,256]{1,0:T(8,128)(2,1)S(1)} %get-tuple-element.292.refs_1_, ...), custom_call_target="tpu_custom_call", output_to_operand_aliasing={{1}: (0, {}), {0}: (2, {})} | custom-call | flops 3000000000 | tf_op jit(solution)/shard_map/frames_back/pallas_call | solution.py:85
  122.9 2.7 %frames_back.7 = (bf16[21,1344,256]{2,1,0:T(8,128)(2,1)}, bf16[10,10,128,256]{3,2,1,0:T(8,128)(2,1)S(1)}) custom-call(bf16[10,10,128,256]{3,2,1,0:T(8,128)(2,1)S(1)} %get-tuple-element.313.refs_0_, bf16[192,256]{1,0:T(8,128)(2,1)S(1)} %get-tuple-element.292.refs_1_, ...), custom_call_target="tpu_custom_call", output_to_operand_aliasing={{1}: (0, {}), {0}: (2, {})} | custom-call | flops 4000000000 | tf_op jit(solution)/shard_map/frames_back/pallas_call | solution.py:85
  129.5 3.1 %steps.2 = (f32[64,576]{1,0:T(8,128)}, f32[64,576]{1,0:T(8,128)}, f32[64,576]{1,0:T(8,128)}, f32[64,576]{1,0:T(8,128)}, f32[19,512]{1,0:T(8,128)}, /*index=5*/f3...) custom-call(bf16[160,640]{1,0:T(8,128)(2,1)S(1)} %pad_maximum_fusion, ...), custom_call_target="tpu_custom_call" | custom-call | flops 5000000000 | tf_op jit(solution)/shard_map/steps/pallas_call | solution.py:980
  (157 shorter events, 15.8 us)
Async XLA Ops:
  1.3 8.4 %copy-start.35 = (f32[691]{0:T(1024)S(1)}, f32[691]{0:T(1024)}, u32[]{:S(2)}) copy-start(f32[691]{0:T(1024)} %param.46) | copy-start | bytes 8296
  1.3 8.4 %copy-start.7 = (f32[256,32]{0,1:T(8,128)S(1)}, f32[256,32]{0,1:T(8,128)}, u32[]{:S(2)}) copy-start(f32[256,32]{0,1:T(8,128)} %param.41) | copy-start | bytes 98308
  4.0 16.0 %copy-start.31 = (f32[1,256]{1,0:T(1,128)}, f32[1,256]{1,0:T(1,128)S(1)}, u32[]{:S(2)}) copy-start(f32[1,256]{1,0:T(1,128)S(1)} %get-tuple-element.197.refs_5_) | copy-start | bytes 3076
  4.0 16.0 %collective-permute-start.2 = (bf16[400,128]{1,0:T(8,128)(2,1)S(1)}, bf16[400,128]{1,0:T(8,128)(2,1)S(1)}, u32[]{:S(2)}, u32[]{:S(2)}) collective-permute-start(bf16[400,128]{1,0:T(8,128)(2,1)S(1)} %get-tuple-element.204), channel_id=1, source_target_pairs={{0,24},{4,28},{8,16},{12,20},{16,8},{20,12},{24,0},{28,4},{1,25},{... | collective-permute-start | bytes 307208 | tf_op jit(solution)/shard_map/ppermute | solution.py:1020
  9.1 10.9 %collective-permute-start.1 = (bf16[400,128]{1,0:T(8,128)(2,1)S(1)}, bf16[400,128]{1,0:T(8,128)(2,1)S(1)}, u32[]{:S(2)}, u32[]{:S(2)}) collective-permute-start(bf16[400,128]{1,0:T(8,128)(2,1)S(1)} %get-tuple-element.204), channel_id=1, source_target_pairs={{0,16},{4,20},{8,24},{12,28},{16,0},{20,4},{24,8},{28,12},{1,17},{... | collective-permute-start | bytes 307208 | tf_op jit(solution)/shard_map/ppermute | solution.py:1020
  9.1 10.9 %collective-permute-start = (bf16[400,128]{1,0:T(8,128)(2,1)S(1)}, bf16[400,128]{1,0:T(8,128)(2,1)S(1)}, u32[]{:S(2)}, u32[]{:S(2)}) collective-permute-start(bf16[400,128]{1,0:T(8,128)(2,1)S(1)} %get-tuple-element.204), channel_id=1, source_target_pairs={{0,8},{4,12},{8,0},{12,4},{16,24},{20,28},{24,16},{28,20},{1,9},{5... | collective-permute-start | bytes 307208 | tf_op jit(solution)/shard_map/ppermute | solution.py:1020
  9.8 24.7 %copy-start.8 = (f32[1,691]{1,0:T(1,128)}, f32[1,691]{1,0:T(1,128)S(1)}, u32[]{:S(2)}) copy-start(f32[1,691]{1,0:T(1,128)S(1)} %reshape.64.bias_ref.refs_3_) | copy-start | bytes 8296
  9.8 13.6 %copy-start.18 = (f32[512,64]{0,1:T(8,128)S(1)}, f32[512,64]{0,1:T(8,128)}, u32[]{:S(2)}) copy-start(f32[512,64]{0,1:T(8,128)} %param.42) | copy-start | bytes 393220
  20.1 10.7 %collective-permute-start.4 = (bf16[4,400,128]{2,1,0:T(8,128)(2,1)S(1)}, bf16[4,400,128]{2,1,0:T(8,128)(2,1)S(1)}, u32[]{:S(2)}, u32[]{:S(2)}) collective-permute-start(bf16[4,400,128]{2,1,0:T(8,128)(2,1)S(1)} %pad_maximum_fusion.1), channel_id=1, source_target_pairs={{0,2},{1,3},{2,0},{3,1},{4,6},{5,7},{6,4},{7,5},{8,10},{9,11},{10,... | collective-permute-start | bytes 1228808 | tf_op jit(solution)/shard_map/ppermute | solution.py:1020
  21.9 10.2 %collective-permute-start.3 = (bf16[4,400,128]{2,1,0:T(8,128)(2,1)S(1)}, bf16[4,400,128]{2,1,0:T(8,128)(2,1)S(1)}, u32[]{:S(2)}, u32[]{:S(2)}) collective-permute-start(bf16[4,400,128]{2,1,0:T(8,128)(2,1)S(1)} %pad_maximum_fusion.1), channel_id=1, source_target_pairs={{0,4},{4,0},{8,12},{12,8},{16,20},{20,16},{24,28},{28,24},{1,5},{5... | collective-permute-start | bytes 1228808 | tf_op jit(solution)/shard_map/ppermute | solution.py:1020
  32.3 7.6 %copy-start.33 = (bf16[12,400,128]{2,1,0:T(8,128)(2,1)}, bf16[12,400,128]{2,1,0:T(8,128)(2,1)S(1)}, u32[]{:S(2)}) copy-start(bf16[12,400,128]{2,1,0:T(8,128)(2,1)S(1)} %pad_maximum_fusion.refs_11_) | copy-start | bytes 3686404
  32.3 9.7 %collective-permute-start.7 = (bf16[12,400,128]{2,1,0:T(8,128)(2,1)S(1)}, bf16[12,400,128]{2,1,0:T(8,128)(2,1)}, u32[]{:S(2)}, u32[]{:S(2)}) collective-permute-start(bf16[12,400,128]{2,1,0:T(8,128)(2,1)S(1)} %pad_maximum_fusion.refs_11_), channel_id=1, source_target_pairs={{0,1},{1,0},{2,3},{3,2},{4,5},{5,4},{6,7},{7,6},{8,9},{9,8},{10,11... | collective-permute-start | bytes 3686408 | tf_op jit(solution)/shard_map/ppermute | solution.py:1020
  32.4 7.5 %collective-permute-start.5 = (bf16[2,400,128]{2,1,0:T(8,128)(2,1)S(1)}, bf16[2,400,128]{2,1,0:T(8,128)(2,1)S(1)}, u32[]{:S(2)}, u32[]{:S(2)}) collective-permute-start(bf16[2,400,128]{2,1,0:T(8,128)(2,1)S(1)} %slice.144), channel_id=1, source_target_pairs={{0,2},{1,3},{2,0},{3,1},{4,6},{5,7},{6,4},{7,5},{8,10},{9,11},{10,... | collective-permute-start | bytes 614408 | tf_op jit(solution)/shard_map/ppermute | solution.py:1020
  32.9 7.1 %collective-permute-start.6 = (bf16[2,400,128]{2,1,0:T(8,128)(2,1)S(1)}, bf16[2,400,128]{2,1,0:T(8,128)(2,1)S(1)}, u32[]{:S(2)}, u32[]{:S(2)}) collective-permute-start(bf16[2,400,128]{2,1,0:T(8,128)(2,1)S(1)} %slice.145), channel_id=1, source_target_pairs={{0,4},{4,0},{8,12},{12,8},{16,20},{20,16},{24,28},{28,24},{1,5},{5... | collective-permute-start | bytes 614408 | tf_op jit(solution)/shard_map/ppermute | solution.py:1020
  40.1 1.8 %collective-permute-start.8 = (bf16[4,400,128]{2,1,0:T(8,128)(2,1)S(1)}, bf16[4,400,128]{2,1,0:T(8,128)(2,1)S(1)}, u32[]{:S(2)}, u32[]{:S(2)}) collective-permute-start(bf16[4,400,128]{2,1,0:T(8,128)(2,1)S(1)} %constant_dynamic-update-slice_fusion.refs_12_), channel_id=1, source_target_pairs={{0,1},{1,0},{2,3},{3,2},{4,5},{5,4},{6,7},{7,6},{8,9},{9,8},{10,11... | collective-permute-start | bytes 1228808 | tf_op jit(solution)/shard_map/ppermute | solution.py:1020
  52.2 8.6 %collective-permute-start.9 = (bf16[2,8,392,128]{3,2,1,0:T(8,128)(2,1)}, bf16[2,8,392,128]{3,2,1,0:T(8,128)(2,1)}, u32[]{:S(2)}, u32[]{:S(2)}) collective-permute-start(bf16[2,8,392,128]{3,2,1,0:T(8,128)(2,1)} %get-tuple-element.239), channel_id=1, source_target_pairs={{0,1},{1,0},{2,3},{3,2},{4,5},{5,4},{6,7},{7,6},{8,9},{9,8},{10,11... | collective-permute-start | bytes 4816904 | tf_op jit(solution)/shard_map/ppermute | solution.py:1020
  52.4 8.4 %copy-start.32 = (bf16[2,8,392,128]{3,2,1,0:T(8,128)(2,1)S(1)}, bf16[2,8,392,128]{3,2,1,0:T(8,128)(2,1)}, u32[]{:S(2)}) copy-start(bf16[2,8,392,128]{3,2,1,0:T(8,128)(2,1)} %get-tuple-element.243) | copy-start | bytes 4816900
  62.8 14.2 %collective-permute-start.10 = (bf16[2,392,128]{2,1,0:T(8,128)(2,1)S(1)}, bf16[2,392,128]{2,1,0:T(8,128)(2,1)S(1)}, u32[]{:S(2)}, u32[]{:S(2)}) collective-permute-start(bf16[2,392,128]{2,1,0:T(8,128)(2,1)S(1)} %get-tuple-element.252), channel_id=1, source_target_pairs={{0,4},{4,0},{8,12},{12,8},{16,20},{20,16},{24,28},{28,24},{1,5},{5... | collective-permute-start | bytes 602120 | tf_op jit(solution)/shard_map/ppermute | solution.py:1020
  64.3 12.6 %collective-permute-start.11 = (bf16[2,392,128]{2,1,0:T(8,128)(2,1)S(1)}, bf16[2,392,128]{2,1,0:T(8,128)(2,1)S(1)}, u32[]{:S(2)}, u32[]{:S(2)}) collective-permute-start(bf16[2,392,128]{2,1,0:T(8,128)(2,1)S(1)} %get-tuple-element.253), channel_id=1, source_target_pairs={{0,2},{1,3},{2,0},{3,1},{4,6},{5,7},{6,4},{7,5},{8,10},{9,11},{10,... | collective-permute-start | bytes 602120 | tf_op jit(solution)/shard_map/ppermute | solution.py:1020
  77.2 9.6 %collective-permute-start.12 = (bf16[80,640]{1,0:T(8,128)(2,1)S(1)}, bf16[80,640]{1,0:T(8,128)(2,1)S(1)}, u32[]{:S(2)}, u32[]{:S(2)}) collective-permute-start(bf16[80,640]{1,0:T(8,128)(2,1)S(1)} %get-tuple-element.264), channel_id=1, source_target_pairs={{0,1},{1,0},{2,3},{3,2},{4,5},{5,4},{6,7},{7,6},{8,9},{9,8},{10,11... | collective-permute-start | bytes 307208 | tf_op jit(solution)/shard_map/ppermute | solution.py:1020
  77.3 26.7 %collective-permute-start.13 = (bf16[4,392,128]{2,1,0:T(8,128)(2,1)S(1)}, bf16[4,392,128]{2,1,0:T(8,128)(2,1)S(1)}, u32[]{:S(2)}, u32[]{:S(2)}) collective-permute-start(bf16[4,392,128]{2,1,0:T(8,128)(2,1)S(1)} %get-tuple-element.279), channel_id=1, source_target_pairs={{0,4},{4,0},{8,12},{12,8},{16,20},{20,16},{24,28},{28,24},{1,5},{5... | collective-permute-start | bytes 1204232 | tf_op jit(solution)/shard_map/ppermute | solution.py:1020
  77.9 26.1 %collective-permute-start.14 = (bf16[4,392,128]{2,1,0:T(8,128)(2,1)S(1)}, bf16[4,392,128]{2,1,0:T(8,128)(2,1)S(1)}, u32[]{:S(2)}, u32[]{:S(2)}) collective-permute-start(bf16[4,392,128]{2,1,0:T(8,128)(2,1)S(1)} %get-tuple-element.280), channel_id=1, source_target_pairs={{0,2},{1,3},{2,0},{3,1},{4,6},{5,7},{6,4},{7,5},{8,10},{9,11},{10,... | collective-permute-start | bytes 1204232 | tf_op jit(solution)/shard_map/ppermute | solution.py:1020
  86.8 17.2 %collective-permute-start.15 = (bf16[80,640]{1,0:T(8,128)(2,1)S(1)}, bf16[80,640]{1,0:T(8,128)(2,1)S(1)}, u32[]{:S(2)}, u32[]{:S(2)}) collective-permute-start(bf16[80,640]{1,0:T(8,128)(2,1)S(1)} %add_convert_fusion.6), channel_id=1, source_target_pairs={{0,16},{4,20},{8,24},{12,28},{16,0},{20,4},{24,8},{28,12},{1,17},{... | collective-permute-start | bytes 307208 | tf_op jit(solution)/shard_map/ppermute | solution.py:1020
  104.3 12.0 %collective-permute-start.17 = (f32[16,640]{1,0:T(8,128)S(1)}, f32[16,640]{1,0:T(8,128)S(1)}, u32[]{:S(2)}, u32[]{:S(2)}) collective-permute-start(f32[16,640]{1,0:T(8,128)S(1)} %get-tuple-element.302), channel_id=1, source_target_pairs={{0,16},{4,20},{8,24},{12,28},{16,0},{20,4},{24,8},{28,12},{1,17},{... | collective-permute-start | bytes 122888 | tf_op jit(solution)/shard_map/ppermute | solution.py:1020
  105.0 11.3 %collective-permute-start.16 = (bf16[80,640]{1,0:T(8,128)(2,1)S(1)}, bf16[80,640]{1,0:T(8,128)(2,1)S(1)}, u32[]{:S(2)}, u32[]{:S(2)}) collective-permute-start(bf16[80,640]{1,0:T(8,128)(2,1)S(1)} %add_convert_fusion.5), channel_id=1, source_target_pairs={{0,2},{1,3},{2,0},{3,1},{4,6},{5,7},{6,4},{7,5},{8,10},{9,11},{10,... | collective-permute-start | bytes 307208 | tf_op jit(solution)/shard_map/ppermute | solution.py:1020
  106.5 19.0 %collective-permute-start.21 = (bf16[392,128]{1,0:T(8,128)(2,1)S(1)}, bf16[392,128]{1,0:T(8,128)(2,1)S(1)}, u32[]{:S(2)}, u32[]{:S(2)}) collective-permute-start(bf16[392,128]{1,0:T(8,128)(2,1)S(1)} %get-tuple-element.382), channel_id=1, source_target_pairs={{0,24},{4,28},{8,16},{12,20},{16,8},{20,12},{24,0},{28,4},{1,25},{... | collective-permute-start | bytes 301064 | tf_op jit(solution)/shard_map/ppermute | solution.py:1020
  110.1 15.5 %collective-permute-start.20 = (bf16[392,128]{1,0:T(8,128)(2,1)S(1)}, bf16[392,128]{1,0:T(8,128)(2,1)S(1)}, u32[]{:S(2)}, u32[]{:S(2)}) collective-permute-start(bf16[392,128]{1,0:T(8,128)(2,1)S(1)} %get-tuple-element.383), channel_id=1, source_target_pairs={{0,16},{4,20},{8,24},{12,28},{16,0},{20,4},{24,8},{28,12},{1,17},{... | collective-permute-start | bytes 301064 | tf_op jit(solution)/shard_map/ppermute | solution.py:1020
  110.1 15.5 %collective-permute-start.19 = (bf16[392,128]{1,0:T(8,128)(2,1)S(1)}, bf16[392,128]{1,0:T(8,128)(2,1)S(1)}, u32[]{:S(2)}, u32[]{:S(2)}) collective-permute-start(bf16[392,128]{1,0:T(8,128)(2,1)S(1)} %get-tuple-element.384), channel_id=1, source_target_pairs={{0,8},{4,12},{8,0},{12,4},{16,24},{20,28},{24,16},{28,20},{1,9},{5... | collective-permute-start | bytes 301064 | tf_op jit(solution)/shard_map/ppermute | solution.py:1020
  116.4 5.2 %collective-permute-start.18 = (bf16[112,640]{1,0:T(8,128)(2,1)S(1)}, bf16[112,640]{1,0:T(8,128)(2,1)S(1)}, u32[]{:S(2)}, u32[]{:S(2)}) collective-permute-start(bf16[112,640]{1,0:T(8,128)(2,1)S(1)} %pad_maximum_fusion.5), channel_id=1, source_target_pairs={{0,4},{4,0},{8,12},{12,8},{16,20},{20,16},{24,28},{28,24},{1,5},{5... | collective-permute-start | bytes 430088 | tf_op jit(solution)/shard_map/ppermute | solution.py:1020
  121.7 5.2 %collective-permute-start.22 = (bf16[112,640]{1,0:T(8,128)(2,1)S(1)}, bf16[112,640]{1,0:T(8,128)(2,1)S(1)}, u32[]{:S(2)}, u32[]{:S(2)}) collective-permute-start(bf16[112,640]{1,0:T(8,128)(2,1)S(1)} %pad_maximum_fusion.6), channel_id=1, source_target_pairs={{0,8},{4,12},{8,0},{12,4},{16,24},{20,28},{24,16},{28,20},{1,9},{5... | collective-permute-start | bytes 430088 | tf_op jit(solution)/shard_map/ppermute | solution.py:1020
  127.1 1.5 %collective-permute-start.23 = (bf16[112,640]{1,0:T(8,128)(2,1)S(1)}, bf16[112,640]{1,0:T(8,128)(2,1)S(1)}, u32[]{:S(2)}, u32[]{:S(2)}) collective-permute-start(bf16[112,640]{1,0:T(8,128)(2,1)S(1)} %pad_maximum_fusion.7), channel_id=1, source_target_pairs={{0,1},{1,0},{2,3},{3,2},{4,5},{5,4},{6,7},{7,6},{8,9},{9,8},{10,11... | collective-permute-start | bytes 430088 | tf_op jit(solution)/shard_map/ppermute | solution.py:1020
  128.7 4.1 %collective-permute-start.24 = (f32[16,640]{1,0:T(8,128)S(1)}, f32[16,640]{1,0:T(8,128)S(1)}, u32[]{:S(2)}, u32[]{:S(2)}) collective-permute-start(f32[16,640]{1,0:T(8,128)S(1)} %fusion.2), channel_id=1, source_target_pairs={{0,2},{1,3},{2,0},{3,1},{4,6},{5,7},{6,4},{7,5},{8,10},{9,11},{10,... | collective-permute-start | bytes 122888 | tf_op jit(solution)/shard_map/ppermute | solution.py:1020
  (33 other events, 102.3 us)
